TPU v7x, 256 devices: a whole 4x4x8 slice. The times are simulated.
256 devices in a mesh: ctx: 16 (over z, x_lo), tp: 16 (over x_hi, y, core).
Axes of the slice: x: 4 (x_hi: 2, x_lo: 2; x = x_hi * 2 + x_lo), y: 4, z: 8, core: 2. Of those that a mesh axis runs over, the one named last changes fastest.
Arguments:
- residual: bfloat16 [2048, 8192], P('ctx', 'tp'), may hold values from -17 to 17
- features: bfloat16 [2048, 3, 8192], P('ctx', None, 'tp'), may hold values from -5 to 5
- filters: float32 [2048, 8192], P('ctx', 'tp'), may hold values from -1.5 to 1.5
- skip_gain: float32 [8192], P('tp'), may hold values from 0.3 to 1.5
- w_out: bfloat16 [8192, 8192], P(None, 'tp'), may hold values from -0.0625 to 0.0625
- norm_gain: float32 [8192], P('tp'), may hold values from 0.25 to 1.75
- w_gate: bfloat16 [8192, 21888], P('tp', 'ctx'), may hold values from -0.0625 to 0.0625
- w_up: bfloat16 [8192, 21888], P('tp', 'ctx'), may hold values from -0.0625 to 0.0625
Outputs:
- stream: bfloat16 [2048, 8192], P('ctx', 'tp')
- hidden: bfloat16 [2048, 21888], P('tp', 'ctx')
All inputs are finite; a program needn't handle non-finite values.
Results may differ from a plain program's by a relative error of at most 0.034.
Values may be sent and summed in bfloat16 or wider, within the bound.
No kernel may reach another device: no remote copies, remote signals or barrier semaphores. Data moves between devices by JAX's collectives and lax.ppermute only.
A program may use at most 128 MiB of HBM per device.

v0:
```python
import math

import jax
import jax.numpy as jnp
import numpy as np
from jax import lax
from jax.experimental import pallas as pl
from jax.experimental.pallas import tpu as pltpu
from jax.sharding import PartitionSpec as P

F32 = jnp.float32
BF16 = jnp.bfloat16
AXES = ("ctx", "tp")
N_CTX = 16
N_TP = 16
ROWS = 128
CH = 512
SUB = 32
FF_LOC = 1368
FF_PAD = 1376
EPS = 1e-06
PLANE_GROUPS = [[xh * 8 + y * 2 + k for xh in range(2) for y in range(4)] for k in range(2)]


def split_index(i):
    c, t = divmod(i, N_TP)
    z, x_lo = divmod(c, 2)
    x_hi, r = divmod(t, 8)
    y, k = divmod(r, 2)
    return z, x_hi * 2 + x_lo, y, k


def join_index(z, x, y, k):
    x = x % 4
    return ((z % 8) * 2 + x % 2) * N_TP + (x // 2) * 8 + (y % 4) * 2 + k % 2


def shift(arr, z=0, x=0, y=0, k=0):
    pairs = []
    for i in range(N_CTX * N_TP):
        az, ax, ay, ak = split_index(i)
        pairs.append((i, join_index(az + z, ax + x, ay + y, ak + k)))
    return lax.ppermute(arr, AXES, pairs)


def split_bf16(table):
    high = np.asarray(table, np.float32).astype(jnp.bfloat16)
    low = (np.asarray(table, np.float32) - high.astype(np.float32)).astype(jnp.bfloat16)
    return high, low


def dft_tables():
    size = 2 * ROWS
    pos = np.arange(ROWS)
    freq = np.arange(ROWS)
    phase = (pos[:, None] * freq[None, :]) % size
    angle = 2.0 * math.pi / size * phase
    cos, sin = np.cos(angle), np.sin(angle)
    sign = np.where(pos % 2 == 0, 1.0, -1.0)
    fwd_im = -sin
    fwd_im[:, 0] = sign
    forward = np.concatenate([cos, fwd_im], axis=1)
    weight = np.where(freq == 0, 1.0, 2.0)[:, None] / size
    inv_re = cos.T * weight
    inv_im = -sin.T * weight
    inv_im[0, :] = sign / size
    inverse = np.concatenate([inv_re, inv_im], axis=0)
    return split_bf16(forward) + split_bf16(inverse)


def dot(a, b):
    return jnp.dot(a, b, preferred_element_type=F32)


def dot_nt(a, b):
    return lax.dot_general(a, b, (((1,), (1,)), ((), ())), preferred_element_type=F32)


def prep_kernel(feat_ref, filt_ref, out_ref):
    prod = feat_ref[1].astype(F32) * feat_ref[2].astype(F32)
    filt = filt_ref[...]
    for j in range(CH // 128):
        cols = slice(128 * j, 128 * j + 128)
        out_ref[4 * j : 4 * j + 4, 0:SUB, :] = prod[:, cols].T.astype(BF16).reshape(4, SUB, 128)
        out_ref[4 * j : 4 * j + 4, SUB : 2 * SUB, :] = (
            filt[:, cols].T.astype(BF16).reshape(4, SUB, 128)
        )


def conv_kernel(x_ref, fh_ref, fl_ref, gh_ref, gl_ref, out_ref, spec, filt, outs):
    x = x_ref[...].reshape(N_CTX * 2 * SUB, ROWS)
    spec[...] = (dot(x, fh_ref[...]) + dot(x, fl_ref[...])).reshape(N_CTX, 2 * SUB, 256)
    lane = lax.broadcasted_iota(jnp.int32, (SUB, 128), 1)
    sign = jnp.where(lane % 2 == 0, 1.0, -1.0).astype(F32)
    first = lane == 0
    for d in range(N_CTX):
        re = spec[d, SUB:, 0:128]
        im = spec[d, SUB:, 128:256]
        if d > 0:
            re = re + sign * spec[d - 1, SUB:, 0:128]
            im = im + sign * spec[d - 1, SUB:, 128:256]
        filt[d, 0] = re
        filt[d, 1] = jnp.where(first, 0.0, im)
        filt[d, 2] = jnp.where(first, im, re)
    for m in range(N_CTX):
        acc_re = jnp.zeros((SUB, 128), F32)
        acc_im = jnp.zeros((SUB, 128), F32)
        for n in range(m + 1):
            pr = spec[n, 0:SUB, 0:128]
            pi = spec[n, 0:SUB, 128:256]
            hr, hz, hq = filt[m - n, 0], filt[m - n, 1], filt[m - n, 2]
            acc_re = acc_re + (pr * hr - pi * hz)
            acc_im = acc_im + (pr * hz + pi * hq)
        outs[m, :, 0:128] = acc_re
        outs[m, :, 128:256] = acc_im
    total = outs[...].reshape(N_CTX * SUB, 256)
    high = total.astype(BF16)
    low = (total - high.astype(F32)).astype(BF16)
    y = dot(high, gh_ref[...]) + dot(high, gl_ref[...]) + dot(low, gh_ref[...])
    out_ref[...] = y.astype(BF16).reshape(N_CTX, SUB, ROWS)


def mix_kernel(conv_ref, feat_ref, skip_ref, out_ref):
    conv = conv_ref[...].reshape(CH, ROWS).astype(F32)
    for j in range(CH // 128):
        cols = slice(128 * j, 128 * j + 128)
        prod = feat_ref[1, :, cols].astype(F32) * feat_ref[2, :, cols].astype(F32)
        long = conv[cols, :].T
        gate = feat_ref[0, :, cols].astype(F32)
        out_ref[:, cols] = (gate * (long + skip_ref[:, cols] * prod)).astype(BF16)


def out_proj_kernel(mixed_ref, w_ref, res_ref, out_ref, acc):
    t = pl.program_id(0)

    @pl.when(t == 0)
    def _():
        acc[...] = res_ref[...].astype(F32)

    acc[...] += dot(mixed_ref[0], w_ref[...])

    @pl.when(t == pl.num_programs(0) - 1)
    def _():
        out_ref[...] = acc[...].astype(BF16)


def mlp_kernel(own_ref, oth_ref, gain_ref, wo_ref, wx_ref, out_ref, so, sx, aux):
    part = pl.program_id(1)

    @pl.when(part == 0)
    def _():
        own = own_ref[0].astype(F32)
        oth = oth_ref[0].astype(F32)
        so[...] = (own * gain_ref[0:1, :]).astype(BF16)
        sx[...] = (oth * gain_ref[1:2, :]).astype(BF16)
        ones = jnp.ones((8, CH), BF16)
        sq = own * own
        hi = sq.astype(BF16)
        total = dot_nt(ones, hi) + dot_nt(ones, (sq - hi.astype(F32)).astype(BF16))
        sq = oth * oth
        hi = sq.astype(BF16)
        total += dot_nt(ones, hi) + dot_nt(ones, (sq - hi.astype(F32)).astype(BF16))
        hi = total.astype(BF16).astype(F32)
        row = lax.broadcasted_iota(jnp.int32, (8, ROWS), 0)
        aux[...] = jnp.where(row == 0, hi, jnp.where(row == 1, total - hi, 0.0))

    res = dot_nt(wo_ref[0], so[...]) + dot_nt(wx_ref[0], sx[...])
    tail = jnp.where(part == 0, aux[...], jnp.zeros_like(aux))
    res = jnp.concatenate([res[:FF_LOC], res[FF_LOC:] + tail], axis=0)
    out_ref[0] = res.astype(BF16)


def finish_kernel(part_ref, out_ref):
    gate = part_ref[0:FF_PAD].astype(F32)
    up = part_ref[FF_PAD:].astype(F32)
    sums = gate[FF_LOC : FF_LOC + 1] + gate[FF_LOC + 1 : FF_LOC + 2]
    scale = lax.rsqrt(sums * (1.0 / (N_TP * CH)) + EPS)
    g = gate[:FF_LOC] * scale
    u = up[:FF_LOC] * scale
    out_ref[...] = (g / (1.0 + jnp.exp(-g)) * u).astype(BF16)


def params(mib):
    return pltpu.CompilerParams(vmem_limit_bytes=mib * 1024 * 1024)


def whole(shape):
    zeros = (0,) * len(shape)
    return pl.BlockSpec(shape, lambda *_: zeros)


def shards(residual, features, filters, skip_gain, w_out, norm_gain, w_gate, w_up):
    core = lax.axis_index("tp") % 2
    x_lo = lax.axis_index("ctx") % 2
    feat = features.transpose(1, 0, 2)

    pad = jnp.zeros((FF_PAD - FF_LOC, CH), BF16)
    w_own = jnp.concatenate([w_gate.T, pad, w_up.T, pad], axis=0)

    sent = pl.pallas_call(
        prep_kernel,
        out_shape=jax.ShapeDtypeStruct((N_CTX, 2 * SUB, ROWS), BF16),
        name="prep",
    )(feat, filters)
    recv = lax.all_to_all(sent, "ctx", 0, 0, tiled=True)
    w_oth = shift(w_own, k=1)
    tables = [jnp.asarray(t) for t in dft_tables()]
    conv = pl.pallas_call(
        conv_kernel,
        out_shape=jax.ShapeDtypeStruct((N_CTX, SUB, ROWS), BF16),
        scratch_shapes=[
            pltpu.VMEM((N_CTX, 2 * SUB, 256), F32),
            pltpu.VMEM((N_CTX, 3, SUB, 128), F32),
            pltpu.VMEM((N_CTX, SUB, 256), F32),
        ],
        compiler_params=params(32),
        name="conv",
    )(recv, *tables)
    conv_rows = lax.all_to_all(conv, "ctx", 0, 0, tiled=True)
    mixed = pl.pallas_call(
        mix_kernel,
        out_shape=jax.ShapeDtypeStruct((ROWS, CH), BF16),
        name="mix",
    )(conv_rows, feat, skip_gain[None, :])

    mixed_all = lax.all_gather(mixed, "tp")
    stream = pl.pallas_call(
        out_proj_kernel,
        out_shape=jax.ShapeDtypeStruct((ROWS, CH), BF16),
        grid=(N_TP,),
        in_specs=[
            pl.BlockSpec((1, ROWS, CH), lambda t: (t, 0, 0)),
            pl.BlockSpec((CH, CH), lambda t: (t, 0)),
            whole((ROWS, CH)),
        ],
        out_specs=whole((ROWS, CH)),
        scratch_shapes=[pltpu.VMEM((ROWS, CH), F32)],
        compiler_params=params(32),
        name="out_proj",
    )(mixed_all, w_out, residual)

    gain_oth = shift(norm_gain[None, :], k=1)
    gains = jnp.concatenate([norm_gain[None, :], gain_oth], axis=0)
    stream_oth = shift(stream, k=1)
    both = jnp.stack([stream, stream_oth])
    across = shift(both, x=0) if False else lax.ppermute(
        both,
        AXES,
        [
            (i, join_index(z, x ^ 1, y, k))
            for i in range(N_CTX * N_TP)
            for z, x, y, k in [split_index(i)]
        ],
    )
    held = jnp.where(x_lo == core, both, across)
    z_groups = [[z * 2 + xl for z in range(8)] for xl in range(2)]
    gathered = lax.all_gather(held, "ctx", axis_index_groups=z_groups)

    partial = pl.pallas_call(
        mlp_kernel,
        out_shape=jax.ShapeDtypeStruct((8, 2 * FF_PAD, ROWS), BF16),
        grid=(8, 2),
        in_specs=[
            pl.BlockSpec((None, 1, ROWS, CH), lambda b, p: (b, 0, 0, 0)),
            pl.BlockSpec((None, 1, ROWS, CH), lambda b, p: (b, 1, 0, 0)),
            whole((2, CH)),
            pl.BlockSpec((1, FF_PAD, CH), lambda b, p: (p, 0, 0)),
            pl.BlockSpec((1, FF_PAD, CH), lambda b, p: (p, 0, 0)),
        ],
        out_specs=pl.BlockSpec((1, FF_PAD, ROWS), lambda b, p: (b, p, 0)),
        scratch_shapes=[
            pltpu.VMEM((ROWS, CH), BF16),
            pltpu.VMEM((ROWS, CH), BF16),
            pltpu.VMEM((8, ROWS), F32),
        ],
        compiler_params=params(48),
        name="mlp",
    )(
        gathered,
        gathered,
        gains,
        w_own.reshape(2, FF_PAD, CH),
        w_oth.reshape(2, FF_PAD, CH),
    )
    reduced = lax.psum_scatter(
        partial, "tp", scatter_dimension=0, axis_index_groups=PLANE_GROUPS, tiled=True
    )[0]
    hidden_t = pl.pallas_call(
        finish_kernel,
        out_shape=jax.ShapeDtypeStruct((FF_LOC, ROWS), BF16),
        compiler_params=params(32),
        name="finish",
    )(reduced)
    return stream, hidden_t.T


def solution(mesh):
    placed = (
        P("ctx", "tp"),
        P("ctx", None, "tp"),
        P("ctx", "tp"),
        P("tp"),
        P(None, "tp"),
        P("tp"),
        P("tp", "ctx"),
        P("tp", "ctx"),
    )
    return jax.shard_map(
        shards,
        mesh=mesh,
        in_specs=placed,
        out_specs=(P("ctx", "tp"), P("tp", "ctx")),
        check_vma=False,
    )
```

profile of v0, /device:TPU:24, one launch (start us, length us, event | category | flops | bytes accessed | tf_op | source)
XLA Modules:
  0.0 291.9 jit_solution(9235535882955755607)
XLA Ops:
  7.2 0.0 copy-start.4
  7.2 0.0 all-gather.5.cloned.1.call-start
  7.2 1.9 prep.1
  9.2 21.5 %all_to_all.10.x_ref = bf16[16,64,128]{2,1,0:T(8,128)(2,1)S(1)} all-to-all(bf16[16,64,128]{2,1,0:T(8,128)(2,1)} %prep.1), channel_id=1, replica_groups=mesh['ctx'=16,'tp'=16] {'ctx'}, dimensions={0} | all-to-all | bytes 524288 | tf_op jit(solution)/shard_map/all_to_all | solution.py:205
  30.7 0.0 copy-start.5
  30.7 0.8 copy-done.5
  31.5 0.0 copy-start.6
  31.5 0.8 copy-done.6
  32.4 0.0 copy-start.7
  32.4 0.8 copy-done.7
  33.2 0.0 copy-start.8
  33.2 0.8 copy-done.8
  34.1 1.4 conv.1
  35.5 12.9 %all_to_all.11.conv_ref = bf16[16,32,128]{2,1,0:T(8,128)(2,1)} all-to-all(bf16[16,32,128]{2,1,0:T(8,128)(2,1)S(1)} %conv.1), channel_id=1, replica_groups=mesh['ctx'=16,'tp'=16] {'ctx'}, dimensions={0} | all-to-all | bytes 262144 | tf_op jit(solution)/shard_map/all_to_all | solution.py:219
  48.5 1.8 mix.1
  50.2 0.0 all-gather.5.cloned.1.call-update
  50.3 0.0 all-gather.7.cloned.1.call-start
  50.3 48.3 %all-gather.5.cloned.1.call-done = bf16[2048,512]{1,0:T(8,128)(2,1)} async-done(((bf16[128,512]{1,0:T(8,128)(2,1)}), bf16[2048,512]{1,0:T(8,128)(2,1)}) %all-gather.5.cloned.1.call-update) | async-done | bytes 2097168 | tf_op jit(solution)/shard_map/all_gather | solution.py:226
  98.6 0.0 copy-done.4
  98.6 0.0 copy-start
  98.6 3.4 %copy-done = bf16[8192,512]{1,0:T(8,128)(2,1)S(1)} copy-done((bf16[8192,512]{1,0:T(8,128)(2,1)S(1)}, bf16[8192,512]{1,0:T(8,128)(2,1)}, u32[]{:S(2)}) %copy-start) | copy-done | bytes 8388632
  102.0 0.0 copy-start.2
  102.0 1.6 copy-done.2
  103.6 4.6 %out_proj.1 = bf16[128,512]{1,0:T(8,128)(2,1)} custom-call(bf16[16,128,512]{2,1,0:T(8,128)(2,1)S(1)} %bitcast.16, bf16[8192,512]{1,0:T(8,128)(2,1)S(1)} %copy-done, bf16[128,512]{1,0:T(8,128)(2,1)S(1)} %copy-done.4), custom_call_target="tpu_custom_call" | custom-call | tf_op jit(solution)/shard_map/out_proj/pallas_call | solution.py:227
  108.2 0.3 collective-permute-start
  108.4 1.3 collective-permute-done
  109.7 0.9 pad_maximum_fusion.1
  110.7 0.7 collective-permute-start.1
  111.3 7.9 %collective-permute-done.1 = bf16[2,128,512]{2,1,0:T(8,128)(2,1)S(1)} collective-permute-done((bf16[2,128,512]{2,1,0:T(8,128)(2,1)S(1)}, bf16[2,128,512]{2,1,0:T(8,128)(2,1)S(1)}, u32[]{:S(2)}, u32[]{:S(2)}) %collective-permute-start.1) | collective-permute-done | bytes 262176 | tf_op jit(solution)/shard_map/ppermute | solution.py:246
  119.2 1.6 broadcast_select_fusion
  120.9 0.0 all-gather.7.cloned.1.call-update
  120.9 0.0 reduce-scatter.2.cloned.1.call-start
  120.9 0.0 copy-start.9
  121.0 1.9 pad_maximum_fusion
  122.9 0.1 collective-permute-start.3
  123.0 0.0 copy-done.9
  123.0 0.5 collective-permute-start.2
  123.5 4.3 %collective-permute-done.2 = f32[1,512]{1,0:T(1,128)S(1)} collective-permute-done((f32[1,512]{1,0:T(1,128)S(1)}, f32[1,512]{1,0:T(1,128)S(1)}, u32[]{:S(2)}, u32[]{:S(2)}) %collective-permute-start.2) | collective-permute-done | bytes 2080 | tf_op jit(solution)/shard_map/ppermute | solution.py:43
  127.8 0.5 collective-permute-done.3
  128.3 33.1 %all-gather.7.cloned.1.call-done = bf16[16,128,512]{2,1,0:T(8,128)(2,1)} async-done(((bf16[2,128,512]{2,1,0:T(8,128)(2,1)}), bf16[16,128,512]{2,1,0:T(8,128)(2,1)}) %all-gather.7.cloned.1.call-update) | async-done | bytes 2097168 | tf_op jit(solution)/shard_map/all_gather | solution.py:257
  161.4 0.0 copy-start.1
  161.4 1.6 copy-done.1
  163.0 23.1 %mlp.1 = bf16[8,2752,128]{2,1,0:T(8,128)(2,1)} custom-call(bf16[8,2,128,512]{3,2,1,0:T(8,128)(2,1)S(1)} %bitcast.14, bf16[8,2,128,512]{3,2,1,0:T(8,128)(2,1)S(1)} %bitcast.15, f32[2,512]{1,0:T(2,128)S(1)} %pad_maximum_fusion.2.gain_ref, bf16[2,1376,512]{2,1,0:T(8,128)(2,1)S(1)} %bitcast.13, bf16[2,1376,512]{2,1,0:T(8,128)(2,1)} %bitcast.10.wx_ref), custom_call_target="tpu_custom_call" | custom-call | tf_op jit(solution)/shard_map/mlp/pallas_call | solution.py:259
  186.0 0.0 reduce-scatter.2.cloned.1.call-update
  186.1 97.2 %reduce-scatter.2.cloned.1.call-done = bf16[1,2752,128]{2,1,0:T(8,128)(2,1)} async-done(((bf16[8,2752,128]{2,1,0:T(8,128)(2,1)}), bf16[1,2752,128]{2,1,0:T(8,128)(2,1)}) %reduce-scatter.2.cloned.1.call-update) | async-done | bytes 704528 | tf_op jit(solution)/shard_map/reduce_scatter | solution.py:285
  283.3 0.0 copy-start.3
  283.3 1.1 copy-done.3
  284.4 1.0 finish.1
  (2 shorter events, 0.0 us)
Async XLA Ops:
  7.2 91.5 %copy-start.4 = (bf16[128,512]{1,0:T(8,128)(2,1)S(1)}, bf16[128,512]{1,0:T(8,128)(2,1)}, u32[]{:S(2)}) copy-start(bf16[128,512]{1,0:T(8,128)(2,1)} %res_ref.1) | copy-start | bytes 393220
  7.2 91.4 %all-gather.5.cloned.1.call-start = ((), (), s32[]{:S(2)}) async-start(), calls=%async_computation.4 | async-start | bytes 2228224 | tf_op jit(solution)/shard_map/all_gather | solution.py:226
  30.7 0.8 copy-start.5
  31.5 0.8 copy-start.6
  32.4 0.8 copy-start.7
  33.2 0.8 copy-start.8
  50.3 111.1 %all-gather.7.cloned.1.call-start = ((), (), s32[]{:S(2)}) async-start(), calls=%async_computation.5 | async-start | bytes 2359296 | tf_op jit(solution)/shard_map/all_gather | solution.py:257
  98.6 3.4 %copy-start = (bf16[8192,512]{1,0:T(8,128)(2,1)S(1)}, bf16[8192,512]{1,0:T(8,128)(2,1)}, u32[]{:S(2)}) copy-start(bf16[8192,512]{1,0:T(8,128)(2,1)} %w_ref.1) | copy-start | bytes 25165828
  102.0 1.6 copy-start.2
  108.2 1.6 collective-permute-start
  110.7 8.6 %collective-permute-start.1 = (bf16[2,128,512]{2,1,0:T(8,128)(2,1)S(1)}, bf16[2,128,512]{2,1,0:T(8,128)(2,1)S(1)}, u32[]{:S(2)}, u32[]{:S(2)}) collective-permute-start(bf16[2,128,512]{2,1,0:T(8,128)(2,1)S(1)} %pad_maximum_fusion.1), channel_id=1, source_target_pairs={{0,16},{1,17},{2,18},{3,19},{4,20},{5,21},{6,22},{7,23},{8,24},{9,... | collective-permute-start | bytes 786440 | tf_op jit(solution)/shard_map/ppermute | solution.py:246
  120.9 162.4 %reduce-scatter.2.cloned.1.call-start = ((), (), s32[]{:S(2)}) async-start(), calls=%async_computation.3 | async-start | bytes 6340608 | tf_op jit(solution)/shard_map/reduce_scatter | solution.py:285
  120.9 2.0 copy-start.9
  122.9 5.4 %collective-permute-start.3 = (bf16[2752,512]{1,0:T(8,128)(2,1)S(1)}, bf16[2752,512]{1,0:T(8,128)(2,1)}, u32[]{:S(2)}, u32[]{:S(2)}) collective-permute-start(bf16[2752,512]{1,0:T(8,128)(2,1)S(1)} %pad_maximum_fusion), channel_id=1, source_target_pairs={{0,1},{1,0},{2,3},{3,2},{4,5},{5,4},{6,7},{7,6},{8,9},{9,8},{10,11... | collective-permute-start | bytes 8454152 | tf_op jit(solution)/shard_map/ppermute | solution.py:43
  123.0 4.8 %collective-permute-start.2 = (f32[1,512]{1,0:T(1,128)S(1)}, f32[1,512]{1,0:T(1,128)S(1)}, u32[]{:S(2)}, u32[]{:S(2)}) collective-permute-start(f32[1,512]{1,0:T(1,128)S(1)} %bitcast.28), channel_id=1, source_target_pairs={{0,1},{1,0},{2,3},{3,2},{4,5},{5,4},{6,7},{7,6},{8,9},{9,8},{10,11... | collective-permute-start | bytes 6152 | tf_op jit(solution)/shard_map/ppermute | solution.py:43
  161.4 1.6 copy-start.1
  283.3 1.1 copy-start.3
Sparse Core Ops, SparseCore 0:
  50.4 48.1 all-gather.4
  121.0 40.3 all-gather.6
  186.2 97.0 reduce-scatter.1
where the time goes:
time: 294 us; the launch traced here: 292 us
  waiting for transfers between devices  193 us (66%)
  blocking collectives  34.5 us (12%)
  Pallas kernels  33.9 us (12%)
  between operations  13.8 us (5%)
  local copies, waits for them, and re-layouts  11 us (4%)
  other arithmetic  4.46 us (2%)
    reduce_scatter x1, waiting for transfers between devices, shards(): lax.psum_scatter(partial, 'tp', scatter_dimension=0, axis_index_groups=PL...  97.2 us
    all_gather x1, waiting for transfers between devices, shards(): mixed_all = lax.all_gather(mixed, 'tp')  48.3 us
    all_gather x1, waiting for transfers between devices, shards(): gathered = lax.all_gather(held, 'ctx', axis_index_groups=z_groups)  33.1 us
    pallas_call x1, Pallas kernels, shards(): pl.pallas_call(mlp_kernel, out_shape=jax.ShapeDtypeStruct((8, 2 * FF_PAD,...  23.1 us
    all_to_all x1, blocking collectives, shards(): recv = lax.all_to_all(sent, 'ctx', 0, 0, tiled=True)  21.5 us
    all_to_all x1, blocking collectives, shards(): conv_rows = lax.all_to_all(conv, 'ctx', 0, 0, tiled=True)  12.9 us
    unnamed x20, local copies, waits for them, and re-layouts  11 us
    ppermute x1, waiting for transfers between devices, shards(): lax.ppermute(both, AXES, [(i, join_index(z, x ^ 1, y, k)) for i in range(...  7.9 us
  transfers between devices with their start and end apart: 7, of which 7 were waited for; matrix products, arithmetic and copies ran while one was open for 1% of the time, Pallas kernels for 0%

commit v1 on v0

v1 whole, which is shorter than its diff:
```python
import math

import jax
import jax.numpy as jnp
import numpy as np
from jax import lax
from jax.experimental import pallas as pl
from jax.experimental.pallas import tpu as pltpu
from jax.sharding import PartitionSpec as P

F32 = jnp.float32
BF16 = jnp.bfloat16
AXES = ("ctx", "tp")
N_CTX = 16
N_TP = 16
ROWS = 128
CH = 512
SUB = 32
FF_LOC = 1368
FF_PAD = 1376
EPS = 1e-06
PLANE_GROUPS = [[xh * 8 + y * 2 + k for xh in range(2) for y in range(4)] for k in range(2)]
Z_GROUPS = [[z * 2 + x_lo for z in range(8)] for x_lo in range(2)]


def split_index(i):
    c, t = divmod(i, N_TP)
    z, x_lo = divmod(c, 2)
    x_hi, r = divmod(t, 8)
    y, k = divmod(r, 2)
    return z, x_hi * 2 + x_lo, y, k


def join_index(z, x, y, k):
    x = x % 4
    return ((z % 8) * 2 + x % 2) * N_TP + (x // 2) * 8 + (y % 4) * 2 + k % 2


def shift(arr, z=0, x=0, y=0, k=0):
    pairs = []
    for i in range(N_CTX * N_TP):
        az, ax, ay, ak = split_index(i)
        pairs.append((i, join_index(az + z, ax + x, ay + y, ak + k)))
    return lax.ppermute(arr, AXES, pairs)


def split_bf16(table):
    high = np.asarray(table, np.float32).astype(jnp.bfloat16)
    low = (np.asarray(table, np.float32) - high.astype(np.float32)).astype(jnp.bfloat16)
    return high, low


def dft_tables():
    size = 2 * ROWS
    pos = np.arange(ROWS)
    freq = np.arange(ROWS)
    phase = (pos[:, None] * freq[None, :]) % size
    angle = 2.0 * math.pi / size * phase
    cos, sin = np.cos(angle), np.sin(angle)
    sign = np.where(pos % 2 == 0, 1.0, -1.0)
    fwd_im = -sin
    fwd_im[:, 0] = sign
    forward = np.concatenate([cos, fwd_im], axis=1)
    weight = np.where(freq == 0, 1.0, 2.0)[:, None] / size
    inv_re = cos.T * weight
    inv_im = -sin.T * weight
    inv_im[0, :] = sign / size
    inverse = np.concatenate([inv_re, inv_im], axis=0)
    return np.concatenate(split_bf16(forward) + split_bf16(inverse.T), axis=1)


def dot(a, b):
    return jnp.dot(a, b, preferred_element_type=F32)


def dot_nt(a, b):
    return lax.dot_general(a, b, (((1,), (1,)), ((), ())), preferred_element_type=F32)


def prep_kernel(feat_ref, filt_ref, out_ref):
    prod = feat_ref[1].astype(F32) * feat_ref[2].astype(F32)
    filt = filt_ref[...]
    for j in range(CH // 128):
        cols = slice(128 * j, 128 * j + 128)
        out_ref[4 * j : 4 * j + 4, 0:SUB, :] = prod[:, cols].T.astype(BF16).reshape(4, SUB, 128)
        out_ref[4 * j : 4 * j + 4, SUB : 2 * SUB, :] = (
            filt[:, cols].T.astype(BF16).reshape(4, SUB, 128)
        )


def conv_kernel(x_ref, tab_ref, out_ref, spec, filt, outs):
    x = x_ref[...].reshape(N_CTX * 2 * SUB, ROWS)
    spec[...] = (dot(x, tab_ref[:, 0:256]) + dot(x, tab_ref[:, 256:512])).reshape(N_CTX, 2 * SUB, 256)
    lane = lax.broadcasted_iota(jnp.int32, (SUB, 128), 1)
    sign = jnp.where(lane % 2 == 0, 1.0, -1.0).astype(F32)
    first = lane == 0
    for d in range(N_CTX):
        re = spec[d, SUB:, 0:128]
        im = spec[d, SUB:, 128:256]
        if d > 0:
            re = re + sign * spec[d - 1, SUB:, 0:128]
            im = im + sign * spec[d - 1, SUB:, 128:256]
        filt[d, 0] = re
        filt[d, 1] = jnp.where(first, 0.0, im)
        filt[d, 2] = jnp.where(first, im, re)
    for m in range(N_CTX):
        acc_re = jnp.zeros((SUB, 128), F32)
        acc_im = jnp.zeros((SUB, 128), F32)
        for n in range(m + 1):
            pr = spec[n, 0:SUB, 0:128]
            pi = spec[n, 0:SUB, 128:256]
            hr, hz, hq = filt[m - n, 0], filt[m - n, 1], filt[m - n, 2]
            acc_re = acc_re + (pr * hr - pi * hz)
            acc_im = acc_im + (pr * hz + pi * hq)
        outs[m, :, 0:128] = acc_re
        outs[m, :, 128:256] = acc_im
    total = outs[...].reshape(N_CTX * SUB, 256)
    high = total.astype(BF16)
    low = (total - high.astype(F32)).astype(BF16)
    inv_high, inv_low = tab_ref[:, 512:768], tab_ref[:, 768:1024]
    y = dot_nt(high, inv_high) + dot_nt(high, inv_low) + dot_nt(low, inv_high)
    out_ref[...] = y.astype(BF16).reshape(N_CTX, SUB, ROWS)


def mix_kernel(conv_ref, feat_ref, skip_ref, out_ref):
    conv = conv_ref[...].reshape(CH, ROWS).astype(F32)
    for j in range(CH // 128):
        cols = slice(128 * j, 128 * j + 128)
        prod = feat_ref[1, :, cols].astype(F32) * feat_ref[2, :, cols].astype(F32)
        long = conv[cols, :].T
        gate = feat_ref[0, :, cols].astype(F32)
        mixed = (gate * (long + skip_ref[:, cols] * prod)).astype(BF16)
        for copy in range(8):
            out_ref[copy, :, cols] = mixed


def out_proj_first_kernel(core_ref, mixed_ref, w_ref, res_ref, out_ref):
    del core_ref
    j = pl.program_id(0)

    @pl.when(j == 0)
    def _():
        out_ref[...] = res_ref[...].astype(F32)

    out_ref[...] += dot(mixed_ref[0], w_ref[...])


def out_proj_second_kernel(core_ref, mixed_ref, w_ref, sum_ref, out_ref, acc):
    del core_ref
    j = pl.program_id(0)

    @pl.when(j == 0)
    def _():
        acc[...] = sum_ref[...]

    acc[...] += dot(mixed_ref[0], w_ref[...])

    @pl.when(j == pl.num_programs(0) - 1)
    def _():
        out_ref[...] = acc[...].astype(BF16)


def square_sums(values):
    ones = jnp.ones((8, CH), BF16)
    sq = values * values
    high = sq.astype(BF16)
    return dot_nt(ones, high) + dot_nt(ones, (sq - high.astype(F32)).astype(BF16))


def two_rows(total):
    high = total.astype(BF16).astype(F32)
    row = lax.broadcasted_iota(jnp.int32, total.shape, 0)
    return jnp.where(row == 0, high, jnp.where(row == 1, total - high, 0.0))


def with_tail(rows, tail):
    return jnp.concatenate([rows, tail], axis=0).astype(BF16)


def mlp_kernel(
    idx_ref, own0_ref, oth0_ref, own1_ref, oth1_ref, gain_ref, gain_oth_ref,
    wg_ref, wgx_ref, wu_ref, wux_ref, g0_ref, g1_ref, *rest
):
    del idx_ref
    up_refs, (so, sx, aux) = rest[:4], rest[4:]
    b = pl.program_id(0)
    for a, (own_ref, oth_ref) in enumerate(((own0_ref, oth0_ref), (own1_ref, oth1_ref))):
        own = own_ref[...].astype(F32)
        oth = oth_ref[...].astype(F32)
        rows = slice(a * ROWS, a * ROWS + ROWS)
        so[rows, :] = (own * gain_ref[...]).astype(BF16)
        sx[rows, :] = (oth * gain_oth_ref[...]).astype(BF16)
        aux[:, rows] = two_rows(square_sums(own) + square_sums(oth))
    zeros = jnp.zeros((FF_PAD - FF_LOC, ROWS), F32)
    gate = dot_nt(wg_ref[...], so[...]) + dot_nt(wgx_ref[...], sx[...])
    g0_ref[0] = with_tail(gate[:, :ROWS], zeros)
    g1_ref[0] = with_tail(gate[:, ROWS:], zeros)
    up = dot_nt(wu_ref[...], so[...]) + dot_nt(wux_ref[...], sx[...])
    for step, up_ref in enumerate(up_refs):

        @pl.when(b == step)
        def _():
            up_ref[0] = with_tail(up[:, :ROWS], aux[:, :ROWS])
            up_ref[1] = with_tail(up[:, ROWS:], aux[:, ROWS:])


def gate_mid_kernel(own_ref, recv_ref, *out_refs):
    for b, out_ref in enumerate(out_refs):
        out_ref[...] = (own_ref[b].astype(F32) + recv_ref[b].astype(F32)).astype(BF16)


def up_mid_kernel(own_ref, r1_ref, r2_ref, r3_ref, keep_ref, send_ref):
    for a, out_ref in enumerate((keep_ref, send_ref)):
        total = own_ref[a].astype(F32) + r1_ref[a].astype(F32)
        total = total + (r2_ref[a].astype(F32) + r3_ref[a].astype(F32))
        tail = total[FF_LOC:]
        out_ref[...] = with_tail(total[:FF_LOC], two_rows(tail[0:1] + tail[1:2] + jnp.zeros_like(tail)))


def finish_kernel(g0_ref, g1_ref, g2_ref, g3_ref, u0_ref, u1_ref, out_ref):
    gate = (g0_ref[...].astype(F32) + g1_ref[...].astype(F32)) + (
        g2_ref[...].astype(F32) + g3_ref[...].astype(F32)
    )
    up = u0_ref[...].astype(F32) + u1_ref[...].astype(F32)
    sums = up[FF_LOC : FF_LOC + 1] + up[FF_LOC + 1 : FF_LOC + 2]
    scale = lax.rsqrt(sums * (1.0 / (N_TP * CH)) + EPS)
    g = gate[:FF_LOC] * scale
    u = up[:FF_LOC] * scale
    out_ref[...] = (g / (1.0 + jnp.exp(-g)) * u).astype(BF16)


def params(mib):
    return pltpu.CompilerParams(vmem_limit_bytes=mib * 1024 * 1024)


def whole(shape):
    zeros = (0,) * len(shape)
    return pl.BlockSpec(shape, lambda *_: zeros)


def pairs_of(rule):
    pairs = []
    for i in range(N_CTX * N_TP):
        target = rule(*split_index(i))
        if target is not None:
            pairs.append((i, join_index(*target)))
    return pairs


def to_row_owner_first(z, x, y, k):
    return (z, x ^ 1, y, k) if k == x % 2 else (z, x, y, k ^ 1)


def to_row_owner_second(z, x, y, k):
    return None if k == x % 2 else (z, x ^ 1, y, k ^ 1)


def out_proj(kernel, offset, core, mixed, w_out, start, dtype, scratch):
    return pl.pallas_call(
        kernel,
        out_shape=jax.ShapeDtypeStruct((ROWS, CH), dtype),
        grid_spec=pltpu.PrefetchScalarGridSpec(
            num_scalar_prefetch=1,
            grid=(N_TP // 2,),
            in_specs=[
                pl.BlockSpec((1, ROWS, CH), lambda j, c: (j, 0, 0)),
                pl.BlockSpec((CH, CH), lambda j, c: (2 * j + jnp.bitwise_xor(c[0], offset), 0)),
                whole((ROWS, CH)),
            ],
            out_specs=whole((ROWS, CH)),
            scratch_shapes=scratch,
        ),
        compiler_params=params(56),
        name="out_proj",
    )(core, mixed, w_out, start)


def shards(residual, features, filters, skip_gain, w_out, norm_gain, w_gate, w_up):
    ctx = lax.axis_index("ctx")
    tp = lax.axis_index("tp")
    core, x_lo = tp % 2, ctx % 2
    x_hi, y = tp // 8, (tp // 2) % 4
    feat = features.transpose(1, 0, 2)
    wg, wu = w_gate.T, w_up.T
    gain = norm_gain[None, :]
    wg_oth, wu_oth, gain_oth = shift(wg, k=1), shift(wu, k=1), shift(gain, k=1)

    sent = pl.pallas_call(
        prep_kernel,
        out_shape=jax.ShapeDtypeStruct((N_CTX, 2 * SUB, ROWS), BF16),
        compiler_params=params(56),
        name="prep",
    )(feat, filters)
    recv = lax.all_to_all(sent, "ctx", 0, 0, tiled=True)
    conv = pl.pallas_call(
        conv_kernel,
        out_shape=jax.ShapeDtypeStruct((N_CTX, SUB, ROWS), BF16),
        scratch_shapes=[
            pltpu.VMEM((N_CTX, 2 * SUB, 256), F32),
            pltpu.VMEM((N_CTX, 3, SUB, 128), F32),
            pltpu.VMEM((N_CTX, SUB, 256), F32),
        ],
        compiler_params=params(56),
        name="conv",
    )(recv, jnp.asarray(dft_tables()))
    conv_rows = lax.all_to_all(conv, "ctx", 0, 0, tiled=True)
    copies = pl.pallas_call(
        mix_kernel,
        out_shape=jax.ShapeDtypeStruct((8, ROWS, CH), BF16),
        compiler_params=params(56),
        name="mix",
    )(conv_rows, feat, skip_gain[None, :])

    mixed = lax.all_to_all(
        copies, "tp", 0, 0, axis_index_groups=PLANE_GROUPS, tiled=True
    )
    mixed_oth = shift(mixed, k=1)
    core_arr = core.astype(jnp.int32)[None]
    half = out_proj(out_proj_first_kernel, 0, core_arr, mixed, w_out, residual, F32, [])
    stream = out_proj(
        out_proj_second_kernel, 1, core_arr, mixed_oth, w_out, half, BF16,
        [pltpu.VMEM((ROWS, CH), F32)],
    )

    first = lax.ppermute(stream, AXES, pairs_of(to_row_owner_first))
    second = lax.ppermute(stream, AXES, pairs_of(to_row_owner_second))
    here = x_lo == core
    held = jnp.stack([jnp.where(here, stream, first), jnp.where(here, first, second)])
    gathered = lax.all_gather(held, "ctx", axis_index_groups=Z_GROUPS)

    order = [4 * ((x_hi + a) % 2) + (y + b) % 4 for b in range(4) for a in range(2)]
    idx = jnp.stack(order).astype(jnp.int32)

    def rows_spec(a, part):
        return pl.BlockSpec((None, None, ROWS, CH), lambda b, i: (i[2 * b + a], part, 0, 0))

    part_shape = (FF_PAD, ROWS)
    outs = pl.pallas_call(
        mlp_kernel,
        out_shape=[jax.ShapeDtypeStruct((4,) + part_shape, BF16)] * 2
        + [jax.ShapeDtypeStruct((2,) + part_shape, BF16)] * 4,
        grid_spec=pltpu.PrefetchScalarGridSpec(
            num_scalar_prefetch=1,
            grid=(4,),
            in_specs=[rows_spec(0, 0), rows_spec(0, 1), rows_spec(1, 0), rows_spec(1, 1)]
            + [whole((1, CH))] * 2
            + [whole((FF_LOC, CH))] * 4,
            out_specs=[pl.BlockSpec((1,) + part_shape, lambda b, i: (b, 0, 0))] * 2
            + [whole((2,) + part_shape)] * 4,
            scratch_shapes=[
                pltpu.VMEM((2 * ROWS, CH), BF16),
                pltpu.VMEM((2 * ROWS, CH), BF16),
                pltpu.VMEM((8, 2 * ROWS), F32),
            ],
        ),
        compiler_params=params(56),
        name="mlp",
    )(idx, gathered, gathered, gathered, gathered, gain, gain_oth, wg, wg_oth, wu, wu_oth)
    g_keep, g_send, u_parts = outs[0], outs[1], outs[2:]

    g_recv = shift(g_send, x=2)
    u_recv = [shift(u_parts[b], y=b) for b in (2, 1, 3)]
    g_mid = pl.pallas_call(
        gate_mid_kernel,
        out_shape=[jax.ShapeDtypeStruct(part_shape, BF16)] * 4,
        compiler_params=params(56),
        name="gate_mid",
    )(g_keep, g_recv)
    u_keep, u_send = pl.pallas_call(
        up_mid_kernel,
        out_shape=[jax.ShapeDtypeStruct(part_shape, BF16)] * 2,
        compiler_params=params(56),
        name="up_mid",
    )(u_parts[0], *u_recv)
    u_last = shift(u_send, x=2)
    g_last = [shift(g_mid[b], y=b) for b in (2, 1, 3)]
    hidden_t = pl.pallas_call(
        finish_kernel,
        out_shape=jax.ShapeDtypeStruct((FF_LOC, ROWS), BF16),
        compiler_params=params(56),
        name="finish",
    )(g_mid[0], *g_last, u_keep, u_last)
    return stream, hidden_t.T


def solution(mesh):
    placed = (
        P("ctx", "tp"),
        P("ctx", None, "tp"),
        P("ctx", "tp"),
        P("tp"),
        P(None, "tp"),
        P("tp"),
        P("tp", "ctx"),
        P("tp", "ctx"),
    )
    return jax.shard_map(
        shards,
        mesh=mesh,
        in_specs=placed,
        out_specs=(P("ctx", "tp"), P("tp", "ctx")),
        check_vma=False,
    )
```

time: 294 us -> 214 us (0.73)
  waiting for transfers between devices: 193 us -> 79.5 us
  blocking collectives: 34.5 us -> 54.1 us
  starting transfers between devices: 1.62 us -> 15.3 us
  Pallas kernels: 33.9 us -> 42.9 us
  local copies, waits for them, and re-layouts: 11 us -> 4.35 us
    reduce_scatter x1 -> x0, waiting for transfers between devices: 97.2 us -> none  [shards(): lax.psum_scatter(partial, 'tp', scatter_dimension=0, axis_index_groups=PL...]
    all_gather x2 -> x1, waiting for transfers between devices: 81.4 us -> 30.6 us  [shards(): gathered = lax.all_gather(held, 'ctx', axis_index_groups=Z_GROUPS)]
    ppermute x3 -> x12, waiting for transfers between devices: 6.1 us -> 46 us  [shift(): return lax.ppermute(arr, AXES, pairs)]
    all_to_all x0 -> x1, blocking collectives: none -> 18.6 us  [shards(): lax.all_to_all(copies, 'tp', 0, 0, axis_index_groups=PLANE_GROUPS, tiled=...]
    ppermute x3 -> x12, starting transfers between devices: 0.84 us -> 12 us  [shift(): return lax.ppermute(arr, AXES, pairs)]
    unnamed x20 -> x26, local copies, waits for them, and re-layouts: 11 us -> 3.72 us
    pallas_call x3 -> x6, Pallas kernels: 29.5 us -> 35.1 us  [the longest x1 14 us: shards(): pl.pallas_call(mlp_kernel, out_shape=[jax.ShapeDtypeStruct((4,) + part_sh...]
    ppermute x1 -> x2, waiting for transfers between devices: 7.9 us -> 2.84 us  [the longest x1 2.83 us: shards(): first = lax.ppermute(stream, AXES, pairs_of(to_row_owner_first))]
  transfers between devices with their start and end apart: 7 -> 15, of which waited for: 7 -> 12; matrix products, arithmetic and copies ran while one was open for 1% -> 0% of each run, Pallas kernels for 0% -> 6%
where the time goes in v1:
time: 214 us; the launch traced here: 212 us
  waiting for transfers between devices  79.5 us (37%)
  blocking collectives  54.1 us (25%)
  Pallas kernels  42.9 us (20%)
  starting transfers between devices  15.3 us (7%)
  between operations  14.1 us (7%)
  local copies, waits for them, and re-layouts  4.35 us (2%)
    ppermute x12, waiting for transfers between devices, shift(): return lax.ppermute(arr, AXES, pairs)  46 us
    all_gather x1, waiting for transfers between devices, shards(): gathered = lax.all_gather(held, 'ctx', axis_index_groups=Z_GROUPS)  30.6 us
    all_to_all x1, blocking collectives, shards(): recv = lax.all_to_all(sent, 'ctx', 0, 0, tiled=True)  21.6 us
    all_to_all x1, blocking collectives, shards(): lax.all_to_all(copies, 'tp', 0, 0, axis_index_groups=PLANE_GROUPS, tiled=...  18.6 us
    pallas_call x1, Pallas kernels, shards(): pl.pallas_call(mlp_kernel, out_shape=[jax.ShapeDtypeStruct((4,) + part_sh...  14 us
    all_to_all x1, blocking collectives, shards(): conv_rows = lax.all_to_all(conv, 'ctx', 0, 0, tiled=True)  13.8 us
    pallas_call x2, Pallas kernels, out_proj(): pl.pallas_call(kernel, out_shape=jax.ShapeDtypeStruct((ROWS, CH), dtype),...  13.1 us
    ppermute x12, starting transfers between devices, shift(): return lax.ppermute(arr, AXES, pairs)  12 us
  transfers between devices with their start and end apart: 15, of which 12 were waited for; matrix products, arithmetic and copies ran while one was open for 0% of the time, Pallas kernels for 6%

profile of v1, /device:TPU:24, one launch (start us, length us, event | category | flops | bytes accessed | tf_op | source)
XLA Modules:
  0.0 211.8 jit_solution(8579979198419235337)
XLA Ops:
  7.2 0.0 all-gather.3.cloned.1.call-start
  7.2 1.9 prep.1
  9.1 21.6 %all_to_all.15.x_ref = bf16[16,64,128]{2,1,0:T(8,128)(2,1)} all-to-all(bf16[16,64,128]{2,1,0:T(8,128)(2,1)} %prep.1), channel_id=1, replica_groups=mesh['ctx'=16,'tp'=16] {'ctx'}, dimensions={0} | all-to-all | bytes 524288 | tf_op jit(solution)/shard_map/all_to_all | solution.py:294
  30.8 3.1 %conv.1 = bf16[16,32,128]{2,1,0:T(8,128)(2,1)} custom-call(bf16[16,64,128]{2,1,0:T(8,128)(2,1)} %all_to_all.15.x_ref, bf16[128,1024]{1,0:T(8,128)(2,1)} %constant.103.clone.tab_ref), custom_call_target="tpu_custom_call" | custom-call | tf_op jit(solution)/shard_map/conv/pallas_call | solution.py:295
  33.9 13.8 %all_to_all.16.conv_ref = bf16[16,32,128]{2,1,0:T(8,128)(2,1)} all-to-all(bf16[16,32,128]{2,1,0:T(8,128)(2,1)} %conv.1), channel_id=1, replica_groups=mesh['ctx'=16,'tp'=16] {'ctx'}, dimensions={0} | all-to-all | bytes 262144 | tf_op jit(solution)/shard_map/all_to_all | solution.py:306
  47.7 2.2 %mix.1 = bf16[8,128,512]{2,1,0:T(8,128)(2,1)} custom-call(bf16[16,32,128]{2,1,0:T(8,128)(2,1)} %all_to_all.16.conv_ref, bf16[3,128,512]{2,1,0:T(8,128)(2,1)} %bitcast.25, f32[1,512]{1,0:T(1,128)} %bitcast.31), custom_call_target="tpu_custom_call" | custom-call | tf_op jit(solution)/shard_map/mix/pallas_call | solution.py:307
  49.9 18.6 %all_to_all.17.mixed_ref = bf16[8,128,512]{2,1,0:T(8,128)(2,1)S(1)} all-to-all(bf16[8,128,512]{2,1,0:T(8,128)(2,1)} %mix.1), channel_id=1, replica_groups={{0,2,4,6,8,10,12,14},{1,3,5,7,9,11,13,15},{16,18,20,22,24,26,28,30},{17..., dimensions={0} | all-to-all | bytes 2097152 | tf_op jit(solution)/shard_map/all_to_all | solution.py:314
  68.6 0.0 copy-start
  68.6 0.0 collective-permute-start
  68.6 1.0 copy-done
  69.6 6.5 %out_proj.2.sum_ref = f32[128,512]{1,0:T(8,128)} custom-call(s32[1]{0:T(128)} %bitcast.core_ref, bf16[8,128,512]{2,1,0:T(8,128)(2,1)} %copy-done, bf16[8192,512]{1,0:T(8,128)(2,1)} %w_ref.3, bf16[128,512]{1,0:T(8,128)(2,1)} %res_ref.1), custom_call_target="tpu_custom_call" | custom-call | tf_op jit(solution)/shard_map/out_proj/pallas_call | solution.py:259
  76.0 0.0 collective-permute-done.mixed_ref
  76.0 0.0 copy-start.3
  76.0 6.6 %out_proj.3 = bf16[128,512]{1,0:T(8,128)(2,1)} custom-call(s32[1]{0:T(128)} %bitcast.core_ref, bf16[8,128,512]{2,1,0:T(8,128)(2,1)} %collective-permute-done.mixed_ref, bf16[8192,512]{1,0:T(8,128)(2,1)} %w_ref.3, f32[128,512]{1,0:T(8,128)} %out_proj.2.sum_ref), custom_call_target="tpu_custom_call" | custom-call | tf_op jit(solution)/shard_map/out_proj/pallas_call | solution.py:259
  82.7 0.0 copy-start.2
  82.7 0.0 copy-start.11
  82.7 0.8 collective-permute-start.2
  83.5 2.5 %collective-permute-start.1 = (bf16[128,512]{1,0:T(8,128)(2,1)}, bf16[128,512]{1,0:T(8,128)(2,1)S(1)}, u32[]{:S(2)}, u32[]{:S(2)}) collective-permute-start(bf16[128,512]{1,0:T(8,128)(2,1)} %out_proj.3), channel_id=1, source_target_pairs={{0,16},{1,0},{2,18},{3,2},{4,20},{5,4},{6,22},{7,6},{8,24},{9,8},{... | collective-permute-start | bytes 393224 | tf_op jit(solution)/shard_map/ppermute | solution.py:325
  86.0 0.0 collective-permute-done.2
  86.0 2.8 %collective-permute-done.1 = bf16[128,512]{1,0:T(8,128)(2,1)S(1)} collective-permute-done((bf16[128,512]{1,0:T(8,128)(2,1)}, bf16[128,512]{1,0:T(8,128)(2,1)S(1)}, u32[]{:S(2)}, u32[]{:S(2)}) %collective-permute-start.1) | collective-permute-done | bytes 131104 | tf_op jit(solution)/shard_map/ppermute | solution.py:325
  88.8 0.9 select_bitcast_fusion.1
  89.7 0.7 pad_maximum_fusion
  90.5 0.0 all-gather.3.cloned.1.call-update
  90.5 0.0 copy-done.2
  90.5 0.6 collective-permute-start.4
  91.1 0.0 copy-done.3
  91.1 0.1 collective-permute-start.5
  91.2 0.0 copy-done.11
  91.2 0.4 collective-permute-start.3
  91.6 0.6 stack.44.idx_ref
  92.2 1.7 collective-permute-done.3.gain_oth_ref
  93.9 0.0 copy-start.12
  93.9 0.1 collective-permute-done.4.wgx_ref
  94.0 2.0 collective-permute-done.5.wux_ref
  96.0 30.6 %all-gather.3.cloned.1.call-done = bf16[16,128,512]{2,1,0:T(8,128)(2,1)} async-done(((bf16[2,128,512]{2,1,0:T(8,128)(2,1)}), bf16[16,128,512]{2,1,0:T(8,128)(2,1)}) %all-gather.3.cloned.1.call-update) | async-done | bytes 2097168 | tf_op jit(solution)/shard_map/all_gather | solution.py:329
  126.6 0.0 copy-done.12
  126.6 14.0 %mlp.1 = (bf16[4,1376,128]{2,1,0:T(8,128)(2,1)}, bf16[4,1376,128]{2,1,0:T(8,128)(2,1)}, bf16[2,1376,128]{2,1,0:T(8,128)(2,1)}, bf16[2,1376,128]{2,1,0:T(8,128)(2...) custom-call(s32[8]{0:T(128)} %stack.44.idx_ref, bf16[8,2,128,512]{3,2,1,0:T(8,128)(2,1)} %bitcast.20, ...), custom_call_target="tpu_custom_call" | custom-call | tf_op jit(solution)/shard_map/mlp/pallas_call | solution.py:338
  140.6 3.1 %collective-permute-start.6 = (bf16[4,1376,128]{2,1,0:T(8,128)(2,1)}, bf16[4,1376,128]{2,1,0:T(8,128)(2,1)S(1)}, u32[]{:S(2)}, u32[]{:S(2)}) collective-permute-start(bf16[4,1376,128]{2,1,0:T(8,128)(2,1)} %get-tuple-element.15), channel_id=1, source_target_pairs={{0,8},{1,9},{2,10},{3,11},{4,12},{5,13},{6,14},{7,15},{8,0},{9,1},... | collective-permute-start | bytes 4227080 | tf_op jit(solution)/shard_map/ppermute | solution.py:44
  143.7 1.4 collective-permute-start.10
  145.1 2.1 collective-permute-start.11
  147.2 0.0 collective-permute-start.12
  147.2 16.9 %collective-permute-done.10.r1_ref = bf16[2,1376,128]{2,1,0:T(8,128)(2,1)S(1)} collective-permute-done((bf16[2,1376,128]{2,1,0:T(8,128)(2,1)}, bf16[2,1376,128]{2,1,0:T(8,128)(2,1)S(1)}, u32[]{:S(2)}, u32[]{:S(2)}) %collective-permute-start.10) | collective-permute-done | bytes 704544 | tf_op jit(solution)/shard_map/ppermute | solution.py:44
  164.1 7.8 %collective-permute-done.11.r2_ref = bf16[2,1376,128]{2,1,0:T(8,128)(2,1)S(1)} collective-permute-done((bf16[2,1376,128]{2,1,0:T(8,128)(2,1)}, bf16[2,1376,128]{2,1,0:T(8,128)(2,1)S(1)}, u32[]{:S(2)}, u32[]{:S(2)}) %collective-permute-start.11) | collective-permute-done | bytes 704544 | tf_op jit(solution)/shard_map/ppermute | solution.py:44
  171.9 2.1 %collective-permute-done.12.r3_ref = bf16[2,1376,128]{2,1,0:T(8,128)(2,1)S(1)} collective-permute-done((bf16[2,1376,128]{2,1,0:T(8,128)(2,1)}, bf16[2,1376,128]{2,1,0:T(8,128)(2,1)S(1)}, u32[]{:S(2)}, u32[]{:S(2)}) %collective-permute-start.12) | collective-permute-done | bytes 704544 | tf_op jit(solution)/shard_map/ppermute | solution.py:44
  174.1 0.0 copy-done.4
  174.1 0.0 copy-done.5
  174.1 0.9 copy-done.6
  174.9 2.8 %up_mid.1 = (bf16[1376,128]{1,0:T(8,128)(2,1)}, bf16[1376,128]{1,0:T(8,128)(2,1)}) custom-call(bf16[2,1376,128]{2,1,0:T(8,128)(2,1)} %get-tuple-element.20.own_ref, bf16[2,1376,128]{2,1,0:T(8,128)(2,1)} %copy-done.4, bf16[2,1376,128]{2,1,0:T(8,128)(2,1)} %copy-done.5, bf16[2,1376,128]{2,1,0:T(8,128)(2,1)} %copy-done.6), custom_call_target="tpu_custom_call" | custom-call | tf_op jit(solution)/shard_map/up_mid/pallas_call | solution.py:369
  177.8 0.6 collective-permute-start.13
  178.3 0.0 collective-permute-done.6.recv_ref
  178.3 1.1 copy-done.1
  179.4 3.0 %gate_mid.1 = (bf16[1376,128]{1,0:T(8,128)(2,1)}, bf16[1376,128]{1,0:T(8,128)(2,1)}, bf16[1376,128]{1,0:T(8,128)(2,1)}, bf16[1376,128]{1,0:T(8,128)(2,1)}) custom-call(bf16[4,1376,128]{2,1,0:T(8,128)(2,1)} %get-tuple-element.14.own_ref, bf16[4,1376,128]{2,1,0:T(8,128)(2,1)} %copy-done.1), custom_call_target="tpu_custom_call" | custom-call | tf_op jit(solution)/shard_map/gate_mid/pallas_call | solution.py:363
  182.4 1.7 collective-permute-start.7
  184.1 1.1 collective-permute-start.8
  185.3 0.9 collective-permute-start.9
  186.1 3.5 %collective-permute-done.13.u1_ref = bf16[1376,128]{1,0:T(8,128)(2,1)S(1)} collective-permute-done((bf16[1376,128]{1,0:T(8,128)(2,1)}, bf16[1376,128]{1,0:T(8,128)(2,1)S(1)}, u32[]{:S(2)}, u32[]{:S(2)}) %collective-permute-start.13) | collective-permute-done | bytes 352288 | tf_op jit(solution)/shard_map/ppermute | solution.py:44
  189.7 5.7 %collective-permute-done.7.g1_ref = bf16[1376,128]{1,0:T(8,128)(2,1)S(1)} collective-permute-done((bf16[1376,128]{1,0:T(8,128)(2,1)}, bf16[1376,128]{1,0:T(8,128)(2,1)S(1)}, u32[]{:S(2)}, u32[]{:S(2)}) %collective-permute-start.7) | collective-permute-done | bytes 352288 | tf_op jit(solution)/shard_map/ppermute | solution.py:44
  195.3 4.3 %collective-permute-done.8.g2_ref = bf16[1376,128]{1,0:T(8,128)(2,1)S(1)} collective-permute-done((bf16[1376,128]{1,0:T(8,128)(2,1)}, bf16[1376,128]{1,0:T(8,128)(2,1)S(1)}, u32[]{:S(2)}, u32[]{:S(2)}) %collective-permute-start.8) | collective-permute-done | bytes 352288 | tf_op jit(solution)/shard_map/ppermute | solution.py:44
  199.6 1.9 collective-permute-done.9.g3_ref
  201.6 0.0 copy-done.7
  201.6 0.0 copy-done.8
  201.6 0.0 copy-done.9
  201.6 0.7 copy-done.10
  202.3 2.7 %finish.1 = bf16[1368,128]{1,0:T(8,128)(2,1)} custom-call(bf16[1376,128]{1,0:T(8,128)(2,1)} %get-tuple-element.16.g0_ref, bf16[1376,128]{1,0:T(8,128)(2,1)} %copy-done.8, bf16[1376,128]{1,0:T(8,128)(2,1)} %copy-done.9, bf16[1376,128]{1,0:T(8,128)(2,1)} %copy-done.10, bf16[1376,128]{1,0:T(8,128)(2,1)} %get-tuple-element.24.u0_ref, bf16[1376,128]{1,0:T(8,128)(2,1)} %copy-done.7), custom_call_target="tpu_custom_call" | custom-call | tf_op jit(solution)/shard_map/finish/pallas_call | solution.py:377
  (8 shorter events, 0.0 us)
Async XLA Ops:
  7.2 119.5 %all-gather.3.cloned.1.call-start = ((), (), s32[]{:S(2)}) async-start(), calls=%async_computation.3 | async-start | bytes 2359296 | tf_op jit(solution)/shard_map/all_gather | solution.py:329
  68.6 1.0 copy-start
  68.6 7.5 %collective-permute-start = (bf16[8,128,512]{2,1,0:T(8,128)(2,1)S(1)}, bf16[8,128,512]{2,1,0:T(8,128)(2,1)}, u32[]{:S(2)}, u32[]{:S(2)}) collective-permute-start(bf16[8,128,512]{2,1,0:T(8,128)(2,1)S(1)} %all_to_all.17.mixed_ref), channel_id=1, source_target_pairs={{0,1},{1,0},{2,3},{3,2},{4,5},{5,4},{6,7},{7,6},{8,9},{9,8},{10,11... | collective-permute-start | bytes 3145736 | tf_op jit(solution)/shard_map/ppermute | solution.py:44
  76.0 15.1 %copy-start.3 = (bf16[512,1368]{0,1:T(8,128)(2,1)S(1)}, bf16[512,1368]{0,1:T(8,128)(2,1)}, u32[]{:S(2)}) copy-start(bf16[512,1368]{0,1:T(8,128)(2,1)} %param.16) | copy-start | bytes 4202500
  82.7 7.8 %copy-start.2 = (bf16[512,1368]{0,1:T(8,128)(2,1)S(1)}, bf16[512,1368]{0,1:T(8,128)(2,1)}, u32[]{:S(2)}) copy-start(bf16[512,1368]{0,1:T(8,128)(2,1)} %param.15) | copy-start | bytes 4202500
  82.7 8.6 %copy-start.11 = (f32[512]{0:T(512)S(1)}, f32[512]{0:T(512)}, u32[]{:S(2)}) copy-start(f32[512]{0:T(512)} %param.14) | copy-start | bytes 6148
  82.7 3.3 %collective-permute-start.2 = (bf16[128,512]{1,0:T(8,128)(2,1)}, bf16[128,512]{1,0:T(8,128)(2,1)S(1)}, u32[]{:S(2)}, u32[]{:S(2)}) collective-permute-start(bf16[128,512]{1,0:T(8,128)(2,1)} %out_proj.3), channel_id=1, source_target_pairs={{1,16},{3,18},{5,20},{7,22},{9,24},{11,26},{13,28},{15,30},{16,1},... | collective-permute-start | bytes 393224 | tf_op jit(solution)/shard_map/ppermute | solution.py:326
  83.5 5.3 %collective-permute-start.1 = (bf16[128,512]{1,0:T(8,128)(2,1)}, bf16[128,512]{1,0:T(8,128)(2,1)S(1)}, u32[]{:S(2)}, u32[]{:S(2)}) collective-permute-start(bf16[128,512]{1,0:T(8,128)(2,1)} %out_proj.3), channel_id=1, source_target_pairs={{0,16},{1,0},{2,18},{3,2},{4,20},{5,4},{6,22},{7,6},{8,24},{9,8},{... | collective-permute-start | bytes 393224 | tf_op jit(solution)/shard_map/ppermute | solution.py:325
  90.5 3.5 %collective-permute-start.4 = (bf16[1368,512]{1,0:T(8,128)(2,1)S(1)}, bf16[1368,512]{1,0:T(8,128)(2,1)}, u32[]{:S(2)}, u32[]{:S(2)}) collective-permute-start(bf16[1368,512]{1,0:T(8,128)(2,1)S(1)} %bitcast.27), channel_id=1, source_target_pairs={{0,1},{1,0},{2,3},{3,2},{4,5},{5,4},{6,7},{7,6},{8,9},{9,8},{10,11... | collective-permute-start | bytes 4202504 | tf_op jit(solution)/shard_map/ppermute | solution.py:44
  91.1 4.9 %collective-permute-start.5 = (bf16[1368,512]{1,0:T(8,128)(2,1)S(1)}, bf16[1368,512]{1,0:T(8,128)(2,1)}, u32[]{:S(2)}, u32[]{:S(2)}) collective-permute-start(bf16[1368,512]{1,0:T(8,128)(2,1)S(1)} %bitcast.29), channel_id=1, source_target_pairs={{0,1},{1,0},{2,3},{3,2},{4,5},{5,4},{6,7},{7,6},{8,9},{9,8},{10,11... | collective-permute-start | bytes 4202504 | tf_op jit(solution)/shard_map/ppermute | solution.py:44
  91.2 2.7 %collective-permute-start.3 = (f32[1,512]{1,0:T(1,128)S(1)}, f32[1,512]{1,0:T(1,128)S(1)}, u32[]{:S(2)}, u32[]{:S(2)}) collective-permute-start(f32[1,512]{1,0:T(1,128)S(1)} %bitcast.33), channel_id=1, source_target_pairs={{0,1},{1,0},{2,3},{3,2},{4,5},{5,4},{6,7},{7,6},{8,9},{9,8},{10,11... | collective-permute-start | bytes 6152 | tf_op jit(solution)/shard_map/ppermute | solution.py:44
  93.9 32.7 %copy-start.12 = (f32[1,512]{1,0:T(1,128)}, f32[1,512]{1,0:T(1,128)S(1)}, u32[]{:S(2)}) copy-start(f32[1,512]{1,0:T(1,128)S(1)} %collective-permute-done.3.gain_oth_ref) | copy-start | bytes 6148
  140.6 37.7 %collective-permute-start.6 = (bf16[4,1376,128]{2,1,0:T(8,128)(2,1)}, bf16[4,1376,128]{2,1,0:T(8,128)(2,1)S(1)}, u32[]{:S(2)}, u32[]{:S(2)}) collective-permute-start(bf16[4,1376,128]{2,1,0:T(8,128)(2,1)} %get-tuple-element.15), channel_id=1, source_target_pairs={{0,8},{1,9},{2,10},{3,11},{4,12},{5,13},{6,14},{7,15},{8,0},{9,1},... | collective-permute-start | bytes 4227080 | tf_op jit(solution)/shard_map/ppermute | solution.py:44
  143.7 20.4 %collective-permute-start.10 = (bf16[2,1376,128]{2,1,0:T(8,128)(2,1)}, bf16[2,1376,128]{2,1,0:T(8,128)(2,1)S(1)}, u32[]{:S(2)}, u32[]{:S(2)}) collective-permute-start(bf16[2,1376,128]{2,1,0:T(8,128)(2,1)} %get-tuple-element.21), channel_id=1, source_target_pairs={{0,4},{1,5},{2,6},{3,7},{4,0},{5,1},{6,2},{7,3},{8,12},{9,13},{10,... | collective-permute-start | bytes 2113544 | tf_op jit(solution)/shard_map/ppermute | solution.py:44
  145.1 26.8 %collective-permute-start.11 = (bf16[2,1376,128]{2,1,0:T(8,128)(2,1)}, bf16[2,1376,128]{2,1,0:T(8,128)(2,1)S(1)}, u32[]{:S(2)}, u32[]{:S(2)}) collective-permute-start(bf16[2,1376,128]{2,1,0:T(8,128)(2,1)} %get-tuple-element.22), channel_id=1, source_target_pairs={{0,2},{1,3},{2,4},{3,5},{4,6},{5,7},{6,0},{7,1},{8,10},{9,11},{10,... | collective-permute-start | bytes 2113544 | tf_op jit(solution)/shard_map/ppermute | solution.py:44
  147.2 26.8 %collective-permute-start.12 = (bf16[2,1376,128]{2,1,0:T(8,128)(2,1)}, bf16[2,1376,128]{2,1,0:T(8,128)(2,1)S(1)}, u32[]{:S(2)}, u32[]{:S(2)}) collective-permute-start(bf16[2,1376,128]{2,1,0:T(8,128)(2,1)} %get-tuple-element.23), channel_id=1, source_target_pairs={{0,6},{1,7},{2,0},{3,1},{4,2},{5,3},{6,4},{7,5},{8,14},{9,15},{10,... | collective-permute-start | bytes 2113544 | tf_op jit(solution)/shard_map/ppermute | solution.py:44
  164.1 9.9 %copy-start.4 = (bf16[2,1376,128]{2,1,0:T(8,128)(2,1)}, bf16[2,1376,128]{2,1,0:T(8,128)(2,1)S(1)}, u32[]{:S(2)}) copy-start(bf16[2,1376,128]{2,1,0:T(8,128)(2,1)S(1)} %collective-permute-done.10.r1_ref) | copy-start | bytes 2113540
  171.9 2.1 %copy-start.5 = (bf16[2,1376,128]{2,1,0:T(8,128)(2,1)}, bf16[2,1376,128]{2,1,0:T(8,128)(2,1)S(1)}, u32[]{:S(2)}) copy-start(bf16[2,1376,128]{2,1,0:T(8,128)(2,1)S(1)} %collective-permute-done.11.r2_ref) | copy-start | bytes 2113540
  174.0 0.9 copy-start.6
  177.8 11.9 %collective-permute-start.13 = (bf16[1376,128]{1,0:T(8,128)(2,1)}, bf16[1376,128]{1,0:T(8,128)(2,1)S(1)}, u32[]{:S(2)}, u32[]{:S(2)}) collective-permute-start(bf16[1376,128]{1,0:T(8,128)(2,1)} %get-tuple-element.25), channel_id=1, source_target_pairs={{0,8},{1,9},{2,10},{3,11},{4,12},{5,13},{6,14},{7,15},{8,0},{9,1},... | collective-permute-start | bytes 1056776 | tf_op jit(solution)/shard_map/ppermute | solution.py:44
  178.3 1.1 copy-start.1
  182.4 12.9 %collective-permute-start.7 = (bf16[1376,128]{1,0:T(8,128)(2,1)}, bf16[1376,128]{1,0:T(8,128)(2,1)S(1)}, u32[]{:S(2)}, u32[]{:S(2)}) collective-permute-start(bf16[1376,128]{1,0:T(8,128)(2,1)} %get-tuple-element.17), channel_id=1, source_target_pairs={{0,4},{1,5},{2,6},{3,7},{4,0},{5,1},{6,2},{7,3},{8,12},{9,13},{10,... | collective-permute-start | bytes 1056776 | tf_op jit(solution)/shard_map/ppermute | solution.py:44
  184.1 15.5 %collective-permute-start.8 = (bf16[1376,128]{1,0:T(8,128)(2,1)}, bf16[1376,128]{1,0:T(8,128)(2,1)S(1)}, u32[]{:S(2)}, u32[]{:S(2)}) collective-permute-start(bf16[1376,128]{1,0:T(8,128)(2,1)} %get-tuple-element.18), channel_id=1, source_target_pairs={{0,2},{1,3},{2,4},{3,5},{4,6},{5,7},{6,0},{7,1},{8,10},{9,11},{10,... | collective-permute-start | bytes 1056776 | tf_op jit(solution)/shard_map/ppermute | solution.py:44
  185.3 16.3 %collective-permute-start.9 = (bf16[1376,128]{1,0:T(8,128)(2,1)}, bf16[1376,128]{1,0:T(8,128)(2,1)S(1)}, u32[]{:S(2)}, u32[]{:S(2)}) collective-permute-start(bf16[1376,128]{1,0:T(8,128)(2,1)} %get-tuple-element.19), channel_id=1, source_target_pairs={{0,6},{1,7},{2,0},{3,1},{4,2},{5,3},{6,4},{7,5},{8,14},{9,15},{10,... | collective-permute-start | bytes 1056776 | tf_op jit(solution)/shard_map/ppermute | solution.py:44
  189.6 11.9 %copy-start.7 = (bf16[1376,128]{1,0:T(8,128)(2,1)}, bf16[1376,128]{1,0:T(8,128)(2,1)S(1)}, u32[]{:S(2)}) copy-start(bf16[1376,128]{1,0:T(8,128)(2,1)S(1)} %collective-permute-done.13.u1_ref) | copy-start | bytes 1056772
  195.3 6.2 %copy-start.8 = (bf16[1376,128]{1,0:T(8,128)(2,1)}, bf16[1376,128]{1,0:T(8,128)(2,1)S(1)}, u32[]{:S(2)}) copy-start(bf16[1376,128]{1,0:T(8,128)(2,1)S(1)} %collective-permute-done.7.g1_ref) | copy-start | bytes 1056772
  199.6 1.9 copy-start.9
  201.6 0.7 copy-start.10
Sparse Core Ops, SparseCore 0:
  90.6 35.9 all-gather.2

commit v2 on v1

--- a/solution.py
+++ b/solution.py
@@ -1,3 +1,4 @@
+import functools
 import math
 
 import jax
@@ -20,7 +21,6 @@
 FF_PAD = 1376
 EPS = 1e-06
 PLANE_GROUPS = [[xh * 8 + y * 2 + k for xh in range(2) for y in range(4)] for k in range(2)]
-Z_GROUPS = [[z * 2 + x_lo for z in range(8)] for x_lo in range(2)]
 
 
 def split_index(i):
@@ -134,30 +134,26 @@
             out_ref[copy, :, cols] = mixed
 
 
-def out_proj_first_kernel(core_ref, mixed_ref, w_ref, res_ref, out_ref):
-    del core_ref
-    j = pl.program_id(0)
-
-    @pl.when(j == 0)
-    def _():
-        out_ref[...] = res_ref[...].astype(F32)
-
-    out_ref[...] += dot(mixed_ref[0], w_ref[...])
-
-
-def out_proj_second_kernel(core_ref, mixed_ref, w_ref, sum_ref, out_ref, acc):
-    del core_ref
-    j = pl.program_id(0)
-
-    @pl.when(j == 0)
-    def _():
-        acc[...] = sum_ref[...]
-
-    acc[...] += dot(mixed_ref[0], w_ref[...])
-
-    @pl.when(j == pl.num_programs(0) - 1)
-    def _():
-        out_ref[...] = acc[...].astype(BF16)
+def out_proj_kernel(offset, core_ref, mixed_hbm, w_hbm, start_ref, out_ref, mixed, w_buf, sem):
+    first = jnp.bitwise_xor(core_ref[0], offset)
+    copies = []
+    for j in range(N_TP // 2):
+        rows = pl.ds(pl.multiple_of((2 * j + first) * CH, CH), CH)
+        copies.append(
+            (
+                pltpu.make_async_copy(mixed_hbm.at[j], mixed.at[j], sem.at[0, j]),
+                pltpu.make_async_copy(w_hbm.at[rows], w_buf.at[j], sem.at[1, j]),
+            )
+        )
+    for pair in copies:
+        for copy in pair:
+            copy.start()
+    acc = start_ref[...].astype(F32)
+    for j, pair in enumerate(copies):
+        for copy in pair:
+            copy.wait()
+        acc = acc + dot(mixed[j], w_buf[j])
+    out_ref[...] = acc.astype(out_ref.dtype)
 
 
 def square_sums(values):
@@ -177,65 +173,50 @@
     return jnp.concatenate([rows, tail], axis=0).astype(BF16)
 
 
-def mlp_kernel(
-    idx_ref, own0_ref, oth0_ref, own1_ref, oth1_ref, gain_ref, gain_oth_ref,
-    wg_ref, wgx_ref, wu_ref, wux_ref, g0_ref, g1_ref, *rest
-):
-    del idx_ref
-    up_refs, (so, sx, aux) = rest[:4], rest[4:]
-    b = pl.program_id(0)
-    for a, (own_ref, oth_ref) in enumerate(((own0_ref, oth0_ref), (own1_ref, oth1_ref))):
-        own = own_ref[...].astype(F32)
-        oth = oth_ref[...].astype(F32)
-        rows = slice(a * ROWS, a * ROWS + ROWS)
-        so[rows, :] = (own * gain_ref[...]).astype(BF16)
-        sx[rows, :] = (oth * gain_oth_ref[...]).astype(BF16)
-        aux[:, rows] = two_rows(square_sums(own) + square_sums(oth))
-    zeros = jnp.zeros((FF_PAD - FF_LOC, ROWS), F32)
-    gate = dot_nt(wg_ref[...], so[...]) + dot_nt(wgx_ref[...], sx[...])
-    g0_ref[0] = with_tail(gate[:, :ROWS], zeros)
-    g1_ref[0] = with_tail(gate[:, ROWS:], zeros)
-    up = dot_nt(wu_ref[...], so[...]) + dot_nt(wux_ref[...], sx[...])
-    for step, up_ref in enumerate(up_refs):
-
-        @pl.when(b == step)
-        def _():
-            up_ref[0] = with_tail(up[:, :ROWS], aux[:, :ROWS])
-            up_ref[1] = with_tail(up[:, ROWS:], aux[:, ROWS:])
-
-
-def gate_mid_kernel(own_ref, recv_ref, *out_refs):
-    for b, out_ref in enumerate(out_refs):
-        out_ref[...] = (own_ref[b].astype(F32) + recv_ref[b].astype(F32)).astype(BF16)
-
-
-def up_mid_kernel(own_ref, r1_ref, r2_ref, r3_ref, keep_ref, send_ref):
-    for a, out_ref in enumerate((keep_ref, send_ref)):
-        total = own_ref[a].astype(F32) + r1_ref[a].astype(F32)
-        total = total + (r2_ref[a].astype(F32) + r3_ref[a].astype(F32))
-        tail = total[FF_LOC:]
-        out_ref[...] = with_tail(total[:FF_LOC], two_rows(tail[0:1] + tail[1:2] + jnp.zeros_like(tail)))
-
-
-def finish_kernel(g0_ref, g1_ref, g2_ref, g3_ref, u0_ref, u1_ref, out_ref):
-    gate = (g0_ref[...].astype(F32) + g1_ref[...].astype(F32)) + (
-        g2_ref[...].astype(F32) + g3_ref[...].astype(F32)
-    )
-    up = u0_ref[...].astype(F32) + u1_ref[...].astype(F32)
-    sums = up[FF_LOC : FF_LOC + 1] + up[FF_LOC + 1 : FF_LOC + 2]
-    scale = lax.rsqrt(sums * (1.0 / (N_TP * CH)) + EPS)
-    g = gate[:FF_LOC] * scale
-    u = up[:FF_LOC] * scale
-    out_ref[...] = (g / (1.0 + jnp.exp(-g)) * u).astype(BF16)
+def mlp_kernel(slots, with_squares, idx_ref, *refs):
+    blocks, (gain_ref, gain_oth_ref, w_ref, wx_ref) = refs[:9], refs[9:13]
+    n = len(slots)
+    out_ref, rows_in, so, sx, row_sem = refs[13:]
+
+    def halves(d):
+        if d == 4:
+            return blocks[4], blocks[5]
+        whole_block = blocks[d if d < 4 else d + 1]
+        return whole_block.at[0], whole_block.at[1]
+
+    def row_copy(d, at, part):
+        return pltpu.make_async_copy(halves(d)[part], rows_in.at[at, part], row_sem.at[at, part])
+
+    for at, slot in enumerate(slots):
+        which = idx_ref[slot]
+        for d in range(8):
+
+            @pl.when(which == d)
+            def _():
+                row_copy(d, at, 0).start()
+                row_copy(d, at, 1).start()
+    tails = []
+    for at in range(n):
+        row_copy(0, at, 0).wait()
+        row_copy(0, at, 1).wait()
+        own = rows_in[at, 0].astype(F32)
+        oth = rows_in[at, 1].astype(F32)
+        span = slice(at * ROWS, at * ROWS + ROWS)
+        so[span, :] = (own * gain_ref[...]).astype(BF16)
+        sx[span, :] = (oth * gain_oth_ref[...]).astype(BF16)
+        if with_squares:
+            tails.append(two_rows(square_sums(own) + square_sums(oth)))
+        else:
+            tails.append(jnp.zeros((FF_PAD - FF_LOC, ROWS), F32))
+    for at in range(0, n, 2):
+        span = slice(at * ROWS, at * ROWS + 2 * ROWS)
+        res = dot_nt(w_ref[...], so[span, :]) + dot_nt(wx_ref[...], sx[span, :])
+        out_ref[at] = with_tail(res[:, :ROWS], tails[at])
+        out_ref[at + 1] = with_tail(res[:, ROWS:], tails[at + 1])
 
 
 def params(mib):
     return pltpu.CompilerParams(vmem_limit_bytes=mib * 1024 * 1024)
-
-
-def whole(shape):
-    zeros = (0,) * len(shape)
-    return pl.BlockSpec(shape, lambda *_: zeros)
 
 
 def pairs_of(rule):
@@ -255,24 +236,56 @@
     return None if k == x % 2 else (z, x ^ 1, y, k ^ 1)
 
 
-def out_proj(kernel, offset, core, mixed, w_out, start, dtype, scratch):
+def in_smem():
+    return pl.BlockSpec(memory_space=pltpu.SMEM)
+
+
+def anywhere():
+    return pl.BlockSpec(memory_space=pl.ANY)
+
+
+def out_proj(offset, core, mixed, w_out, start, dtype):
     return pl.pallas_call(
-        kernel,
+        functools.partial(out_proj_kernel, offset),
         out_shape=jax.ShapeDtypeStruct((ROWS, CH), dtype),
-        grid_spec=pltpu.PrefetchScalarGridSpec(
-            num_scalar_prefetch=1,
-            grid=(N_TP // 2,),
-            in_specs=[
-                pl.BlockSpec((1, ROWS, CH), lambda j, c: (j, 0, 0)),
-                pl.BlockSpec((CH, CH), lambda j, c: (2 * j + jnp.bitwise_xor(c[0], offset), 0)),
-                whole((ROWS, CH)),
-            ],
-            out_specs=whole((ROWS, CH)),
-            scratch_shapes=scratch,
+        in_specs=[
+            in_smem(),
+            anywhere(),
+            pl.BlockSpec(memory_space=pltpu.HBM),
+            pl.BlockSpec(memory_space=pltpu.VMEM),
+        ],
+        scratch_shapes=[
+            pltpu.VMEM((N_TP // 2, ROWS, CH), BF16),
+            pltpu.VMEM((N_TP // 2, CH, CH), BF16),
+            pltpu.SemaphoreType.DMA((2, N_TP // 2)),
+        ],
+        compiler_params=params(51),
+        cost_estimate=pl.CostEstimate(
+            flops=2 * ROWS * CH * N_TP // 2 * CH, bytes_accessed=5 << 20, transcendentals=0
         ),
-        compiler_params=params(56),
         name="out_proj",
     )(core, mixed, w_out, start)
+
+
+def mlp_part(slots, with_squares, idx, blocks, gains, weights):
+    n = len(slots)
+    vmem = pl.BlockSpec(memory_space=pltpu.VMEM)
+    return pl.pallas_call(
+        functools.partial(mlp_kernel, tuple(slots), with_squares),
+        out_shape=jax.ShapeDtypeStruct((n, FF_PAD, ROWS), BF16),
+        in_specs=[in_smem()] + [anywhere()] * 9 + [vmem] * 4,
+        scratch_shapes=[
+            pltpu.VMEM((n, 2, ROWS, CH), BF16),
+            pltpu.VMEM((n * ROWS, CH), BF16),
+            pltpu.VMEM((n * ROWS, CH), BF16),
+            pltpu.SemaphoreType.DMA((n, 2)),
+        ],
+        compiler_params=params(24),
+        cost_estimate=pl.CostEstimate(
+            flops=4 * n * ROWS * CH * FF_LOC, bytes_accessed=5 << 20, transcendentals=0
+        ),
+        name="mlp",
+    )(idx, *blocks, *gains, *weights)
 
 
 def shards(residual, features, filters, skip_gain, w_out, norm_gain, w_gate, w_up):
@@ -292,6 +305,7 @@
         name="prep",
     )(feat, filters)
     recv = lax.all_to_all(sent, "ctx", 0, 0, tiled=True)
+    recv, wg_oth, wu_oth, gain_oth = lax.optimization_barrier((recv, wg_oth, wu_oth, gain_oth))
     conv = pl.pallas_call(
         conv_kernel,
         out_shape=jax.ShapeDtypeStruct((N_CTX, SUB, ROWS), BF16),
@@ -316,70 +330,69 @@
     )
     mixed_oth = shift(mixed, k=1)
     core_arr = core.astype(jnp.int32)[None]
-    half = out_proj(out_proj_first_kernel, 0, core_arr, mixed, w_out, residual, F32, [])
-    stream = out_proj(
-        out_proj_second_kernel, 1, core_arr, mixed_oth, w_out, half, BF16,
-        [pltpu.VMEM((ROWS, CH), F32)],
-    )
+    half = out_proj(0, core_arr, mixed, w_out, residual, F32)
+    stream = out_proj(1, core_arr, mixed_oth, w_out, half, BF16)
 
     first = lax.ppermute(stream, AXES, pairs_of(to_row_owner_first))
     second = lax.ppermute(stream, AXES, pairs_of(to_row_owner_second))
     here = x_lo == core
     held = jnp.stack([jnp.where(here, stream, first), jnp.where(here, first, second)])
-    gathered = lax.all_gather(held, "ctx", axis_index_groups=Z_GROUPS)
-
-    order = [4 * ((x_hi + a) % 2) + (y + b) % 4 for b in range(4) for a in range(2)]
-    idx = jnp.stack(order).astype(jnp.int32)
-
-    def rows_spec(a, part):
-        return pl.BlockSpec((None, None, ROWS, CH), lambda b, i: (i[2 * b + a], part, 0, 0))
-
-    part_shape = (FF_PAD, ROWS)
-    outs = pl.pallas_call(
-        mlp_kernel,
-        out_shape=[jax.ShapeDtypeStruct((4,) + part_shape, BF16)] * 2
-        + [jax.ShapeDtypeStruct((2,) + part_shape, BF16)] * 4,
-        grid_spec=pltpu.PrefetchScalarGridSpec(
-            num_scalar_prefetch=1,
-            grid=(4,),
-            in_specs=[rows_spec(0, 0), rows_spec(0, 1), rows_spec(1, 0), rows_spec(1, 1)]
-            + [whole((1, CH))] * 2
-            + [whole((FF_LOC, CH))] * 4,
-            out_specs=[pl.BlockSpec((1,) + part_shape, lambda b, i: (b, 0, 0))] * 2
-            + [whole((2,) + part_shape)] * 4,
-            scratch_shapes=[
-                pltpu.VMEM((2 * ROWS, CH), BF16),
-                pltpu.VMEM((2 * ROWS, CH), BF16),
-                pltpu.VMEM((8, 2 * ROWS), F32),
-            ],
-        ),
-        compiler_params=params(56),
-        name="mlp",
-    )(idx, gathered, gathered, gathered, gathered, gain, gain_oth, wg, wg_oth, wu, wu_oth)
-    g_keep, g_send, u_parts = outs[0], outs[1], outs[2:]
-
-    g_recv = shift(g_send, x=2)
-    u_recv = [shift(u_parts[b], y=b) for b in (2, 1, 3)]
-    g_mid = pl.pallas_call(
-        gate_mid_kernel,
-        out_shape=[jax.ShapeDtypeStruct(part_shape, BF16)] * 4,
-        compiler_params=params(56),
-        name="gate_mid",
-    )(g_keep, g_recv)
-    u_keep, u_send = pl.pallas_call(
-        up_mid_kernel,
-        out_shape=[jax.ShapeDtypeStruct(part_shape, BF16)] * 2,
-        compiler_params=params(56),
-        name="up_mid",
-    )(u_parts[0], *u_recv)
+    below, above = [held], [held]
+    for step in (1, 2):
+        below.append(shift(held, z=step))
+        above.append(shift(held, z=-step))
+    below.append(shift(below[2], z=1))
+    above.append(shift(above[2], z=-1))
+    opposite = (shift(below[2][0], z=2), shift(above[2][1], z=-2))
+    blocks = above + list(opposite) + [below[3], below[2], below[1]]
+
+    z = ctx // 2
+    idx = jnp.stack(
+        [
+            (4 * ((x_hi + a) % 2) + (y + b) % 4 - z) % 8
+            for b in range(4)
+            for a in range(2)
+        ]
+    ).astype(jnp.int32)
+    part = functools.partial(
+        mlp_part, idx=idx, blocks=blocks, gains=(gain, gain_oth)
+    )
+    gate_w, up_w = (wg, wg_oth), (wu, wu_oth)
+
+    g_send_a = part((5, 3), False, weights=gate_w)
+    idx_up, g_send_a = lax.optimization_barrier((idx, g_send_a))
+    g_recv_a = shift(g_send_a, x=2)
+    part_up = functools.partial(part, idx=idx_up)
+    u_sends = {b: part_up((2 * b, 2 * b + 1), True, weights=up_w) for b in (2, 1, 3)}
+    u_recv = {b: shift(u_sends[b], y=b) for b in (2, 1, 3)}
+    g_send_b = part((7, 1), False, weights=gate_w)
+    g_recv_b = shift(g_send_b, x=2)
+    g_keep_a = part((4, 2), False, weights=gate_w)
+    g_keep_b = part((6, 0), False, weights=gate_w)
+    u_keep = part((0, 1), True, weights=up_w)
+
+    def add(*terms):
+        total = terms[0].astype(F32)
+        for term in terms[1:]:
+            total = total + term.astype(F32)
+        return total
+
+    g_last = [
+        shift(add(g_keep_a[0], g_recv_a[0]).astype(BF16), y=2),
+        shift(add(g_keep_a[1], g_recv_a[1]).astype(BF16), y=1),
+        shift(add(g_keep_b[0], g_recv_b[0]).astype(BF16), y=3),
+    ]
+    g_own = add(g_keep_b[1], g_recv_b[1])
+    u_send = add(u_keep[1], *(u_recv[b][1] for b in (2, 1, 3))).astype(BF16)
     u_last = shift(u_send, x=2)
-    g_last = [shift(g_mid[b], y=b) for b in (2, 1, 3)]
-    hidden_t = pl.pallas_call(
-        finish_kernel,
-        out_shape=jax.ShapeDtypeStruct((FF_LOC, ROWS), BF16),
-        compiler_params=params(56),
-        name="finish",
-    )(g_mid[0], *g_last, u_keep, u_last)
+    u_own = add(u_keep[0], *(u_recv[b][0] for b in (2, 1, 3)))
+    gate = add(g_own, *g_last)
+    up = add(u_own, u_last)
+    sums = up[FF_LOC : FF_LOC + 1] + up[FF_LOC + 1 : FF_LOC + 2]
+    scale = lax.rsqrt(sums * (1.0 / (N_TP * CH)) + EPS)
+    gate_vals = gate[:FF_LOC] * scale
+    up_vals = up[:FF_LOC] * scale
+    hidden_t = (jax.nn.silu(gate_vals) * up_vals).astype(BF16)
     return stream, hidden_t.T
 
 

time: 214 us -> 170 us (0.79)
  waiting for transfers between devices: 79.5 us -> 49.1 us
  starting transfers between devices: 15.3 us -> 39.6 us
  blocking collectives: 54.1 us -> 33.2 us
  between operations: 14.1 us -> 0.88 us
  Pallas kernels: 42.9 us -> 36.8 us
    all_gather x1 -> x0, waiting for transfers between devices: 30.6 us -> none  [shards(): gathered = lax.all_gather(held, 'ctx', axis_index_groups=Z_GROUPS)]
    all_to_all x1 -> x0, blocking collectives: 21.6 us -> none  [shards(): recv = lax.all_to_all(sent, 'ctx', 0, 0, tiled=True)]
    ppermute x12 -> x21, starting transfers between devices: 12 us -> 29.1 us  [shift(): return lax.ppermute(arr, AXES, pairs)]
    all_to_all x0 -> x1, waiting for transfers between devices: none -> 11 us  [shards(): recv = lax.all_to_all(sent, 'ctx', 0, 0, tiled=True)]
    ppermute x12 -> x21, waiting for transfers between devices: 46 us -> 36.1 us  [shift(): return lax.ppermute(arr, AXES, pairs)]
    all_to_all x0 -> x1, starting transfers between devices: none -> 9.5 us  [shards(): recv = lax.all_to_all(sent, 'ctx', 0, 0, tiled=True)]
    pallas_call x6 -> x10, Pallas kernels: 35.6 us -> 29.2 us  [the longest x8 22.8 us: mlp_part(): pl.pallas_call(functools.partial(mlp_kernel, tuple(slots), with_squares),...]
    ppermute x1, starting transfers between devices: 2.5 us -> 0.15 us  [shards(): first = lax.ppermute(stream, AXES, pairs_of(to_row_owner_first))]
  transfers between devices with their start and end apart: 15 -> 24, of which waited for: 12 -> 13; matrix products, arithmetic and copies ran while one was open for 0% -> 2% of each run, Pallas kernels for 6% -> 15%
where the time goes in v2:
time: 170 us; the launch traced here: 167 us
  waiting for transfers between devices  49.1 us (29%)
  starting transfers between devices  39.6 us (23%)
  Pallas kernels  36.8 us (22%)
  blocking collectives  33.2 us (20%)
  local copies, waits for them, and re-layouts  4.71 us (3%)
  other arithmetic  2.84 us (2%)
    ppermute x21, waiting for transfers between devices, shift(): return lax.ppermute(arr, AXES, pairs)  36.1 us
    ppermute x21, starting transfers between devices, shift(): return lax.ppermute(arr, AXES, pairs)  29.1 us
    pallas_call x8, Pallas kernels, mlp_part(): pl.pallas_call(functools.partial(mlp_kernel, tuple(slots), with_squares),...  22.8 us
    all_to_all x1, blocking collectives, shards(): lax.all_to_all(copies, 'tp', 0, 0, axis_index_groups=PLANE_GROUPS, tiled=...  19.4 us
    all_to_all x1, blocking collectives, shards(): conv_rows = lax.all_to_all(conv, 'ctx', 0, 0, tiled=True)  13.8 us
    all_to_all x1, waiting for transfers between devices, shards(): recv = lax.all_to_all(sent, 'ctx', 0, 0, tiled=True)  11 us
    all_to_all x1, starting transfers between devices, shards(): recv = lax.all_to_all(sent, 'ctx', 0, 0, tiled=True)  9.5 us
    pallas_call x2, Pallas kernels, out_proj(): pl.pallas_call(functools.partial(out_proj_kernel, offset), out_shape=jax....  6.4 us
  transfers between devices with their start and end apart: 24, of which 13 were waited for; matrix products, arithmetic and copies ran while one was open for 2% of the time, Pallas kernels for 15%

profile of v2, /device:TPU:24, one launch (start us, length us, event | category | flops | bytes accessed | tf_op | source)
XLA Modules:
  0.0 167.1 jit_solution(16828151495357219254)
XLA Ops:
  0.6 0.1 collective-permute-start
  0.7 0.5 collective-permute-start.1
  1.2 1.9 %prep.1 = bf16[16,64,128]{2,1,0:T(8,128)(2,1)} custom-call(bf16[3,128,512]{2,1,0:T(8,128)(2,1)} %bitcast.57, f32[128,512]{1,0:T(8,128)} %filt_ref.1), custom_call_target="tpu_custom_call" | custom-call | tf_op jit(solution)/shard_map/prep/pallas_call | solution.py:301
  3.1 9.5 %all-to-all-start = ((bf16[16,64,128]{2,1,0:T(8,128)(2,1)}), bf16[16,64,128]{2,1,0:T(8,128)(2,1)S(1)}, u32[]{:S(2)}, u32[]{:S(2)}) async-start(bf16[16,64,128]{2,1,0:T(8,128)(2,1)} %prep.1), calls=%async_computation | async-start | bytes 524288 | tf_op jit(solution)/shard_map/all_to_all | solution.py:307
  12.7 0.1 collective-permute-start.2
  12.8 1.1 collective-permute-done.2.refs_10_
  13.9 11.0 %all-to-all-done.x_ref = bf16[16,64,128]{2,1,0:T(8,128)(2,1)S(1)} async-done(((bf16[16,64,128]{2,1,0:T(8,128)(2,1)}), bf16[16,64,128]{2,1,0:T(8,128)(2,1)S(1)}, u32[]{:S(2)}, u32[]{:S(2)}) %all-to-all-start) | async-done | bytes 262176 | tf_op jit(solution)/shard_map/all_to_all | solution.py:307
  24.9 0.0 collective-permute-done.refs_12_
  24.9 0.7 copy-done.8
  25.6 3.5 %conv.1 = bf16[16,32,128]{2,1,0:T(8,128)(2,1)} custom-call(bf16[16,64,128]{2,1,0:T(8,128)(2,1)} %copy-done.8, bf16[128,1024]{1,0:T(8,128)(2,1)} %constant.153.clone.tab_ref), custom_call_target="tpu_custom_call" | custom-call | tf_op jit(solution)/shard_map/conv/pallas_call | solution.py:309
  29.1 13.8 %all_to_all.15.conv_ref = bf16[16,32,128]{2,1,0:T(8,128)(2,1)} all-to-all(bf16[16,32,128]{2,1,0:T(8,128)(2,1)} %conv.1), channel_id=1, replica_groups=mesh['ctx'=16,'tp'=16] {'ctx'}, dimensions={0} | all-to-all | bytes 262144 | tf_op jit(solution)/shard_map/all_to_all | solution.py:320
  42.9 2.2 %mix.1 = bf16[8,128,512]{2,1,0:T(8,128)(2,1)} custom-call(bf16[16,32,128]{2,1,0:T(8,128)(2,1)} %all_to_all.15.conv_ref, bf16[3,128,512]{2,1,0:T(8,128)(2,1)} %bitcast.58, f32[1,512]{1,0:T(1,128)} %bitcast.59), custom_call_target="tpu_custom_call" | custom-call | tf_op jit(solution)/shard_map/mix/pallas_call | solution.py:321
  45.1 19.4 %all_to_all.16.mixed_hbm = bf16[8,128,512]{2,1,0:T(8,128)(2,1)} all-to-all(bf16[8,128,512]{2,1,0:T(8,128)(2,1)} %mix.1), channel_id=1, replica_groups={{0,2,4,6,8,10,12,14},{1,3,5,7,9,11,13,15},{16,18,20,22,24,26,28,30},{17..., dimensions={0} | all-to-all | bytes 2097152 | tf_op jit(solution)/shard_map/all_to_all | solution.py:328
  64.5 2.9 %out_proj.2.start_ref = f32[128,512]{1,0:T(8,128)S(1)} custom-call(s32[1]{0:T(128)} %bitcast.core_ref, bf16[8,128,512]{2,1,0:T(8,128)(2,1)} %all_to_all.16.mixed_hbm, bf16[8192,512]{1,0:T(8,128)(2,1)} %w_hbm.3, bf16[128,512]{1,0:T(8,128)(2,1)S(1)} %copy-done.7), custom_call_target="tpu_custom_call" | custom-call | flops 536870912 | bytes 5242880 | tf_op jit(solution)/shard_map/out_proj/pallas_call | solution.py:248
  67.4 0.1 collective-permute-done.3.mixed_hbm
  67.5 3.5 %out_proj.3 = bf16[128,512]{1,0:T(8,128)(2,1)} custom-call(s32[1]{0:T(128)} %bitcast.core_ref, bf16[8,128,512]{2,1,0:T(8,128)(2,1)} %collective-permute-done.3.mixed_hbm, bf16[8192,512]{1,0:T(8,128)(2,1)} %w_hbm.3, f32[128,512]{1,0:T(8,128)S(1)} %out_proj.2.start_ref), custom_call_target="tpu_custom_call" | custom-call | flops 536870912 | bytes 5242880 | tf_op jit(solution)/shard_map/out_proj/pallas_call | solution.py:248
  71.1 0.0 copy-start
  71.1 0.2 collective-permute-start.4
  71.2 0.8 collective-permute-start.5
  72.0 2.0 %collective-permute-done.4 = bf16[128,512]{1,0:T(8,128)(2,1)S(1)} collective-permute-done((bf16[128,512]{1,0:T(8,128)(2,1)}, bf16[128,512]{1,0:T(8,128)(2,1)S(1)}, u32[]{:S(2)}, u32[]{:S(2)}) %collective-permute-start.4) | collective-permute-done | bytes 131104 | tf_op jit(solution)/shard_map/ppermute | solution.py:336
  74.1 0.9 select_bitcast_fusion.1
  75.0 0.6 collective-permute-start.9
  75.6 3.6 %collective-permute-start.7 = (bf16[2,128,512]{2,1,0:T(8,128)(2,1)S(1)}, bf16[2,128,512]{2,1,0:T(8,128)(2,1)}, u32[]{:S(2)}, u32[]{:S(2)}) collective-permute-start(bf16[2,128,512]{2,1,0:T(8,128)(2,1)S(1)} %pad_maximum_fusion.refs_0_), channel_id=1, source_target_pairs={{0,192},{1,193},{2,194},{3,195},{4,196},{5,197},{6,198},{7,199},{8... | collective-permute-start | bytes 786440 | tf_op jit(solution)/shard_map/ppermute | solution.py:44
  79.2 0.3 collective-permute-start.13
  79.6 2.9 %collective-permute-start.6 = (bf16[2,128,512]{2,1,0:T(8,128)(2,1)S(1)}, bf16[2,128,512]{2,1,0:T(8,128)(2,1)}, u32[]{:S(2)}, u32[]{:S(2)}) collective-permute-start(bf16[2,128,512]{2,1,0:T(8,128)(2,1)S(1)} %pad_maximum_fusion.refs_0_), channel_id=1, source_target_pairs={{0,224},{1,225},{2,226},{3,227},{4,228},{5,229},{6,230},{7,231},{8... | collective-permute-start | bytes 786440 | tf_op jit(solution)/shard_map/ppermute | solution.py:44
  82.5 7.6 %collective-permute-done.9.refs_7_ = bf16[2,128,512]{2,1,0:T(8,128)(2,1)S(1)} collective-permute-done((bf16[2,128,512]{2,1,0:T(8,128)(2,1)S(1)}, bf16[2,128,512]{2,1,0:T(8,128)(2,1)S(1)}, u32[]{:S(2)}, u32[]{:S(2)}) %collective-permute-start.9) | collective-permute-done | bytes 262176 | tf_op jit(solution)/shard_map/ppermute | solution.py:44
  90.1 0.7 slice_bitcast_fusion.1
  90.8 0.2 collective-permute-start.12
  91.0 3.0 %collective-permute-start.8 = (bf16[2,128,512]{2,1,0:T(8,128)(2,1)}, bf16[2,128,512]{2,1,0:T(8,128)(2,1)}, u32[]{:S(2)}, u32[]{:S(2)}) collective-permute-start(bf16[2,128,512]{2,1,0:T(8,128)(2,1)} %collective-permute-done.7.refs_2_), channel_id=1, source_target_pairs={{0,224},{1,225},{2,226},{3,227},{4,228},{5,229},{6,230},{7,231},{8... | collective-permute-start | bytes 786440 | tf_op jit(solution)/shard_map/ppermute | solution.py:44
  94.0 1.6 slice_bitcast_fusion
  95.6 0.7 copy-done.4
  96.3 2.9 %collective-permute-start.11 = (bf16[128,512]{1,0:T(8,128)(2,1)}, bf16[128,512]{1,0:T(8,128)(2,1)}, u32[]{:S(2)}, u32[]{:S(2)}) collective-permute-start(bf16[128,512]{1,0:T(8,128)(2,1)} %slice_bitcast_fusion), channel_id=1, source_target_pairs={{0,192},{1,193},{2,194},{3,195},{4,196},{5,197},{6,198},{7,199},{8... | collective-permute-start | bytes 393224 | tf_op jit(solution)/shard_map/ppermute | solution.py:44
  99.3 0.1 stack.44.idx_ref
  99.4 3.1 %collective-permute-done.10.refs_4_ = bf16[128,512]{1,0:T(8,128)(2,1)S(1)} collective-permute-done((bf16[128,512]{1,0:T(8,128)(2,1)}, bf16[128,512]{1,0:T(8,128)(2,1)S(1)}, u32[]{:S(2)}, u32[]{:S(2)}) %collective-permute-start.10) | collective-permute-done | bytes 131104 | tf_op jit(solution)/shard_map/ppermute | solution.py:44
  102.5 3.3 %collective-permute-done.11.refs_5_ = bf16[128,512]{1,0:T(8,128)(2,1)} collective-permute-done((bf16[128,512]{1,0:T(8,128)(2,1)}, bf16[128,512]{1,0:T(8,128)(2,1)}, u32[]{:S(2)}, u32[]{:S(2)}) %collective-permute-start.11) | collective-permute-done | bytes 131104 | tf_op jit(solution)/shard_map/ppermute | solution.py:44
  105.8 0.8 collective-permute-done.12.refs_6_
  106.6 0.9 copy-done.5
  107.5 2.7 %mlp.11 = bf16[2,1376,128]{2,1,0:T(8,128)(2,1)S(1)} custom-call(s32[8]{0:T(128)S(1)} %stack.44.idx_ref, bf16[2,128,512]{2,1,0:T(8,128)(2,1)S(1)} %pad_maximum_fusion.refs_0_, bf16[2,128,512]{2,1,0:T(8,128)(2,1)} %collective-permute-done.6.refs_1_, bf16[2,128,512]{2,1,0:T(8,128)(2,1)} %collective-permute-done.7.refs_2_, ...), custom_call_target="tpu_custom_call" | custom-call | flops 717225984 | bytes 5242880 | tf_op jit(solution)/shard_map/mlp/pallas_call | solution.py:273
  110.2 3.1 %collective-permute-start.15 = (bf16[2,1376,128]{2,1,0:T(8,128)(2,1)S(1)}, bf16[2,1376,128]{2,1,0:T(8,128)(2,1)S(1)}, u32[]{:S(2)}, u32[]{:S(2)}) collective-permute-start(bf16[2,1376,128]{2,1,0:T(8,128)(2,1)S(1)} %mlp.11), channel_id=1, source_target_pairs={{0,8},{1,9},{2,10},{3,11},{4,12},{5,13},{6,14},{7,15},{8,0},{9,1},... | collective-permute-start | bytes 2113544 | tf_op jit(solution)/shard_map/ppermute | solution.py:44
  113.3 3.2 %mlp.13 = bf16[2,1376,128]{2,1,0:T(8,128)(2,1)S(1)} custom-call(s32[8]{0:T(128)S(1)} %stack.44.idx_ref, bf16[2,128,512]{2,1,0:T(8,128)(2,1)S(1)} %pad_maximum_fusion.refs_0_, bf16[2,128,512]{2,1,0:T(8,128)(2,1)} %collective-permute-done.6.refs_1_, bf16[2,128,512]{2,1,0:T(8,128)(2,1)} %collective-permute-done.7.refs_2_, ...), custom_call_target="tpu_custom_call" | custom-call | flops 717225984 | bytes 5242880 | tf_op jit(solution)/shard_map/mlp/pallas_call | solution.py:273
  116.4 2.2 %collective-permute-start.19 = (bf16[2,1376,128]{2,1,0:T(8,128)(2,1)S(1)}, bf16[2,1376,128]{2,1,0:T(8,128)(2,1)S(1)}, u32[]{:S(2)}, u32[]{:S(2)}) collective-permute-start(bf16[2,1376,128]{2,1,0:T(8,128)(2,1)S(1)} %mlp.13), channel_id=1, source_target_pairs={{0,4},{1,5},{2,6},{3,7},{4,0},{5,1},{6,2},{7,3},{8,12},{9,13},{10,... | collective-permute-start | bytes 2113544 | tf_op jit(solution)/shard_map/ppermute | solution.py:44
  118.7 3.2 %mlp.14 = bf16[2,1376,128]{2,1,0:T(8,128)(2,1)S(1)} custom-call(s32[8]{0:T(128)S(1)} %stack.44.idx_ref, bf16[2,128,512]{2,1,0:T(8,128)(2,1)S(1)} %pad_maximum_fusion.refs_0_, bf16[2,128,512]{2,1,0:T(8,128)(2,1)} %collective-permute-done.6.refs_1_, bf16[2,128,512]{2,1,0:T(8,128)(2,1)} %collective-permute-done.7.refs_2_, ...), custom_call_target="tpu_custom_call" | custom-call | flops 717225984 | bytes 5242880 | tf_op jit(solution)/shard_map/mlp/pallas_call | solution.py:273
  121.9 1.1 collective-permute-start.20
  123.0 3.2 %mlp.15 = bf16[2,1376,128]{2,1,0:T(8,128)(2,1)S(1)} custom-call(s32[8]{0:T(128)S(1)} %stack.44.idx_ref, bf16[2,128,512]{2,1,0:T(8,128)(2,1)S(1)} %pad_maximum_fusion.refs_0_, bf16[2,128,512]{2,1,0:T(8,128)(2,1)} %collective-permute-done.6.refs_1_, bf16[2,128,512]{2,1,0:T(8,128)(2,1)} %collective-permute-done.7.refs_2_, ...), custom_call_target="tpu_custom_call" | custom-call | flops 717225984 | bytes 5242880 | tf_op jit(solution)/shard_map/mlp/pallas_call | solution.py:273
  126.2 1.1 collective-permute-start.21
  127.3 2.3 %mlp.9 = bf16[2,1376,128]{2,1,0:T(8,128)(2,1)S(1)} custom-call(s32[8]{0:T(128)S(1)} %stack.44.idx_ref, bf16[2,128,512]{2,1,0:T(8,128)(2,1)S(1)} %pad_maximum_fusion.refs_0_, bf16[2,128,512]{2,1,0:T(8,128)(2,1)} %collective-permute-done.6.refs_1_, bf16[2,128,512]{2,1,0:T(8,128)(2,1)} %collective-permute-done.7.refs_2_, ...), custom_call_target="tpu_custom_call" | custom-call | flops 717225984 | bytes 5242880 | tf_op jit(solution)/shard_map/mlp/pallas_call | solution.py:273
  129.6 0.5 collective-permute-start.14
  130.1 2.5 %mlp.10 = bf16[2,1376,128]{2,1,0:T(8,128)(2,1)S(1)} custom-call(s32[8]{0:T(128)S(1)} %stack.44.idx_ref, bf16[2,128,512]{2,1,0:T(8,128)(2,1)S(1)} %pad_maximum_fusion.refs_0_, bf16[2,128,512]{2,1,0:T(8,128)(2,1)} %collective-permute-done.6.refs_1_, bf16[2,128,512]{2,1,0:T(8,128)(2,1)} %collective-permute-done.7.refs_2_, ...), custom_call_target="tpu_custom_call" | custom-call | flops 717225984 | bytes 5242880 | tf_op jit(solution)/shard_map/mlp/pallas_call | solution.py:273
  132.6 2.6 %mlp.8 = bf16[2,1376,128]{2,1,0:T(8,128)(2,1)S(1)} custom-call(s32[8]{0:T(128)S(1)} %stack.44.idx_ref, bf16[2,128,512]{2,1,0:T(8,128)(2,1)S(1)} %pad_maximum_fusion.refs_0_, bf16[2,128,512]{2,1,0:T(8,128)(2,1)} %collective-permute-done.6.refs_1_, bf16[2,128,512]{2,1,0:T(8,128)(2,1)} %collective-permute-done.7.refs_2_, ...), custom_call_target="tpu_custom_call" | custom-call | flops 717225984 | bytes 5242880 | tf_op jit(solution)/shard_map/mlp/pallas_call | solution.py:273
  135.2 3.2 %mlp.12 = bf16[2,1376,128]{2,1,0:T(8,128)(2,1)S(1)} custom-call(s32[8]{0:T(128)S(1)} %stack.44.idx_ref, bf16[2,128,512]{2,1,0:T(8,128)(2,1)S(1)} %pad_maximum_fusion.refs_0_, bf16[2,128,512]{2,1,0:T(8,128)(2,1)} %collective-permute-done.6.refs_1_, bf16[2,128,512]{2,1,0:T(8,128)(2,1)} %collective-permute-done.7.refs_2_, ...), custom_call_target="tpu_custom_call" | custom-call | flops 717225984 | bytes 5242880 | tf_op jit(solution)/shard_map/mlp/pallas_call | solution.py:273
  138.4 0.2 fusion.5
  138.6 2.4 %collective-permute-start.16 = (bf16[1376,128]{1,0:T(8,128)(2,1)S(1)}, bf16[1376,128]{1,0:T(8,128)(2,1)S(1)}, u32[]{:S(2)}, u32[]{:S(2)}) collective-permute-start(bf16[1376,128]{1,0:T(8,128)(2,1)S(1)} %get-tuple-element.16), channel_id=1, source_target_pairs={{0,4},{1,5},{2,6},{3,7},{4,0},{5,1},{6,2},{7,3},{8,12},{9,13},{10,... | collective-permute-start | bytes 1056776 | tf_op jit(solution)/shard_map/ppermute | solution.py:44
  141.0 2.4 %collective-permute-start.17 = (bf16[1376,128]{1,0:T(8,128)(2,1)S(1)}, bf16[1376,128]{1,0:T(8,128)(2,1)S(1)}, u32[]{:S(2)}, u32[]{:S(2)}) collective-permute-start(bf16[1376,128]{1,0:T(8,128)(2,1)S(1)} %get-tuple-element.17), channel_id=1, source_target_pairs={{0,2},{1,3},{2,4},{3,5},{4,6},{5,7},{6,0},{7,1},{8,10},{9,11},{10,... | collective-permute-start | bytes 1056776 | tf_op jit(solution)/shard_map/ppermute | solution.py:44
  143.4 7.6 %collective-permute-done.20 = bf16[2,1376,128]{2,1,0:T(8,128)(2,1)S(1)} collective-permute-done((bf16[2,1376,128]{2,1,0:T(8,128)(2,1)S(1)}, bf16[2,1376,128]{2,1,0:T(8,128)(2,1)S(1)}, u32[]{:S(2)}, u32[]{:S(2)}) %collective-permute-start.20) | collective-permute-done | bytes 704544 | tf_op jit(solution)/shard_map/ppermute | solution.py:44
  151.0 0.7 collective-permute-done.21
  151.7 0.2 fusion.8
  151.9 1.2 collective-permute-start.22
  153.2 0.2 add_bitcast_fusion
  153.3 0.8 collective-permute-start.18
  154.1 9.5 %collective-permute-done.22 = bf16[1376,128]{1,0:T(8,128)(2,1)S(1)} collective-permute-done((bf16[1376,128]{1,0:T(8,128)(2,1)S(1)}, bf16[1376,128]{1,0:T(8,128)(2,1)S(1)}, u32[]{:S(2)}, u32[]{:S(2)}) %collective-permute-start.22) | collective-permute-done | bytes 352288 | tf_op jit(solution)/shard_map/ppermute | solution.py:44
  163.6 0.2 bitcast_add_fusion
  163.8 1.4 collective-permute-done.17
  165.2 0.8 collective-permute-done.18
  166.0 1.1 fusion.9
  (28 shorter events, 0.1 us)
Async XLA Ops:
  0.6 12.0 %copy-start.6 = (f32[512]{0:T(512)S(1)}, f32[512]{0:T(512)}, u32[]{:S(2)}) copy-start(f32[512]{0:T(512)} %param.14) | copy-start | bytes 6148
  0.6 24.3 %collective-permute-start = (bf16[1368,512]{1,0:T(8,128)(2,1)}, bf16[1368,512]{1,0:T(8,128)(2,1)S(1)}, u32[]{:S(2)}, u32[]{:S(2)}) collective-permute-start(bf16[1368,512]{1,0:T(8,128)(2,1)} %bitcast.38), channel_id=1, source_target_pairs={{0,1},{1,0},{2,3},{3,2},{4,5},{5,4},{6,7},{7,6},{8,9},{9,8},{10,11... | collective-permute-start | bytes 4202504 | tf_op jit(solution)/shard_map/ppermute | solution.py:44
  0.7 24.2 %collective-permute-start.1 = (bf16[1368,512]{1,0:T(8,128)(2,1)}, bf16[1368,512]{1,0:T(8,128)(2,1)S(1)}, u32[]{:S(2)}, u32[]{:S(2)}) collective-permute-start(bf16[1368,512]{1,0:T(8,128)(2,1)} %bitcast.43), channel_id=1, source_target_pairs={{0,1},{1,0},{2,3},{3,2},{4,5},{5,4},{6,7},{7,6},{8,9},{9,8},{10,11... | collective-permute-start | bytes 4202504 | tf_op jit(solution)/shard_map/ppermute | solution.py:44
  3.1 21.8 %all-to-all-start = ((bf16[16,64,128]{2,1,0:T(8,128)(2,1)}), bf16[16,64,128]{2,1,0:T(8,128)(2,1)S(1)}, u32[]{:S(2)}, u32[]{:S(2)}) async-start(bf16[16,64,128]{2,1,0:T(8,128)(2,1)} %prep.1), calls=%async_computation | async-start | bytes 524288 | tf_op jit(solution)/shard_map/all_to_all | solution.py:307
  12.7 1.2 collective-permute-start.2
  24.9 0.7 copy-start.8
  25.6 38.9 %copy-start.2 = (bf16[1368,512]{1,0:T(8,128)(2,1)}, bf16[1368,512]{1,0:T(8,128)(2,1)S(1)}, u32[]{:S(2)}) copy-start(bf16[1368,512]{1,0:T(8,128)(2,1)S(1)} %collective-permute-done.1.refs_12_) | copy-start | bytes 4202500
  45.1 19.4 %copy-start.7 = (bf16[128,512]{1,0:T(8,128)(2,1)S(1)}, bf16[128,512]{1,0:T(8,128)(2,1)}, u32[]{:S(2)}) copy-start(bf16[128,512]{1,0:T(8,128)(2,1)} %start_ref.1) | copy-start | bytes 393220
  64.5 3.0 %collective-permute-start.3 = (bf16[8,128,512]{2,1,0:T(8,128)(2,1)}, bf16[8,128,512]{2,1,0:T(8,128)(2,1)}, u32[]{:S(2)}, u32[]{:S(2)}) collective-permute-start(bf16[8,128,512]{2,1,0:T(8,128)(2,1)} %all_to_all.16.mixed_hbm), channel_id=1, source_target_pairs={{0,1},{1,0},{2,3},{3,2},{4,5},{5,4},{6,7},{7,6},{8,9},{9,8},{10,11... | collective-permute-start | bytes 3145736 | tf_op jit(solution)/shard_map/ppermute | solution.py:44
  71.1 35.5 %copy-start = (bf16[512,1368]{0,1:T(8,128)(2,1)S(1)}, bf16[512,1368]{0,1:T(8,128)(2,1)}, u32[]{:S(2)}) copy-start(bf16[512,1368]{0,1:T(8,128)(2,1)} %param.15) | copy-start | bytes 4202500
  71.1 3.0 %collective-permute-start.4 = (bf16[128,512]{1,0:T(8,128)(2,1)}, bf16[128,512]{1,0:T(8,128)(2,1)S(1)}, u32[]{:S(2)}, u32[]{:S(2)}) collective-permute-start(bf16[128,512]{1,0:T(8,128)(2,1)} %out_proj.3), channel_id=1, source_target_pairs={{0,16},{1,0},{2,18},{3,2},{4,20},{5,4},{6,22},{7,6},{8,24},{9,8},{... | collective-permute-start | bytes 393224 | tf_op jit(solution)/shard_map/ppermute | solution.py:336
  71.2 2.8 %collective-permute-start.5 = (bf16[128,512]{1,0:T(8,128)(2,1)}, bf16[128,512]{1,0:T(8,128)(2,1)S(1)}, u32[]{:S(2)}, u32[]{:S(2)}) collective-permute-start(bf16[128,512]{1,0:T(8,128)(2,1)} %out_proj.3), channel_id=1, source_target_pairs={{1,16},{3,18},{5,20},{7,22},{9,24},{11,26},{13,28},{15,30},{16,1},... | collective-permute-start | bytes 393224 | tf_op jit(solution)/shard_map/ppermute | solution.py:337
  75.0 15.1 %collective-permute-start.9 = (bf16[2,128,512]{2,1,0:T(8,128)(2,1)S(1)}, bf16[2,128,512]{2,1,0:T(8,128)(2,1)S(1)}, u32[]{:S(2)}, u32[]{:S(2)}) collective-permute-start(bf16[2,128,512]{2,1,0:T(8,128)(2,1)S(1)} %pad_maximum_fusion.refs_0_), channel_id=1, source_target_pairs={{0,64},{1,65},{2,66},{3,67},{4,68},{5,69},{6,70},{7,71},{8,72},{9,... | collective-permute-start | bytes 786440 | tf_op jit(solution)/shard_map/ppermute | solution.py:44
  75.6 15.4 %collective-permute-start.7 = (bf16[2,128,512]{2,1,0:T(8,128)(2,1)S(1)}, bf16[2,128,512]{2,1,0:T(8,128)(2,1)}, u32[]{:S(2)}, u32[]{:S(2)}) collective-permute-start(bf16[2,128,512]{2,1,0:T(8,128)(2,1)S(1)} %pad_maximum_fusion.refs_0_), channel_id=1, source_target_pairs={{0,192},{1,193},{2,194},{3,195},{4,196},{5,197},{6,198},{7,199},{8... | collective-permute-start | bytes 786440 | tf_op jit(solution)/shard_map/ppermute | solution.py:44
  79.2 16.4 %collective-permute-start.13 = (bf16[2,128,512]{2,1,0:T(8,128)(2,1)S(1)}, bf16[2,128,512]{2,1,0:T(8,128)(2,1)S(1)}, u32[]{:S(2)}, u32[]{:S(2)}) collective-permute-start(bf16[2,128,512]{2,1,0:T(8,128)(2,1)S(1)} %pad_maximum_fusion.refs_0_), channel_id=1, source_target_pairs={{0,32},{1,33},{2,34},{3,35},{4,36},{5,37},{6,38},{7,39},{8,40},{9,... | collective-permute-start | bytes 786440 | tf_op jit(solution)/shard_map/ppermute | solution.py:44
  79.6 19.8 %collective-permute-start.6 = (bf16[2,128,512]{2,1,0:T(8,128)(2,1)S(1)}, bf16[2,128,512]{2,1,0:T(8,128)(2,1)}, u32[]{:S(2)}, u32[]{:S(2)}) collective-permute-start(bf16[2,128,512]{2,1,0:T(8,128)(2,1)S(1)} %pad_maximum_fusion.refs_0_), channel_id=1, source_target_pairs={{0,224},{1,225},{2,226},{3,227},{4,228},{5,229},{6,230},{7,231},{8... | collective-permute-start | bytes 786440 | tf_op jit(solution)/shard_map/ppermute | solution.py:44
  90.8 11.7 %collective-permute-start.10 = (bf16[128,512]{1,0:T(8,128)(2,1)}, bf16[128,512]{1,0:T(8,128)(2,1)S(1)}, u32[]{:S(2)}, u32[]{:S(2)}) collective-permute-start(bf16[128,512]{1,0:T(8,128)(2,1)} %slice_bitcast_fusion.1), channel_id=1, source_target_pairs={{0,64},{1,65},{2,66},{3,67},{4,68},{5,69},{6,70},{7,71},{8,72},{9,... | collective-permute-start | bytes 393224 | tf_op jit(solution)/shard_map/ppermute | solution.py:44
  90.8 15.8 %collective-permute-start.12 = (bf16[2,128,512]{2,1,0:T(8,128)(2,1)S(1)}, bf16[2,128,512]{2,1,0:T(8,128)(2,1)}, u32[]{:S(2)}, u32[]{:S(2)}) collective-permute-start(bf16[2,128,512]{2,1,0:T(8,128)(2,1)S(1)} %collective-permute-done.9.refs_7_), channel_id=1, source_target_pairs={{0,32},{1,33},{2,34},{3,35},{4,36},{5,37},{6,38},{7,39},{8,40},{9,... | collective-permute-start | bytes 786440 | tf_op jit(solution)/shard_map/ppermute | solution.py:44
  91.0 15.5 %collective-permute-start.8 = (bf16[2,128,512]{2,1,0:T(8,128)(2,1)}, bf16[2,128,512]{2,1,0:T(8,128)(2,1)}, u32[]{:S(2)}, u32[]{:S(2)}) collective-permute-start(bf16[2,128,512]{2,1,0:T(8,128)(2,1)} %collective-permute-done.7.refs_2_), channel_id=1, source_target_pairs={{0,224},{1,225},{2,226},{3,227},{4,228},{5,229},{6,230},{7,231},{8... | collective-permute-start | bytes 786440 | tf_op jit(solution)/shard_map/ppermute | solution.py:44
  95.6 0.7 copy-start.4
  96.3 9.4 %collective-permute-start.11 = (bf16[128,512]{1,0:T(8,128)(2,1)}, bf16[128,512]{1,0:T(8,128)(2,1)}, u32[]{:S(2)}, u32[]{:S(2)}) collective-permute-start(bf16[128,512]{1,0:T(8,128)(2,1)} %slice_bitcast_fusion), channel_id=1, source_target_pairs={{0,192},{1,193},{2,194},{3,195},{4,196},{5,197},{6,198},{7,199},{8... | collective-permute-start | bytes 393224 | tf_op jit(solution)/shard_map/ppermute | solution.py:44
  99.3 13.9 %copy-start.1 = (bf16[512,1368]{0,1:T(8,128)(2,1)S(1)}, bf16[512,1368]{0,1:T(8,128)(2,1)}, u32[]{:S(2)}) copy-start(bf16[512,1368]{0,1:T(8,128)(2,1)} %param.16) | copy-start | bytes 4202500
  99.3 13.9 %copy-start.3 = (bf16[1368,512]{1,0:T(8,128)(2,1)S(1)}, bf16[1368,512]{1,0:T(8,128)(2,1)}, u32[]{:S(2)}) copy-start(bf16[1368,512]{1,0:T(8,128)(2,1)} %copy-done.2) | copy-start | bytes 4202500
  106.6 1.0 copy-start.5
  110.2 28.2 %collective-permute-start.15 = (bf16[2,1376,128]{2,1,0:T(8,128)(2,1)S(1)}, bf16[2,1376,128]{2,1,0:T(8,128)(2,1)S(1)}, u32[]{:S(2)}, u32[]{:S(2)}) collective-permute-start(bf16[2,1376,128]{2,1,0:T(8,128)(2,1)S(1)} %mlp.11), channel_id=1, source_target_pairs={{0,8},{1,9},{2,10},{3,11},{4,12},{5,13},{6,14},{7,15},{8,0},{9,1},... | collective-permute-start | bytes 2113544 | tf_op jit(solution)/shard_map/ppermute | solution.py:44
  116.4 24.6 %collective-permute-start.19 = (bf16[2,1376,128]{2,1,0:T(8,128)(2,1)S(1)}, bf16[2,1376,128]{2,1,0:T(8,128)(2,1)S(1)}, u32[]{:S(2)}, u32[]{:S(2)}) collective-permute-start(bf16[2,1376,128]{2,1,0:T(8,128)(2,1)S(1)} %mlp.13), channel_id=1, source_target_pairs={{0,4},{1,5},{2,6},{3,7},{4,0},{5,1},{6,2},{7,3},{8,12},{9,13},{10,... | collective-permute-start | bytes 2113544 | tf_op jit(solution)/shard_map/ppermute | solution.py:44
  121.9 29.1 %collective-permute-start.20 = (bf16[2,1376,128]{2,1,0:T(8,128)(2,1)S(1)}, bf16[2,1376,128]{2,1,0:T(8,128)(2,1)S(1)}, u32[]{:S(2)}, u32[]{:S(2)}) collective-permute-start(bf16[2,1376,128]{2,1,0:T(8,128)(2,1)S(1)} %mlp.14), channel_id=1, source_target_pairs={{0,2},{1,3},{2,4},{3,5},{4,6},{5,7},{6,0},{7,1},{8,10},{9,11},{10,... | collective-permute-start | bytes 2113544 | tf_op jit(solution)/shard_map/ppermute | solution.py:44
  126.2 25.5 %collective-permute-start.21 = (bf16[2,1376,128]{2,1,0:T(8,128)(2,1)S(1)}, bf16[2,1376,128]{2,1,0:T(8,128)(2,1)S(1)}, u32[]{:S(2)}, u32[]{:S(2)}) collective-permute-start(bf16[2,1376,128]{2,1,0:T(8,128)(2,1)S(1)} %mlp.15), channel_id=1, source_target_pairs={{0,6},{1,7},{2,0},{3,1},{4,2},{5,3},{6,4},{7,5},{8,14},{9,15},{10,... | collective-permute-start | bytes 2113544 | tf_op jit(solution)/shard_map/ppermute | solution.py:44
  129.6 23.6 %collective-permute-start.14 = (bf16[2,1376,128]{2,1,0:T(8,128)(2,1)S(1)}, bf16[2,1376,128]{2,1,0:T(8,128)(2,1)S(1)}, u32[]{:S(2)}, u32[]{:S(2)}) collective-permute-start(bf16[2,1376,128]{2,1,0:T(8,128)(2,1)S(1)} %mlp.9), channel_id=1, source_target_pairs={{0,8},{1,9},{2,10},{3,11},{4,12},{5,13},{6,14},{7,15},{8,0},{9,1},... | collective-permute-start | bytes 2113544 | tf_op jit(solution)/shard_map/ppermute | solution.py:44
  138.6 25.2 %collective-permute-start.16 = (bf16[1376,128]{1,0:T(8,128)(2,1)S(1)}, bf16[1376,128]{1,0:T(8,128)(2,1)S(1)}, u32[]{:S(2)}, u32[]{:S(2)}) collective-permute-start(bf16[1376,128]{1,0:T(8,128)(2,1)S(1)} %get-tuple-element.16), channel_id=1, source_target_pairs={{0,4},{1,5},{2,6},{3,7},{4,0},{5,1},{6,2},{7,3},{8,12},{9,13},{10,... | collective-permute-start | bytes 1056776 | tf_op jit(solution)/shard_map/ppermute | solution.py:44
  141.0 24.2 %collective-permute-start.17 = (bf16[1376,128]{1,0:T(8,128)(2,1)S(1)}, bf16[1376,128]{1,0:T(8,128)(2,1)S(1)}, u32[]{:S(2)}, u32[]{:S(2)}) collective-permute-start(bf16[1376,128]{1,0:T(8,128)(2,1)S(1)} %get-tuple-element.17), channel_id=1, source_target_pairs={{0,2},{1,3},{2,4},{3,5},{4,6},{5,7},{6,0},{7,1},{8,10},{9,11},{10,... | collective-permute-start | bytes 1056776 | tf_op jit(solution)/shard_map/ppermute | solution.py:44
  151.9 11.7 %collective-permute-start.22 = (bf16[1376,128]{1,0:T(8,128)(2,1)S(1)}, bf16[1376,128]{1,0:T(8,128)(2,1)S(1)}, u32[]{:S(2)}, u32[]{:S(2)}) collective-permute-start(bf16[1376,128]{1,0:T(8,128)(2,1)S(1)} %fusion.8), channel_id=1, source_target_pairs={{0,8},{1,9},{2,10},{3,11},{4,12},{5,13},{6,14},{7,15},{8,0},{9,1},... | collective-permute-start | bytes 1056776 | tf_op jit(solution)/shard_map/ppermute | solution.py:44
  153.3 12.7 %collective-permute-start.18 = (bf16[1376,128]{1,0:T(8,128)(2,1)S(1)}, bf16[1376,128]{1,0:T(8,128)(2,1)S(1)}, u32[]{:S(2)}, u32[]{:S(2)}) collective-permute-start(bf16[1376,128]{1,0:T(8,128)(2,1)S(1)} %get-tuple-element.15), channel_id=1, source_target_pairs={{0,6},{1,7},{2,0},{3,1},{4,2},{5,3},{6,4},{7,5},{8,14},{9,15},{10,... | collective-permute-start | bytes 1056776 | tf_op jit(solution)/shard_map/ppermute | solution.py:44

commit v3 on v2

--- a/solution.py
+++ b/solution.py
@@ -20,6 +20,7 @@
 FF_LOC = 1368
 FF_PAD = 1376
 EPS = 1e-06
+NEAR = 5
 PLANE_GROUPS = [[xh * 8 + y * 2 + k for xh in range(2) for y in range(4)] for k in range(2)]
 
 
@@ -173,46 +174,47 @@
     return jnp.concatenate([rows, tail], axis=0).astype(BF16)
 
 
-def mlp_kernel(slots, with_squares, idx_ref, *refs):
-    blocks, (gain_ref, gain_oth_ref, w_ref, wx_ref) = refs[:9], refs[9:13]
-    n = len(slots)
-    out_ref, rows_in, so, sx, row_sem = refs[13:]
-
-    def halves(d):
-        if d == 4:
-            return blocks[4], blocks[5]
-        whole_block = blocks[d if d < 4 else d + 1]
-        return whole_block.at[0], whole_block.at[1]
-
-    def row_copy(d, at, part):
-        return pltpu.make_async_copy(halves(d)[part], rows_in.at[at, part], row_sem.at[at, part])
-
+def scale_kernel(n, *refs):
+    blocks, (gain_ref, gain_oth_ref, out_ref, tail_ref) = refs[:-4], refs[-4:]
+    halves = []
+    for ref in blocks:
+        halves += [ref.at[0], ref.at[1]] if len(ref.shape) == 3 else [ref]
+    for i in range(n):
+        own = halves[2 * i][...].astype(F32)
+        oth = halves[2 * i + 1][...].astype(F32)
+        out_ref[i, 0] = (own * gain_ref[...]).astype(BF16)
+        out_ref[i, 1] = (oth * gain_oth_ref[...]).astype(BF16)
+        tail_ref[i] = two_rows(square_sums(own) + square_sums(oth))
+
+
+def mlp_kernel(groups, with_squares, idx_ref, near_ref, far_ref, near_tail_ref, far_tail_ref, *refs):
+    w_ref, wx_ref = refs[:2]
+    out_refs = refs[2:-3]
+    so, sx, tail = refs[-3:]
+    slots = [slot for group in groups for slot in group]
     for at, slot in enumerate(slots):
         which = idx_ref[slot]
-        for d in range(8):
-
-            @pl.when(which == d)
-            def _():
-                row_copy(d, at, 0).start()
-                row_copy(d, at, 1).start()
-    tails = []
-    for at in range(n):
-        row_copy(0, at, 0).wait()
-        row_copy(0, at, 1).wait()
-        own = rows_in[at, 0].astype(F32)
-        oth = rows_in[at, 1].astype(F32)
         span = slice(at * ROWS, at * ROWS + ROWS)
-        so[span, :] = (own * gain_ref[...]).astype(BF16)
-        sx[span, :] = (oth * gain_oth_ref[...]).astype(BF16)
-        if with_squares:
-            tails.append(two_rows(square_sums(own) + square_sums(oth)))
-        else:
-            tails.append(jnp.zeros((FF_PAD - FF_LOC, ROWS), F32))
-    for at in range(0, n, 2):
-        span = slice(at * ROWS, at * ROWS + 2 * ROWS)
-        res = dot_nt(w_ref[...], so[span, :]) + dot_nt(wx_ref[...], sx[span, :])
-        out_ref[at] = with_tail(res[:, :ROWS], tails[at])
-        out_ref[at + 1] = with_tail(res[:, ROWS:], tails[at + 1])
+
+        @pl.when(which < NEAR)
+        def _():
+            so[span, :] = near_ref[which, 0]
+            sx[span, :] = near_ref[which, 1]
+            tail[at] = near_tail_ref[which]
+
+        @pl.when(which >= NEAR)
+        def _():
+            so[span, :] = far_ref[which - NEAR, 0]
+            sx[span, :] = far_ref[which - NEAR, 1]
+            tail[at] = far_tail_ref[which - NEAR]
+
+    res = dot_nt(w_ref[...], so[...]) + dot_nt(wx_ref[...], sx[...])
+    at = 0
+    for group, out_ref in zip(groups, out_refs):
+        for i in range(len(group)):
+            end = tail[at] if with_squares else jnp.zeros((FF_PAD - FF_LOC, ROWS), F32)
+            out_ref[i] = with_tail(res[:, at * ROWS : at * ROWS + ROWS], end)
+            at += 1
 
 
 def params(mib):
@@ -267,25 +269,39 @@
     )(core, mixed, w_out, start)
 
 
-def mlp_part(slots, with_squares, idx, blocks, gains, weights):
-    n = len(slots)
+def scale(blocks, gains, n):
+    return pl.pallas_call(
+        functools.partial(scale_kernel, n),
+        out_shape=[
+            jax.ShapeDtypeStruct((n, 2, ROWS, CH), BF16),
+            jax.ShapeDtypeStruct((n, 8, ROWS), F32),
+        ],
+        compiler_params=params(24),
+        cost_estimate=pl.CostEstimate(
+            flops=8 * n * ROWS * CH * 8, bytes_accessed=n << 19, transcendentals=0
+        ),
+        name="scale",
+    )(*blocks, *gains)
+
+
+def mlp_part(groups, with_squares, idx, rows, weights):
+    n = sum(len(group) for group in groups)
     vmem = pl.BlockSpec(memory_space=pltpu.VMEM)
     return pl.pallas_call(
-        functools.partial(mlp_kernel, tuple(slots), with_squares),
-        out_shape=jax.ShapeDtypeStruct((n, FF_PAD, ROWS), BF16),
-        in_specs=[in_smem()] + [anywhere()] * 9 + [vmem] * 4,
+        functools.partial(mlp_kernel, groups, with_squares),
+        out_shape=[jax.ShapeDtypeStruct((len(g), FF_PAD, ROWS), BF16) for g in groups],
+        in_specs=[in_smem()] + [vmem] * 6,
         scratch_shapes=[
-            pltpu.VMEM((n, 2, ROWS, CH), BF16),
             pltpu.VMEM((n * ROWS, CH), BF16),
             pltpu.VMEM((n * ROWS, CH), BF16),
-            pltpu.SemaphoreType.DMA((n, 2)),
+            pltpu.VMEM((n, 8, ROWS), F32),
         ],
         compiler_params=params(24),
         cost_estimate=pl.CostEstimate(
             flops=4 * n * ROWS * CH * FF_LOC, bytes_accessed=5 << 20, transcendentals=0
         ),
         name="mlp",
-    )(idx, *blocks, *gains, *weights)
+    )(idx, *rows, *weights)
 
 
 def shards(residual, features, filters, skip_gain, w_out, norm_gain, w_gate, w_up):
@@ -338,38 +354,31 @@
     here = x_lo == core
     held = jnp.stack([jnp.where(here, stream, first), jnp.where(here, first, second)])
     below, above = [held], [held]
-    for step in (1, 2):
-        below.append(shift(held, z=step))
-        above.append(shift(held, z=-step))
+    for step in (2, 1):
+        below.insert(1, shift(held, z=step))
+        above.insert(1, shift(held, z=-step))
     below.append(shift(below[2], z=1))
     above.append(shift(above[2], z=-1))
     opposite = (shift(below[2][0], z=2), shift(above[2][1], z=-2))
-    blocks = above + list(opposite) + [below[3], below[2], below[1]]
+    gains = (gain, gain_oth)
+    near, near_tail = scale([held, above[1], above[2], below[2], below[1]], gains, NEAR)
+    far, far_tail = scale([above[3], *opposite, below[3]], gains, 8 - NEAR)
+    rows = (near, far, near_tail, far_tail)
 
     z = ctx // 2
-    idx = jnp.stack(
-        [
-            (4 * ((x_hi + a) % 2) + (y + b) % 4 - z) % 8
-            for b in range(4)
-            for a in range(2)
-        ]
-    ).astype(jnp.int32)
-    part = functools.partial(
-        mlp_part, idx=idx, blocks=blocks, gains=(gain, gain_oth)
-    )
+    order = []
+    for b in range(4):
+        for a in range(2):
+            d = (4 * ((x_hi + a) % 2) + (y + b) % 4 - z) % 8
+            order.append(jnp.where(d <= 2, d, jnp.where(d >= 6, d - 3, d + 2)))
+    idx = jnp.stack(order).astype(jnp.int32)
     gate_w, up_w = (wg, wg_oth), (wu, wu_oth)
 
-    g_send_a = part((5, 3), False, weights=gate_w)
-    idx_up, g_send_a = lax.optimization_barrier((idx, g_send_a))
-    g_recv_a = shift(g_send_a, x=2)
-    part_up = functools.partial(part, idx=idx_up)
-    u_sends = {b: part_up((2 * b, 2 * b + 1), True, weights=up_w) for b in (2, 1, 3)}
-    u_recv = {b: shift(u_sends[b], y=b) for b in (2, 1, 3)}
-    g_send_b = part((7, 1), False, weights=gate_w)
-    g_recv_b = shift(g_send_b, x=2)
-    g_keep_a = part((4, 2), False, weights=gate_w)
-    g_keep_b = part((6, 0), False, weights=gate_w)
-    u_keep = part((0, 1), True, weights=up_w)
+    def gate_part(*groups):
+        return mlp_part(groups, False, idx, rows, gate_w)
+
+    def up_part(*groups):
+        return mlp_part(groups, True, idx, rows, up_w)
 
     def add(*terms):
         total = terms[0].astype(F32)
@@ -377,21 +386,30 @@
             total = total + term.astype(F32)
         return total
 
-    g_last = [
-        shift(add(g_keep_a[0], g_recv_a[0]).astype(BF16), y=2),
-        shift(add(g_keep_a[1], g_recv_a[1]).astype(BF16), y=1),
-        shift(add(g_keep_b[0], g_recv_b[0]).astype(BF16), y=3),
-    ]
-    g_own = add(g_keep_b[1], g_recv_b[1])
-    u_send = add(u_keep[1], *(u_recv[b][1] for b in (2, 1, 3))).astype(BF16)
-    u_last = shift(u_send, x=2)
-    u_own = add(u_keep[0], *(u_recv[b][0] for b in (2, 1, 3)))
-    gate = add(g_own, *g_last)
-    up = add(u_own, u_last)
+    (u_plus,) = up_part((4, 3))
+    u_plus = shift(u_plus, y=1)
+    (u_minus,) = up_part((5, 6))
+    u_minus = shift(u_minus, y=-1)
+    (g_send_a,) = gate_part((5, 1))
+    g_recv_a = shift(g_send_a, x=2)
+    (g_send_b,) = gate_part((3, 7))
+    g_recv_b = shift(g_send_b, x=2)
+    (u_pair,) = up_part((2, 7))
+    (g_keep_a,) = gate_part((4, 0))
+    (g_keep_b,) = gate_part((2, 6))
+    (u_keep,) = up_part((0, 1))
+    u_plus_2 = shift(add(u_pair[0], u_plus[0]).astype(BF16), y=1)
+    u_minus_2 = shift(add(u_pair[1], u_minus[0]).astype(BF16), y=-1)
+    g_last_2 = shift(add(g_keep_a[0], g_recv_a[0]).astype(BF16), y=2)
+    g_last_1 = shift(add(g_keep_b[0], g_recv_b[0]).astype(BF16), y=1)
+    g_last_3 = shift(add(g_keep_b[1], g_recv_b[1]).astype(BF16), y=-1)
+    u_last = shift(add(u_keep[1], u_plus[1], u_minus_2).astype(BF16), x=2)
+    up = add(u_keep[0], u_plus_2, u_minus[1], u_last)
+    gate = add(g_keep_a[1], g_recv_a[1], g_last_1, g_last_2, g_last_3)
     sums = up[FF_LOC : FF_LOC + 1] + up[FF_LOC + 1 : FF_LOC + 2]
-    scale = lax.rsqrt(sums * (1.0 / (N_TP * CH)) + EPS)
-    gate_vals = gate[:FF_LOC] * scale
-    up_vals = up[:FF_LOC] * scale
+    row_scale = lax.rsqrt(sums * (1.0 / (N_TP * CH)) + EPS)
+    gate_vals = gate[:FF_LOC] * row_scale
+    up_vals = up[:FF_LOC] * row_scale
     hidden_t = (jax.nn.silu(gate_vals) * up_vals).astype(BF16)
     return stream, hidden_t.T
 

time: 170 us -> 175 us (1.029)
  the two profiles are of different devices: /device:TPU:24 before, /device:TPU:1 now
where the time goes in v3:
time: 175 us
  waiting for transfers between devices  64.4 us (37%)
  starting transfers between devices  40.4 us (23%)
  blocking collectives  32.2 us (18%)
  Pallas kernels  29.8 us (17%)
  local copies, waits for them, and re-layouts  4.83 us (3%)
  other arithmetic  2.08 us (1%)
    ppermute x22, waiting for transfers between devices, shift(): return lax.ppermute(arr, AXES, pairs)  50.6 us
    ppermute x22, starting transfers between devices, shift(): return lax.ppermute(arr, AXES, pairs)  30.8 us
    all_to_all x1, blocking collectives, shards(): lax.all_to_all(copies, 'tp', 0, 0, axis_index_groups=PLANE_GROUPS, tiled=...  19.5 us
    all_to_all x1, blocking collectives, shards(): conv_rows = lax.all_to_all(conv, 'ctx', 0, 0, tiled=True)  12.7 us
    pallas_call x8, Pallas kernels, mlp_part(): pl.pallas_call(functools.partial(mlp_kernel, groups, with_squares), out_s...  12.3 us
    all_to_all x1, waiting for transfers between devices, shards(): recv = lax.all_to_all(sent, 'ctx', 0, 0, tiled=True)  9.32 us
    all_to_all x1, starting transfers between devices, shards(): recv = lax.all_to_all(sent, 'ctx', 0, 0, tiled=True)  7.48 us
    pallas_call x2, Pallas kernels, out_proj(): pl.pallas_call(functools.partial(out_proj_kernel, offset), out_shape=jax....  6.4 us
  transfers between devices with their start and end apart: 25, of which 14 were waited for; matrix products, arithmetic and copies ran while one was open for 2% of the time, Pallas kernels for 9%

profile of v3, /device:TPU:1, one launch (start us, length us, event | category | flops | bytes accessed | tf_op | source)
XLA Modules:
  0.0 174.7 jit_solution(1538417268758182296)
XLA Ops:
  0.6 3.3 %collective-permute-start = (bf16[1368,512]{1,0:T(8,128)(2,1)}, bf16[1368,512]{1,0:T(8,128)(2,1)S(1)}, u32[]{:S(2)}, u32[]{:S(2)}) collective-permute-start(bf16[1368,512]{1,0:T(8,128)(2,1)} %bitcast.57), channel_id=1, source_target_pairs={{0,1},{1,0},{2,3},{3,2},{4,5},{5,4},{6,7},{7,6},{8,9},{9,8},{10,11... | collective-permute-start | bytes 4202504 | tf_op jit(solution)/shard_map/ppermute | solution.py:45
  4.0 0.1 collective-permute-start.1
  4.1 1.9 %prep.1 = bf16[16,64,128]{2,1,0:T(8,128)(2,1)} custom-call(bf16[3,128,512]{2,1,0:T(8,128)(2,1)} %bitcast.65, f32[128,512]{1,0:T(8,128)} %filt_ref.1), custom_call_target="tpu_custom_call" | custom-call | tf_op jit(solution)/shard_map/prep/pallas_call | solution.py:317
  6.0 7.5 %all-to-all-start = ((bf16[16,64,128]{2,1,0:T(8,128)(2,1)}), bf16[16,64,128]{2,1,0:T(8,128)(2,1)S(1)}, u32[]{:S(2)}, u32[]{:S(2)}) async-start(bf16[16,64,128]{2,1,0:T(8,128)(2,1)} %prep.1), calls=%async_computation | async-start | bytes 524288 | tf_op jit(solution)/shard_map/all_to_all | solution.py:323
  13.5 0.8 collective-permute-start.2
  14.3 0.8 collective-permute-done.2.refs_6_.refs_5_
  15.1 9.3 %all-to-all-done.x_ref = bf16[16,64,128]{2,1,0:T(8,128)(2,1)S(1)} async-done(((bf16[16,64,128]{2,1,0:T(8,128)(2,1)}), bf16[16,64,128]{2,1,0:T(8,128)(2,1)S(1)}, u32[]{:S(2)}, u32[]{:S(2)}) %all-to-all-start) | async-done | bytes 262176 | tf_op jit(solution)/shard_map/all_to_all | solution.py:323
  24.4 0.7 copy-done.8
  25.1 3.5 %conv.1 = bf16[16,32,128]{2,1,0:T(8,128)(2,1)} custom-call(bf16[16,64,128]{2,1,0:T(8,128)(2,1)} %copy-done.8, bf16[128,1024]{1,0:T(8,128)(2,1)} %constant.164.clone.tab_ref), custom_call_target="tpu_custom_call" | custom-call | tf_op jit(solution)/shard_map/conv/pallas_call | solution.py:325
  28.6 12.7 %all_to_all.15.conv_ref = bf16[16,32,128]{2,1,0:T(8,128)(2,1)} all-to-all(bf16[16,32,128]{2,1,0:T(8,128)(2,1)} %conv.1), channel_id=1, replica_groups=mesh['ctx'=16,'tp'=16] {'ctx'}, dimensions={0} | all-to-all | bytes 262144 | tf_op jit(solution)/shard_map/all_to_all | solution.py:336
  41.3 2.2 %mix.1 = bf16[8,128,512]{2,1,0:T(8,128)(2,1)} custom-call(bf16[16,32,128]{2,1,0:T(8,128)(2,1)} %all_to_all.15.conv_ref, bf16[3,128,512]{2,1,0:T(8,128)(2,1)} %bitcast.66, f32[1,512]{1,0:T(1,128)} %bitcast.67), custom_call_target="tpu_custom_call" | custom-call | tf_op jit(solution)/shard_map/mix/pallas_call | solution.py:337
  43.5 19.5 %all_to_all.16.mixed_hbm = bf16[8,128,512]{2,1,0:T(8,128)(2,1)} all-to-all(bf16[8,128,512]{2,1,0:T(8,128)(2,1)} %mix.1), channel_id=1, replica_groups={{0,2,4,6,8,10,12,14},{1,3,5,7,9,11,13,15},{16,18,20,22,24,26,28,30},{17..., dimensions={0} | all-to-all | bytes 2097152 | tf_op jit(solution)/shard_map/all_to_all | solution.py:344
  63.0 5.2 %collective-permute-start.3 = (bf16[8,128,512]{2,1,0:T(8,128)(2,1)}, bf16[8,128,512]{2,1,0:T(8,128)(2,1)}, u32[]{:S(2)}, u32[]{:S(2)}) collective-permute-start(bf16[8,128,512]{2,1,0:T(8,128)(2,1)} %all_to_all.16.mixed_hbm), channel_id=1, source_target_pairs={{0,1},{1,0},{2,3},{3,2},{4,5},{5,4},{6,7},{7,6},{8,9},{9,8},{10,11... | collective-permute-start | bytes 3145736 | tf_op jit(solution)/shard_map/ppermute | solution.py:45
  68.2 2.9 %out_proj.2.start_ref = f32[128,512]{1,0:T(8,128)S(1)} custom-call(s32[1]{0:T(128)} %bitcast.core_ref, bf16[8,128,512]{2,1,0:T(8,128)(2,1)} %all_to_all.16.mixed_hbm, bf16[8192,512]{1,0:T(8,128)(2,1)} %w_hbm.3, bf16[128,512]{1,0:T(8,128)(2,1)S(1)} %copy-done.6), custom_call_target="tpu_custom_call" | custom-call | flops 536870912 | bytes 5242880 | tf_op jit(solution)/shard_map/out_proj/pallas_call | solution.py:250
  71.1 3.5 %out_proj.3 = bf16[128,512]{1,0:T(8,128)(2,1)} custom-call(s32[1]{0:T(128)} %bitcast.core_ref, bf16[8,128,512]{2,1,0:T(8,128)(2,1)} %collective-permute-done.3.mixed_hbm, bf16[8192,512]{1,0:T(8,128)(2,1)} %w_hbm.3, f32[128,512]{1,0:T(8,128)S(1)} %out_proj.2.start_ref), custom_call_target="tpu_custom_call" | custom-call | flops 536870912 | bytes 5242880 | tf_op jit(solution)/shard_map/out_proj/pallas_call | solution.py:250
  74.7 0.2 collective-permute-start.4
  74.9 2.0 %collective-permute-start.5 = (bf16[128,512]{1,0:T(8,128)(2,1)}, bf16[128,512]{1,0:T(8,128)(2,1)S(1)}, u32[]{:S(2)}, u32[]{:S(2)}) collective-permute-start(bf16[128,512]{1,0:T(8,128)(2,1)} %out_proj.3), channel_id=1, source_target_pairs={{1,16},{3,18},{5,20},{7,22},{9,24},{11,26},{13,28},{15,30},{16,1},... | collective-permute-start | bytes 393224 | tf_op jit(solution)/shard_map/ppermute | solution.py:353
  76.9 1.9 %collective-permute-done.4 = bf16[128,512]{1,0:T(8,128)(2,1)S(1)} collective-permute-done((bf16[128,512]{1,0:T(8,128)(2,1)}, bf16[128,512]{1,0:T(8,128)(2,1)S(1)}, u32[]{:S(2)}, u32[]{:S(2)}) %collective-permute-start.4) | collective-permute-done | bytes 131104 | tf_op jit(solution)/shard_map/ppermute | solution.py:352
  78.8 2.6 %collective-permute-done.5 = bf16[128,512]{1,0:T(8,128)(2,1)S(1)} collective-permute-done((bf16[128,512]{1,0:T(8,128)(2,1)}, bf16[128,512]{1,0:T(8,128)(2,1)S(1)}, u32[]{:S(2)}, u32[]{:S(2)}) %collective-permute-start.5) | collective-permute-done | bytes 131104 | tf_op jit(solution)/shard_map/ppermute | solution.py:353
  81.4 0.4 collective-permute-start.8
  81.8 3.3 %collective-permute-start.7 = (bf16[2,128,512]{2,1,0:T(8,128)(2,1)S(1)}, bf16[2,128,512]{2,1,0:T(8,128)(2,1)}, u32[]{:S(2)}, u32[]{:S(2)}) collective-permute-start(bf16[2,128,512]{2,1,0:T(8,128)(2,1)S(1)} %pad_maximum_fusion.refs_0_), channel_id=1, source_target_pairs={{0,192},{1,193},{2,194},{3,195},{4,196},{5,197},{6,198},{7,199},{8... | collective-permute-start | bytes 786440 | tf_op jit(solution)/shard_map/ppermute | solution.py:45
  85.1 1.5 collective-permute-start.9
  86.5 10.2 %collective-permute-done.8.refs_3_ = bf16[2,128,512]{2,1,0:T(8,128)(2,1)S(1)} collective-permute-done((bf16[2,128,512]{2,1,0:T(8,128)(2,1)S(1)}, bf16[2,128,512]{2,1,0:T(8,128)(2,1)S(1)}, u32[]{:S(2)}, u32[]{:S(2)}) %collective-permute-start.8) | collective-permute-done | bytes 262176 | tf_op jit(solution)/shard_map/ppermute | solution.py:45
  96.7 0.7 slice_bitcast_fusion.3
  97.4 2.7 %collective-permute-start.10 = (bf16[2,128,512]{2,1,0:T(8,128)(2,1)}, bf16[2,128,512]{2,1,0:T(8,128)(2,1)}, u32[]{:S(2)}, u32[]{:S(2)}) collective-permute-start(bf16[2,128,512]{2,1,0:T(8,128)(2,1)} %collective-permute-done.7.refs_2_), channel_id=1, source_target_pairs={{0,224},{1,225},{2,226},{3,227},{4,228},{5,229},{6,230},{7,231},{8... | collective-permute-start | bytes 786440 | tf_op jit(solution)/shard_map/ppermute | solution.py:45
  100.0 1.6 slice_bitcast_fusion.2
  101.6 0.2 collective-permute-done.6.refs_1_
  101.8 0.7 copy-done.4
  102.5 2.2 %collective-permute-start.12 = (bf16[128,512]{1,0:T(8,128)(2,1)}, bf16[128,512]{1,0:T(8,128)(2,1)}, u32[]{:S(2)}, u32[]{:S(2)}) collective-permute-start(bf16[128,512]{1,0:T(8,128)(2,1)} %slice_bitcast_fusion.2), channel_id=1, source_target_pairs={{0,192},{1,193},{2,194},{3,195},{4,196},{5,197},{6,198},{7,199},{8... | collective-permute-start | bytes 393224 | tf_op jit(solution)/shard_map/ppermute | solution.py:45
  104.7 0.1 stack.44.idx_ref
  104.8 1.1 copy-done.5
  105.9 1.9 %scale.2 = (bf16[5,2,128,512]{3,2,1,0:T(8,128)(2,1)S(1)}, f32[5,8,128]{2,1,0:T(8,128)S(1)}) custom-call(bf16[2,128,512]{2,1,0:T(8,128)(2,1)S(1)} %pad_maximum_fusion.refs_0_, bf16[2,128,512]{2,1,0:T(8,128)(2,1)S(1)} %copy-done.5, bf16[2,128,512]{2,1,0:T(8,128)(2,1)} %collective-permute-done.7.refs_2_, ...), custom_call_target="tpu_custom_call" | custom-call | flops 20971520 | bytes 2621440 | tf_op jit(solution)/shard_map/scale/pallas_call | solution.py:273
  107.7 3.9 %collective-permute-done.12.refs_2_ = bf16[128,512]{1,0:T(8,128)(2,1)} collective-permute-done((bf16[128,512]{1,0:T(8,128)(2,1)}, bf16[128,512]{1,0:T(8,128)(2,1)}, u32[]{:S(2)}, u32[]{:S(2)}) %collective-permute-start.12) | collective-permute-done | bytes 131104 | tf_op jit(solution)/shard_map/ppermute | solution.py:45
  111.6 1.7 scale.3
  113.3 1.5 mlp.14
  114.9 1.5 mlp.15
  116.4 0.1 collective-permute-start.19
  116.5 2.7 %collective-permute-start.21 = (bf16[2,1376,128]{2,1,0:T(8,128)(2,1)S(1)}, bf16[2,1376,128]{2,1,0:T(8,128)(2,1)S(1)}, u32[]{:S(2)}, u32[]{:S(2)}) collective-permute-start(bf16[2,1376,128]{2,1,0:T(8,128)(2,1)S(1)} %mlp.15), channel_id=1, source_target_pairs={{0,6},{1,7},{2,0},{3,1},{4,2},{5,3},{6,4},{7,5},{8,14},{9,15},{10,... | collective-permute-start | bytes 2113544 | tf_op jit(solution)/shard_map/ppermute | solution.py:45
  119.2 1.5 mlp.11
  120.7 0.7 collective-permute-start.15
  121.4 1.5 mlp.9
  123.0 2.4 %collective-permute-start.14 = (bf16[2,1376,128]{2,1,0:T(8,128)(2,1)S(1)}, bf16[2,1376,128]{2,1,0:T(8,128)(2,1)S(1)}, u32[]{:S(2)}, u32[]{:S(2)}) collective-permute-start(bf16[2,1376,128]{2,1,0:T(8,128)(2,1)S(1)} %mlp.9), channel_id=1, source_target_pairs={{0,8},{1,9},{2,10},{3,11},{4,12},{5,13},{6,14},{7,15},{8,0},{9,1},... | collective-permute-start | bytes 2113544 | tf_op jit(solution)/shard_map/ppermute | solution.py:45
  125.4 1.5 mlp.13
  126.9 1.5 mlp.12
  128.5 1.5 mlp.10
  130.0 1.5 mlp.8
  131.6 3.7 %collective-permute-done.19 = bf16[2,1376,128]{2,1,0:T(8,128)(2,1)S(1)} collective-permute-done((bf16[2,1376,128]{2,1,0:T(8,128)(2,1)S(1)}, bf16[2,1376,128]{2,1,0:T(8,128)(2,1)S(1)}, u32[]{:S(2)}, u32[]{:S(2)}) %collective-permute-start.19) | collective-permute-done | bytes 704544 | tf_op jit(solution)/shard_map/ppermute | solution.py:45
  135.3 0.2 fusion.10
  135.5 2.5 %collective-permute-start.22 = (bf16[1376,128]{1,0:T(8,128)(2,1)S(1)}, bf16[1376,128]{1,0:T(8,128)(2,1)S(1)}, u32[]{:S(2)}, u32[]{:S(2)}) collective-permute-start(bf16[1376,128]{1,0:T(8,128)(2,1)S(1)} %get-tuple-element.23), channel_id=1, source_target_pairs={{0,6},{1,7},{2,0},{3,1},{4,2},{5,3},{6,4},{7,5},{8,14},{9,15},{10,... | collective-permute-start | bytes 1056776 | tf_op jit(solution)/shard_map/ppermute | solution.py:45
  138.1 1.3 collective-permute-done.15
  139.4 0.2 fusion.7
  139.6 1.4 collective-permute-start.18
  141.0 3.8 %collective-permute-done.22 = bf16[1376,128]{1,0:T(8,128)(2,1)S(1)} collective-permute-done((bf16[1376,128]{1,0:T(8,128)(2,1)S(1)}, bf16[1376,128]{1,0:T(8,128)(2,1)S(1)}, u32[]{:S(2)}, u32[]{:S(2)}) %collective-permute-start.22) | collective-permute-done | bytes 352288 | tf_op jit(solution)/shard_map/ppermute | solution.py:45
  144.8 0.2 fusion.1
  145.0 0.6 collective-permute-start.23
  145.6 8.9 %collective-permute-done.14 = bf16[2,1376,128]{2,1,0:T(8,128)(2,1)S(1)} collective-permute-done((bf16[2,1376,128]{2,1,0:T(8,128)(2,1)S(1)}, bf16[2,1376,128]{2,1,0:T(8,128)(2,1)S(1)}, u32[]{:S(2)}, u32[]{:S(2)}) %collective-permute-start.14) | collective-permute-done | bytes 704544 | tf_op jit(solution)/shard_map/ppermute | solution.py:45
  154.5 0.2 add_bitcast_fusion
  154.7 0.1 collective-permute-start.17
  154.8 0.9 collective-permute-start.16
  155.7 6.4 %collective-permute-done.23 = bf16[1376,128]{1,0:T(8,128)(2,1)S(1)} collective-permute-done((bf16[1376,128]{1,0:T(8,128)(2,1)S(1)}, bf16[1376,128]{1,0:T(8,128)(2,1)S(1)}, u32[]{:S(2)}, u32[]{:S(2)}) %collective-permute-start.23) | collective-permute-done | bytes 352288 | tf_op jit(solution)/shard_map/ppermute | solution.py:45
  162.0 0.2 fusion
  162.2 2.0 %collective-permute-done.17 = bf16[1376,128]{1,0:T(8,128)(2,1)S(1)} collective-permute-done((bf16[1376,128]{1,0:T(8,128)(2,1)S(1)}, bf16[1376,128]{1,0:T(8,128)(2,1)S(1)}, u32[]{:S(2)}, u32[]{:S(2)}) %collective-permute-start.17) | collective-permute-done | bytes 352288 | tf_op jit(solution)/shard_map/ppermute | solution.py:45
  164.2 9.3 %collective-permute-done.16 = bf16[1376,128]{1,0:T(8,128)(2,1)S(1)} collective-permute-done((bf16[1376,128]{1,0:T(8,128)(2,1)S(1)}, bf16[1376,128]{1,0:T(8,128)(2,1)S(1)}, u32[]{:S(2)}, u32[]{:S(2)}) %collective-permute-start.16) | collective-permute-done | bytes 352288 | tf_op jit(solution)/shard_map/ppermute | solution.py:45
  173.6 1.1 fusion.12
  (33 shorter events, 0.2 us)
Async XLA Ops:
  0.6 12.8 %copy-start.7 = (f32[512]{0:T(512)S(1)}, f32[512]{0:T(512)}, u32[]{:S(2)}) copy-start(f32[512]{0:T(512)} %param.14) | copy-start | bytes 6148
  0.6 23.8 %collective-permute-start = (bf16[1368,512]{1,0:T(8,128)(2,1)}, bf16[1368,512]{1,0:T(8,128)(2,1)S(1)}, u32[]{:S(2)}, u32[]{:S(2)}) collective-permute-start(bf16[1368,512]{1,0:T(8,128)(2,1)} %bitcast.57), channel_id=1, source_target_pairs={{0,1},{1,0},{2,3},{3,2},{4,5},{5,4},{6,7},{7,6},{8,9},{9,8},{10,11... | collective-permute-start | bytes 4202504 | tf_op jit(solution)/shard_map/ppermute | solution.py:45
  4.0 20.4 %collective-permute-start.1 = (bf16[1368,512]{1,0:T(8,128)(2,1)}, bf16[1368,512]{1,0:T(8,128)(2,1)S(1)}, u32[]{:S(2)}, u32[]{:S(2)}) collective-permute-start(bf16[1368,512]{1,0:T(8,128)(2,1)} %bitcast.52), channel_id=1, source_target_pairs={{0,1},{1,0},{2,3},{3,2},{4,5},{5,4},{6,7},{7,6},{8,9},{9,8},{10,11... | collective-permute-start | bytes 4202504 | tf_op jit(solution)/shard_map/ppermute | solution.py:45
  6.0 18.4 %all-to-all-start = ((bf16[16,64,128]{2,1,0:T(8,128)(2,1)}), bf16[16,64,128]{2,1,0:T(8,128)(2,1)S(1)}, u32[]{:S(2)}, u32[]{:S(2)}) async-start(bf16[16,64,128]{2,1,0:T(8,128)(2,1)} %prep.1), calls=%async_computation | async-start | bytes 524288 | tf_op jit(solution)/shard_map/all_to_all | solution.py:323
  13.5 1.6 collective-permute-start.2
  24.4 0.7 copy-start.8
  25.1 37.9 %copy-start.2 = (bf16[1368,512]{1,0:T(8,128)(2,1)}, bf16[1368,512]{1,0:T(8,128)(2,1)S(1)}, u32[]{:S(2)}) copy-start(bf16[1368,512]{1,0:T(8,128)(2,1)S(1)} %collective-permute-done.1.refs_1_) | copy-start | bytes 4202500
  43.5 24.7 %copy-start.6 = (bf16[128,512]{1,0:T(8,128)(2,1)S(1)}, bf16[128,512]{1,0:T(8,128)(2,1)}, u32[]{:S(2)}) copy-start(bf16[128,512]{1,0:T(8,128)(2,1)} %start_ref.1) | copy-start | bytes 393220
  63.0 8.1 %collective-permute-start.3 = (bf16[8,128,512]{2,1,0:T(8,128)(2,1)}, bf16[8,128,512]{2,1,0:T(8,128)(2,1)}, u32[]{:S(2)}, u32[]{:S(2)}) collective-permute-start(bf16[8,128,512]{2,1,0:T(8,128)(2,1)} %all_to_all.16.mixed_hbm), channel_id=1, source_target_pairs={{0,1},{1,0},{2,3},{3,2},{4,5},{5,4},{6,7},{7,6},{8,9},{9,8},{10,11... | collective-permute-start | bytes 3145736 | tf_op jit(solution)/shard_map/ppermute | solution.py:45
  74.7 4.1 %collective-permute-start.4 = (bf16[128,512]{1,0:T(8,128)(2,1)}, bf16[128,512]{1,0:T(8,128)(2,1)S(1)}, u32[]{:S(2)}, u32[]{:S(2)}) collective-permute-start(bf16[128,512]{1,0:T(8,128)(2,1)} %out_proj.3), channel_id=1, source_target_pairs={{0,16},{1,0},{2,18},{3,2},{4,20},{5,4},{6,22},{7,6},{8,24},{9,8},{... | collective-permute-start | bytes 393224 | tf_op jit(solution)/shard_map/ppermute | solution.py:352
  74.9 6.5 %collective-permute-start.5 = (bf16[128,512]{1,0:T(8,128)(2,1)}, bf16[128,512]{1,0:T(8,128)(2,1)S(1)}, u32[]{:S(2)}, u32[]{:S(2)}) collective-permute-start(bf16[128,512]{1,0:T(8,128)(2,1)} %out_proj.3), channel_id=1, source_target_pairs={{1,16},{3,18},{5,20},{7,22},{9,24},{11,26},{13,28},{15,30},{16,1},... | collective-permute-start | bytes 393224 | tf_op jit(solution)/shard_map/ppermute | solution.py:353
  81.4 15.3 %collective-permute-start.8 = (bf16[2,128,512]{2,1,0:T(8,128)(2,1)S(1)}, bf16[2,128,512]{2,1,0:T(8,128)(2,1)S(1)}, u32[]{:S(2)}, u32[]{:S(2)}) collective-permute-start(bf16[2,128,512]{2,1,0:T(8,128)(2,1)S(1)} %pad_maximum_fusion.refs_0_), channel_id=1, source_target_pairs={{0,64},{1,65},{2,66},{3,67},{4,68},{5,69},{6,70},{7,71},{8,72},{9,... | collective-permute-start | bytes 786440 | tf_op jit(solution)/shard_map/ppermute | solution.py:45
  81.8 15.6 %collective-permute-start.7 = (bf16[2,128,512]{2,1,0:T(8,128)(2,1)S(1)}, bf16[2,128,512]{2,1,0:T(8,128)(2,1)}, u32[]{:S(2)}, u32[]{:S(2)}) collective-permute-start(bf16[2,128,512]{2,1,0:T(8,128)(2,1)S(1)} %pad_maximum_fusion.refs_0_), channel_id=1, source_target_pairs={{0,192},{1,193},{2,194},{3,195},{4,196},{5,197},{6,198},{7,199},{8... | collective-permute-start | bytes 786440 | tf_op jit(solution)/shard_map/ppermute | solution.py:45
  85.1 16.8 %collective-permute-start.6 = (bf16[2,128,512]{2,1,0:T(8,128)(2,1)S(1)}, bf16[2,128,512]{2,1,0:T(8,128)(2,1)S(1)}, u32[]{:S(2)}, u32[]{:S(2)}) collective-permute-start(bf16[2,128,512]{2,1,0:T(8,128)(2,1)S(1)} %pad_maximum_fusion.refs_0_), channel_id=1, source_target_pairs={{0,224},{1,225},{2,226},{3,227},{4,228},{5,229},{6,230},{7,231},{8... | collective-permute-start | bytes 786440 | tf_op jit(solution)/shard_map/ppermute | solution.py:45
  85.1 19.7 %collective-permute-start.9 = (bf16[2,128,512]{2,1,0:T(8,128)(2,1)S(1)}, bf16[2,128,512]{2,1,0:T(8,128)(2,1)}, u32[]{:S(2)}, u32[]{:S(2)}) collective-permute-start(bf16[2,128,512]{2,1,0:T(8,128)(2,1)S(1)} %pad_maximum_fusion.refs_0_), channel_id=1, source_target_pairs={{0,32},{1,33},{2,34},{3,35},{4,36},{5,37},{6,38},{7,39},{8,40},{9,... | collective-permute-start | bytes 786440 | tf_op jit(solution)/shard_map/ppermute | solution.py:45
  97.3 16.0 %copy-start = (bf16[512,1368]{0,1:T(8,128)(2,1)S(1)}, bf16[512,1368]{0,1:T(8,128)(2,1)}, u32[]{:S(2)}) copy-start(bf16[512,1368]{0,1:T(8,128)(2,1)} %param.16) | copy-start | bytes 4202500
  97.3 10.4 %collective-permute-start.11 = (bf16[128,512]{1,0:T(8,128)(2,1)}, bf16[128,512]{1,0:T(8,128)(2,1)S(1)}, u32[]{:S(2)}, u32[]{:S(2)}) collective-permute-start(bf16[128,512]{1,0:T(8,128)(2,1)} %slice_bitcast_fusion.3), channel_id=1, source_target_pairs={{0,64},{1,65},{2,66},{3,67},{4,68},{5,69},{6,70},{7,71},{8,72},{9,... | collective-permute-start | bytes 393224 | tf_op jit(solution)/shard_map/ppermute | solution.py:45
  97.4 14.3 %collective-permute-start.13 = (bf16[2,128,512]{2,1,0:T(8,128)(2,1)S(1)}, bf16[2,128,512]{2,1,0:T(8,128)(2,1)}, u32[]{:S(2)}, u32[]{:S(2)}) collective-permute-start(bf16[2,128,512]{2,1,0:T(8,128)(2,1)S(1)} %collective-permute-done.8.refs_3_), channel_id=1, source_target_pairs={{0,32},{1,33},{2,34},{3,35},{4,36},{5,37},{6,38},{7,39},{8,40},{9,... | collective-permute-start | bytes 786440 | tf_op jit(solution)/shard_map/ppermute | solution.py:45
  97.4 14.3 %collective-permute-start.10 = (bf16[2,128,512]{2,1,0:T(8,128)(2,1)}, bf16[2,128,512]{2,1,0:T(8,128)(2,1)}, u32[]{:S(2)}, u32[]{:S(2)}) collective-permute-start(bf16[2,128,512]{2,1,0:T(8,128)(2,1)} %collective-permute-done.7.refs_2_), channel_id=1, source_target_pairs={{0,224},{1,225},{2,226},{3,227},{4,228},{5,229},{6,230},{7,231},{8... | collective-permute-start | bytes 786440 | tf_op jit(solution)/shard_map/ppermute | solution.py:45
  101.8 0.7 copy-start.4
  102.5 9.1 %collective-permute-start.12 = (bf16[128,512]{1,0:T(8,128)(2,1)}, bf16[128,512]{1,0:T(8,128)(2,1)}, u32[]{:S(2)}, u32[]{:S(2)}) collective-permute-start(bf16[128,512]{1,0:T(8,128)(2,1)} %slice_bitcast_fusion.2), channel_id=1, source_target_pairs={{0,192},{1,193},{2,194},{3,195},{4,196},{5,197},{6,198},{7,199},{8... | collective-permute-start | bytes 393224 | tf_op jit(solution)/shard_map/ppermute | solution.py:45
  104.8 8.5 %copy-start.3 = (bf16[1368,512]{1,0:T(8,128)(2,1)S(1)}, bf16[1368,512]{1,0:T(8,128)(2,1)}, u32[]{:S(2)}) copy-start(bf16[1368,512]{1,0:T(8,128)(2,1)} %copy-done.2) | copy-start | bytes 4202500
  104.8 1.1 copy-start.5
  114.9 4.3 %copy-start.1 = (bf16[512,1368]{0,1:T(8,128)(2,1)S(1)}, bf16[512,1368]{0,1:T(8,128)(2,1)}, u32[]{:S(2)}) copy-start(bf16[512,1368]{0,1:T(8,128)(2,1)} %param.15) | copy-start | bytes 4202500
  116.4 18.9 %collective-permute-start.19 = (bf16[2,1376,128]{2,1,0:T(8,128)(2,1)S(1)}, bf16[2,1376,128]{2,1,0:T(8,128)(2,1)S(1)}, u32[]{:S(2)}, u32[]{:S(2)}) collective-permute-start(bf16[2,1376,128]{2,1,0:T(8,128)(2,1)S(1)} %mlp.14), channel_id=1, source_target_pairs={{0,2},{1,3},{2,4},{3,5},{4,6},{5,7},{6,0},{7,1},{8,10},{9,11},{10,... | collective-permute-start | bytes 2113544 | tf_op jit(solution)/shard_map/ppermute | solution.py:45
  116.5 18.8 %collective-permute-start.21 = (bf16[2,1376,128]{2,1,0:T(8,128)(2,1)S(1)}, bf16[2,1376,128]{2,1,0:T(8,128)(2,1)S(1)}, u32[]{:S(2)}, u32[]{:S(2)}) collective-permute-start(bf16[2,1376,128]{2,1,0:T(8,128)(2,1)S(1)} %mlp.15), channel_id=1, source_target_pairs={{0,6},{1,7},{2,0},{3,1},{4,2},{5,3},{6,4},{7,5},{8,14},{9,15},{10,... | collective-permute-start | bytes 2113544 | tf_op jit(solution)/shard_map/ppermute | solution.py:45
  120.7 18.7 %collective-permute-start.15 = (bf16[2,1376,128]{2,1,0:T(8,128)(2,1)S(1)}, bf16[2,1376,128]{2,1,0:T(8,128)(2,1)S(1)}, u32[]{:S(2)}, u32[]{:S(2)}) collective-permute-start(bf16[2,1376,128]{2,1,0:T(8,128)(2,1)S(1)} %mlp.11), channel_id=1, source_target_pairs={{0,8},{1,9},{2,10},{3,11},{4,12},{5,13},{6,14},{7,15},{8,0},{9,1},... | collective-permute-start | bytes 2113544 | tf_op jit(solution)/shard_map/ppermute | solution.py:45
  123.0 31.5 %collective-permute-start.14 = (bf16[2,1376,128]{2,1,0:T(8,128)(2,1)S(1)}, bf16[2,1376,128]{2,1,0:T(8,128)(2,1)S(1)}, u32[]{:S(2)}, u32[]{:S(2)}) collective-permute-start(bf16[2,1376,128]{2,1,0:T(8,128)(2,1)S(1)} %mlp.9), channel_id=1, source_target_pairs={{0,8},{1,9},{2,10},{3,11},{4,12},{5,13},{6,14},{7,15},{8,0},{9,1},... | collective-permute-start | bytes 2113544 | tf_op jit(solution)/shard_map/ppermute | solution.py:45
  135.5 9.3 %collective-permute-start.22 = (bf16[1376,128]{1,0:T(8,128)(2,1)S(1)}, bf16[1376,128]{1,0:T(8,128)(2,1)S(1)}, u32[]{:S(2)}, u32[]{:S(2)}) collective-permute-start(bf16[1376,128]{1,0:T(8,128)(2,1)S(1)} %get-tuple-element.23), channel_id=1, source_target_pairs={{0,6},{1,7},{2,0},{3,1},{4,2},{5,3},{6,4},{7,5},{8,14},{9,15},{10,... | collective-permute-start | bytes 1056776 | tf_op jit(solution)/shard_map/ppermute | solution.py:45
  138.0 17.6 %collective-permute-start.20 = (bf16[1376,128]{1,0:T(8,128)(2,1)S(1)}, bf16[1376,128]{1,0:T(8,128)(2,1)S(1)}, u32[]{:S(2)}, u32[]{:S(2)}) collective-permute-start(bf16[1376,128]{1,0:T(8,128)(2,1)S(1)} %get-tuple-element.22), channel_id=1, source_target_pairs={{0,2},{1,3},{2,4},{3,5},{4,6},{5,7},{6,0},{7,1},{8,10},{9,11},{10,... | collective-permute-start | bytes 1056776 | tf_op jit(solution)/shard_map/ppermute | solution.py:45
  139.6 22.6 %collective-permute-start.18 = (bf16[1376,128]{1,0:T(8,128)(2,1)S(1)}, bf16[1376,128]{1,0:T(8,128)(2,1)S(1)}, u32[]{:S(2)}, u32[]{:S(2)}) collective-permute-start(bf16[1376,128]{1,0:T(8,128)(2,1)S(1)} %get-tuple-element.21), channel_id=1, source_target_pairs={{0,6},{1,7},{2,0},{3,1},{4,2},{5,3},{6,4},{7,5},{8,14},{9,15},{10,... | collective-permute-start | bytes 1056776 | tf_op jit(solution)/shard_map/ppermute | solution.py:45
  145.0 17.0 %collective-permute-start.23 = (bf16[1376,128]{1,0:T(8,128)(2,1)S(1)}, bf16[1376,128]{1,0:T(8,128)(2,1)S(1)}, u32[]{:S(2)}, u32[]{:S(2)}) collective-permute-start(bf16[1376,128]{1,0:T(8,128)(2,1)S(1)} %fusion.1), channel_id=1, source_target_pairs={{0,8},{1,9},{2,10},{3,11},{4,12},{5,13},{6,14},{7,15},{8,0},{9,1},... | collective-permute-start | bytes 1056776 | tf_op jit(solution)/shard_map/ppermute | solution.py:45
  154.7 9.6 %collective-permute-start.17 = (bf16[1376,128]{1,0:T(8,128)(2,1)S(1)}, bf16[1376,128]{1,0:T(8,128)(2,1)S(1)}, u32[]{:S(2)}, u32[]{:S(2)}) collective-permute-start(bf16[1376,128]{1,0:T(8,128)(2,1)S(1)} %get-tuple-element.19), channel_id=1, source_target_pairs={{0,4},{1,5},{2,6},{3,7},{4,0},{5,1},{6,2},{7,3},{8,12},{9,13},{10,... | collective-permute-start | bytes 1056776 | tf_op jit(solution)/shard_map/ppermute | solution.py:45
  154.8 18.8 %collective-permute-start.16 = (bf16[1376,128]{1,0:T(8,128)(2,1)S(1)}, bf16[1376,128]{1,0:T(8,128)(2,1)S(1)}, u32[]{:S(2)}, u32[]{:S(2)}) collective-permute-start(bf16[1376,128]{1,0:T(8,128)(2,1)S(1)} %get-tuple-element.20), channel_id=1, source_target_pairs={{0,2},{1,3},{2,4},{3,5},{4,6},{5,7},{6,0},{7,1},{8,10},{9,11},{10,... | collective-permute-start | bytes 1056776 | tf_op jit(solution)/shard_map/ppermute | solution.py:45

commit v4 on v3

--- a/solution.py
+++ b/solution.py
@@ -174,14 +174,11 @@
     return jnp.concatenate([rows, tail], axis=0).astype(BF16)
 
 
-def scale_kernel(n, *refs):
+def scale_kernel(*refs):
     blocks, (gain_ref, gain_oth_ref, out_ref, tail_ref) = refs[:-4], refs[-4:]
-    halves = []
-    for ref in blocks:
-        halves += [ref.at[0], ref.at[1]] if len(ref.shape) == 3 else [ref]
-    for i in range(n):
-        own = halves[2 * i][...].astype(F32)
-        oth = halves[2 * i + 1][...].astype(F32)
+    for i, block in enumerate(blocks):
+        own = block[0].astype(F32)
+        oth = block[1].astype(F32)
         out_ref[i, 0] = (own * gain_ref[...]).astype(BF16)
         out_ref[i, 1] = (oth * gain_oth_ref[...]).astype(BF16)
         tail_ref[i] = two_rows(square_sums(own) + square_sums(oth))
@@ -189,8 +186,10 @@
 
 def mlp_kernel(groups, with_squares, idx_ref, near_ref, far_ref, near_tail_ref, far_tail_ref, *refs):
     w_ref, wx_ref = refs[:2]
-    out_refs = refs[2:-3]
+    out_refs, order_ref = refs[2:-4], refs[-4]
     so, sx, tail = refs[-3:]
+    for slot in range(8):
+        order_ref[slot] = idx_ref[slot]
     slots = [slot for group in groups for slot in group]
     for at, slot in enumerate(slots):
         which = idx_ref[slot]
@@ -244,6 +243,10 @@
 
 def anywhere():
     return pl.BlockSpec(memory_space=pl.ANY)
+
+
+def to_opposite(z, x, y, k):
+    return (z + 2, x, y, k) if z % 2 == 0 else (z - 2, x, y, k)
 
 
 def out_proj(offset, core, mixed, w_out, start, dtype):
@@ -269,14 +272,15 @@
     )(core, mixed, w_out, start)
 
 
-def scale(blocks, gains, n):
+def scale(blocks, gains):
+    n = len(blocks)
     return pl.pallas_call(
-        functools.partial(scale_kernel, n),
+        scale_kernel,
         out_shape=[
             jax.ShapeDtypeStruct((n, 2, ROWS, CH), BF16),
             jax.ShapeDtypeStruct((n, 8, ROWS), F32),
         ],
-        compiler_params=params(24),
+        compiler_params=params(14),
         cost_estimate=pl.CostEstimate(
             flops=8 * n * ROWS * CH * 8, bytes_accessed=n << 19, transcendentals=0
         ),
@@ -289,16 +293,18 @@
     vmem = pl.BlockSpec(memory_space=pltpu.VMEM)
     return pl.pallas_call(
         functools.partial(mlp_kernel, groups, with_squares),
-        out_shape=[jax.ShapeDtypeStruct((len(g), FF_PAD, ROWS), BF16) for g in groups],
+        out_shape=[jax.ShapeDtypeStruct((len(g), FF_PAD, ROWS), BF16) for g in groups]
+        + [jax.ShapeDtypeStruct((8,), jnp.int32)],
         in_specs=[in_smem()] + [vmem] * 6,
+        out_specs=[vmem] * len(groups) + [in_smem()],
         scratch_shapes=[
             pltpu.VMEM((n * ROWS, CH), BF16),
             pltpu.VMEM((n * ROWS, CH), BF16),
             pltpu.VMEM((n, 8, ROWS), F32),
         ],
-        compiler_params=params(24),
+        compiler_params=params(18),
         cost_estimate=pl.CostEstimate(
-            flops=4 * n * ROWS * CH * FF_LOC, bytes_accessed=5 << 20, transcendentals=0
+            flops=10**8, bytes_accessed=1 << 19, transcendentals=0
         ),
         name="mlp",
     )(idx, *rows, *weights)
@@ -330,7 +336,7 @@
             pltpu.VMEM((N_CTX, 3, SUB, 128), F32),
             pltpu.VMEM((N_CTX, SUB, 256), F32),
         ],
-        compiler_params=params(56),
+        compiler_params=params(14),
         name="conv",
     )(recv, jnp.asarray(dft_tables()))
     conv_rows = lax.all_to_all(conv, "ctx", 0, 0, tiled=True)
@@ -359,13 +365,14 @@
         above.insert(1, shift(held, z=-step))
     below.append(shift(below[2], z=1))
     above.append(shift(above[2], z=-1))
-    opposite = (shift(below[2][0], z=2), shift(above[2][1], z=-2))
+    z = ctx // 2
+    onward = jnp.where(z % 2 == 0, below[2], above[2])
+    opposite = lax.ppermute(onward, AXES, pairs_of(to_opposite))
     gains = (gain, gain_oth)
-    near, near_tail = scale([held, above[1], above[2], below[2], below[1]], gains, NEAR)
-    far, far_tail = scale([above[3], *opposite, below[3]], gains, 8 - NEAR)
+    near, near_tail = scale([held, above[1], above[2], below[2], below[1]], gains)
+    far, far_tail = scale([above[3], opposite, below[3]], gains)
     rows = (near, far, near_tail, far_tail)
 
-    z = ctx // 2
     order = []
     for b in range(4):
         for a in range(2):
@@ -374,11 +381,13 @@
     idx = jnp.stack(order).astype(jnp.int32)
     gate_w, up_w = (wg, wg_oth), (wu, wu_oth)
 
-    def gate_part(*groups):
-        return mlp_part(groups, False, idx, rows, gate_w)
-
-    def up_part(*groups):
-        return mlp_part(groups, True, idx, rows, up_w)
+    def gate_part(order, *groups):
+        *outs, token = mlp_part(groups, False, order, rows, gate_w)
+        return outs + [token]
+
+    def up_part(order, *groups):
+        *outs, token = mlp_part(groups, True, order, rows, up_w)
+        return outs + [token]
 
     def add(*terms):
         total = terms[0].astype(F32)
@@ -386,25 +395,24 @@
             total = total + term.astype(F32)
         return total
 
-    (u_plus,) = up_part((4, 3))
-    u_plus = shift(u_plus, y=1)
-    (u_minus,) = up_part((5, 6))
-    u_minus = shift(u_minus, y=-1)
-    (g_send_a,) = gate_part((5, 1))
+    u_two, _ = up_part(idx, (4, 5))
+    g_send_a, _ = gate_part(idx, (5, 1))
+    u_one, _ = up_part(idx, (2, 3))
+    u_three, _ = up_part(idx, (6, 7))
+    g_send_b, then = gate_part(idx, (3, 7))
+    u_two = shift(u_two, y=2)
     g_recv_a = shift(g_send_a, x=2)
-    (g_send_b,) = gate_part((3, 7))
+    u_one = shift(u_one, y=1)
+    u_three = shift(u_three, y=-1)
     g_recv_b = shift(g_send_b, x=2)
-    (u_pair,) = up_part((2, 7))
-    (g_keep_a,) = gate_part((4, 0))
-    (g_keep_b,) = gate_part((2, 6))
-    (u_keep,) = up_part((0, 1))
-    u_plus_2 = shift(add(u_pair[0], u_plus[0]).astype(BF16), y=1)
-    u_minus_2 = shift(add(u_pair[1], u_minus[0]).astype(BF16), y=-1)
+    g_keep_a, _ = gate_part(then, (4, 0))
+    g_keep_b, _ = gate_part(then, (2, 6))
+    u_keep, _ = up_part(then, (0, 1))
     g_last_2 = shift(add(g_keep_a[0], g_recv_a[0]).astype(BF16), y=2)
     g_last_1 = shift(add(g_keep_b[0], g_recv_b[0]).astype(BF16), y=1)
     g_last_3 = shift(add(g_keep_b[1], g_recv_b[1]).astype(BF16), y=-1)
-    u_last = shift(add(u_keep[1], u_plus[1], u_minus_2).astype(BF16), x=2)
-    up = add(u_keep[0], u_plus_2, u_minus[1], u_last)
+    u_last = shift(add(u_keep[1], u_one[1], u_two[1], u_three[1]).astype(BF16), x=2)
+    up = add(u_keep[0], u_one[0], u_two[0], u_three[0], u_last)
     gate = add(g_keep_a[1], g_recv_a[1], g_last_1, g_last_2, g_last_3)
     sums = up[FF_LOC : FF_LOC + 1] + up[FF_LOC + 1 : FF_LOC + 2]
     row_scale = lax.rsqrt(sums * (1.0 / (N_TP * CH)) + EPS)

time: 175 us -> 170 us (0.971)
  the two profiles are of different devices: /device:TPU:1 before, /device:TPU:24 now
where the time goes in v4:
time: 170 us
  waiting for transfers between devices  65.5 us (39%)
  starting transfers between devices  36.4 us (21%)
  blocking collectives  32.4 us (19%)
  Pallas kernels  27.9 us (16%)
  other arithmetic  3.6 us (2%)
  local copies, waits for them, and re-layouts  3.12 us (2%)
    ppermute x19, waiting for transfers between devices, shift(): return lax.ppermute(arr, AXES, pairs)  52.4 us
    ppermute x19, starting transfers between devices, shift(): return lax.ppermute(arr, AXES, pairs)  24.4 us
    all_to_all x1, blocking collectives, shards(): lax.all_to_all(copies, 'tp', 0, 0, axis_index_groups=PLANE_GROUPS, tiled=...  19.5 us
    all_to_all x1, blocking collectives, shards(): conv_rows = lax.all_to_all(conv, 'ctx', 0, 0, tiled=True)  12.9 us
    pallas_call x8, Pallas kernels, mlp_part(): pl.pallas_call(functools.partial(mlp_kernel, groups, with_squares), out_s...  12.4 us
    all_to_all x1, waiting for transfers between devices, shards(): recv = lax.all_to_all(sent, 'ctx', 0, 0, tiled=True)  11 us
    all_to_all x1, starting transfers between devices, shards(): recv = lax.all_to_all(sent, 'ctx', 0, 0, tiled=True)  9.5 us
    pallas_call x2, Pallas kernels, out_proj(): pl.pallas_call(functools.partial(out_proj_kernel, offset), out_shape=jax....  6.4 us
  transfers between devices with their start and end apart: 23, of which 13 were waited for; matrix products, arithmetic and copies ran while one was open for 1% of the time, Pallas kernels for 10%

profile of v4, /device:TPU:24, one launch (start us, length us, event | category | flops | bytes accessed | tf_op | source)
XLA Modules:
  0.0 169.9 jit_solution(7519045532088946467)
XLA Ops:
  0.6 0.0 copy-start.6
  0.7 0.1 collective-permute-start
  0.8 0.5 collective-permute-start.1
  1.2 1.9 %prep.1 = bf16[16,64,128]{2,1,0:T(8,128)(2,1)} custom-call(bf16[3,128,512]{2,1,0:T(8,128)(2,1)} %bitcast.47, f32[128,512]{1,0:T(8,128)} %filt_ref.1), custom_call_target="tpu_custom_call" | custom-call | tf_op jit(solution)/shard_map/prep/pallas_call | solution.py:323
  3.2 9.5 %all-to-all-start = ((bf16[16,64,128]{2,1,0:T(8,128)(2,1)}), bf16[16,64,128]{2,1,0:T(8,128)(2,1)S(1)}, u32[]{:S(2)}, u32[]{:S(2)}) async-start(bf16[16,64,128]{2,1,0:T(8,128)(2,1)} %prep.1), calls=%async_computation | async-start | bytes 524288 | tf_op jit(solution)/shard_map/all_to_all | solution.py:329
  12.7 0.1 collective-permute-start.2
  12.8 1.1 collective-permute-done.2.refs_6_.refs_4_
  13.9 11.0 %all-to-all-done.x_ref = bf16[16,64,128]{2,1,0:T(8,128)(2,1)S(1)} async-done(((bf16[16,64,128]{2,1,0:T(8,128)(2,1)}), bf16[16,64,128]{2,1,0:T(8,128)(2,1)S(1)}, u32[]{:S(2)}, u32[]{:S(2)}) %all-to-all-start) | async-done | bytes 262176 | tf_op jit(solution)/shard_map/all_to_all | solution.py:329
  24.9 1.5 conv.1
  26.4 12.9 %all_to_all.15.conv_ref = bf16[16,32,128]{2,1,0:T(8,128)(2,1)} all-to-all(bf16[16,32,128]{2,1,0:T(8,128)(2,1)S(1)} %conv.1), channel_id=1, replica_groups=mesh['ctx'=16,'tp'=16] {'ctx'}, dimensions={0} | all-to-all | bytes 262144 | tf_op jit(solution)/shard_map/all_to_all | solution.py:342
  39.3 2.2 %mix.1 = bf16[8,128,512]{2,1,0:T(8,128)(2,1)} custom-call(bf16[16,32,128]{2,1,0:T(8,128)(2,1)} %all_to_all.15.conv_ref, bf16[3,128,512]{2,1,0:T(8,128)(2,1)} %bitcast.48, f32[1,512]{1,0:T(1,128)} %bitcast.49), custom_call_target="tpu_custom_call" | custom-call | tf_op jit(solution)/shard_map/mix/pallas_call | solution.py:343
  41.5 19.5 %all_to_all.16.mixed_hbm = bf16[8,128,512]{2,1,0:T(8,128)(2,1)} all-to-all(bf16[8,128,512]{2,1,0:T(8,128)(2,1)} %mix.1), channel_id=1, replica_groups={{0,2,4,6,8,10,12,14},{1,3,5,7,9,11,13,15},{16,18,20,22,24,26,28,30},{17..., dimensions={0} | all-to-all | bytes 2097152 | tf_op jit(solution)/shard_map/all_to_all | solution.py:350
  61.1 2.9 %out_proj.2.start_ref = f32[128,512]{1,0:T(8,128)S(1)} custom-call(s32[1]{0:T(128)} %bitcast.core_ref, bf16[8,128,512]{2,1,0:T(8,128)(2,1)} %all_to_all.16.mixed_hbm, bf16[8192,512]{1,0:T(8,128)(2,1)} %w_hbm.3, bf16[128,512]{1,0:T(8,128)(2,1)S(1)} %copy-done.7), custom_call_target="tpu_custom_call" | custom-call | flops 536870912 | bytes 5242880 | tf_op jit(solution)/shard_map/out_proj/pallas_call | solution.py:253
  63.9 0.1 collective-permute-done.3.mixed_hbm
  64.1 3.5 %out_proj.3 = bf16[128,512]{1,0:T(8,128)(2,1)} custom-call(s32[1]{0:T(128)} %bitcast.core_ref, bf16[8,128,512]{2,1,0:T(8,128)(2,1)} %collective-permute-done.3.mixed_hbm, bf16[8192,512]{1,0:T(8,128)(2,1)} %w_hbm.3, f32[128,512]{1,0:T(8,128)S(1)} %out_proj.2.start_ref), custom_call_target="tpu_custom_call" | custom-call | flops 536870912 | bytes 5242880 | tf_op jit(solution)/shard_map/out_proj/pallas_call | solution.py:253
  67.6 0.2 collective-permute-start.4
  67.8 0.7 collective-permute-start.5
  68.4 2.2 %collective-permute-done.4 = bf16[128,512]{1,0:T(8,128)(2,1)S(1)} collective-permute-done((bf16[128,512]{1,0:T(8,128)(2,1)}, bf16[128,512]{1,0:T(8,128)(2,1)S(1)}, u32[]{:S(2)}, u32[]{:S(2)}) %collective-permute-start.4) | collective-permute-done | bytes 131104 | tf_op jit(solution)/shard_map/ppermute | solution.py:358
  70.6 0.9 select_bitcast_fusion.1
  71.6 0.7 collective-permute-start.7
  72.3 2.3 %collective-permute-start.8 = (bf16[2,128,512]{2,1,0:T(8,128)(2,1)S(1)}, bf16[2,128,512]{2,1,0:T(8,128)(2,1)S(1)}, u32[]{:S(2)}, u32[]{:S(2)}) collective-permute-start(bf16[2,128,512]{2,1,0:T(8,128)(2,1)S(1)} %pad_maximum_fusion.refs_0_), channel_id=1, source_target_pairs={{0,64},{1,65},{2,66},{3,67},{4,68},{5,69},{6,70},{7,71},{8,72},{9,... | collective-permute-start | bytes 786440 | tf_op jit(solution)/shard_map/ppermute | solution.py:45
  74.6 1.8 %collective-permute-start.6 = (bf16[2,128,512]{2,1,0:T(8,128)(2,1)S(1)}, bf16[2,128,512]{2,1,0:T(8,128)(2,1)}, u32[]{:S(2)}, u32[]{:S(2)}) collective-permute-start(bf16[2,128,512]{2,1,0:T(8,128)(2,1)S(1)} %pad_maximum_fusion.refs_0_), channel_id=1, source_target_pairs={{0,224},{1,225},{2,226},{3,227},{4,228},{5,229},{6,230},{7,231},{8... | collective-permute-start | bytes 786440 | tf_op jit(solution)/shard_map/ppermute | solution.py:45
  76.3 0.3 collective-permute-start.9
  76.6 8.9 %collective-permute-done.7.refs_2_ = bf16[2,128,512]{2,1,0:T(8,128)(2,1)S(1)} collective-permute-done((bf16[2,128,512]{2,1,0:T(8,128)(2,1)S(1)}, bf16[2,128,512]{2,1,0:T(8,128)(2,1)S(1)}, u32[]{:S(2)}, u32[]{:S(2)}) %collective-permute-start.7) | collective-permute-done | bytes 262176 | tf_op jit(solution)/shard_map/ppermute | solution.py:45
  85.5 0.7 copy-done.4
  86.2 0.8 broadcast_select_fusion
  86.9 1.7 collective-permute-start.11
  88.6 3.1 %collective-permute-start.10 = (bf16[2,128,512]{2,1,0:T(8,128)(2,1)S(1)}, bf16[2,128,512]{2,1,0:T(8,128)(2,1)}, u32[]{:S(2)}, u32[]{:S(2)}) collective-permute-start(bf16[2,128,512]{2,1,0:T(8,128)(2,1)S(1)} %collective-permute-done.7.refs_2_), channel_id=1, source_target_pairs={{0,224},{1,225},{2,226},{3,227},{4,228},{5,229},{6,230},{7,231},{8... | collective-permute-start | bytes 786440 | tf_op jit(solution)/shard_map/ppermute | solution.py:45
  91.6 0.1 stack.44.idx_ref
  91.7 4.6 %collective-permute-done.9.refs_4_ = bf16[2,128,512]{2,1,0:T(8,128)(2,1)} collective-permute-done((bf16[2,128,512]{2,1,0:T(8,128)(2,1)S(1)}, bf16[2,128,512]{2,1,0:T(8,128)(2,1)}, u32[]{:S(2)}, u32[]{:S(2)}) %collective-permute-start.9) | collective-permute-done | bytes 262176 | tf_op jit(solution)/shard_map/ppermute | solution.py:45
  96.3 0.9 copy-done.5
  97.2 1.9 %scale.2 = (bf16[5,2,128,512]{3,2,1,0:T(8,128)(2,1)S(1)}, f32[5,8,128]{2,1,0:T(8,128)S(1)}) custom-call(bf16[2,128,512]{2,1,0:T(8,128)(2,1)S(1)} %pad_maximum_fusion.refs_0_, bf16[2,128,512]{2,1,0:T(8,128)(2,1)} %collective-permute-done.6.refs_1_, bf16[2,128,512]{2,1,0:T(8,128)(2,1)S(1)} %collective-permute-done.7.refs_2_, ...), custom_call_target="tpu_custom_call" | custom-call | flops 20971520 | bytes 2621440 | tf_op jit(solution)/shard_map/scale/pallas_call | solution.py:277
  99.1 0.0 collective-permute-done.11.refs_1_
  99.1 3.9 %collective-permute-done.10.refs_0_ = bf16[2,128,512]{2,1,0:T(8,128)(2,1)} collective-permute-done((bf16[2,128,512]{2,1,0:T(8,128)(2,1)S(1)}, bf16[2,128,512]{2,1,0:T(8,128)(2,1)}, u32[]{:S(2)}, u32[]{:S(2)}) %collective-permute-start.10) | collective-permute-done | bytes 262176 | tf_op jit(solution)/shard_map/ppermute | solution.py:45
  103.0 2.5 %collective-permute-done.12.refs_2_ = bf16[2,128,512]{2,1,0:T(8,128)(2,1)} collective-permute-done((bf16[2,128,512]{2,1,0:T(8,128)(2,1)}, bf16[2,128,512]{2,1,0:T(8,128)(2,1)}, u32[]{:S(2)}, u32[]{:S(2)}) %collective-permute-start.12) | collective-permute-done | bytes 262176 | tf_op jit(solution)/shard_map/ppermute | solution.py:45
  105.5 1.7 scale.3
  107.2 0.0 copy-done
  107.2 1.3 copy-done.3
  108.5 1.5 mlp.10
  110.1 1.7 %collective-permute-start.13 = (bf16[2,1376,128]{2,1,0:T(8,128)(2,1)S(1)}, bf16[2,1376,128]{2,1,0:T(8,128)(2,1)S(1)}, u32[]{:S(2)}, u32[]{:S(2)}) collective-permute-start(bf16[2,1376,128]{2,1,0:T(8,128)(2,1)S(1)} %get-tuple-element.28), channel_id=1, source_target_pairs={{0,8},{1,9},{2,10},{3,11},{4,12},{5,13},{6,14},{7,15},{8,0},{9,1},... | collective-permute-start | bytes 2113544 | tf_op jit(solution)/shard_map/ppermute | solution.py:45
  111.8 1.6 mlp.13
  113.4 1.9 %collective-permute-start.18 = (bf16[2,1376,128]{2,1,0:T(8,128)(2,1)S(1)}, bf16[2,1376,128]{2,1,0:T(8,128)(2,1)S(1)}, u32[]{:S(2)}, u32[]{:S(2)}) collective-permute-start(bf16[2,1376,128]{2,1,0:T(8,128)(2,1)S(1)} %get-tuple-element.33), channel_id=1, source_target_pairs={{0,2},{1,3},{2,4},{3,5},{4,6},{5,7},{6,0},{7,1},{8,10},{9,11},{10,... | collective-permute-start | bytes 2113544 | tf_op jit(solution)/shard_map/ppermute | solution.py:45
  115.3 1.5 mlp.14
  116.8 1.6 mlp.15
  118.4 0.6 collective-permute-start.19
  119.0 1.2 collective-permute-start.20
  120.2 1.5 mlp.8
  121.7 2.0 %collective-permute-start.14 = (bf16[2,1376,128]{2,1,0:T(8,128)(2,1)S(1)}, bf16[2,1376,128]{2,1,0:T(8,128)(2,1)S(1)}, u32[]{:S(2)}, u32[]{:S(2)}) collective-permute-start(bf16[2,1376,128]{2,1,0:T(8,128)(2,1)S(1)} %get-tuple-element.30), channel_id=1, source_target_pairs={{0,8},{1,9},{2,10},{3,11},{4,12},{5,13},{6,14},{7,15},{8,0},{9,1},... | collective-permute-start | bytes 2113544 | tf_op jit(solution)/shard_map/ppermute | solution.py:45
  123.7 1.5 mlp.9
  125.3 1.5 mlp.11
  126.8 1.6 mlp.12
  128.4 1.9 %collective-permute-done.13 = bf16[2,1376,128]{2,1,0:T(8,128)(2,1)S(1)} collective-permute-done((bf16[2,1376,128]{2,1,0:T(8,128)(2,1)S(1)}, bf16[2,1376,128]{2,1,0:T(8,128)(2,1)S(1)}, u32[]{:S(2)}, u32[]{:S(2)}) %collective-permute-start.13) | collective-permute-done | bytes 704544 | tf_op jit(solution)/shard_map/ppermute | solution.py:45
  130.3 0.2 add_bitcast_fusion
  130.5 2.2 %collective-permute-start.16 = (bf16[1376,128]{1,0:T(8,128)(2,1)S(1)}, bf16[1376,128]{1,0:T(8,128)(2,1)S(1)}, u32[]{:S(2)}, u32[]{:S(2)}) collective-permute-start(bf16[1376,128]{1,0:T(8,128)(2,1)S(1)} %get-tuple-element.37), channel_id=1, source_target_pairs={{0,4},{1,5},{2,6},{3,7},{4,0},{5,1},{6,2},{7,3},{8,12},{9,13},{10,... | collective-permute-start | bytes 1056776 | tf_op jit(solution)/shard_map/ppermute | solution.py:45
  132.6 20.6 %collective-permute-done.18 = bf16[2,1376,128]{2,1,0:T(8,128)(2,1)S(1)} collective-permute-done((bf16[2,1376,128]{2,1,0:T(8,128)(2,1)S(1)}, bf16[2,1376,128]{2,1,0:T(8,128)(2,1)S(1)}, u32[]{:S(2)}, u32[]{:S(2)}) %collective-permute-start.18) | collective-permute-done | bytes 704544 | tf_op jit(solution)/shard_map/ppermute | solution.py:45
  153.2 0.5 collective-permute-done.20
  153.7 0.2 fusion.8
  153.9 2.4 %collective-permute-start.21 = (bf16[1376,128]{1,0:T(8,128)(2,1)S(1)}, bf16[1376,128]{1,0:T(8,128)(2,1)S(1)}, u32[]{:S(2)}, u32[]{:S(2)}) collective-permute-start(bf16[1376,128]{1,0:T(8,128)(2,1)S(1)} %fusion.8), channel_id=1, source_target_pairs={{0,8},{1,9},{2,10},{3,11},{4,12},{5,13},{6,14},{7,15},{8,0},{9,1},... | collective-permute-start | bytes 1056776 | tf_op jit(solution)/shard_map/ppermute | solution.py:45
  156.3 0.2 fusion.5
  156.5 3.7 %collective-permute-start.15 = (bf16[1376,128]{1,0:T(8,128)(2,1)S(1)}, bf16[1376,128]{1,0:T(8,128)(2,1)S(1)}, u32[]{:S(2)}, u32[]{:S(2)}) collective-permute-start(bf16[1376,128]{1,0:T(8,128)(2,1)S(1)} %get-tuple-element.38), channel_id=1, source_target_pairs={{0,2},{1,3},{2,4},{3,5},{4,6},{5,7},{6,0},{7,1},{8,10},{9,11},{10,... | collective-permute-start | bytes 1056776 | tf_op jit(solution)/shard_map/ppermute | solution.py:45
  160.2 5.5 %collective-permute-done.21 = bf16[1376,128]{1,0:T(8,128)(2,1)S(1)} collective-permute-done((bf16[1376,128]{1,0:T(8,128)(2,1)S(1)}, bf16[1376,128]{1,0:T(8,128)(2,1)S(1)}, u32[]{:S(2)}, u32[]{:S(2)}) %collective-permute-start.21) | collective-permute-done | bytes 352288 | tf_op jit(solution)/shard_map/ppermute | solution.py:45
  165.8 0.2 bitcast_add_fusion
  166.0 2.8 %collective-permute-done.17 = bf16[1376,128]{1,0:T(8,128)(2,1)S(1)} collective-permute-done((bf16[1376,128]{1,0:T(8,128)(2,1)S(1)}, bf16[1376,128]{1,0:T(8,128)(2,1)S(1)}, u32[]{:S(2)}, u32[]{:S(2)}) %collective-permute-start.17) | collective-permute-done | bytes 352288 | tf_op jit(solution)/shard_map/ppermute | solution.py:45
  168.8 1.1 fusion.9
  (27 shorter events, 0.1 us)
Async XLA Ops:
  0.6 24.3 %copy-start.6 = (bf16[128,1024]{1,0:T(8,128)(2,1)S(1)}, bf16[128,1024]{1,0:T(8,128)(2,1)}, u32[]{:S(2)}) copy-start(bf16[128,1024]{1,0:T(8,128)(2,1)} %constant.169.clone.tab_ref) | copy-start | bytes 786436
  0.6 12.0 %copy-start.8 = (f32[512]{0:T(512)S(1)}, f32[512]{0:T(512)}, u32[]{:S(2)}) copy-start(f32[512]{0:T(512)} %param.14) | copy-start | bytes 6148
  0.7 24.3 %collective-permute-start = (bf16[1368,512]{1,0:T(8,128)(2,1)}, bf16[1368,512]{1,0:T(8,128)(2,1)S(1)}, u32[]{:S(2)}, u32[]{:S(2)}) collective-permute-start(bf16[1368,512]{1,0:T(8,128)(2,1)} %bitcast.34), channel_id=1, source_target_pairs={{0,1},{1,0},{2,3},{3,2},{4,5},{5,4},{6,7},{7,6},{8,9},{9,8},{10,11... | collective-permute-start | bytes 4202504 | tf_op jit(solution)/shard_map/ppermute | solution.py:45
  0.8 24.2 %collective-permute-start.1 = (bf16[1368,512]{1,0:T(8,128)(2,1)}, bf16[1368,512]{1,0:T(8,128)(2,1)S(1)}, u32[]{:S(2)}, u32[]{:S(2)}) collective-permute-start(bf16[1368,512]{1,0:T(8,128)(2,1)} %bitcast.39), channel_id=1, source_target_pairs={{0,1},{1,0},{2,3},{3,2},{4,5},{5,4},{6,7},{7,6},{8,9},{9,8},{10,11... | collective-permute-start | bytes 4202504 | tf_op jit(solution)/shard_map/ppermute | solution.py:45
  3.2 21.8 %all-to-all-start = ((bf16[16,64,128]{2,1,0:T(8,128)(2,1)}), bf16[16,64,128]{2,1,0:T(8,128)(2,1)S(1)}, u32[]{:S(2)}, u32[]{:S(2)}) async-start(bf16[16,64,128]{2,1,0:T(8,128)(2,1)} %prep.1), calls=%async_computation | async-start | bytes 524288 | tf_op jit(solution)/shard_map/all_to_all | solution.py:329
  12.7 1.2 collective-permute-start.2
  24.9 36.1 %copy-start.2 = (bf16[1368,512]{1,0:T(8,128)(2,1)}, bf16[1368,512]{1,0:T(8,128)(2,1)S(1)}, u32[]{:S(2)}) copy-start(bf16[1368,512]{1,0:T(8,128)(2,1)S(1)} %collective-permute-done.refs_1_) | copy-start | bytes 4202500
  41.5 19.5 %copy-start.7 = (bf16[128,512]{1,0:T(8,128)(2,1)S(1)}, bf16[128,512]{1,0:T(8,128)(2,1)}, u32[]{:S(2)}) copy-start(bf16[128,512]{1,0:T(8,128)(2,1)} %start_ref.1) | copy-start | bytes 393220
  61.1 3.0 %collective-permute-start.3 = (bf16[8,128,512]{2,1,0:T(8,128)(2,1)}, bf16[8,128,512]{2,1,0:T(8,128)(2,1)}, u32[]{:S(2)}, u32[]{:S(2)}) collective-permute-start(bf16[8,128,512]{2,1,0:T(8,128)(2,1)} %all_to_all.16.mixed_hbm), channel_id=1, source_target_pairs={{0,1},{1,0},{2,3},{3,2},{4,5},{5,4},{6,7},{7,6},{8,9},{9,8},{10,11... | collective-permute-start | bytes 3145736 | tf_op jit(solution)/shard_map/ppermute | solution.py:45
  67.6 3.0 %collective-permute-start.4 = (bf16[128,512]{1,0:T(8,128)(2,1)}, bf16[128,512]{1,0:T(8,128)(2,1)S(1)}, u32[]{:S(2)}, u32[]{:S(2)}) collective-permute-start(bf16[128,512]{1,0:T(8,128)(2,1)} %out_proj.3), channel_id=1, source_target_pairs={{0,16},{1,0},{2,18},{3,2},{4,20},{5,4},{6,22},{7,6},{8,24},{9,8},{... | collective-permute-start | bytes 393224 | tf_op jit(solution)/shard_map/ppermute | solution.py:358
  67.8 2.8 %collective-permute-start.5 = (bf16[128,512]{1,0:T(8,128)(2,1)}, bf16[128,512]{1,0:T(8,128)(2,1)S(1)}, u32[]{:S(2)}, u32[]{:S(2)}) collective-permute-start(bf16[128,512]{1,0:T(8,128)(2,1)} %out_proj.3), channel_id=1, source_target_pairs={{1,16},{3,18},{5,20},{7,22},{9,24},{11,26},{13,28},{15,30},{16,1},... | collective-permute-start | bytes 393224 | tf_op jit(solution)/shard_map/ppermute | solution.py:359
  71.6 13.9 %collective-permute-start.7 = (bf16[2,128,512]{2,1,0:T(8,128)(2,1)S(1)}, bf16[2,128,512]{2,1,0:T(8,128)(2,1)S(1)}, u32[]{:S(2)}, u32[]{:S(2)}) collective-permute-start(bf16[2,128,512]{2,1,0:T(8,128)(2,1)S(1)} %pad_maximum_fusion.refs_0_), channel_id=1, source_target_pairs={{0,192},{1,193},{2,194},{3,195},{4,196},{5,197},{6,198},{7,199},{8... | collective-permute-start | bytes 786440 | tf_op jit(solution)/shard_map/ppermute | solution.py:45
  72.3 13.2 %collective-permute-start.8 = (bf16[2,128,512]{2,1,0:T(8,128)(2,1)S(1)}, bf16[2,128,512]{2,1,0:T(8,128)(2,1)S(1)}, u32[]{:S(2)}, u32[]{:S(2)}) collective-permute-start(bf16[2,128,512]{2,1,0:T(8,128)(2,1)S(1)} %pad_maximum_fusion.refs_0_), channel_id=1, source_target_pairs={{0,64},{1,65},{2,66},{3,67},{4,68},{5,69},{6,70},{7,71},{8,72},{9,... | collective-permute-start | bytes 786440 | tf_op jit(solution)/shard_map/ppermute | solution.py:45
  74.6 17.2 %collective-permute-start.6 = (bf16[2,128,512]{2,1,0:T(8,128)(2,1)S(1)}, bf16[2,128,512]{2,1,0:T(8,128)(2,1)}, u32[]{:S(2)}, u32[]{:S(2)}) collective-permute-start(bf16[2,128,512]{2,1,0:T(8,128)(2,1)S(1)} %pad_maximum_fusion.refs_0_), channel_id=1, source_target_pairs={{0,224},{1,225},{2,226},{3,227},{4,228},{5,229},{6,230},{7,231},{8... | collective-permute-start | bytes 786440 | tf_op jit(solution)/shard_map/ppermute | solution.py:45
  76.3 20.0 %collective-permute-start.9 = (bf16[2,128,512]{2,1,0:T(8,128)(2,1)S(1)}, bf16[2,128,512]{2,1,0:T(8,128)(2,1)}, u32[]{:S(2)}, u32[]{:S(2)}) collective-permute-start(bf16[2,128,512]{2,1,0:T(8,128)(2,1)S(1)} %pad_maximum_fusion.refs_0_), channel_id=1, source_target_pairs={{0,32},{1,33},{2,34},{3,35},{4,36},{5,37},{6,38},{7,39},{8,40},{9,... | collective-permute-start | bytes 786440 | tf_op jit(solution)/shard_map/ppermute | solution.py:45
  85.5 0.7 copy-start.4
  86.9 20.2 %copy-start = (bf16[512,1368]{0,1:T(8,128)(2,1)S(1)}, bf16[512,1368]{0,1:T(8,128)(2,1)}, u32[]{:S(2)}) copy-start(bf16[512,1368]{0,1:T(8,128)(2,1)} %param.15) | copy-start | bytes 4202500
  86.9 12.2 %collective-permute-start.11 = (bf16[2,128,512]{2,1,0:T(8,128)(2,1)}, bf16[2,128,512]{2,1,0:T(8,128)(2,1)}, u32[]{:S(2)}, u32[]{:S(2)}) collective-permute-start(bf16[2,128,512]{2,1,0:T(8,128)(2,1)} %broadcast_select_fusion), channel_id=1, source_target_pairs={{0,64},{1,65},{2,66},{3,67},{4,68},{5,69},{6,70},{7,71},{8,72},{9,... | collective-permute-start | bytes 786440 | tf_op jit(solution)/shard_map/ppermute | solution.py:370
  88.6 14.4 %collective-permute-start.10 = (bf16[2,128,512]{2,1,0:T(8,128)(2,1)S(1)}, bf16[2,128,512]{2,1,0:T(8,128)(2,1)}, u32[]{:S(2)}, u32[]{:S(2)}) collective-permute-start(bf16[2,128,512]{2,1,0:T(8,128)(2,1)S(1)} %collective-permute-done.7.refs_2_), channel_id=1, source_target_pairs={{0,224},{1,225},{2,226},{3,227},{4,228},{5,229},{6,230},{7,231},{8... | collective-permute-start | bytes 786440 | tf_op jit(solution)/shard_map/ppermute | solution.py:45
  91.6 13.9 %collective-permute-start.12 = (bf16[2,128,512]{2,1,0:T(8,128)(2,1)}, bf16[2,128,512]{2,1,0:T(8,128)(2,1)}, u32[]{:S(2)}, u32[]{:S(2)}) collective-permute-start(bf16[2,128,512]{2,1,0:T(8,128)(2,1)} %copy-done.4), channel_id=1, source_target_pairs={{0,32},{1,33},{2,34},{3,35},{4,36},{5,37},{6,38},{7,39},{8,40},{9,... | collective-permute-start | bytes 786440 | tf_op jit(solution)/shard_map/ppermute | solution.py:45
  96.3 1.0 copy-start.5
  107.2 1.3 copy-start.3
  108.5 3.3 %copy-start.1 = (bf16[512,1368]{0,1:T(8,128)(2,1)S(1)}, bf16[512,1368]{0,1:T(8,128)(2,1)}, u32[]{:S(2)}) copy-start(bf16[512,1368]{0,1:T(8,128)(2,1)} %param.16) | copy-start | bytes 4202500
  110.1 20.2 %collective-permute-start.13 = (bf16[2,1376,128]{2,1,0:T(8,128)(2,1)S(1)}, bf16[2,1376,128]{2,1,0:T(8,128)(2,1)S(1)}, u32[]{:S(2)}, u32[]{:S(2)}) collective-permute-start(bf16[2,1376,128]{2,1,0:T(8,128)(2,1)S(1)} %get-tuple-element.28), channel_id=1, source_target_pairs={{0,8},{1,9},{2,10},{3,11},{4,12},{5,13},{6,14},{7,15},{8,0},{9,1},... | collective-permute-start | bytes 2113544 | tf_op jit(solution)/shard_map/ppermute | solution.py:45
  113.4 39.8 %collective-permute-start.18 = (bf16[2,1376,128]{2,1,0:T(8,128)(2,1)S(1)}, bf16[2,1376,128]{2,1,0:T(8,128)(2,1)S(1)}, u32[]{:S(2)}, u32[]{:S(2)}) collective-permute-start(bf16[2,1376,128]{2,1,0:T(8,128)(2,1)S(1)} %get-tuple-element.33), channel_id=1, source_target_pairs={{0,2},{1,3},{2,4},{3,5},{4,6},{5,7},{6,0},{7,1},{8,10},{9,11},{10,... | collective-permute-start | bytes 2113544 | tf_op jit(solution)/shard_map/ppermute | solution.py:45
  118.4 34.8 %collective-permute-start.19 = (bf16[2,1376,128]{2,1,0:T(8,128)(2,1)S(1)}, bf16[2,1376,128]{2,1,0:T(8,128)(2,1)S(1)}, u32[]{:S(2)}, u32[]{:S(2)}) collective-permute-start(bf16[2,1376,128]{2,1,0:T(8,128)(2,1)S(1)} %get-tuple-element.34), channel_id=1, source_target_pairs={{0,4},{1,5},{2,6},{3,7},{4,0},{5,1},{6,2},{7,3},{8,12},{9,13},{10,... | collective-permute-start | bytes 2113544 | tf_op jit(solution)/shard_map/ppermute | solution.py:45
  119.0 34.7 %collective-permute-start.20 = (bf16[2,1376,128]{2,1,0:T(8,128)(2,1)S(1)}, bf16[2,1376,128]{2,1,0:T(8,128)(2,1)S(1)}, u32[]{:S(2)}, u32[]{:S(2)}) collective-permute-start(bf16[2,1376,128]{2,1,0:T(8,128)(2,1)S(1)} %get-tuple-element.35), channel_id=1, source_target_pairs={{0,6},{1,7},{2,0},{3,1},{4,2},{5,3},{6,4},{7,5},{8,14},{9,15},{10,... | collective-permute-start | bytes 2113544 | tf_op jit(solution)/shard_map/ppermute | solution.py:45
  121.7 34.6 %collective-permute-start.14 = (bf16[2,1376,128]{2,1,0:T(8,128)(2,1)S(1)}, bf16[2,1376,128]{2,1,0:T(8,128)(2,1)S(1)}, u32[]{:S(2)}, u32[]{:S(2)}) collective-permute-start(bf16[2,1376,128]{2,1,0:T(8,128)(2,1)S(1)} %get-tuple-element.30), channel_id=1, source_target_pairs={{0,8},{1,9},{2,10},{3,11},{4,12},{5,13},{6,14},{7,15},{8,0},{9,1},... | collective-permute-start | bytes 2113544 | tf_op jit(solution)/shard_map/ppermute | solution.py:45
  130.5 35.5 %collective-permute-start.16 = (bf16[1376,128]{1,0:T(8,128)(2,1)S(1)}, bf16[1376,128]{1,0:T(8,128)(2,1)S(1)}, u32[]{:S(2)}, u32[]{:S(2)}) collective-permute-start(bf16[1376,128]{1,0:T(8,128)(2,1)S(1)} %get-tuple-element.37), channel_id=1, source_target_pairs={{0,4},{1,5},{2,6},{3,7},{4,0},{5,1},{6,2},{7,3},{8,12},{9,13},{10,... | collective-permute-start | bytes 1056776 | tf_op jit(solution)/shard_map/ppermute | solution.py:45
  153.9 11.9 %collective-permute-start.21 = (bf16[1376,128]{1,0:T(8,128)(2,1)S(1)}, bf16[1376,128]{1,0:T(8,128)(2,1)S(1)}, u32[]{:S(2)}, u32[]{:S(2)}) collective-permute-start(bf16[1376,128]{1,0:T(8,128)(2,1)S(1)} %fusion.8), channel_id=1, source_target_pairs={{0,8},{1,9},{2,10},{3,11},{4,12},{5,13},{6,14},{7,15},{8,0},{9,1},... | collective-permute-start | bytes 1056776 | tf_op jit(solution)/shard_map/ppermute | solution.py:45
  156.5 9.5 %collective-permute-start.15 = (bf16[1376,128]{1,0:T(8,128)(2,1)S(1)}, bf16[1376,128]{1,0:T(8,128)(2,1)S(1)}, u32[]{:S(2)}, u32[]{:S(2)}) collective-permute-start(bf16[1376,128]{1,0:T(8,128)(2,1)S(1)} %get-tuple-element.38), channel_id=1, source_target_pairs={{0,2},{1,3},{2,4},{3,5},{4,6},{5,7},{6,0},{7,1},{8,10},{9,11},{10,... | collective-permute-start | bytes 1056776 | tf_op jit(solution)/shard_map/ppermute | solution.py:45
  160.2 8.5 %collective-permute-start.17 = (bf16[1376,128]{1,0:T(8,128)(2,1)S(1)}, bf16[1376,128]{1,0:T(8,128)(2,1)S(1)}, u32[]{:S(2)}, u32[]{:S(2)}) collective-permute-start(bf16[1376,128]{1,0:T(8,128)(2,1)S(1)} %get-tuple-element.39), channel_id=1, source_target_pairs={{0,6},{1,7},{2,0},{3,1},{4,2},{5,3},{6,4},{7,5},{8,14},{9,15},{10,... | collective-permute-start | bytes 1056776 | tf_op jit(solution)/shard_map/ppermute | solution.py:45

commit v5 on v4

--- a/solution.py
+++ b/solution.py
@@ -174,46 +174,75 @@
     return jnp.concatenate([rows, tail], axis=0).astype(BF16)
 
 
+def load_kernel(wg_ref, wgx_ref, wu_ref, wux_ref, mark_ref, gate_ref, up_ref, out_mark_ref, sem):
+    copies = []
+    pieces = ((wg_ref, gate_ref, 0), (wgx_ref, gate_ref, CH), (wu_ref, up_ref, 0), (wux_ref, up_ref, CH))
+    for i, (src, dst, at) in enumerate(pieces):
+        copies.append(pltpu.make_async_copy(src, dst.at[:, pl.ds(at, CH)], sem.at[i]))
+        copies[-1].start()
+    for copy in copies:
+        copy.wait()
+    out_mark_ref[...] = mark_ref[...]
+
+
 def scale_kernel(*refs):
     blocks, (gain_ref, gain_oth_ref, out_ref, tail_ref) = refs[:-4], refs[-4:]
     for i, block in enumerate(blocks):
         own = block[0].astype(F32)
         oth = block[1].astype(F32)
-        out_ref[i, 0] = (own * gain_ref[...]).astype(BF16)
-        out_ref[i, 1] = (oth * gain_oth_ref[...]).astype(BF16)
+        out_ref[i, :, 0:CH] = (own * gain_ref[...]).astype(BF16)
+        out_ref[i, :, CH:] = (oth * gain_oth_ref[...]).astype(BF16)
         tail_ref[i] = two_rows(square_sums(own) + square_sums(oth))
 
 
-def mlp_kernel(groups, with_squares, idx_ref, near_ref, far_ref, near_tail_ref, far_tail_ref, *refs):
-    w_ref, wx_ref = refs[:2]
-    out_refs, order_ref = refs[2:-4], refs[-4]
-    so, sx, tail = refs[-3:]
+def mlp_kernel(slots, idx_ref, *refs):
+    rows, (gate_ref, up_ref) = refs[:8], refs[8:10]
+    out_refs, order_ref = refs[10:-3], refs[-3]
+    scaled, tail = refs[-2:]
     for slot in range(8):
         order_ref[slot] = idx_ref[slot]
-    slots = [slot for group in groups for slot in group]
     for at, slot in enumerate(slots):
         which = idx_ref[slot]
         span = slice(at * ROWS, at * ROWS + ROWS)
 
         @pl.when(which < NEAR)
         def _():
-            so[span, :] = near_ref[which, 0]
-            sx[span, :] = near_ref[which, 1]
-            tail[at] = near_tail_ref[which]
-
-        @pl.when(which >= NEAR)
-        def _():
-            so[span, :] = far_ref[which - NEAR, 0]
-            sx[span, :] = far_ref[which - NEAR, 1]
-            tail[at] = far_tail_ref[which - NEAR]
-
-    res = dot_nt(w_ref[...], so[...]) + dot_nt(wx_ref[...], sx[...])
-    at = 0
-    for group, out_ref in zip(groups, out_refs):
-        for i in range(len(group)):
-            end = tail[at] if with_squares else jnp.zeros((FF_PAD - FF_LOC, ROWS), F32)
-            out_ref[i] = with_tail(res[:, at * ROWS : at * ROWS + ROWS], end)
-            at += 1
+            scaled[span, :] = rows[0][which]
+            tail[at] = rows[1][which]
+
+        for i in range(3):
+
+            @pl.when(which == NEAR + i)
+            def _():
+                scaled[span, :] = rows[2 + 2 * i][0]
+                tail[at] = rows[3 + 2 * i][0]
+
+    zeros = jnp.zeros((FF_PAD - FF_LOC, ROWS), F32)
+    gate = dot_nt(gate_ref[...], scaled[...])
+    for at, out_ref in enumerate(out_refs):
+        out_ref[0] = with_tail(gate[:, at * ROWS : at * ROWS + ROWS], zeros)
+    up = dot_nt(up_ref[...], scaled[...])
+    for at, out_ref in enumerate(out_refs):
+        out_ref[1] = with_tail(up[:, at * ROWS : at * ROWS + ROWS], tail[at])
+
+
+def sum_kernel(*refs):
+    total = refs[0][...].astype(F32)
+    for ref in refs[1:-1]:
+        total = total + ref[...].astype(F32)
+    refs[-1][...] = total.astype(BF16)
+
+
+def finish_kernel(*refs):
+    gate = refs[0][0].astype(F32)
+    up = refs[0][1].astype(F32)
+    for ref in refs[1:-1]:
+        gate = gate + ref[0].astype(F32)
+        up = up + ref[1].astype(F32)
+    sums = up[FF_LOC : FF_LOC + 1] + up[FF_LOC + 1 : FF_LOC + 2]
+    scale = lax.rsqrt(sums * (1.0 / (N_TP * CH)) + EPS)
+    gate = gate[:FF_LOC] * scale
+    refs[-1][...] = (gate / (1.0 + jnp.exp(-gate)) * (up[:FF_LOC] * scale)).astype(BF16)
 
 
 def params(mib):
@@ -272,12 +301,27 @@
     )(core, mixed, w_out, start)
 
 
+def load_weights(weights, mark):
+    vmem = pl.BlockSpec(memory_space=pltpu.VMEM)
+    return pl.pallas_call(
+        load_kernel,
+        out_shape=[jax.ShapeDtypeStruct((FF_LOC, 2 * CH), BF16)] * 2
+        + [jax.ShapeDtypeStruct(mark.shape, mark.dtype)],
+        in_specs=[anywhere()] * 4 + [vmem],
+        out_specs=[vmem] * 3,
+        scratch_shapes=[pltpu.SemaphoreType.DMA((4,))],
+        compiler_params=params(16),
+        cost_estimate=pl.CostEstimate(flops=1, bytes_accessed=12 << 20, transcendentals=0),
+        name="load",
+    )(*weights, mark)
+
+
 def scale(blocks, gains):
     n = len(blocks)
     return pl.pallas_call(
         scale_kernel,
         out_shape=[
-            jax.ShapeDtypeStruct((n, 2, ROWS, CH), BF16),
+            jax.ShapeDtypeStruct((n, ROWS, 2 * CH), BF16),
             jax.ShapeDtypeStruct((n, 8, ROWS), F32),
         ],
         compiler_params=params(14),
@@ -288,18 +332,17 @@
     )(*blocks, *gains)
 
 
-def mlp_part(groups, with_squares, idx, rows, weights):
-    n = sum(len(group) for group in groups)
+def mlp_part(slots, idx, rows, weights):
+    n = len(slots)
     vmem = pl.BlockSpec(memory_space=pltpu.VMEM)
-    return pl.pallas_call(
-        functools.partial(mlp_kernel, groups, with_squares),
-        out_shape=[jax.ShapeDtypeStruct((len(g), FF_PAD, ROWS), BF16) for g in groups]
+    *outs, token = pl.pallas_call(
+        functools.partial(mlp_kernel, slots),
+        out_shape=[jax.ShapeDtypeStruct((2, FF_PAD, ROWS), BF16)] * n
         + [jax.ShapeDtypeStruct((8,), jnp.int32)],
-        in_specs=[in_smem()] + [vmem] * 6,
-        out_specs=[vmem] * len(groups) + [in_smem()],
+        in_specs=[in_smem()] + [vmem] * 10,
+        out_specs=[vmem] * n + [in_smem()],
         scratch_shapes=[
-            pltpu.VMEM((n * ROWS, CH), BF16),
-            pltpu.VMEM((n * ROWS, CH), BF16),
+            pltpu.VMEM((n * ROWS, 2 * CH), BF16),
             pltpu.VMEM((n, 8, ROWS), F32),
         ],
         compiler_params=params(18),
@@ -308,6 +351,20 @@
         ),
         name="mlp",
     )(idx, *rows, *weights)
+    return outs, token
+
+
+def in_vmem_call(kernel, shape, name, parts):
+    vmem = pl.BlockSpec(memory_space=pltpu.VMEM)
+    return pl.pallas_call(
+        kernel,
+        out_shape=jax.ShapeDtypeStruct(shape, BF16),
+        in_specs=[vmem] * len(parts),
+        out_specs=vmem,
+        compiler_params=params(16),
+        cost_estimate=pl.CostEstimate(flops=1, bytes_accessed=1 << 19, transcendentals=0),
+        name=name,
+    )(*parts)
 
 
 def shards(residual, features, filters, skip_gain, w_out, norm_gain, w_gate, w_up):
@@ -359,6 +416,8 @@
     second = lax.ppermute(stream, AXES, pairs_of(to_row_owner_second))
     here = x_lo == core
     held = jnp.stack([jnp.where(here, stream, first), jnp.where(here, first, second)])
+    gate_w, up_w, mark = load_weights((wg, wg_oth, wu, wu_oth), held[0, :16])
+    gain, _ = lax.optimization_barrier((gain, mark))
     below, above = [held], [held]
     for step in (2, 1):
         below.insert(1, shift(held, z=step))
@@ -369,9 +428,9 @@
     onward = jnp.where(z % 2 == 0, below[2], above[2])
     opposite = lax.ppermute(onward, AXES, pairs_of(to_opposite))
     gains = (gain, gain_oth)
-    near, near_tail = scale([held, above[1], above[2], below[2], below[1]], gains)
-    far, far_tail = scale([above[3], opposite, below[3]], gains)
-    rows = (near, far, near_tail, far_tail)
+    rows = scale([held, above[1], above[2], below[2], below[1]], gains)
+    for block in (above[3], opposite, below[3]):
+        rows = rows + scale([block], gains)
 
     order = []
     for b in range(4):
@@ -379,46 +438,29 @@
             d = (4 * ((x_hi + a) % 2) + (y + b) % 4 - z) % 8
             order.append(jnp.where(d <= 2, d, jnp.where(d >= 6, d - 3, d + 2)))
     idx = jnp.stack(order).astype(jnp.int32)
-    gate_w, up_w = (wg, wg_oth), (wu, wu_oth)
-
-    def gate_part(order, *groups):
-        *outs, token = mlp_part(groups, False, order, rows, gate_w)
-        return outs + [token]
-
-    def up_part(order, *groups):
-        *outs, token = mlp_part(groups, True, order, rows, up_w)
-        return outs + [token]
-
-    def add(*terms):
-        total = terms[0].astype(F32)
-        for term in terms[1:]:
-            total = total + term.astype(F32)
-        return total
-
-    u_two, _ = up_part(idx, (4, 5))
-    g_send_a, _ = gate_part(idx, (5, 1))
-    u_one, _ = up_part(idx, (2, 3))
-    u_three, _ = up_part(idx, (6, 7))
-    g_send_b, then = gate_part(idx, (3, 7))
-    u_two = shift(u_two, y=2)
-    g_recv_a = shift(g_send_a, x=2)
-    u_one = shift(u_one, y=1)
-    u_three = shift(u_three, y=-1)
-    g_recv_b = shift(g_send_b, x=2)
-    g_keep_a, _ = gate_part(then, (4, 0))
-    g_keep_b, _ = gate_part(then, (2, 6))
-    u_keep, _ = up_part(then, (0, 1))
-    g_last_2 = shift(add(g_keep_a[0], g_recv_a[0]).astype(BF16), y=2)
-    g_last_1 = shift(add(g_keep_b[0], g_recv_b[0]).astype(BF16), y=1)
-    g_last_3 = shift(add(g_keep_b[1], g_recv_b[1]).astype(BF16), y=-1)
-    u_last = shift(add(u_keep[1], u_one[1], u_two[1], u_three[1]).astype(BF16), x=2)
-    up = add(u_keep[0], u_one[0], u_two[0], u_three[0], u_last)
-    gate = add(g_keep_a[1], g_recv_a[1], g_last_1, g_last_2, g_last_3)
-    sums = up[FF_LOC : FF_LOC + 1] + up[FF_LOC + 1 : FF_LOC + 2]
-    row_scale = lax.rsqrt(sums * (1.0 / (N_TP * CH)) + EPS)
-    gate_vals = gate[:FF_LOC] * row_scale
-    up_vals = up[:FF_LOC] * row_scale
-    hidden_t = (jax.nn.silu(gate_vals) * up_vals).astype(BF16)
+
+    weights = (gate_w, up_w)
+    shape = (2, FF_PAD, ROWS)
+    (one_far, three_far), then = mlp_part((3, 7), idx, rows, weights)
+    (two_far,), then = mlp_part((5,), then, rows, weights)
+    (one_near, three_near), then = mlp_part((2, 6), then, rows, weights)
+    (two_near, own_far), then = mlp_part((4, 1), then, rows, weights)
+    (own_near,), _ = mlp_part((0,), then, rows, weights)
+    one_far = shift(one_far, y=1)
+    three_far = shift(three_far, y=-1)
+    two_far = shift(two_far, x=2)
+    one_near = shift(one_near, y=1)
+    three_near = shift(three_near, y=-1)
+    across = in_vmem_call(sum_kernel, shape, "sum", (own_far, one_far, three_far))
+    two_near = in_vmem_call(sum_kernel, shape, "sum", (two_near, two_far))
+    across = shift(across, x=2)
+    two_near = shift(two_near, y=2)
+    hidden_t = in_vmem_call(
+        finish_kernel,
+        (FF_LOC, ROWS),
+        "finish",
+        (own_near, one_near, three_near, across, two_near),
+    )
     return stream, hidden_t.T
 
 

time: 170 us -> 168 us (0.988)
  waiting for transfers between devices: 65.5 us -> 59.6 us
  Pallas kernels: 27.9 us -> 32.5 us
    ppermute x19 -> x17, waiting for transfers between devices: 52.4 us -> 41.2 us  [shift(): return lax.ppermute(arr, AXES, pairs)]
    ppermute x1, waiting for transfers between devices: 0.01 us -> 4.6 us  [shards(): opposite = lax.ppermute(onward, AXES, pairs_of(to_opposite))]
    pallas_call x10 -> x13, Pallas kernels: 15.9 us -> 20.3 us  [the longest x5 11.4 us: mlp_part(): pl.pallas_call(functools.partial(mlp_kernel, slots), out_shape=[jax.Shape...]
    ppermute x19 -> x17, starting transfers between devices: 24.4 us -> 20.2 us  [shift(): return lax.ppermute(arr, AXES, pairs)]
    ppermute x1, starting transfers between devices: 0.17 us -> 3.44 us  [shards(): first = lax.ppermute(stream, AXES, pairs_of(to_row_owner_first))]
  transfers between devices with their start and end apart: 23 -> 21, of which waited for: 13 -> 10; matrix products, arithmetic and copies ran while one was open for 1% -> 1% of each run, Pallas kernels for 10% -> 12%
where the time goes in v5:
time: 168 us; the launch traced here: 167 us
  waiting for transfers between devices  59.6 us (35%)
  starting transfers between devices  35 us (21%)
  Pallas kernels  32.5 us (19%)
  blocking collectives  32.3 us (19%)
  local copies, waits for them, and re-layouts  3.95 us (2%)
  other arithmetic  2.66 us (2%)
    ppermute x17, waiting for transfers between devices, shift(): return lax.ppermute(arr, AXES, pairs)  41.2 us
    ppermute x17, starting transfers between devices, shift(): return lax.ppermute(arr, AXES, pairs)  20.2 us
    all_to_all x1, blocking collectives, shards(): lax.all_to_all(copies, 'tp', 0, 0, axis_index_groups=PLANE_GROUPS, tiled=...  19.4 us
    all_to_all x1, blocking collectives, shards(): conv_rows = lax.all_to_all(conv, 'ctx', 0, 0, tiled=True)  12.9 us
    pallas_call x5, Pallas kernels, mlp_part(): pl.pallas_call(functools.partial(mlp_kernel, slots), out_shape=[jax.Shape...  11.4 us
    all_to_all x1, waiting for transfers between devices, shards(): recv = lax.all_to_all(sent, 'ctx', 0, 0, tiled=True)  11 us
    all_to_all x1, starting transfers between devices, shards(): recv = lax.all_to_all(sent, 'ctx', 0, 0, tiled=True)  9.5 us
    pallas_call x2, Pallas kernels, out_proj(): pl.pallas_call(functools.partial(out_proj_kernel, offset), out_shape=jax....  6.58 us
  transfers between devices with their start and end apart: 21, of which 10 were waited for; matrix products, arithmetic and copies ran while one was open for 1% of the time, Pallas kernels for 12%

profile of v5, /device:TPU:24, one launch (start us, length us, event | category | flops | bytes accessed | tf_op | source)
XLA Modules:
  0.0 166.9 jit_solution(6392890944836606935)
XLA Ops:
  0.6 0.0 copy-start.6
  0.7 0.1 collective-permute-start
  0.8 0.5 collective-permute-start.1
  1.2 1.9 %prep.1 = bf16[16,64,128]{2,1,0:T(8,128)(2,1)} custom-call(bf16[3,128,512]{2,1,0:T(8,128)(2,1)} %bitcast.30, f32[128,512]{1,0:T(8,128)} %filt_ref.1), custom_call_target="tpu_custom_call" | custom-call | tf_op jit(solution)/shard_map/prep/pallas_call | solution.py:380
  3.2 9.5 %all-to-all-start = ((bf16[16,64,128]{2,1,0:T(8,128)(2,1)}), bf16[16,64,128]{2,1,0:T(8,128)(2,1)S(1)}, u32[]{:S(2)}, u32[]{:S(2)}) async-start(bf16[16,64,128]{2,1,0:T(8,128)(2,1)} %prep.1), calls=%async_computation | async-start | bytes 524288 | tf_op jit(solution)/shard_map/all_to_all | solution.py:386
  12.7 0.1 collective-permute-start.2
  12.8 1.1 collective-permute-done.2.refs_6_.refs_2_
  13.9 11.0 %all-to-all-done.x_ref = bf16[16,64,128]{2,1,0:T(8,128)(2,1)S(1)} async-done(((bf16[16,64,128]{2,1,0:T(8,128)(2,1)}), bf16[16,64,128]{2,1,0:T(8,128)(2,1)S(1)}, u32[]{:S(2)}, u32[]{:S(2)}) %all-to-all-start) | async-done | bytes 262176 | tf_op jit(solution)/shard_map/all_to_all | solution.py:386
  24.9 1.1 copy-done.2
  26.1 0.0 collective-permute-done.1.wux_ref
  26.1 1.5 conv.1
  27.5 12.9 %all_to_all.15.conv_ref = bf16[16,32,128]{2,1,0:T(8,128)(2,1)} all-to-all(bf16[16,32,128]{2,1,0:T(8,128)(2,1)S(1)} %conv.1), channel_id=1, replica_groups=mesh['ctx'=16,'tp'=16] {'ctx'}, dimensions={0} | all-to-all | bytes 262144 | tf_op jit(solution)/shard_map/all_to_all | solution.py:399
  40.4 2.2 %mix.1 = bf16[8,128,512]{2,1,0:T(8,128)(2,1)} custom-call(bf16[16,32,128]{2,1,0:T(8,128)(2,1)} %all_to_all.15.conv_ref, bf16[3,128,512]{2,1,0:T(8,128)(2,1)} %bitcast.31, f32[1,512]{1,0:T(1,128)} %bitcast.33), custom_call_target="tpu_custom_call" | custom-call | tf_op jit(solution)/shard_map/mix/pallas_call | solution.py:400
  42.6 19.4 %all_to_all.16.mixed_hbm = bf16[8,128,512]{2,1,0:T(8,128)(2,1)S(1)} all-to-all(bf16[8,128,512]{2,1,0:T(8,128)(2,1)} %mix.1), channel_id=1, replica_groups={{0,2,4,6,8,10,12,14},{1,3,5,7,9,11,13,15},{16,18,20,22,24,26,28,30},{17..., dimensions={0} | all-to-all | bytes 2097152 | tf_op jit(solution)/shard_map/all_to_all | solution.py:407
  62.1 0.0 collective-permute-start.3
  62.1 3.0 %out_proj.2.start_ref = f32[128,512]{1,0:T(8,128)S(1)} custom-call(s32[1]{0:T(128)} %bitcast.core_ref, bf16[8,128,512]{2,1,0:T(8,128)(2,1)S(1)} %all_to_all.16.mixed_hbm, bf16[8192,512]{1,0:T(8,128)(2,1)} %w_hbm.3, bf16[128,512]{1,0:T(8,128)(2,1)S(1)} %copy-done.7), custom_call_target="tpu_custom_call" | custom-call | flops 536870912 | bytes 5242880 | tf_op jit(solution)/shard_map/out_proj/pallas_call | solution.py:282
  65.0 0.0 collective-permute-done.3.mixed_hbm
  65.0 0.0 copy-start.1
  65.1 3.6 %out_proj.3 = bf16[128,512]{1,0:T(8,128)(2,1)} custom-call(s32[1]{0:T(128)} %bitcast.core_ref, bf16[8,128,512]{2,1,0:T(8,128)(2,1)} %collective-permute-done.3.mixed_hbm, bf16[8192,512]{1,0:T(8,128)(2,1)} %w_hbm.3, f32[128,512]{1,0:T(8,128)S(1)} %out_proj.2.start_ref), custom_call_target="tpu_custom_call" | custom-call | flops 536870912 | bytes 5242880 | tf_op jit(solution)/shard_map/out_proj/pallas_call | solution.py:282
  68.7 0.0 copy-start
  68.7 0.8 collective-permute-start.5
  69.5 3.4 %collective-permute-start.4 = (bf16[128,512]{1,0:T(8,128)(2,1)}, bf16[128,512]{1,0:T(8,128)(2,1)S(1)}, u32[]{:S(2)}, u32[]{:S(2)}) collective-permute-start(bf16[128,512]{1,0:T(8,128)(2,1)} %out_proj.3), channel_id=1, source_target_pairs={{0,16},{1,0},{2,18},{3,2},{4,20},{5,4},{6,22},{7,6},{8,24},{9,8},{... | collective-permute-start | bytes 393224 | tf_op jit(solution)/shard_map/ppermute | solution.py:415
  72.9 0.0 collective-permute-done.5
  72.9 2.8 %collective-permute-done.4 = bf16[128,512]{1,0:T(8,128)(2,1)S(1)} collective-permute-done((bf16[128,512]{1,0:T(8,128)(2,1)}, bf16[128,512]{1,0:T(8,128)(2,1)S(1)}, u32[]{:S(2)}, u32[]{:S(2)}) %collective-permute-start.4) | collective-permute-done | bytes 131104 | tf_op jit(solution)/shard_map/ppermute | solution.py:415
  75.8 0.9 select_bitcast_fusion.1
  76.7 0.7 collective-permute-start.8
  77.4 3.5 %collective-permute-start.7 = (bf16[2,128,512]{2,1,0:T(8,128)(2,1)S(1)}, bf16[2,128,512]{2,1,0:T(8,128)(2,1)S(1)}, u32[]{:S(2)}, u32[]{:S(2)}) collective-permute-start(bf16[2,128,512]{2,1,0:T(8,128)(2,1)S(1)} %pad_maximum_fusion.refs_0_), channel_id=1, source_target_pairs={{0,192},{1,193},{2,194},{3,195},{4,196},{5,197},{6,198},{7,199},{8... | collective-permute-start | bytes 786440 | tf_op jit(solution)/shard_map/ppermute | solution.py:45
  81.0 0.4 collective-permute-start.9
  81.4 2.8 %collective-permute-start.6 = (bf16[2,128,512]{2,1,0:T(8,128)(2,1)S(1)}, bf16[2,128,512]{2,1,0:T(8,128)(2,1)}, u32[]{:S(2)}, u32[]{:S(2)}) collective-permute-start(bf16[2,128,512]{2,1,0:T(8,128)(2,1)S(1)} %pad_maximum_fusion.refs_0_), channel_id=1, source_target_pairs={{0,224},{1,225},{2,226},{3,227},{4,228},{5,229},{6,230},{7,231},{8... | collective-permute-start | bytes 786440 | tf_op jit(solution)/shard_map/ppermute | solution.py:45
  84.2 8.9 %collective-permute-done.8.refs_3_ = bf16[2,128,512]{2,1,0:T(8,128)(2,1)} collective-permute-done((bf16[2,128,512]{2,1,0:T(8,128)(2,1)S(1)}, bf16[2,128,512]{2,1,0:T(8,128)(2,1)}, u32[]{:S(2)}, u32[]{:S(2)}) %collective-permute-start.8) | collective-permute-done | bytes 262176 | tf_op jit(solution)/shard_map/ppermute | solution.py:45
  93.1 0.3 collective-permute-start.12
  93.4 1.7 %broadcast_select_fusion = bf16[2,128,512]{2,1,0:T(8,128)(2,1)} fusion(bf16[2,128,512]{2,1,0:T(8,128)(2,1)} %collective-permute-done.8.refs_3_, bf16[2,128,512]{2,1,0:T(8,128)(2,1)S(1)} %collective-permute-done.7.refs_2_, pred[]{:T(512)S(6)} %eq.36), kind=kLoop, calls=%fused_computation.1 | loop fusion | flops 131072 | bytes 786433 | tf_op jit(solution)/shard_map/jit(_where)/select_n | solution.py:428
  95.1 1.1 collective-permute-start.11
  96.3 0.8 collective-permute-start.10
  97.1 0.1 stack.44.idx_ref
  97.2 1.3 copy-done.3
  98.5 1.3 copy-done.5
  99.9 1.5 load.1
  101.4 0.4 collective-permute-done.6.refs_1_
  101.8 1.9 %scale.4 = (bf16[5,128,1024]{2,1,0:T(8,128)(2,1)S(1)}, f32[5,8,128]{2,1,0:T(8,128)S(1)}) custom-call(bf16[2,128,512]{2,1,0:T(8,128)(2,1)S(1)} %pad_maximum_fusion.refs_0_, bf16[2,128,512]{2,1,0:T(8,128)(2,1)} %collective-permute-done.6.refs_1_, bf16[2,128,512]{2,1,0:T(8,128)(2,1)S(1)} %collective-permute-done.7.refs_2_, ...), custom_call_target="tpu_custom_call" | custom-call | flops 20971520 | bytes 2621440 | tf_op jit(solution)/shard_map/scale/pallas_call | solution.py:321
  103.8 0.0 collective-permute-done.12.refs_0_
  103.8 1.2 scale.7
  105.0 4.6 %collective-permute-done.11.refs_0_ = bf16[2,128,512]{2,1,0:T(8,128)(2,1)} collective-permute-done((bf16[2,128,512]{2,1,0:T(8,128)(2,1)}, bf16[2,128,512]{2,1,0:T(8,128)(2,1)}, u32[]{:S(2)}, u32[]{:S(2)}) %collective-permute-start.11) | collective-permute-done | bytes 262176 | tf_op jit(solution)/shard_map/ppermute | solution.py:429
  109.6 1.2 scale.6
  110.9 0.0 collective-permute-done.10.refs_0_
  110.9 1.2 scale.5
  112.1 2.3 %mlp.5 = (bf16[2,1376,128]{2,1,0:T(8,128)(2,1)S(1)}, bf16[2,1376,128]{2,1,0:T(8,128)(2,1)S(1)}, s32[8]{0:T(128)S(1)}) custom-call(s32[8]{0:T(128)S(1)} %stack.44.idx_ref, bf16[5,128,1024]{2,1,0:T(8,128)(2,1)S(1)} %get-tuple-element.30.refs_0_, f32[5,8,128]{2,1,0:T(8,128)S(1)} %get-tuple-element.31.refs_1_, ...), custom_call_target="tpu_custom_call" | custom-call | flops 100000000 | bytes 524288 | tf_op jit(solution)/shard_map/mlp/pallas_call | solution.py:338
  114.4 2.5 %collective-permute-start.15 = (bf16[2,1376,128]{2,1,0:T(8,128)(2,1)S(1)}, bf16[2,1376,128]{2,1,0:T(8,128)(2,1)S(1)}, u32[]{:S(2)}, u32[]{:S(2)}) collective-permute-start(bf16[2,1376,128]{2,1,0:T(8,128)(2,1)S(1)} %get-tuple-element.50), channel_id=1, source_target_pairs={{0,2},{1,3},{2,4},{3,5},{4,6},{5,7},{6,0},{7,1},{8,10},{9,11},{10,... | collective-permute-start | bytes 2113544 | tf_op jit(solution)/shard_map/ppermute | solution.py:45
  116.9 2.2 %mlp.6 = (bf16[2,1376,128]{2,1,0:T(8,128)(2,1)S(1)}, s32[8]{0:T(128)S(1)}) custom-call(s32[8]{0:T(128)S(1)} %get-tuple-element.42.idx_ref, bf16[5,128,1024]{2,1,0:T(8,128)(2,1)S(1)} %get-tuple-element.30.refs_0_, f32[5,8,128]{2,1,0:T(8,128)S(1)} %get-tuple-element.31.refs_1_, bf16[1,128,1024]{2,1,0:T(8,128)(2,1)S(1)} %get-tuple-element.32.refs_2_, ...), custom_call_target="tpu_custom_call" | custom-call | flops 100000000 | bytes 524288 | tf_op jit(solution)/shard_map/mlp/pallas_call | solution.py:338
  119.2 1.2 collective-permute-start.18
  120.4 2.3 %mlp.7 = (bf16[2,1376,128]{2,1,0:T(8,128)(2,1)S(1)}, bf16[2,1376,128]{2,1,0:T(8,128)(2,1)S(1)}, s32[8]{0:T(128)S(1)}) custom-call(s32[8]{0:T(128)S(1)} %get-tuple-element.43.idx_ref, bf16[5,128,1024]{2,1,0:T(8,128)(2,1)S(1)} %get-tuple-element.30.refs_0_, f32[5,8,128]{2,1,0:T(8,128)S(1)} %get-tuple-element.31.refs_1_, ...), custom_call_target="tpu_custom_call" | custom-call | flops 100000000 | bytes 524288 | tf_op jit(solution)/shard_map/mlp/pallas_call | solution.py:338
  122.7 3.1 %collective-permute-start.13 = (bf16[2,1376,128]{2,1,0:T(8,128)(2,1)S(1)}, bf16[2,1376,128]{2,1,0:T(8,128)(2,1)S(1)}, u32[]{:S(2)}, u32[]{:S(2)}) collective-permute-start(bf16[2,1376,128]{2,1,0:T(8,128)(2,1)S(1)} %get-tuple-element.47), channel_id=1, source_target_pairs={{0,2},{1,3},{2,4},{3,5},{4,6},{5,7},{6,0},{7,1},{8,10},{9,11},{10,... | collective-permute-start | bytes 2113544 | tf_op jit(solution)/shard_map/ppermute | solution.py:45
  125.8 0.0 collective-permute-start.14
  125.8 2.3 %mlp.8 = (bf16[2,1376,128]{2,1,0:T(8,128)(2,1)S(1)}, bf16[2,1376,128]{2,1,0:T(8,128)(2,1)S(1)}, s32[8]{0:T(128)S(1)}) custom-call(s32[8]{0:T(128)S(1)} %get-tuple-element.44.idx_ref, bf16[5,128,1024]{2,1,0:T(8,128)(2,1)S(1)} %get-tuple-element.30.refs_0_, f32[5,8,128]{2,1,0:T(8,128)S(1)} %get-tuple-element.31.refs_1_, ...), custom_call_target="tpu_custom_call" | custom-call | flops 100000000 | bytes 524288 | tf_op jit(solution)/shard_map/mlp/pallas_call | solution.py:338
  128.1 5.1 %collective-permute-done.15.refs_1_ = bf16[2,1376,128]{2,1,0:T(8,128)(2,1)S(1)} collective-permute-done((bf16[2,1376,128]{2,1,0:T(8,128)(2,1)S(1)}, bf16[2,1376,128]{2,1,0:T(8,128)(2,1)S(1)}, u32[]{:S(2)}, u32[]{:S(2)}) %collective-permute-start.15) | collective-permute-done | bytes 704544 | tf_op jit(solution)/shard_map/ppermute | solution.py:45
  133.2 3.7 %collective-permute-done.16.refs_2_ = bf16[2,1376,128]{2,1,0:T(8,128)(2,1)S(1)} collective-permute-done((bf16[2,1376,128]{2,1,0:T(8,128)(2,1)S(1)}, bf16[2,1376,128]{2,1,0:T(8,128)(2,1)S(1)}, u32[]{:S(2)}, u32[]{:S(2)}) %collective-permute-start.16) | collective-permute-done | bytes 704544 | tf_op jit(solution)/shard_map/ppermute | solution.py:45
  136.9 0.3 sum.2
  137.1 1.0 collective-permute-start.17
  138.1 0.2 sum.3
  138.3 3.1 %collective-permute-start.19 = (bf16[2,1376,128]{2,1,0:T(8,128)(2,1)S(1)}, bf16[2,1376,128]{2,1,0:T(8,128)(2,1)S(1)}, u32[]{:S(2)}, u32[]{:S(2)}) collective-permute-start(bf16[2,1376,128]{2,1,0:T(8,128)(2,1)S(1)} %sum.3), channel_id=1, source_target_pairs={{0,4},{1,5},{2,6},{3,7},{4,0},{5,1},{6,2},{7,3},{8,12},{9,13},{10,... | collective-permute-start | bytes 2113544 | tf_op jit(solution)/shard_map/ppermute | solution.py:45
  141.4 2.2 %mlp.9 = (bf16[2,1376,128]{2,1,0:T(8,128)(2,1)S(1)}, s32[8]{0:T(128)}) custom-call(s32[8]{0:T(128)S(1)} %get-tuple-element.45.idx_ref, bf16[5,128,1024]{2,1,0:T(8,128)(2,1)S(1)} %get-tuple-element.30.refs_0_, f32[5,8,128]{2,1,0:T(8,128)S(1)} %get-tuple-element.31.refs_1_, bf16[1,128,1024]{2,1,0:T(8,128)(2,1)S(1)} %get-tuple-element.32.refs_2_, ...), custom_call_target="tpu_custom_call" | custom-call | flops 100000000 | bytes 524288 | tf_op jit(solution)/shard_map/mlp/pallas_call | solution.py:338
  143.6 18.5 %collective-permute-done.13.refs_1_ = bf16[2,1376,128]{2,1,0:T(8,128)(2,1)S(1)} collective-permute-done((bf16[2,1376,128]{2,1,0:T(8,128)(2,1)S(1)}, bf16[2,1376,128]{2,1,0:T(8,128)(2,1)S(1)}, u32[]{:S(2)}, u32[]{:S(2)}) %collective-permute-start.13) | collective-permute-done | bytes 704544 | tf_op jit(solution)/shard_map/ppermute | solution.py:45
  162.2 3.4 %collective-permute-done.14.refs_2_ = bf16[2,1376,128]{2,1,0:T(8,128)(2,1)S(1)} collective-permute-done((bf16[2,1376,128]{2,1,0:T(8,128)(2,1)S(1)}, bf16[2,1376,128]{2,1,0:T(8,128)(2,1)S(1)}, u32[]{:S(2)}, u32[]{:S(2)}) %collective-permute-start.14) | collective-permute-done | bytes 704544 | tf_op jit(solution)/shard_map/ppermute | solution.py:45
  165.5 1.4 finish.1
  (21 shorter events, 0.1 us)
Async XLA Ops:
  0.6 25.4 %copy-start.6 = (bf16[128,1024]{1,0:T(8,128)(2,1)S(1)}, bf16[128,1024]{1,0:T(8,128)(2,1)}, u32[]{:S(2)}) copy-start(bf16[128,1024]{1,0:T(8,128)(2,1)} %constant.162.clone.tab_ref) | copy-start | bytes 786436
  0.6 12.0 %copy-start.8 = (f32[512]{0:T(512)S(1)}, f32[512]{0:T(512)}, u32[]{:S(2)}) copy-start(f32[512]{0:T(512)} %param.14) | copy-start | bytes 6148
  0.7 24.3 %collective-permute-start = (bf16[1368,512]{1,0:T(8,128)(2,1)}, bf16[1368,512]{1,0:T(8,128)(2,1)S(1)}, u32[]{:S(2)}, u32[]{:S(2)}) collective-permute-start(bf16[1368,512]{1,0:T(8,128)(2,1)} %bitcast.21), channel_id=1, source_target_pairs={{0,1},{1,0},{2,3},{3,2},{4,5},{5,4},{6,7},{7,6},{8,9},{9,8},{10,11... | collective-permute-start | bytes 4202504 | tf_op jit(solution)/shard_map/ppermute | solution.py:45
  0.8 25.3 %collective-permute-start.1 = (bf16[1368,512]{1,0:T(8,128)(2,1)}, bf16[1368,512]{1,0:T(8,128)(2,1)S(1)}, u32[]{:S(2)}, u32[]{:S(2)}) collective-permute-start(bf16[1368,512]{1,0:T(8,128)(2,1)} %bitcast.23), channel_id=1, source_target_pairs={{0,1},{1,0},{2,3},{3,2},{4,5},{5,4},{6,7},{7,6},{8,9},{9,8},{10,11... | collective-permute-start | bytes 4202504 | tf_op jit(solution)/shard_map/ppermute | solution.py:45
  3.2 21.8 %all-to-all-start = ((bf16[16,64,128]{2,1,0:T(8,128)(2,1)}), bf16[16,64,128]{2,1,0:T(8,128)(2,1)S(1)}, u32[]{:S(2)}, u32[]{:S(2)}) async-start(bf16[16,64,128]{2,1,0:T(8,128)(2,1)} %prep.1), calls=%async_computation | async-start | bytes 524288 | tf_op jit(solution)/shard_map/all_to_all | solution.py:386
  12.7 1.2 collective-permute-start.2
  24.9 1.1 copy-start.2
  26.1 36.0 %copy-start.4 = (bf16[1368,512]{1,0:T(8,128)(2,1)}, bf16[1368,512]{1,0:T(8,128)(2,1)S(1)}, u32[]{:S(2)}) copy-start(bf16[1368,512]{1,0:T(8,128)(2,1)S(1)} %collective-permute-done.1.wux_ref) | copy-start | bytes 4202500
  42.6 19.4 %copy-start.7 = (bf16[128,512]{1,0:T(8,128)(2,1)S(1)}, bf16[128,512]{1,0:T(8,128)(2,1)}, u32[]{:S(2)}) copy-start(bf16[128,512]{1,0:T(8,128)(2,1)} %start_ref.1) | copy-start | bytes 393220
  62.1 3.0 %collective-permute-start.3 = (bf16[8,128,512]{2,1,0:T(8,128)(2,1)S(1)}, bf16[8,128,512]{2,1,0:T(8,128)(2,1)}, u32[]{:S(2)}, u32[]{:S(2)}) collective-permute-start(bf16[8,128,512]{2,1,0:T(8,128)(2,1)S(1)} %all_to_all.16.mixed_hbm), channel_id=1, source_target_pairs={{0,1},{1,0},{2,3},{3,2},{4,5},{5,4},{6,7},{7,6},{8,9},{9,8},{10,11... | collective-permute-start | bytes 3145736 | tf_op jit(solution)/shard_map/ppermute | solution.py:45
  65.0 32.1 %copy-start.1 = (bf16[512,1368]{0,1:T(8,128)(2,1)S(1)}, bf16[512,1368]{0,1:T(8,128)(2,1)}, u32[]{:S(2)}) copy-start(bf16[512,1368]{0,1:T(8,128)(2,1)} %param.16) | copy-start | bytes 4202500
  68.7 28.5 %copy-start = (bf16[512,1368]{0,1:T(8,128)(2,1)S(1)}, bf16[512,1368]{0,1:T(8,128)(2,1)}, u32[]{:S(2)}) copy-start(bf16[512,1368]{0,1:T(8,128)(2,1)} %param.15) | copy-start | bytes 4202500
  68.7 4.2 %collective-permute-start.5 = (bf16[128,512]{1,0:T(8,128)(2,1)}, bf16[128,512]{1,0:T(8,128)(2,1)S(1)}, u32[]{:S(2)}, u32[]{:S(2)}) collective-permute-start(bf16[128,512]{1,0:T(8,128)(2,1)} %out_proj.3), channel_id=1, source_target_pairs={{1,16},{3,18},{5,20},{7,22},{9,24},{11,26},{13,28},{15,30},{16,1},... | collective-permute-start | bytes 393224 | tf_op jit(solution)/shard_map/ppermute | solution.py:416
  69.5 6.3 %collective-permute-start.4 = (bf16[128,512]{1,0:T(8,128)(2,1)}, bf16[128,512]{1,0:T(8,128)(2,1)S(1)}, u32[]{:S(2)}, u32[]{:S(2)}) collective-permute-start(bf16[128,512]{1,0:T(8,128)(2,1)} %out_proj.3), channel_id=1, source_target_pairs={{0,16},{1,0},{2,18},{3,2},{4,20},{5,4},{6,22},{7,6},{8,24},{9,8},{... | collective-permute-start | bytes 393224 | tf_op jit(solution)/shard_map/ppermute | solution.py:415
  76.7 16.3 %collective-permute-start.8 = (bf16[2,128,512]{2,1,0:T(8,128)(2,1)S(1)}, bf16[2,128,512]{2,1,0:T(8,128)(2,1)}, u32[]{:S(2)}, u32[]{:S(2)}) collective-permute-start(bf16[2,128,512]{2,1,0:T(8,128)(2,1)S(1)} %pad_maximum_fusion.refs_0_), channel_id=1, source_target_pairs={{0,64},{1,65},{2,66},{3,67},{4,68},{5,69},{6,70},{7,71},{8,72},{9,... | collective-permute-start | bytes 786440 | tf_op jit(solution)/shard_map/ppermute | solution.py:45
  77.4 16.0 %collective-permute-start.7 = (bf16[2,128,512]{2,1,0:T(8,128)(2,1)S(1)}, bf16[2,128,512]{2,1,0:T(8,128)(2,1)S(1)}, u32[]{:S(2)}, u32[]{:S(2)}) collective-permute-start(bf16[2,128,512]{2,1,0:T(8,128)(2,1)S(1)} %pad_maximum_fusion.refs_0_), channel_id=1, source_target_pairs={{0,192},{1,193},{2,194},{3,195},{4,196},{5,197},{6,198},{7,199},{8... | collective-permute-start | bytes 786440 | tf_op jit(solution)/shard_map/ppermute | solution.py:45
  81.0 20.4 %collective-permute-start.9 = (bf16[2,128,512]{2,1,0:T(8,128)(2,1)S(1)}, bf16[2,128,512]{2,1,0:T(8,128)(2,1)}, u32[]{:S(2)}, u32[]{:S(2)}) collective-permute-start(bf16[2,128,512]{2,1,0:T(8,128)(2,1)S(1)} %pad_maximum_fusion.refs_0_), channel_id=1, source_target_pairs={{0,32},{1,33},{2,34},{3,35},{4,36},{5,37},{6,38},{7,39},{8,40},{9,... | collective-permute-start | bytes 786440 | tf_op jit(solution)/shard_map/ppermute | solution.py:45
  81.4 20.4 %collective-permute-start.6 = (bf16[2,128,512]{2,1,0:T(8,128)(2,1)S(1)}, bf16[2,128,512]{2,1,0:T(8,128)(2,1)}, u32[]{:S(2)}, u32[]{:S(2)}) collective-permute-start(bf16[2,128,512]{2,1,0:T(8,128)(2,1)S(1)} %pad_maximum_fusion.refs_0_), channel_id=1, source_target_pairs={{0,224},{1,225},{2,226},{3,227},{4,228},{5,229},{6,230},{7,231},{8... | collective-permute-start | bytes 786440 | tf_op jit(solution)/shard_map/ppermute | solution.py:45
  93.1 10.7 %collective-permute-start.12 = (bf16[2,128,512]{2,1,0:T(8,128)(2,1)}, bf16[2,128,512]{2,1,0:T(8,128)(2,1)}, u32[]{:S(2)}, u32[]{:S(2)}) collective-permute-start(bf16[2,128,512]{2,1,0:T(8,128)(2,1)} %collective-permute-done.8.refs_3_), channel_id=1, source_target_pairs={{0,32},{1,33},{2,34},{3,35},{4,36},{5,37},{6,38},{7,39},{8,40},{9,... | collective-permute-start | bytes 786440 | tf_op jit(solution)/shard_map/ppermute | solution.py:45
  95.1 14.5 %collective-permute-start.11 = (bf16[2,128,512]{2,1,0:T(8,128)(2,1)}, bf16[2,128,512]{2,1,0:T(8,128)(2,1)}, u32[]{:S(2)}, u32[]{:S(2)}) collective-permute-start(bf16[2,128,512]{2,1,0:T(8,128)(2,1)} %broadcast_select_fusion), channel_id=1, source_target_pairs={{0,64},{1,65},{2,66},{3,67},{4,68},{5,69},{6,70},{7,71},{8,72},{9,... | collective-permute-start | bytes 786440 | tf_op jit(solution)/shard_map/ppermute | solution.py:429
  96.3 14.6 %collective-permute-start.10 = (bf16[2,128,512]{2,1,0:T(8,128)(2,1)S(1)}, bf16[2,128,512]{2,1,0:T(8,128)(2,1)}, u32[]{:S(2)}, u32[]{:S(2)}) collective-permute-start(bf16[2,128,512]{2,1,0:T(8,128)(2,1)S(1)} %collective-permute-done.7.refs_2_), channel_id=1, source_target_pairs={{0,224},{1,225},{2,226},{3,227},{4,228},{5,229},{6,230},{7,231},{8... | collective-permute-start | bytes 786440 | tf_op jit(solution)/shard_map/ppermute | solution.py:45
  97.2 1.3 copy-start.3
  98.5 1.3 copy-start.5
  114.4 18.8 %collective-permute-start.15 = (bf16[2,1376,128]{2,1,0:T(8,128)(2,1)S(1)}, bf16[2,1376,128]{2,1,0:T(8,128)(2,1)S(1)}, u32[]{:S(2)}, u32[]{:S(2)}) collective-permute-start(bf16[2,1376,128]{2,1,0:T(8,128)(2,1)S(1)} %get-tuple-element.50), channel_id=1, source_target_pairs={{0,2},{1,3},{2,4},{3,5},{4,6},{5,7},{6,0},{7,1},{8,10},{9,11},{10,... | collective-permute-start | bytes 2113544 | tf_op jit(solution)/shard_map/ppermute | solution.py:45
  116.9 19.9 %collective-permute-start.16 = (bf16[2,1376,128]{2,1,0:T(8,128)(2,1)S(1)}, bf16[2,1376,128]{2,1,0:T(8,128)(2,1)S(1)}, u32[]{:S(2)}, u32[]{:S(2)}) collective-permute-start(bf16[2,1376,128]{2,1,0:T(8,128)(2,1)S(1)} %get-tuple-element.51), channel_id=1, source_target_pairs={{0,6},{1,7},{2,0},{3,1},{4,2},{5,3},{6,4},{7,5},{8,14},{9,15},{10,... | collective-permute-start | bytes 2113544 | tf_op jit(solution)/shard_map/ppermute | solution.py:45
  119.2 18.9 %collective-permute-start.18 = (bf16[2,1376,128]{2,1,0:T(8,128)(2,1)S(1)}, bf16[2,1376,128]{2,1,0:T(8,128)(2,1)S(1)}, u32[]{:S(2)}, u32[]{:S(2)}) collective-permute-start(bf16[2,1376,128]{2,1,0:T(8,128)(2,1)S(1)} %get-tuple-element.53), channel_id=1, source_target_pairs={{0,8},{1,9},{2,10},{3,11},{4,12},{5,13},{6,14},{7,15},{8,0},{9,1},... | collective-permute-start | bytes 2113544 | tf_op jit(solution)/shard_map/ppermute | solution.py:45
  122.7 39.5 %collective-permute-start.13 = (bf16[2,1376,128]{2,1,0:T(8,128)(2,1)S(1)}, bf16[2,1376,128]{2,1,0:T(8,128)(2,1)S(1)}, u32[]{:S(2)}, u32[]{:S(2)}) collective-permute-start(bf16[2,1376,128]{2,1,0:T(8,128)(2,1)S(1)} %get-tuple-element.47), channel_id=1, source_target_pairs={{0,2},{1,3},{2,4},{3,5},{4,6},{5,7},{6,0},{7,1},{8,10},{9,11},{10,... | collective-permute-start | bytes 2113544 | tf_op jit(solution)/shard_map/ppermute | solution.py:45
  125.8 39.8 %collective-permute-start.14 = (bf16[2,1376,128]{2,1,0:T(8,128)(2,1)S(1)}, bf16[2,1376,128]{2,1,0:T(8,128)(2,1)S(1)}, u32[]{:S(2)}, u32[]{:S(2)}) collective-permute-start(bf16[2,1376,128]{2,1,0:T(8,128)(2,1)S(1)} %get-tuple-element.48), channel_id=1, source_target_pairs={{0,6},{1,7},{2,0},{3,1},{4,2},{5,3},{6,4},{7,5},{8,14},{9,15},{10,... | collective-permute-start | bytes 2113544 | tf_op jit(solution)/shard_map/ppermute | solution.py:45
  137.1 28.4 %collective-permute-start.17 = (bf16[2,1376,128]{2,1,0:T(8,128)(2,1)S(1)}, bf16[2,1376,128]{2,1,0:T(8,128)(2,1)S(1)}, u32[]{:S(2)}, u32[]{:S(2)}) collective-permute-start(bf16[2,1376,128]{2,1,0:T(8,128)(2,1)S(1)} %sum.2), channel_id=1, source_target_pairs={{0,8},{1,9},{2,10},{3,11},{4,12},{5,13},{6,14},{7,15},{8,0},{9,1},... | collective-permute-start | bytes 2113544 | tf_op jit(solution)/shard_map/ppermute | solution.py:45
  138.3 27.3 %collective-permute-start.19 = (bf16[2,1376,128]{2,1,0:T(8,128)(2,1)S(1)}, bf16[2,1376,128]{2,1,0:T(8,128)(2,1)S(1)}, u32[]{:S(2)}, u32[]{:S(2)}) collective-permute-start(bf16[2,1376,128]{2,1,0:T(8,128)(2,1)S(1)} %sum.3), channel_id=1, source_target_pairs={{0,4},{1,5},{2,6},{3,7},{4,0},{5,1},{6,2},{7,3},{8,12},{9,13},{10,... | collective-permute-start | bytes 2113544 | tf_op jit(solution)/shard_map/ppermute | solution.py:45

commit v6 on v5

--- a/solution.py
+++ b/solution.py
@@ -21,6 +21,7 @@
 FF_PAD = 1376
 EPS = 1e-06
 NEAR = 5
+ROW_OF = (0, 2, 3, 6, 7, 5, 4, 1)
 PLANE_GROUPS = [[xh * 8 + y * 2 + k for xh in range(2) for y in range(4)] for k in range(2)]
 
 
@@ -195,9 +196,9 @@
         tail_ref[i] = two_rows(square_sums(own) + square_sums(oth))
 
 
-def mlp_kernel(slots, idx_ref, *refs):
-    rows, (gate_ref, up_ref) = refs[:8], refs[8:10]
-    out_refs, order_ref = refs[10:-3], refs[-3]
+def mlp_kernel(slots, split, idx_ref, *refs):
+    rows, (gate_ref, up_ref) = refs[:4], refs[4:6]
+    out_refs, order_ref = refs[6:-3], refs[-3]
     scaled, tail = refs[-2:]
     for slot in range(8):
         order_ref[slot] = idx_ref[slot]
@@ -210,20 +211,20 @@
             scaled[span, :] = rows[0][which]
             tail[at] = rows[1][which]
 
-        for i in range(3):
-
-            @pl.when(which == NEAR + i)
-            def _():
-                scaled[span, :] = rows[2 + 2 * i][0]
-                tail[at] = rows[3 + 2 * i][0]
+        @pl.when(which >= NEAR)
+        def _():
+            scaled[span, :] = rows[2][which - NEAR]
+            tail[at] = rows[3][which - NEAR]
 
     zeros = jnp.zeros((FF_PAD - FF_LOC, ROWS), F32)
     gate = dot_nt(gate_ref[...], scaled[...])
-    for at, out_ref in enumerate(out_refs):
-        out_ref[0] = with_tail(gate[:, at * ROWS : at * ROWS + ROWS], zeros)
+    for at in range(len(slots)):
+        target = out_refs[2 * at] if split else out_refs[at].at[0]
+        target[...] = with_tail(gate[:, at * ROWS : at * ROWS + ROWS], zeros)
     up = dot_nt(up_ref[...], scaled[...])
-    for at, out_ref in enumerate(out_refs):
-        out_ref[1] = with_tail(up[:, at * ROWS : at * ROWS + ROWS], tail[at])
+    for at in range(len(slots)):
+        target = out_refs[2 * at + 1] if split else out_refs[at].at[1]
+        target[...] = with_tail(up[:, at * ROWS : at * ROWS + ROWS], tail[at])
 
 
 def sum_kernel(*refs):
@@ -233,16 +234,20 @@
     refs[-1][...] = total.astype(BF16)
 
 
-def finish_kernel(*refs):
-    gate = refs[0][0].astype(F32)
-    up = refs[0][1].astype(F32)
-    for ref in refs[1:-1]:
-        gate = gate + ref[0].astype(F32)
-        up = up + ref[1].astype(F32)
+def sum_apart_kernel(left_ref, right_ref, gate_ref, up_ref):
+    for i, out_ref in enumerate((gate_ref, up_ref)):
+        out_ref[...] = (left_ref[i].astype(F32) + right_ref[i].astype(F32)).astype(BF16)
+
+
+def finish_kernel(own_ref, across_ref, gate_1_ref, gate_3_ref, up_1_ref, up_3_ref, out_ref):
+    gate = own_ref[0].astype(F32) + across_ref[0].astype(F32)
+    gate = gate + (gate_1_ref[...].astype(F32) + gate_3_ref[...].astype(F32))
+    up = own_ref[1].astype(F32) + across_ref[1].astype(F32)
+    up = up + (up_1_ref[...].astype(F32) + up_3_ref[...].astype(F32))
     sums = up[FF_LOC : FF_LOC + 1] + up[FF_LOC + 1 : FF_LOC + 2]
     scale = lax.rsqrt(sums * (1.0 / (N_TP * CH)) + EPS)
     gate = gate[:FF_LOC] * scale
-    refs[-1][...] = (gate / (1.0 + jnp.exp(-gate)) * (up[:FF_LOC] * scale)).astype(BF16)
+    out_ref[...] = (gate / (1.0 + jnp.exp(-gate)) * (up[:FF_LOC] * scale)).astype(BF16)
 
 
 def params(mib):
@@ -274,8 +279,8 @@
     return pl.BlockSpec(memory_space=pl.ANY)
 
 
-def to_opposite(z, x, y, k):
-    return (z + 2, x, y, k) if z % 2 == 0 else (z - 2, x, y, k)
+def along(steps, z, x, y, k):
+    return (z + steps, x, y, k) if z % 2 == 0 else (z - steps, x, y, k)
 
 
 def out_proj(offset, core, mixed, w_out, start, dtype):
@@ -332,15 +337,16 @@
     )(*blocks, *gains)
 
 
-def mlp_part(slots, idx, rows, weights):
+def mlp_part(slots, idx, rows, weights, split=False):
     n = len(slots)
+    shapes = [(FF_PAD, ROWS)] * (2 * n) if split else [(2, FF_PAD, ROWS)] * n
     vmem = pl.BlockSpec(memory_space=pltpu.VMEM)
     *outs, token = pl.pallas_call(
-        functools.partial(mlp_kernel, slots),
-        out_shape=[jax.ShapeDtypeStruct((2, FF_PAD, ROWS), BF16)] * n
+        functools.partial(mlp_kernel, slots, split),
+        out_shape=[jax.ShapeDtypeStruct(shape, BF16) for shape in shapes]
         + [jax.ShapeDtypeStruct((8,), jnp.int32)],
-        in_specs=[in_smem()] + [vmem] * 10,
-        out_specs=[vmem] * n + [in_smem()],
+        in_specs=[in_smem()] + [vmem] * 6,
+        out_specs=[vmem] * len(shapes) + [in_smem()],
         scratch_shapes=[
             pltpu.VMEM((n * ROWS, 2 * CH), BF16),
             pltpu.VMEM((n, 8, ROWS), F32),
@@ -354,13 +360,13 @@
     return outs, token
 
 
-def in_vmem_call(kernel, shape, name, parts):
+def in_vmem_call(kernel, shapes, name, parts):
     vmem = pl.BlockSpec(memory_space=pltpu.VMEM)
     return pl.pallas_call(
         kernel,
-        out_shape=jax.ShapeDtypeStruct(shape, BF16),
+        out_shape=[jax.ShapeDtypeStruct(shape, BF16) for shape in shapes],
         in_specs=[vmem] * len(parts),
-        out_specs=vmem,
+        out_specs=[vmem] * len(shapes),
         compiler_params=params(16),
         cost_estimate=pl.CostEstimate(flops=1, bytes_accessed=1 << 19, transcendentals=0),
         name=name,
@@ -418,48 +424,53 @@
     held = jnp.stack([jnp.where(here, stream, first), jnp.where(here, first, second)])
     gate_w, up_w, mark = load_weights((wg, wg_oth, wu, wu_oth), held[0, :16])
     gain, _ = lax.optimization_barrier((gain, mark))
-    below, above = [held], [held]
-    for step in (2, 1):
-        below.insert(1, shift(held, z=step))
-        above.insert(1, shift(held, z=-step))
-    below.append(shift(below[2], z=1))
-    above.append(shift(above[2], z=-1))
     z = ctx // 2
-    onward = jnp.where(z % 2 == 0, below[2], above[2])
-    opposite = lax.ppermute(onward, AXES, pairs_of(to_opposite))
+    side = jnp.where(z % 2 == 0, -1, 1)
+    two_first = lax.ppermute(held, AXES, pairs_of(functools.partial(along, 2)))
+    two_second = lax.ppermute(held, AXES, pairs_of(functools.partial(along, -2)))
+    one_first = lax.ppermute(held, AXES, pairs_of(functools.partial(along, 1)))
+    one_second = lax.ppermute(held, AXES, pairs_of(functools.partial(along, -1)))
+    three_first = lax.ppermute(two_first, AXES, pairs_of(functools.partial(along, 1)))
+    three_second = lax.ppermute(two_second, AXES, pairs_of(functools.partial(along, -1)))
+    opposite = lax.ppermute(two_first, AXES, pairs_of(functools.partial(along, 2)))
     gains = (gain, gain_oth)
-    rows = scale([held, above[1], above[2], below[2], below[1]], gains)
-    for block in (above[3], opposite, below[3]):
-        rows = rows + scale([block], gains)
+    rows = scale([held, one_first, one_second, two_first, two_second], gains)
+    rows = rows + scale([three_first, three_second, opposite], gains)
 
     order = []
     for b in range(4):
         for a in range(2):
-            d = (4 * ((x_hi + a) % 2) + (y + b) % 4 - z) % 8
-            order.append(jnp.where(d <= 2, d, jnp.where(d >= 6, d - 3, d + 2)))
-    idx = jnp.stack(order).astype(jnp.int32)
+            d = (side * (4 * ((x_hi + a) % 2) + (y + b) % 4 - z)) % 8
+            order.append(d)
+    seen = jnp.stack(order)
+    idx = sum(jnp.where(seen == d, at, 0) for d, at in enumerate(ROW_OF)).astype(jnp.int32)
 
     weights = (gate_w, up_w)
-    shape = (2, FF_PAD, ROWS)
-    (one_far, three_far), then = mlp_part((3, 7), idx, rows, weights)
-    (two_far,), then = mlp_part((5,), then, rows, weights)
-    (one_near, three_near), then = mlp_part((2, 6), then, rows, weights)
+    both, half = (2, FF_PAD, ROWS), (FF_PAD, ROWS)
+    (two_far,), then = mlp_part((5,), idx, rows, weights)
+    (one_far, three_far), then = mlp_part((3, 7), then, rows, weights)
+    near, then = mlp_part((2, 6), then, rows, weights, split=True)
     (two_near, own_far), then = mlp_part((4, 1), then, rows, weights)
     (own_near,), _ = mlp_part((0,), then, rows, weights)
+    two_far = shift(two_far, x=2)
     one_far = shift(one_far, y=1)
     three_far = shift(three_far, y=-1)
-    two_far = shift(two_far, x=2)
-    one_near = shift(one_near, y=1)
-    three_near = shift(three_near, y=-1)
-    across = in_vmem_call(sum_kernel, shape, "sum", (own_far, one_far, three_far))
-    two_near = in_vmem_call(sum_kernel, shape, "sum", (two_near, two_far))
+    up_1 = shift(near[1], y=1)
+    gate_3 = shift(near[2], y=-1)
+    gate_by, up_by = in_vmem_call(sum_apart_kernel, (half, half), "sum", (two_near, two_far))
+    (across,) = in_vmem_call(sum_kernel, (both,), "sum", (own_far, one_far, three_far))
+    gate_by = shift(gate_by, y=1)
+    up_by = shift(up_by, y=-1)
     across = shift(across, x=2)
-    two_near = shift(two_near, y=2)
-    hidden_t = in_vmem_call(
+    (gate_1,) = in_vmem_call(sum_kernel, (half,), "sum", (near[0], gate_by))
+    (up_3,) = in_vmem_call(sum_kernel, (half,), "sum", (near[3], up_by))
+    gate_1 = shift(gate_1, y=1)
+    up_3 = shift(up_3, y=-1)
+    (hidden_t,) = in_vmem_call(
         finish_kernel,
-        (FF_LOC, ROWS),
+        ((FF_LOC, ROWS),),
         "finish",
-        (own_near, one_near, three_near, across, two_near),
+        (own_near, across, gate_1, gate_3, up_1, up_3),
     )
     return stream, hidden_t.T
 

time: 168 us -> 162 us (0.964)
  waiting for transfers between devices: 59.6 us -> 55.1 us
  starting transfers between devices: 35 us -> 38.8 us
  Pallas kernels: 32.5 us -> 29.2 us
  other arithmetic: 2.66 us -> 0.97 us
    ppermute x17 -> x14, waiting for transfers between devices: 41.2 us -> 24 us  [shift(): return lax.ppermute(arr, AXES, pairs)]
    ppermute x1 -> x7, waiting for transfers between devices: 4.6 us -> 17.3 us  [the longest x1 11.9 us: shards(): two_first = lax.ppermute(held, AXES, pairs_of(functools.partial(along, 2)))]
    ppermute x1 -> x7, starting transfers between devices: 1.14 us -> 9.55 us  [the longest x1 3.54 us: shards(): lax.ppermute(held, AXES, pairs_of(functools.partial(along, -2)))]
    ppermute x17 -> x14, starting transfers between devices: 20.2 us -> 15.5 us  [shift(): return lax.ppermute(arr, AXES, pairs)]
    pallas_call x4 -> x2, Pallas kernels: 5.64 us -> 2.34 us  [scale(): pl.pallas_call(scale_kernel, out_shape=[jax.ShapeDtypeStruct((n, ROWS, 2...]
    select_n x1 -> x0, other arithmetic: 1.71 us -> none  [shards(): onward = jnp.where(z % 2 == 0, below[2], above[2])]
    pallas_call x8 -> x10, Pallas kernels: 13.2 us -> 13.2 us  [the longest x5 11.3 us: mlp_part(): pl.pallas_call(functools.partial(mlp_kernel, slots, split), out_shape=[ja...]
  transfers between devices with their start and end apart: 21 -> 24, of which waited for: 10 -> 12; matrix products, arithmetic and copies ran while one was open for 1% -> 0% of each run, Pallas kernels for 12% -> 11%
where the time goes in v6:
time: 162 us; the launch traced here: 161 us
  waiting for transfers between devices  55.1 us (34%)
  starting transfers between devices  38.8 us (24%)
  blocking collectives  32.3 us (20%)
  Pallas kernels  29.2 us (18%)
  local copies, waits for them, and re-layouts  3.94 us (2%)
    ppermute x14, waiting for transfers between devices, shift(): return lax.ppermute(arr, AXES, pairs)  24 us
    all_to_all x1, blocking collectives, shards(): lax.all_to_all(copies, 'tp', 0, 0, axis_index_groups=PLANE_GROUPS, tiled=...  19.4 us
    ppermute x14, starting transfers between devices, shift(): return lax.ppermute(arr, AXES, pairs)  15.5 us
    all_to_all x1, blocking collectives, shards(): conv_rows = lax.all_to_all(conv, 'ctx', 0, 0, tiled=True)  12.9 us
    ppermute x1, waiting for transfers between devices, shards(): two_first = lax.ppermute(held, AXES, pairs_of(functools.partial(along, 2)))  11.9 us
    pallas_call x5, Pallas kernels, mlp_part(): pl.pallas_call(functools.partial(mlp_kernel, slots, split), out_shape=[ja...  11.3 us
    all_to_all x1, waiting for transfers between devices, shards(): recv = lax.all_to_all(sent, 'ctx', 0, 0, tiled=True)  11 us
    all_to_all x1, starting transfers between devices, shards(): recv = lax.all_to_all(sent, 'ctx', 0, 0, tiled=True)  9.5 us
  transfers between devices with their start and end apart: 24, of which 12 were waited for; matrix products, arithmetic and copies ran while one was open for 0% of the time, Pallas kernels for 11%

profile of v6, /device:TPU:24, one launch (start us, length us, event | category | flops | bytes accessed | tf_op | source)
XLA Modules:
  0.0 161.1 jit_solution(13230039263153976607)
XLA Ops:
  0.6 0.0 copy-start.6
  0.7 0.1 collective-permute-start
  0.8 0.5 collective-permute-start.1
  1.2 1.9 %prep.1 = bf16[16,64,128]{2,1,0:T(8,128)(2,1)} custom-call(bf16[3,128,512]{2,1,0:T(8,128)(2,1)} %bitcast.28, f32[128,512]{1,0:T(8,128)} %filt_ref.1), custom_call_target="tpu_custom_call" | custom-call | tf_op jit(solution)/shard_map/prep/pallas_call | solution.py:386
  3.2 9.5 %all-to-all-start = ((bf16[16,64,128]{2,1,0:T(8,128)(2,1)}), bf16[16,64,128]{2,1,0:T(8,128)(2,1)S(1)}, u32[]{:S(2)}, u32[]{:S(2)}) async-start(bf16[16,64,128]{2,1,0:T(8,128)(2,1)} %prep.1), calls=%async_computation | async-start | bytes 524288 | tf_op jit(solution)/shard_map/all_to_all | solution.py:392
  12.7 0.1 collective-permute-start.2
  12.8 1.1 collective-permute-done.2.refs_6_.refs_4_
  13.9 11.0 %all-to-all-done.x_ref = bf16[16,64,128]{2,1,0:T(8,128)(2,1)S(1)} async-done(((bf16[16,64,128]{2,1,0:T(8,128)(2,1)}), bf16[16,64,128]{2,1,0:T(8,128)(2,1)S(1)}, u32[]{:S(2)}, u32[]{:S(2)}) %all-to-all-start) | async-done | bytes 262176 | tf_op jit(solution)/shard_map/all_to_all | solution.py:392
  24.9 0.0 collective-permute-done.wgx_ref
  24.9 1.1 copy-done.2
  26.1 0.0 collective-permute-done.1.wux_ref
  26.1 1.5 conv.1
  27.5 12.9 %all_to_all.15.conv_ref = bf16[16,32,128]{2,1,0:T(8,128)(2,1)} all-to-all(bf16[16,32,128]{2,1,0:T(8,128)(2,1)S(1)} %conv.1), channel_id=1, replica_groups=mesh['ctx'=16,'tp'=16] {'ctx'}, dimensions={0} | all-to-all | bytes 262144 | tf_op jit(solution)/shard_map/all_to_all | solution.py:405
  40.4 2.2 %mix.1 = bf16[8,128,512]{2,1,0:T(8,128)(2,1)} custom-call(bf16[16,32,128]{2,1,0:T(8,128)(2,1)} %all_to_all.15.conv_ref, bf16[3,128,512]{2,1,0:T(8,128)(2,1)} %bitcast.29, f32[1,512]{1,0:T(1,128)} %bitcast.31), custom_call_target="tpu_custom_call" | custom-call | tf_op jit(solution)/shard_map/mix/pallas_call | solution.py:406
  42.6 19.4 %all_to_all.16.mixed_hbm = bf16[8,128,512]{2,1,0:T(8,128)(2,1)S(1)} all-to-all(bf16[8,128,512]{2,1,0:T(8,128)(2,1)} %mix.1), channel_id=1, replica_groups={{0,2,4,6,8,10,12,14},{1,3,5,7,9,11,13,15},{16,18,20,22,24,26,28,30},{17..., dimensions={0} | all-to-all | bytes 2097152 | tf_op jit(solution)/shard_map/all_to_all | solution.py:413
  62.0 3.0 %out_proj.2.start_ref = f32[128,512]{1,0:T(8,128)S(1)} custom-call(s32[1]{0:T(128)} %bitcast.core_ref, bf16[8,128,512]{2,1,0:T(8,128)(2,1)S(1)} %all_to_all.16.mixed_hbm, bf16[8192,512]{1,0:T(8,128)(2,1)} %w_hbm.3, bf16[128,512]{1,0:T(8,128)(2,1)S(1)} %copy-done.7), custom_call_target="tpu_custom_call" | custom-call | flops 536870912 | bytes 5242880 | tf_op jit(solution)/shard_map/out_proj/pallas_call | solution.py:287
  65.0 0.0 collective-permute-done.3.mixed_hbm
  65.0 0.0 copy-start.1
  65.0 3.6 %out_proj.3 = bf16[128,512]{1,0:T(8,128)(2,1)} custom-call(s32[1]{0:T(128)} %bitcast.core_ref, bf16[8,128,512]{2,1,0:T(8,128)(2,1)} %collective-permute-done.3.mixed_hbm, bf16[8192,512]{1,0:T(8,128)(2,1)} %w_hbm.3, f32[128,512]{1,0:T(8,128)S(1)} %out_proj.2.start_ref), custom_call_target="tpu_custom_call" | custom-call | flops 536870912 | bytes 5242880 | tf_op jit(solution)/shard_map/out_proj/pallas_call | solution.py:287
  68.7 0.0 copy-start
  68.7 0.8 collective-permute-start.5
  69.5 3.4 %collective-permute-start.4 = (bf16[128,512]{1,0:T(8,128)(2,1)}, bf16[128,512]{1,0:T(8,128)(2,1)S(1)}, u32[]{:S(2)}, u32[]{:S(2)}) collective-permute-start(bf16[128,512]{1,0:T(8,128)(2,1)} %out_proj.3), channel_id=1, source_target_pairs={{0,16},{1,0},{2,18},{3,2},{4,20},{5,4},{6,22},{7,6},{8,24},{9,8},{... | collective-permute-start | bytes 393224 | tf_op jit(solution)/shard_map/ppermute | solution.py:421
  72.9 2.8 %collective-permute-done.4 = bf16[128,512]{1,0:T(8,128)(2,1)S(1)} collective-permute-done((bf16[128,512]{1,0:T(8,128)(2,1)}, bf16[128,512]{1,0:T(8,128)(2,1)S(1)}, u32[]{:S(2)}, u32[]{:S(2)}) %collective-permute-start.4) | collective-permute-done | bytes 131104 | tf_op jit(solution)/shard_map/ppermute | solution.py:421
  75.8 0.9 select_bitcast_fusion.1
  76.7 0.7 collective-permute-start.8
  77.4 3.5 %collective-permute-start.9 = (bf16[2,128,512]{2,1,0:T(8,128)(2,1)S(1)}, bf16[2,128,512]{2,1,0:T(8,128)(2,1)}, u32[]{:S(2)}, u32[]{:S(2)}) collective-permute-start(bf16[2,128,512]{2,1,0:T(8,128)(2,1)S(1)} %pad_maximum_fusion.refs_0_), channel_id=1, source_target_pairs={{0,192},{1,193},{2,194},{3,195},{4,196},{5,197},{6,198},{7,199},{8... | collective-permute-start | bytes 786440 | tf_op jit(solution)/shard_map/ppermute | solution.py:430
  80.9 0.1 stack.44
  81.0 0.6 collective-permute-start.7
  81.7 11.9 %collective-permute-done.8.refs_3_ = bf16[2,128,512]{2,1,0:T(8,128)(2,1)S(1)} collective-permute-done((bf16[2,128,512]{2,1,0:T(8,128)(2,1)S(1)}, bf16[2,128,512]{2,1,0:T(8,128)(2,1)S(1)}, u32[]{:S(2)}, u32[]{:S(2)}) %collective-permute-start.8) | collective-permute-done | bytes 262176 | tf_op jit(solution)/shard_map/ppermute | solution.py:429
  93.6 0.0 collective-permute-start.12
  93.6 2.2 %collective-permute-start.10 = (bf16[2,128,512]{2,1,0:T(8,128)(2,1)S(1)}, bf16[2,128,512]{2,1,0:T(8,128)(2,1)S(1)}, u32[]{:S(2)}, u32[]{:S(2)}) collective-permute-start(bf16[2,128,512]{2,1,0:T(8,128)(2,1)S(1)} %collective-permute-done.8.refs_3_), channel_id=1, source_target_pairs={{0,32},{1,33},{2,34},{3,35},{4,36},{5,37},{6,38},{7,39},{8,40},{9,... | collective-permute-start | bytes 786440 | tf_op jit(solution)/shard_map/ppermute | solution.py:433
  95.8 2.5 %collective-permute-start.11 = (bf16[2,128,512]{2,1,0:T(8,128)(2,1)}, bf16[2,128,512]{2,1,0:T(8,128)(2,1)S(1)}, u32[]{:S(2)}, u32[]{:S(2)}) collective-permute-start(bf16[2,128,512]{2,1,0:T(8,128)(2,1)} %collective-permute-done.9.refs_4_), channel_id=1, source_target_pairs={{0,224},{1,225},{2,226},{3,227},{4,228},{5,229},{6,230},{7,231},{8... | collective-permute-start | bytes 786440 | tf_op jit(solution)/shard_map/ppermute | solution.py:434
  98.4 1.3 copy-done.3
  99.7 1.3 copy-done.5
  101.1 1.5 load.1
  102.6 0.8 collective-permute-done.7.refs_2_
  103.4 1.8 %scale.2 = (bf16[5,128,1024]{2,1,0:T(8,128)(2,1)S(1)}, f32[5,8,128]{2,1,0:T(8,128)S(1)}) custom-call(bf16[2,128,512]{2,1,0:T(8,128)(2,1)S(1)} %pad_maximum_fusion.refs_0_, bf16[2,128,512]{2,1,0:T(8,128)(2,1)S(1)} %collective-permute-done.6.refs_1_, bf16[2,128,512]{2,1,0:T(8,128)(2,1)S(1)} %collective-permute-done.7.refs_2_, ...), custom_call_target="tpu_custom_call" | custom-call | flops 20971520 | bytes 2621440 | tf_op jit(solution)/shard_map/scale/pallas_call | solution.py:326
  105.1 4.6 %collective-permute-done.11.refs_1_ = bf16[2,128,512]{2,1,0:T(8,128)(2,1)S(1)} collective-permute-done((bf16[2,128,512]{2,1,0:T(8,128)(2,1)}, bf16[2,128,512]{2,1,0:T(8,128)(2,1)S(1)}, u32[]{:S(2)}, u32[]{:S(2)}) %collective-permute-start.11) | collective-permute-done | bytes 262176 | tf_op jit(solution)/shard_map/ppermute | solution.py:434
  109.7 0.6 scale.3
  110.3 2.2 %mlp.5 = (bf16[2,1376,128]{2,1,0:T(8,128)(2,1)S(1)}, s32[8]{0:T(128)S(1)}) custom-call(s32[8]{0:T(128)S(1)} %fusion.5.idx_ref, bf16[5,128,1024]{2,1,0:T(8,128)(2,1)S(1)} %get-tuple-element.30.refs_0_, f32[5,8,128]{2,1,0:T(8,128)S(1)} %get-tuple-element.31.refs_1_, bf16[3,128,1024]{2,1,0:T(8,128)(2,1)S(1)} %get-tuple-element.32.refs_2_, ...), custom_call_target="tpu_custom_call" | custom-call | flops 100000000 | bytes 524288 | tf_op jit(solution)/shard_map/mlp/pallas_call | solution.py:344
  112.5 1.6 %collective-permute-start.16 = (bf16[2,1376,128]{2,1,0:T(8,128)(2,1)S(1)}, bf16[2,1376,128]{2,1,0:T(8,128)(2,1)S(1)}, u32[]{:S(2)}, u32[]{:S(2)}) collective-permute-start(bf16[2,1376,128]{2,1,0:T(8,128)(2,1)S(1)} %get-tuple-element.48), channel_id=1, source_target_pairs={{0,8},{1,9},{2,10},{3,11},{4,12},{5,13},{6,14},{7,15},{8,0},{9,1},... | collective-permute-start | bytes 2113544 | tf_op jit(solution)/shard_map/ppermute | solution.py:46
  114.1 2.3 %mlp.6 = (bf16[2,1376,128]{2,1,0:T(8,128)(2,1)S(1)}, bf16[2,1376,128]{2,1,0:T(8,128)(2,1)S(1)}, s32[8]{0:T(128)S(1)}) custom-call(s32[8]{0:T(128)S(1)} %get-tuple-element.38.idx_ref, bf16[5,128,1024]{2,1,0:T(8,128)(2,1)S(1)} %get-tuple-element.30.refs_0_, f32[5,8,128]{2,1,0:T(8,128)S(1)} %get-tuple-element.31.refs_1_, ...), custom_call_target="tpu_custom_call" | custom-call | flops 100000000 | bytes 524288 | tf_op jit(solution)/shard_map/mlp/pallas_call | solution.py:344
  116.4 1.9 %collective-permute-start.13 = (bf16[2,1376,128]{2,1,0:T(8,128)(2,1)S(1)}, bf16[2,1376,128]{2,1,0:T(8,128)(2,1)S(1)}, u32[]{:S(2)}, u32[]{:S(2)}) collective-permute-start(bf16[2,1376,128]{2,1,0:T(8,128)(2,1)S(1)} %get-tuple-element.44), channel_id=1, source_target_pairs={{0,2},{1,3},{2,4},{3,5},{4,6},{5,7},{6,0},{7,1},{8,10},{9,11},{10,... | collective-permute-start | bytes 2113544 | tf_op jit(solution)/shard_map/ppermute | solution.py:46
  118.3 0.2 collective-permute-start.14
  118.6 2.3 %mlp.7 = (bf16[1376,128]{1,0:T(8,128)(2,1)S(1)}, bf16[1376,128]{1,0:T(8,128)(2,1)S(1)}, bf16[1376,128]{1,0:T(8,128)(2,1)S(1)}, bf16[1376,128]{1,0:T(8,128)(2,1)S(1)}, s32[8]{0:T(128)S(1)}) custom-call(s32[8]{0:T(128)S(1)} %get-tuple-element.39.idx_ref, bf16[5,128,1024]{2,1,0:T(8,128)(2,1)S(1)} %get-tuple-element.30.refs_0_, ...), custom_call_target="tpu_custom_call" | custom-call | flops 100000000 | bytes 524288 | tf_op jit(solution)/shard_map/mlp/pallas_call | solution.py:344
  120.9 2.3 %mlp.8 = (bf16[2,1376,128]{2,1,0:T(8,128)(2,1)S(1)}, bf16[2,1376,128]{2,1,0:T(8,128)(2,1)S(1)}, s32[8]{0:T(128)S(1)}) custom-call(s32[8]{0:T(128)S(1)} %get-tuple-element.40.idx_ref, bf16[5,128,1024]{2,1,0:T(8,128)(2,1)S(1)} %get-tuple-element.30.refs_0_, f32[5,8,128]{2,1,0:T(8,128)S(1)} %get-tuple-element.31.refs_1_, ...), custom_call_target="tpu_custom_call" | custom-call | flops 100000000 | bytes 524288 | tf_op jit(solution)/shard_map/mlp/pallas_call | solution.py:344
  123.2 8.6 %collective-permute-done.16.right_ref = bf16[2,1376,128]{2,1,0:T(8,128)(2,1)S(1)} collective-permute-done((bf16[2,1376,128]{2,1,0:T(8,128)(2,1)S(1)}, bf16[2,1376,128]{2,1,0:T(8,128)(2,1)S(1)}, u32[]{:S(2)}, u32[]{:S(2)}) %collective-permute-start.16) | collective-permute-done | bytes 704544 | tf_op jit(solution)/shard_map/ppermute | solution.py:46
  131.8 0.2 sum.5
  132.0 2.5 %collective-permute-start.17 = (bf16[1376,128]{1,0:T(8,128)(2,1)S(1)}, bf16[1376,128]{1,0:T(8,128)(2,1)S(1)}, u32[]{:S(2)}, u32[]{:S(2)}) collective-permute-start(bf16[1376,128]{1,0:T(8,128)(2,1)S(1)} %get-tuple-element.49), channel_id=1, source_target_pairs={{0,2},{1,3},{2,4},{3,5},{4,6},{5,7},{6,0},{7,1},{8,10},{9,11},{10,... | collective-permute-start | bytes 1056776 | tf_op jit(solution)/shard_map/ppermute | solution.py:46
  134.5 2.2 %collective-permute-done.14.refs_2_ = bf16[2,1376,128]{2,1,0:T(8,128)(2,1)S(1)} collective-permute-done((bf16[2,1376,128]{2,1,0:T(8,128)(2,1)S(1)}, bf16[2,1376,128]{2,1,0:T(8,128)(2,1)S(1)}, u32[]{:S(2)}, u32[]{:S(2)}) %collective-permute-start.14) | collective-permute-done | bytes 704544 | tf_op jit(solution)/shard_map/ppermute | solution.py:46
  136.7 0.3 sum.4
  136.9 3.9 %collective-permute-start.15 = (bf16[2,1376,128]{2,1,0:T(8,128)(2,1)S(1)}, bf16[2,1376,128]{2,1,0:T(8,128)(2,1)S(1)}, u32[]{:S(2)}, u32[]{:S(2)}) collective-permute-start(bf16[2,1376,128]{2,1,0:T(8,128)(2,1)S(1)} %sum.4), channel_id=1, source_target_pairs={{0,8},{1,9},{2,10},{3,11},{4,12},{5,13},{6,14},{7,15},{8,0},{9,1},... | collective-permute-start | bytes 2113544 | tf_op jit(solution)/shard_map/ppermute | solution.py:46
  140.8 0.0 collective-permute-start.19
  140.8 3.2 %collective-permute-start.20 = (bf16[1376,128]{1,0:T(8,128)(2,1)S(1)}, bf16[1376,128]{1,0:T(8,128)(2,1)S(1)}, u32[]{:S(2)}, u32[]{:S(2)}) collective-permute-start(bf16[1376,128]{1,0:T(8,128)(2,1)S(1)} %get-tuple-element.51), channel_id=1, source_target_pairs={{0,2},{1,3},{2,4},{3,5},{4,6},{5,7},{6,0},{7,1},{8,10},{9,11},{10,... | collective-permute-start | bytes 1056776 | tf_op jit(solution)/shard_map/ppermute | solution.py:46
  144.1 0.1 sum.6
  144.1 1.3 collective-permute-start.18
  145.5 1.4 collective-permute-done.21.refs_1_
  146.9 0.1 sum.7
  147.0 0.1 collective-permute-start.22
  147.1 2.2 %mlp.9 = (bf16[2,1376,128]{2,1,0:T(8,128)(2,1)S(1)}, s32[8]{0:T(128)}) custom-call(s32[8]{0:T(128)S(1)} %get-tuple-element.41.idx_ref, bf16[5,128,1024]{2,1,0:T(8,128)(2,1)S(1)} %get-tuple-element.30.refs_0_, f32[5,8,128]{2,1,0:T(8,128)S(1)} %get-tuple-element.31.refs_1_, bf16[3,128,1024]{2,1,0:T(8,128)(2,1)S(1)} %get-tuple-element.32.refs_2_, ...), custom_call_target="tpu_custom_call" | custom-call | flops 100000000 | bytes 524288 | tf_op jit(solution)/shard_map/mlp/pallas_call | solution.py:344
  149.3 5.2 %collective-permute-done.19.gate_3_ref = bf16[1376,128]{1,0:T(8,128)(2,1)S(1)} collective-permute-done((bf16[1376,128]{1,0:T(8,128)(2,1)S(1)}, bf16[1376,128]{1,0:T(8,128)(2,1)S(1)}, u32[]{:S(2)}, u32[]{:S(2)}) %collective-permute-start.19) | collective-permute-done | bytes 352288 | tf_op jit(solution)/shard_map/ppermute | solution.py:46
  154.4 2.2 %collective-permute-done.18.gate_1_ref = bf16[1376,128]{1,0:T(8,128)(2,1)S(1)} collective-permute-done((bf16[1376,128]{1,0:T(8,128)(2,1)S(1)}, bf16[1376,128]{1,0:T(8,128)(2,1)S(1)}, u32[]{:S(2)}, u32[]{:S(2)}) %collective-permute-start.18) | collective-permute-done | bytes 352288 | tf_op jit(solution)/shard_map/ppermute | solution.py:46
  156.6 3.3 %collective-permute-done.22.up_3_ref = bf16[1376,128]{1,0:T(8,128)(2,1)S(1)} collective-permute-done((bf16[1376,128]{1,0:T(8,128)(2,1)S(1)}, bf16[1376,128]{1,0:T(8,128)(2,1)S(1)}, u32[]{:S(2)}, u32[]{:S(2)}) %collective-permute-start.22) | collective-permute-done | bytes 352288 | tf_op jit(solution)/shard_map/ppermute | solution.py:46
  159.9 1.3 finish.1
  (27 shorter events, 0.1 us)
Async XLA Ops:
  0.6 25.4 %copy-start.6 = (bf16[128,1024]{1,0:T(8,128)(2,1)S(1)}, bf16[128,1024]{1,0:T(8,128)(2,1)}, u32[]{:S(2)}) copy-start(bf16[128,1024]{1,0:T(8,128)(2,1)} %constant.165.clone.tab_ref) | copy-start | bytes 786436
  0.6 12.0 %copy-start.8 = (f32[512]{0:T(512)S(1)}, f32[512]{0:T(512)}, u32[]{:S(2)}) copy-start(f32[512]{0:T(512)} %param.14) | copy-start | bytes 6148
  0.7 24.3 %collective-permute-start = (bf16[1368,512]{1,0:T(8,128)(2,1)}, bf16[1368,512]{1,0:T(8,128)(2,1)S(1)}, u32[]{:S(2)}, u32[]{:S(2)}) collective-permute-start(bf16[1368,512]{1,0:T(8,128)(2,1)} %bitcast.21), channel_id=1, source_target_pairs={{0,1},{1,0},{2,3},{3,2},{4,5},{5,4},{6,7},{7,6},{8,9},{9,8},{10,11... | collective-permute-start | bytes 4202504 | tf_op jit(solution)/shard_map/ppermute | solution.py:46
  0.8 25.3 %collective-permute-start.1 = (bf16[1368,512]{1,0:T(8,128)(2,1)}, bf16[1368,512]{1,0:T(8,128)(2,1)S(1)}, u32[]{:S(2)}, u32[]{:S(2)}) collective-permute-start(bf16[1368,512]{1,0:T(8,128)(2,1)} %bitcast.23), channel_id=1, source_target_pairs={{0,1},{1,0},{2,3},{3,2},{4,5},{5,4},{6,7},{7,6},{8,9},{9,8},{10,11... | collective-permute-start | bytes 4202504 | tf_op jit(solution)/shard_map/ppermute | solution.py:46
  3.2 21.8 %all-to-all-start = ((bf16[16,64,128]{2,1,0:T(8,128)(2,1)}), bf16[16,64,128]{2,1,0:T(8,128)(2,1)S(1)}, u32[]{:S(2)}, u32[]{:S(2)}) async-start(bf16[16,64,128]{2,1,0:T(8,128)(2,1)} %prep.1), calls=%async_computation | async-start | bytes 524288 | tf_op jit(solution)/shard_map/all_to_all | solution.py:392
  12.7 1.2 collective-permute-start.2
  24.9 1.1 copy-start.2
  26.1 36.0 %copy-start.4 = (bf16[1368,512]{1,0:T(8,128)(2,1)}, bf16[1368,512]{1,0:T(8,128)(2,1)S(1)}, u32[]{:S(2)}) copy-start(bf16[1368,512]{1,0:T(8,128)(2,1)S(1)} %collective-permute-done.1.wux_ref) | copy-start | bytes 4202500
  42.6 19.4 %copy-start.7 = (bf16[128,512]{1,0:T(8,128)(2,1)S(1)}, bf16[128,512]{1,0:T(8,128)(2,1)}, u32[]{:S(2)}) copy-start(bf16[128,512]{1,0:T(8,128)(2,1)} %start_ref.1) | copy-start | bytes 393220
  62.0 3.0 %collective-permute-start.3 = (bf16[8,128,512]{2,1,0:T(8,128)(2,1)S(1)}, bf16[8,128,512]{2,1,0:T(8,128)(2,1)}, u32[]{:S(2)}, u32[]{:S(2)}) collective-permute-start(bf16[8,128,512]{2,1,0:T(8,128)(2,1)S(1)} %all_to_all.16.mixed_hbm), channel_id=1, source_target_pairs={{0,1},{1,0},{2,3},{3,2},{4,5},{5,4},{6,7},{7,6},{8,9},{9,8},{10,11... | collective-permute-start | bytes 3145736 | tf_op jit(solution)/shard_map/ppermute | solution.py:46
  65.0 33.3 %copy-start.1 = (bf16[512,1368]{0,1:T(8,128)(2,1)S(1)}, bf16[512,1368]{0,1:T(8,128)(2,1)}, u32[]{:S(2)}) copy-start(bf16[512,1368]{0,1:T(8,128)(2,1)} %param.16) | copy-start | bytes 4202500
  68.7 29.7 %copy-start = (bf16[512,1368]{0,1:T(8,128)(2,1)S(1)}, bf16[512,1368]{0,1:T(8,128)(2,1)}, u32[]{:S(2)}) copy-start(bf16[512,1368]{0,1:T(8,128)(2,1)} %param.15) | copy-start | bytes 4202500
  68.7 4.2 %collective-permute-start.5 = (bf16[128,512]{1,0:T(8,128)(2,1)}, bf16[128,512]{1,0:T(8,128)(2,1)S(1)}, u32[]{:S(2)}, u32[]{:S(2)}) collective-permute-start(bf16[128,512]{1,0:T(8,128)(2,1)} %out_proj.3), channel_id=1, source_target_pairs={{1,16},{3,18},{5,20},{7,22},{9,24},{11,26},{13,28},{15,30},{16,1},... | collective-permute-start | bytes 393224 | tf_op jit(solution)/shard_map/ppermute | solution.py:422
  69.5 6.3 %collective-permute-start.4 = (bf16[128,512]{1,0:T(8,128)(2,1)}, bf16[128,512]{1,0:T(8,128)(2,1)S(1)}, u32[]{:S(2)}, u32[]{:S(2)}) collective-permute-start(bf16[128,512]{1,0:T(8,128)(2,1)} %out_proj.3), channel_id=1, source_target_pairs={{0,16},{1,0},{2,18},{3,2},{4,20},{5,4},{6,22},{7,6},{8,24},{9,8},{... | collective-permute-start | bytes 393224 | tf_op jit(solution)/shard_map/ppermute | solution.py:421
  76.7 16.9 %collective-permute-start.8 = (bf16[2,128,512]{2,1,0:T(8,128)(2,1)S(1)}, bf16[2,128,512]{2,1,0:T(8,128)(2,1)S(1)}, u32[]{:S(2)}, u32[]{:S(2)}) collective-permute-start(bf16[2,128,512]{2,1,0:T(8,128)(2,1)S(1)} %pad_maximum_fusion.refs_0_), channel_id=1, source_target_pairs={{0,64},{1,65},{2,66},{3,67},{4,68},{5,69},{6,70},{7,71},{8,72},{9,... | collective-permute-start | bytes 786440 | tf_op jit(solution)/shard_map/ppermute | solution.py:429
  77.4 18.4 %collective-permute-start.9 = (bf16[2,128,512]{2,1,0:T(8,128)(2,1)S(1)}, bf16[2,128,512]{2,1,0:T(8,128)(2,1)}, u32[]{:S(2)}, u32[]{:S(2)}) collective-permute-start(bf16[2,128,512]{2,1,0:T(8,128)(2,1)S(1)} %pad_maximum_fusion.refs_0_), channel_id=1, source_target_pairs={{0,192},{1,193},{2,194},{3,195},{4,196},{5,197},{6,198},{7,199},{8... | collective-permute-start | bytes 786440 | tf_op jit(solution)/shard_map/ppermute | solution.py:430
  81.0 22.3 %collective-permute-start.7 = (bf16[2,128,512]{2,1,0:T(8,128)(2,1)S(1)}, bf16[2,128,512]{2,1,0:T(8,128)(2,1)S(1)}, u32[]{:S(2)}, u32[]{:S(2)}) collective-permute-start(bf16[2,128,512]{2,1,0:T(8,128)(2,1)S(1)} %pad_maximum_fusion.refs_0_), channel_id=1, source_target_pairs={{0,224},{1,225},{2,226},{3,227},{4,228},{5,229},{6,230},{7,231},{8... | collective-permute-start | bytes 786440 | tf_op jit(solution)/shard_map/ppermute | solution.py:432
  81.7 21.7 %collective-permute-start.6 = (bf16[2,128,512]{2,1,0:T(8,128)(2,1)S(1)}, bf16[2,128,512]{2,1,0:T(8,128)(2,1)S(1)}, u32[]{:S(2)}, u32[]{:S(2)}) collective-permute-start(bf16[2,128,512]{2,1,0:T(8,128)(2,1)S(1)} %pad_maximum_fusion.refs_0_), channel_id=1, source_target_pairs={{0,32},{1,33},{2,34},{3,35},{4,36},{5,37},{6,38},{7,39},{8,40},{9,... | collective-permute-start | bytes 786440 | tf_op jit(solution)/shard_map/ppermute | solution.py:431
  93.6 16.1 %collective-permute-start.12 = (bf16[2,128,512]{2,1,0:T(8,128)(2,1)S(1)}, bf16[2,128,512]{2,1,0:T(8,128)(2,1)S(1)}, u32[]{:S(2)}, u32[]{:S(2)}) collective-permute-start(bf16[2,128,512]{2,1,0:T(8,128)(2,1)S(1)} %collective-permute-done.8.refs_3_), channel_id=1, source_target_pairs={{0,64},{1,65},{2,66},{3,67},{4,68},{5,69},{6,70},{7,71},{8,72},{9,... | collective-permute-start | bytes 786440 | tf_op jit(solution)/shard_map/ppermute | solution.py:435
  93.6 16.1 %collective-permute-start.10 = (bf16[2,128,512]{2,1,0:T(8,128)(2,1)S(1)}, bf16[2,128,512]{2,1,0:T(8,128)(2,1)S(1)}, u32[]{:S(2)}, u32[]{:S(2)}) collective-permute-start(bf16[2,128,512]{2,1,0:T(8,128)(2,1)S(1)} %collective-permute-done.8.refs_3_), channel_id=1, source_target_pairs={{0,32},{1,33},{2,34},{3,35},{4,36},{5,37},{6,38},{7,39},{8,40},{9,... | collective-permute-start | bytes 786440 | tf_op jit(solution)/shard_map/ppermute | solution.py:433
  95.8 13.9 %collective-permute-start.11 = (bf16[2,128,512]{2,1,0:T(8,128)(2,1)}, bf16[2,128,512]{2,1,0:T(8,128)(2,1)S(1)}, u32[]{:S(2)}, u32[]{:S(2)}) collective-permute-start(bf16[2,128,512]{2,1,0:T(8,128)(2,1)} %collective-permute-done.9.refs_4_), channel_id=1, source_target_pairs={{0,224},{1,225},{2,226},{3,227},{4,228},{5,229},{6,230},{7,231},{8... | collective-permute-start | bytes 786440 | tf_op jit(solution)/shard_map/ppermute | solution.py:434
  98.4 1.3 copy-start.3
  99.7 1.3 copy-start.5
  112.5 19.3 %collective-permute-start.16 = (bf16[2,1376,128]{2,1,0:T(8,128)(2,1)S(1)}, bf16[2,1376,128]{2,1,0:T(8,128)(2,1)S(1)}, u32[]{:S(2)}, u32[]{:S(2)}) collective-permute-start(bf16[2,1376,128]{2,1,0:T(8,128)(2,1)S(1)} %get-tuple-element.48), channel_id=1, source_target_pairs={{0,8},{1,9},{2,10},{3,11},{4,12},{5,13},{6,14},{7,15},{8,0},{9,1},... | collective-permute-start | bytes 2113544 | tf_op jit(solution)/shard_map/ppermute | solution.py:46
  116.4 18.0 %collective-permute-start.13 = (bf16[2,1376,128]{2,1,0:T(8,128)(2,1)S(1)}, bf16[2,1376,128]{2,1,0:T(8,128)(2,1)S(1)}, u32[]{:S(2)}, u32[]{:S(2)}) collective-permute-start(bf16[2,1376,128]{2,1,0:T(8,128)(2,1)S(1)} %get-tuple-element.44), channel_id=1, source_target_pairs={{0,2},{1,3},{2,4},{3,5},{4,6},{5,7},{6,0},{7,1},{8,10},{9,11},{10,... | collective-permute-start | bytes 2113544 | tf_op jit(solution)/shard_map/ppermute | solution.py:46
  118.3 18.4 %collective-permute-start.14 = (bf16[2,1376,128]{2,1,0:T(8,128)(2,1)S(1)}, bf16[2,1376,128]{2,1,0:T(8,128)(2,1)S(1)}, u32[]{:S(2)}, u32[]{:S(2)}) collective-permute-start(bf16[2,1376,128]{2,1,0:T(8,128)(2,1)S(1)} %get-tuple-element.45), channel_id=1, source_target_pairs={{0,6},{1,7},{2,0},{3,1},{4,2},{5,3},{6,4},{7,5},{8,14},{9,15},{10,... | collective-permute-start | bytes 2113544 | tf_op jit(solution)/shard_map/ppermute | solution.py:46
  132.0 12.1 %collective-permute-start.17 = (bf16[1376,128]{1,0:T(8,128)(2,1)S(1)}, bf16[1376,128]{1,0:T(8,128)(2,1)S(1)}, u32[]{:S(2)}, u32[]{:S(2)}) collective-permute-start(bf16[1376,128]{1,0:T(8,128)(2,1)S(1)} %get-tuple-element.49), channel_id=1, source_target_pairs={{0,2},{1,3},{2,4},{3,5},{4,6},{5,7},{6,0},{7,1},{8,10},{9,11},{10,... | collective-permute-start | bytes 1056776 | tf_op jit(solution)/shard_map/ppermute | solution.py:46
  134.5 12.4 %collective-permute-start.21 = (bf16[1376,128]{1,0:T(8,128)(2,1)S(1)}, bf16[1376,128]{1,0:T(8,128)(2,1)S(1)}, u32[]{:S(2)}, u32[]{:S(2)}) collective-permute-start(bf16[1376,128]{1,0:T(8,128)(2,1)S(1)} %get-tuple-element.53), channel_id=1, source_target_pairs={{0,6},{1,7},{2,0},{3,1},{4,2},{5,3},{6,4},{7,5},{8,14},{9,15},{10,... | collective-permute-start | bytes 1056776 | tf_op jit(solution)/shard_map/ppermute | solution.py:46
  136.9 22.9 %collective-permute-start.15 = (bf16[2,1376,128]{2,1,0:T(8,128)(2,1)S(1)}, bf16[2,1376,128]{2,1,0:T(8,128)(2,1)S(1)}, u32[]{:S(2)}, u32[]{:S(2)}) collective-permute-start(bf16[2,1376,128]{2,1,0:T(8,128)(2,1)S(1)} %sum.4), channel_id=1, source_target_pairs={{0,8},{1,9},{2,10},{3,11},{4,12},{5,13},{6,14},{7,15},{8,0},{9,1},... | collective-permute-start | bytes 2113544 | tf_op jit(solution)/shard_map/ppermute | solution.py:46
  140.8 13.6 %collective-permute-start.19 = (bf16[1376,128]{1,0:T(8,128)(2,1)S(1)}, bf16[1376,128]{1,0:T(8,128)(2,1)S(1)}, u32[]{:S(2)}, u32[]{:S(2)}) collective-permute-start(bf16[1376,128]{1,0:T(8,128)(2,1)S(1)} %get-tuple-element.50), channel_id=1, source_target_pairs={{0,6},{1,7},{2,0},{3,1},{4,2},{5,3},{6,4},{7,5},{8,14},{9,15},{10,... | collective-permute-start | bytes 1056776 | tf_op jit(solution)/shard_map/ppermute | solution.py:46
  140.8 13.6 %collective-permute-start.20 = (bf16[1376,128]{1,0:T(8,128)(2,1)S(1)}, bf16[1376,128]{1,0:T(8,128)(2,1)S(1)}, u32[]{:S(2)}, u32[]{:S(2)}) collective-permute-start(bf16[1376,128]{1,0:T(8,128)(2,1)S(1)} %get-tuple-element.51), channel_id=1, source_target_pairs={{0,2},{1,3},{2,4},{3,5},{4,6},{5,7},{6,0},{7,1},{8,10},{9,11},{10,... | collective-permute-start | bytes 1056776 | tf_op jit(solution)/shard_map/ppermute | solution.py:46
  144.1 12.5 %collective-permute-start.18 = (bf16[1376,128]{1,0:T(8,128)(2,1)S(1)}, bf16[1376,128]{1,0:T(8,128)(2,1)S(1)}, u32[]{:S(2)}, u32[]{:S(2)}) collective-permute-start(bf16[1376,128]{1,0:T(8,128)(2,1)S(1)} %sum.6), channel_id=1, source_target_pairs={{0,2},{1,3},{2,4},{3,5},{4,6},{5,7},{6,0},{7,1},{8,10},{9,11},{10,... | collective-permute-start | bytes 1056776 | tf_op jit(solution)/shard_map/ppermute | solution.py:46
  147.0 12.9 %collective-permute-start.22 = (bf16[1376,128]{1,0:T(8,128)(2,1)S(1)}, bf16[1376,128]{1,0:T(8,128)(2,1)S(1)}, u32[]{:S(2)}, u32[]{:S(2)}) collective-permute-start(bf16[1376,128]{1,0:T(8,128)(2,1)S(1)} %sum.7), channel_id=1, source_target_pairs={{0,6},{1,7},{2,0},{3,1},{4,2},{5,3},{6,4},{7,5},{8,14},{9,15},{10,... | collective-permute-start | bytes 1056776 | tf_op jit(solution)/shard_map/ppermute | solution.py:46

commit v7 on v6

--- a/solution.py
+++ b/solution.py
@@ -186,6 +186,18 @@
     out_mark_ref[...] = mark_ref[...]
 
 
+def hold_kernel(here_ref, stream_ref, second_ref, first_ref, out_ref):
+    @pl.when(here_ref[0] == 1)
+    def _():
+        out_ref[0] = stream_ref[...]
+        out_ref[1] = first_ref[...]
+
+    @pl.when(here_ref[0] == 0)
+    def _():
+        out_ref[0] = first_ref[...]
+        out_ref[1] = second_ref[...]
+
+
 def scale_kernel(*refs):
     blocks, (gain_ref, gain_oth_ref, out_ref, tail_ref) = refs[:-4], refs[-4:]
     for i, block in enumerate(blocks):
@@ -304,6 +316,19 @@
         ),
         name="out_proj",
     )(core, mixed, w_out, start)
+
+
+def hold(here, *parts):
+    vmem = pl.BlockSpec(memory_space=pltpu.VMEM)
+    return pl.pallas_call(
+        hold_kernel,
+        out_shape=jax.ShapeDtypeStruct((2, ROWS, CH), BF16),
+        in_specs=[in_smem()] + [vmem] * 3,
+        out_specs=vmem,
+        compiler_params=params(14),
+        cost_estimate=pl.CostEstimate(flops=1, bytes_accessed=1 << 19, transcendentals=0),
+        name="hold",
+    )(here, *parts)
 
 
 def load_weights(weights, mark):
@@ -420,8 +445,8 @@
 
     first = lax.ppermute(stream, AXES, pairs_of(to_row_owner_first))
     second = lax.ppermute(stream, AXES, pairs_of(to_row_owner_second))
-    here = x_lo == core
-    held = jnp.stack([jnp.where(here, stream, first), jnp.where(here, first, second)])
+    here = (x_lo == core).astype(jnp.int32)[None]
+    held = hold(here, stream, second, first)
     gate_w, up_w, mark = load_weights((wg, wg_oth, wu, wu_oth), held[0, :16])
     gain, _ = lax.optimization_barrier((gain, mark))
     z = ctx // 2

time: 162 us -> 159 us (0.981)
  starting transfers between devices: 38.8 us -> 34 us
    ppermute x1, waiting for transfers between devices: 11.9 us -> 4.03 us  [shards(): two_first = lax.ppermute(held, AXES, pairs_of(functools.partial(along, 2)))]
    ppermute x1, waiting for transfers between devices: 0.01 us -> 3.84 us  [shards(): lax.ppermute(held, AXES, pairs_of(functools.partial(along, -2)))]
    ppermute x1, starting transfers between devices: 3.44 us -> 0.17 us  [shards(): first = lax.ppermute(stream, AXES, pairs_of(to_row_owner_first))]
    ppermute x1, waiting for transfers between devices: 4.58 us -> 7.84 us  [shards(): lax.ppermute(two_second, AXES, pairs_of(functools.partial(along, -1)))]
    ppermute x1, waiting for transfers between devices: 0.77 us -> 3.8 us  [shards(): lax.ppermute(held, AXES, pairs_of(functools.partial(along, -1)))]
    unnamed x18 -> x20, local copies, waits for them, and re-layouts: 3.86 us -> 4.76 us
  transfers between devices with their start and end apart: 24 -> 24, of which waited for: 12 -> 14; matrix products, arithmetic and copies ran while one was open for 0% -> 0% of each run, Pallas kernels for 11% -> 11%
where the time goes in v7:
time: 159 us; the launch traced here: 158 us
  waiting for transfers between devices  56.7 us (36%)
  starting transfers between devices  34 us (21%)
  blocking collectives  32.3 us (20%)
  Pallas kernels  29.3 us (18%)
  local copies, waits for them, and re-layouts  4.85 us (3%)
    ppermute x14, waiting for transfers between devices, shift(): return lax.ppermute(arr, AXES, pairs)  24.1 us
    all_to_all x1, blocking collectives, shards(): lax.all_to_all(copies, 'tp', 0, 0, axis_index_groups=PLANE_GROUPS, tiled=...  19.4 us
    ppermute x14, starting transfers between devices, shift(): return lax.ppermute(arr, AXES, pairs)  15.9 us
    all_to_all x1, blocking collectives, shards(): conv_rows = lax.all_to_all(conv, 'ctx', 0, 0, tiled=True)  12.9 us
    pallas_call x5, Pallas kernels, mlp_part(): pl.pallas_call(functools.partial(mlp_kernel, slots, split), out_shape=[ja...  11.3 us
    all_to_all x1, waiting for transfers between devices, shards(): recv = lax.all_to_all(sent, 'ctx', 0, 0, tiled=True)  11 us
    all_to_all x1, starting transfers between devices, shards(): recv = lax.all_to_all(sent, 'ctx', 0, 0, tiled=True)  9.5 us
    ppermute x1, waiting for transfers between devices, shards(): lax.ppermute(two_second, AXES, pairs_of(functools.partial(along, -1)))  7.84 us
  transfers between devices with their start and end apart: 24, of which 14 were waited for; matrix products, arithmetic and copies ran while one was open for 0% of the time, Pallas kernels for 11%

profile of v7, /device:TPU:24, one launch (start us, length us, event | category | flops | bytes accessed | tf_op | source)
XLA Modules:
  0.0 158.0 jit_solution(16474525183416890904)
XLA Ops:
  0.6 0.0 copy-start.7
  0.7 0.1 collective-permute-start
  0.8 0.5 collective-permute-start.1
  1.2 1.9 %prep.1 = bf16[16,64,128]{2,1,0:T(8,128)(2,1)} custom-call(bf16[3,128,512]{2,1,0:T(8,128)(2,1)} %bitcast.25, f32[128,512]{1,0:T(8,128)} %filt_ref.1), custom_call_target="tpu_custom_call" | custom-call | tf_op jit(solution)/shard_map/prep/pallas_call | solution.py:411
  3.2 9.5 %all-to-all-start = ((bf16[16,64,128]{2,1,0:T(8,128)(2,1)}), bf16[16,64,128]{2,1,0:T(8,128)(2,1)S(1)}, u32[]{:S(2)}, u32[]{:S(2)}) async-start(bf16[16,64,128]{2,1,0:T(8,128)(2,1)} %prep.1), calls=%async_computation | async-start | bytes 524288 | tf_op jit(solution)/shard_map/all_to_all | solution.py:417
  12.7 0.1 collective-permute-start.2
  12.8 1.1 collective-permute-done.2.refs_6_.refs_4_
  13.9 11.0 %all-to-all-done.x_ref = bf16[16,64,128]{2,1,0:T(8,128)(2,1)S(1)} async-done(((bf16[16,64,128]{2,1,0:T(8,128)(2,1)}), bf16[16,64,128]{2,1,0:T(8,128)(2,1)S(1)}, u32[]{:S(2)}, u32[]{:S(2)}) %all-to-all-start) | async-done | bytes 262176 | tf_op jit(solution)/shard_map/all_to_all | solution.py:417
  24.9 0.0 collective-permute-done.wgx_ref
  24.9 1.1 copy-done.2
  26.1 0.0 collective-permute-done.1.wux_ref
  26.1 1.5 conv.1
  27.5 12.9 %all_to_all.15.conv_ref = bf16[16,32,128]{2,1,0:T(8,128)(2,1)} all-to-all(bf16[16,32,128]{2,1,0:T(8,128)(2,1)S(1)} %conv.1), channel_id=1, replica_groups=mesh['ctx'=16,'tp'=16] {'ctx'}, dimensions={0} | all-to-all | bytes 262144 | tf_op jit(solution)/shard_map/all_to_all | solution.py:430
  40.4 2.2 %mix.1 = bf16[8,128,512]{2,1,0:T(8,128)(2,1)} custom-call(bf16[16,32,128]{2,1,0:T(8,128)(2,1)} %all_to_all.15.conv_ref, bf16[3,128,512]{2,1,0:T(8,128)(2,1)} %bitcast.26, f32[1,512]{1,0:T(1,128)} %bitcast.28), custom_call_target="tpu_custom_call" | custom-call | tf_op jit(solution)/shard_map/mix/pallas_call | solution.py:431
  42.6 19.4 %all_to_all.16.mixed_hbm = bf16[8,128,512]{2,1,0:T(8,128)(2,1)S(1)} all-to-all(bf16[8,128,512]{2,1,0:T(8,128)(2,1)} %mix.1), channel_id=1, replica_groups={{0,2,4,6,8,10,12,14},{1,3,5,7,9,11,13,15},{16,18,20,22,24,26,28,30},{17..., dimensions={0} | all-to-all | bytes 2097152 | tf_op jit(solution)/shard_map/all_to_all | solution.py:438
  62.0 3.0 %out_proj.2.start_ref = f32[128,512]{1,0:T(8,128)S(1)} custom-call(s32[1]{0:T(128)} %bitcast.core_ref, bf16[8,128,512]{2,1,0:T(8,128)(2,1)S(1)} %all_to_all.16.mixed_hbm, bf16[8192,512]{1,0:T(8,128)(2,1)} %w_hbm.3, bf16[128,512]{1,0:T(8,128)(2,1)S(1)} %copy-done.8), custom_call_target="tpu_custom_call" | custom-call | flops 536870912 | bytes 5242880 | tf_op jit(solution)/shard_map/out_proj/pallas_call | solution.py:299
  65.0 0.0 copy-start
  65.0 0.0 copy-start.1
  65.0 3.7 %out_proj.3.stream_ref = bf16[128,512]{1,0:T(8,128)(2,1)} custom-call(s32[1]{0:T(128)} %bitcast.core_ref, bf16[8,128,512]{2,1,0:T(8,128)(2,1)} %collective-permute-done.3.mixed_hbm, bf16[8192,512]{1,0:T(8,128)(2,1)} %w_hbm.3, f32[128,512]{1,0:T(8,128)S(1)} %out_proj.2.start_ref), custom_call_target="tpu_custom_call" | custom-call | flops 536870912 | bytes 5242880 | tf_op jit(solution)/shard_map/out_proj/pallas_call | solution.py:299
  68.7 0.2 collective-permute-start.5
  68.9 0.7 collective-permute-start.4
  69.6 2.2 %collective-permute-done.5.first_ref = bf16[128,512]{1,0:T(8,128)(2,1)S(1)} collective-permute-done((bf16[128,512]{1,0:T(8,128)(2,1)}, bf16[128,512]{1,0:T(8,128)(2,1)S(1)}, u32[]{:S(2)}, u32[]{:S(2)}) %collective-permute-start.5) | collective-permute-done | bytes 131104 | tf_op jit(solution)/shard_map/ppermute | solution.py:446
  71.7 0.9 copy-done.6
  72.7 0.6 collective-permute-start.8
  73.3 3.6 %collective-permute-start.9 = (bf16[2,128,512]{2,1,0:T(8,128)(2,1)S(1)}, bf16[2,128,512]{2,1,0:T(8,128)(2,1)}, u32[]{:S(2)}, u32[]{:S(2)}) collective-permute-start(bf16[2,128,512]{2,1,0:T(8,128)(2,1)S(1)} %hold.1.refs_0_), channel_id=1, source_target_pairs={{0,192},{1,193},{2,194},{3,195},{4,196},{5,197},{6,198},{7,199},{8... | collective-permute-start | bytes 786440 | tf_op jit(solution)/shard_map/ppermute | solution.py:455
  76.9 0.1 stack.35
  77.0 0.6 collective-permute-start.7
  77.5 4.0 %collective-permute-done.8.refs_3_ = bf16[2,128,512]{2,1,0:T(8,128)(2,1)S(1)} collective-permute-done((bf16[2,128,512]{2,1,0:T(8,128)(2,1)S(1)}, bf16[2,128,512]{2,1,0:T(8,128)(2,1)S(1)}, u32[]{:S(2)}, u32[]{:S(2)}) %collective-permute-start.8) | collective-permute-done | bytes 262176 | tf_op jit(solution)/shard_map/ppermute | solution.py:454
  81.6 1.8 %collective-permute-start.10 = (bf16[2,128,512]{2,1,0:T(8,128)(2,1)S(1)}, bf16[2,128,512]{2,1,0:T(8,128)(2,1)S(1)}, u32[]{:S(2)}, u32[]{:S(2)}) collective-permute-start(bf16[2,128,512]{2,1,0:T(8,128)(2,1)S(1)} %collective-permute-done.8.refs_3_), channel_id=1, source_target_pairs={{0,32},{1,33},{2,34},{3,35},{4,36},{5,37},{6,38},{7,39},{8,40},{9,... | collective-permute-start | bytes 786440 | tf_op jit(solution)/shard_map/ppermute | solution.py:458
  83.4 3.8 %collective-permute-done.9.refs_4_ = bf16[2,128,512]{2,1,0:T(8,128)(2,1)} collective-permute-done((bf16[2,128,512]{2,1,0:T(8,128)(2,1)S(1)}, bf16[2,128,512]{2,1,0:T(8,128)(2,1)}, u32[]{:S(2)}, u32[]{:S(2)}) %collective-permute-start.9) | collective-permute-done | bytes 262176 | tf_op jit(solution)/shard_map/ppermute | solution.py:455
  87.2 1.2 collective-permute-start.11
  88.5 1.3 copy-done.3
  89.8 1.3 copy-done.5
  91.1 1.5 load.1
  92.7 3.8 %collective-permute-done.7.refs_2_ = bf16[2,128,512]{2,1,0:T(8,128)(2,1)S(1)} collective-permute-done((bf16[2,128,512]{2,1,0:T(8,128)(2,1)S(1)}, bf16[2,128,512]{2,1,0:T(8,128)(2,1)S(1)}, u32[]{:S(2)}, u32[]{:S(2)}) %collective-permute-start.7) | collective-permute-done | bytes 262176 | tf_op jit(solution)/shard_map/ppermute | solution.py:457
  96.5 1.8 %scale.2 = (bf16[5,128,1024]{2,1,0:T(8,128)(2,1)S(1)}, f32[5,8,128]{2,1,0:T(8,128)S(1)}) custom-call(bf16[2,128,512]{2,1,0:T(8,128)(2,1)S(1)} %hold.1.refs_0_, bf16[2,128,512]{2,1,0:T(8,128)(2,1)S(1)} %collective-permute-done.6.refs_1_, bf16[2,128,512]{2,1,0:T(8,128)(2,1)S(1)} %collective-permute-done.7.refs_2_, ...), custom_call_target="tpu_custom_call" | custom-call | flops 20971520 | bytes 2621440 | tf_op jit(solution)/shard_map/scale/pallas_call | solution.py:351
  98.3 7.8 %collective-permute-done.11.refs_1_ = bf16[2,128,512]{2,1,0:T(8,128)(2,1)S(1)} collective-permute-done((bf16[2,128,512]{2,1,0:T(8,128)(2,1)}, bf16[2,128,512]{2,1,0:T(8,128)(2,1)S(1)}, u32[]{:S(2)}, u32[]{:S(2)}) %collective-permute-start.11) | collective-permute-done | bytes 262176 | tf_op jit(solution)/shard_map/ppermute | solution.py:459
  106.1 0.6 scale.3
  106.7 2.2 %mlp.5 = (bf16[2,1376,128]{2,1,0:T(8,128)(2,1)S(1)}, s32[8]{0:T(128)S(1)}) custom-call(s32[8]{0:T(128)S(1)} %fusion.5.idx_ref, bf16[5,128,1024]{2,1,0:T(8,128)(2,1)S(1)} %get-tuple-element.30.refs_0_, f32[5,8,128]{2,1,0:T(8,128)S(1)} %get-tuple-element.31.refs_1_, bf16[3,128,1024]{2,1,0:T(8,128)(2,1)S(1)} %get-tuple-element.32.refs_2_, ...), custom_call_target="tpu_custom_call" | custom-call | flops 100000000 | bytes 524288 | tf_op jit(solution)/shard_map/mlp/pallas_call | solution.py:369
  108.9 2.3 %collective-permute-start.16 = (bf16[2,1376,128]{2,1,0:T(8,128)(2,1)S(1)}, bf16[2,1376,128]{2,1,0:T(8,128)(2,1)S(1)}, u32[]{:S(2)}, u32[]{:S(2)}) collective-permute-start(bf16[2,1376,128]{2,1,0:T(8,128)(2,1)S(1)} %get-tuple-element.48), channel_id=1, source_target_pairs={{0,8},{1,9},{2,10},{3,11},{4,12},{5,13},{6,14},{7,15},{8,0},{9,1},... | collective-permute-start | bytes 2113544 | tf_op jit(solution)/shard_map/ppermute | solution.py:46
  111.2 2.3 %mlp.6 = (bf16[2,1376,128]{2,1,0:T(8,128)(2,1)S(1)}, bf16[2,1376,128]{2,1,0:T(8,128)(2,1)S(1)}, s32[8]{0:T(128)S(1)}) custom-call(s32[8]{0:T(128)S(1)} %get-tuple-element.38.idx_ref, bf16[5,128,1024]{2,1,0:T(8,128)(2,1)S(1)} %get-tuple-element.30.refs_0_, f32[5,8,128]{2,1,0:T(8,128)S(1)} %get-tuple-element.31.refs_1_, ...), custom_call_target="tpu_custom_call" | custom-call | flops 100000000 | bytes 524288 | tf_op jit(solution)/shard_map/mlp/pallas_call | solution.py:369
  113.5 1.9 %collective-permute-start.13 = (bf16[2,1376,128]{2,1,0:T(8,128)(2,1)S(1)}, bf16[2,1376,128]{2,1,0:T(8,128)(2,1)S(1)}, u32[]{:S(2)}, u32[]{:S(2)}) collective-permute-start(bf16[2,1376,128]{2,1,0:T(8,128)(2,1)S(1)} %get-tuple-element.44), channel_id=1, source_target_pairs={{0,2},{1,3},{2,4},{3,5},{4,6},{5,7},{6,0},{7,1},{8,10},{9,11},{10,... | collective-permute-start | bytes 2113544 | tf_op jit(solution)/shard_map/ppermute | solution.py:46
  115.4 0.2 collective-permute-start.14
  115.6 2.3 %mlp.7 = (bf16[1376,128]{1,0:T(8,128)(2,1)S(1)}, bf16[1376,128]{1,0:T(8,128)(2,1)S(1)}, bf16[1376,128]{1,0:T(8,128)(2,1)S(1)}, bf16[1376,128]{1,0:T(8,128)(2,1)S(1)}, s32[8]{0:T(128)S(1)}) custom-call(s32[8]{0:T(128)S(1)} %get-tuple-element.39.idx_ref, bf16[5,128,1024]{2,1,0:T(8,128)(2,1)S(1)} %get-tuple-element.30.refs_0_, ...), custom_call_target="tpu_custom_call" | custom-call | flops 100000000 | bytes 524288 | tf_op jit(solution)/shard_map/mlp/pallas_call | solution.py:369
  117.9 2.3 %mlp.8 = (bf16[2,1376,128]{2,1,0:T(8,128)(2,1)S(1)}, bf16[2,1376,128]{2,1,0:T(8,128)(2,1)S(1)}, s32[8]{0:T(128)S(1)}) custom-call(s32[8]{0:T(128)S(1)} %get-tuple-element.40.idx_ref, bf16[5,128,1024]{2,1,0:T(8,128)(2,1)S(1)} %get-tuple-element.30.refs_0_, f32[5,8,128]{2,1,0:T(8,128)S(1)} %get-tuple-element.31.refs_1_, ...), custom_call_target="tpu_custom_call" | custom-call | flops 100000000 | bytes 524288 | tf_op jit(solution)/shard_map/mlp/pallas_call | solution.py:369
  120.2 8.3 %collective-permute-done.16.right_ref = bf16[2,1376,128]{2,1,0:T(8,128)(2,1)S(1)} collective-permute-done((bf16[2,1376,128]{2,1,0:T(8,128)(2,1)S(1)}, bf16[2,1376,128]{2,1,0:T(8,128)(2,1)S(1)}, u32[]{:S(2)}, u32[]{:S(2)}) %collective-permute-start.16) | collective-permute-done | bytes 704544 | tf_op jit(solution)/shard_map/ppermute | solution.py:46
  128.5 0.2 sum.5
  128.6 2.5 %collective-permute-start.17 = (bf16[1376,128]{1,0:T(8,128)(2,1)S(1)}, bf16[1376,128]{1,0:T(8,128)(2,1)S(1)}, u32[]{:S(2)}, u32[]{:S(2)}) collective-permute-start(bf16[1376,128]{1,0:T(8,128)(2,1)S(1)} %get-tuple-element.49), channel_id=1, source_target_pairs={{0,2},{1,3},{2,4},{3,5},{4,6},{5,7},{6,0},{7,1},{8,10},{9,11},{10,... | collective-permute-start | bytes 1056776 | tf_op jit(solution)/shard_map/ppermute | solution.py:46
  131.1 0.3 collective-permute-done.13.refs_1_
  131.4 2.4 %collective-permute-done.14.refs_2_ = bf16[2,1376,128]{2,1,0:T(8,128)(2,1)S(1)} collective-permute-done((bf16[2,1376,128]{2,1,0:T(8,128)(2,1)S(1)}, bf16[2,1376,128]{2,1,0:T(8,128)(2,1)S(1)}, u32[]{:S(2)}, u32[]{:S(2)}) %collective-permute-start.14) | collective-permute-done | bytes 704544 | tf_op jit(solution)/shard_map/ppermute | solution.py:46
  133.8 0.3 sum.4
  134.1 2.7 %collective-permute-start.15 = (bf16[2,1376,128]{2,1,0:T(8,128)(2,1)S(1)}, bf16[2,1376,128]{2,1,0:T(8,128)(2,1)S(1)}, u32[]{:S(2)}, u32[]{:S(2)}) collective-permute-start(bf16[2,1376,128]{2,1,0:T(8,128)(2,1)S(1)} %sum.4), channel_id=1, source_target_pairs={{0,8},{1,9},{2,10},{3,11},{4,12},{5,13},{6,14},{7,15},{8,0},{9,1},... | collective-permute-start | bytes 2113544 | tf_op jit(solution)/shard_map/ppermute | solution.py:46
  136.8 0.0 collective-permute-start.19
  136.8 3.2 %collective-permute-start.20 = (bf16[1376,128]{1,0:T(8,128)(2,1)S(1)}, bf16[1376,128]{1,0:T(8,128)(2,1)S(1)}, u32[]{:S(2)}, u32[]{:S(2)}) collective-permute-start(bf16[1376,128]{1,0:T(8,128)(2,1)S(1)} %get-tuple-element.51), channel_id=1, source_target_pairs={{0,2},{1,3},{2,4},{3,5},{4,6},{5,7},{6,0},{7,1},{8,10},{9,11},{10,... | collective-permute-start | bytes 1056776 | tf_op jit(solution)/shard_map/ppermute | solution.py:46
  140.0 0.1 sum.6
  140.1 2.3 %collective-permute-start.18 = (bf16[1376,128]{1,0:T(8,128)(2,1)S(1)}, bf16[1376,128]{1,0:T(8,128)(2,1)S(1)}, u32[]{:S(2)}, u32[]{:S(2)}) collective-permute-start(bf16[1376,128]{1,0:T(8,128)(2,1)S(1)} %sum.6), channel_id=1, source_target_pairs={{0,2},{1,3},{2,4},{3,5},{4,6},{5,7},{6,0},{7,1},{8,10},{9,11},{10,... | collective-permute-start | bytes 1056776 | tf_op jit(solution)/shard_map/ppermute | solution.py:46
  142.4 1.1 collective-permute-done.21.refs_1_
  143.5 0.1 sum.7
  143.6 0.1 collective-permute-start.22
  143.7 2.2 %mlp.9 = (bf16[2,1376,128]{2,1,0:T(8,128)(2,1)S(1)}, s32[8]{0:T(128)}) custom-call(s32[8]{0:T(128)S(1)} %get-tuple-element.41.idx_ref, bf16[5,128,1024]{2,1,0:T(8,128)(2,1)S(1)} %get-tuple-element.30.refs_0_, f32[5,8,128]{2,1,0:T(8,128)S(1)} %get-tuple-element.31.refs_1_, bf16[3,128,1024]{2,1,0:T(8,128)(2,1)S(1)} %get-tuple-element.32.refs_2_, ...), custom_call_target="tpu_custom_call" | custom-call | flops 100000000 | bytes 524288 | tf_op jit(solution)/shard_map/mlp/pallas_call | solution.py:369
  145.9 5.1 %collective-permute-done.19.gate_3_ref = bf16[1376,128]{1,0:T(8,128)(2,1)S(1)} collective-permute-done((bf16[1376,128]{1,0:T(8,128)(2,1)S(1)}, bf16[1376,128]{1,0:T(8,128)(2,1)S(1)}, u32[]{:S(2)}, u32[]{:S(2)}) %collective-permute-start.19) | collective-permute-done | bytes 352288 | tf_op jit(solution)/shard_map/ppermute | solution.py:46
  151.1 2.7 %collective-permute-done.18.gate_1_ref = bf16[1376,128]{1,0:T(8,128)(2,1)S(1)} collective-permute-done((bf16[1376,128]{1,0:T(8,128)(2,1)S(1)}, bf16[1376,128]{1,0:T(8,128)(2,1)S(1)}, u32[]{:S(2)}, u32[]{:S(2)}) %collective-permute-start.18) | collective-permute-done | bytes 352288 | tf_op jit(solution)/shard_map/ppermute | solution.py:46
  153.7 3.0 %collective-permute-done.22.up_3_ref = bf16[1376,128]{1,0:T(8,128)(2,1)S(1)} collective-permute-done((bf16[1376,128]{1,0:T(8,128)(2,1)S(1)}, bf16[1376,128]{1,0:T(8,128)(2,1)S(1)}, u32[]{:S(2)}, u32[]{:S(2)}) %collective-permute-start.22) | collective-permute-done | bytes 352288 | tf_op jit(solution)/shard_map/ppermute | solution.py:46
  156.8 1.3 finish.1
  (28 shorter events, 0.1 us)
Async XLA Ops:
  0.6 25.4 %copy-start.7 = (bf16[128,1024]{1,0:T(8,128)(2,1)S(1)}, bf16[128,1024]{1,0:T(8,128)(2,1)}, u32[]{:S(2)}) copy-start(bf16[128,1024]{1,0:T(8,128)(2,1)} %constant.165.clone.tab_ref) | copy-start | bytes 786436
  0.6 12.0 %copy-start.9 = (f32[512]{0:T(512)S(1)}, f32[512]{0:T(512)}, u32[]{:S(2)}) copy-start(f32[512]{0:T(512)} %param.14) | copy-start | bytes 6148
  0.7 24.3 %collective-permute-start = (bf16[1368,512]{1,0:T(8,128)(2,1)}, bf16[1368,512]{1,0:T(8,128)(2,1)S(1)}, u32[]{:S(2)}, u32[]{:S(2)}) collective-permute-start(bf16[1368,512]{1,0:T(8,128)(2,1)} %bitcast.18), channel_id=1, source_target_pairs={{0,1},{1,0},{2,3},{3,2},{4,5},{5,4},{6,7},{7,6},{8,9},{9,8},{10,11... | collective-permute-start | bytes 4202504 | tf_op jit(solution)/shard_map/ppermute | solution.py:46
  0.8 25.3 %collective-permute-start.1 = (bf16[1368,512]{1,0:T(8,128)(2,1)}, bf16[1368,512]{1,0:T(8,128)(2,1)S(1)}, u32[]{:S(2)}, u32[]{:S(2)}) collective-permute-start(bf16[1368,512]{1,0:T(8,128)(2,1)} %bitcast.20), channel_id=1, source_target_pairs={{0,1},{1,0},{2,3},{3,2},{4,5},{5,4},{6,7},{7,6},{8,9},{9,8},{10,11... | collective-permute-start | bytes 4202504 | tf_op jit(solution)/shard_map/ppermute | solution.py:46
  3.2 21.8 %all-to-all-start = ((bf16[16,64,128]{2,1,0:T(8,128)(2,1)}), bf16[16,64,128]{2,1,0:T(8,128)(2,1)S(1)}, u32[]{:S(2)}, u32[]{:S(2)}) async-start(bf16[16,64,128]{2,1,0:T(8,128)(2,1)} %prep.1), calls=%async_computation | async-start | bytes 524288 | tf_op jit(solution)/shard_map/all_to_all | solution.py:417
  12.7 1.2 collective-permute-start.2
  24.9 1.1 copy-start.2
  26.1 36.0 %copy-start.4 = (bf16[1368,512]{1,0:T(8,128)(2,1)}, bf16[1368,512]{1,0:T(8,128)(2,1)S(1)}, u32[]{:S(2)}) copy-start(bf16[1368,512]{1,0:T(8,128)(2,1)S(1)} %collective-permute-done.1.wux_ref) | copy-start | bytes 4202500
  42.6 19.4 %copy-start.8 = (bf16[128,512]{1,0:T(8,128)(2,1)S(1)}, bf16[128,512]{1,0:T(8,128)(2,1)}, u32[]{:S(2)}) copy-start(bf16[128,512]{1,0:T(8,128)(2,1)} %start_ref.1) | copy-start | bytes 393220
  62.0 3.0 %collective-permute-start.3 = (bf16[8,128,512]{2,1,0:T(8,128)(2,1)S(1)}, bf16[8,128,512]{2,1,0:T(8,128)(2,1)}, u32[]{:S(2)}, u32[]{:S(2)}) collective-permute-start(bf16[8,128,512]{2,1,0:T(8,128)(2,1)S(1)} %all_to_all.16.mixed_hbm), channel_id=1, source_target_pairs={{0,1},{1,0},{2,3},{3,2},{4,5},{5,4},{6,7},{7,6},{8,9},{9,8},{10,11... | collective-permute-start | bytes 3145736 | tf_op jit(solution)/shard_map/ppermute | solution.py:46
  65.0 23.4 %copy-start = (bf16[512,1368]{0,1:T(8,128)(2,1)S(1)}, bf16[512,1368]{0,1:T(8,128)(2,1)}, u32[]{:S(2)}) copy-start(bf16[512,1368]{0,1:T(8,128)(2,1)} %param.15) | copy-start | bytes 4202500
  65.0 23.4 %copy-start.1 = (bf16[512,1368]{0,1:T(8,128)(2,1)S(1)}, bf16[512,1368]{0,1:T(8,128)(2,1)}, u32[]{:S(2)}) copy-start(bf16[512,1368]{0,1:T(8,128)(2,1)} %param.16) | copy-start | bytes 4202500
  68.7 3.0 %collective-permute-start.5 = (bf16[128,512]{1,0:T(8,128)(2,1)}, bf16[128,512]{1,0:T(8,128)(2,1)S(1)}, u32[]{:S(2)}, u32[]{:S(2)}) collective-permute-start(bf16[128,512]{1,0:T(8,128)(2,1)} %out_proj.3.stream_ref), channel_id=1, source_target_pairs={{0,16},{1,0},{2,18},{3,2},{4,20},{5,4},{6,22},{7,6},{8,24},{9,8},{... | collective-permute-start | bytes 393224 | tf_op jit(solution)/shard_map/ppermute | solution.py:446
  68.9 2.8 %collective-permute-start.4 = (bf16[128,512]{1,0:T(8,128)(2,1)}, bf16[128,512]{1,0:T(8,128)(2,1)S(1)}, u32[]{:S(2)}, u32[]{:S(2)}) collective-permute-start(bf16[128,512]{1,0:T(8,128)(2,1)} %out_proj.3.stream_ref), channel_id=1, source_target_pairs={{1,16},{3,18},{5,20},{7,22},{9,24},{11,26},{13,28},{15,30},{16,1},... | collective-permute-start | bytes 393224 | tf_op jit(solution)/shard_map/ppermute | solution.py:447
  71.7 0.9 copy-start.6
  72.7 8.9 %collective-permute-start.8 = (bf16[2,128,512]{2,1,0:T(8,128)(2,1)S(1)}, bf16[2,128,512]{2,1,0:T(8,128)(2,1)S(1)}, u32[]{:S(2)}, u32[]{:S(2)}) collective-permute-start(bf16[2,128,512]{2,1,0:T(8,128)(2,1)S(1)} %hold.1.refs_0_), channel_id=1, source_target_pairs={{0,64},{1,65},{2,66},{3,67},{4,68},{5,69},{6,70},{7,71},{8,72},{9,... | collective-permute-start | bytes 786440 | tf_op jit(solution)/shard_map/ppermute | solution.py:454
  73.3 13.9 %collective-permute-start.9 = (bf16[2,128,512]{2,1,0:T(8,128)(2,1)S(1)}, bf16[2,128,512]{2,1,0:T(8,128)(2,1)}, u32[]{:S(2)}, u32[]{:S(2)}) collective-permute-start(bf16[2,128,512]{2,1,0:T(8,128)(2,1)S(1)} %hold.1.refs_0_), channel_id=1, source_target_pairs={{0,192},{1,193},{2,194},{3,195},{4,196},{5,197},{6,198},{7,199},{8... | collective-permute-start | bytes 786440 | tf_op jit(solution)/shard_map/ppermute | solution.py:455
  77.0 19.5 %collective-permute-start.7 = (bf16[2,128,512]{2,1,0:T(8,128)(2,1)S(1)}, bf16[2,128,512]{2,1,0:T(8,128)(2,1)S(1)}, u32[]{:S(2)}, u32[]{:S(2)}) collective-permute-start(bf16[2,128,512]{2,1,0:T(8,128)(2,1)S(1)} %hold.1.refs_0_), channel_id=1, source_target_pairs={{0,224},{1,225},{2,226},{3,227},{4,228},{5,229},{6,230},{7,231},{8... | collective-permute-start | bytes 786440 | tf_op jit(solution)/shard_map/ppermute | solution.py:457
  77.5 19.0 %collective-permute-start.6 = (bf16[2,128,512]{2,1,0:T(8,128)(2,1)S(1)}, bf16[2,128,512]{2,1,0:T(8,128)(2,1)S(1)}, u32[]{:S(2)}, u32[]{:S(2)}) collective-permute-start(bf16[2,128,512]{2,1,0:T(8,128)(2,1)S(1)} %hold.1.refs_0_), channel_id=1, source_target_pairs={{0,32},{1,33},{2,34},{3,35},{4,36},{5,37},{6,38},{7,39},{8,40},{9,... | collective-permute-start | bytes 786440 | tf_op jit(solution)/shard_map/ppermute | solution.py:456
  81.6 24.5 %collective-permute-start.12 = (bf16[2,128,512]{2,1,0:T(8,128)(2,1)S(1)}, bf16[2,128,512]{2,1,0:T(8,128)(2,1)S(1)}, u32[]{:S(2)}, u32[]{:S(2)}) collective-permute-start(bf16[2,128,512]{2,1,0:T(8,128)(2,1)S(1)} %collective-permute-done.8.refs_3_), channel_id=1, source_target_pairs={{0,64},{1,65},{2,66},{3,67},{4,68},{5,69},{6,70},{7,71},{8,72},{9,... | collective-permute-start | bytes 786440 | tf_op jit(solution)/shard_map/ppermute | solution.py:460
  81.6 24.5 %collective-permute-start.10 = (bf16[2,128,512]{2,1,0:T(8,128)(2,1)S(1)}, bf16[2,128,512]{2,1,0:T(8,128)(2,1)S(1)}, u32[]{:S(2)}, u32[]{:S(2)}) collective-permute-start(bf16[2,128,512]{2,1,0:T(8,128)(2,1)S(1)} %collective-permute-done.8.refs_3_), channel_id=1, source_target_pairs={{0,32},{1,33},{2,34},{3,35},{4,36},{5,37},{6,38},{7,39},{8,40},{9,... | collective-permute-start | bytes 786440 | tf_op jit(solution)/shard_map/ppermute | solution.py:458
  87.2 18.9 %collective-permute-start.11 = (bf16[2,128,512]{2,1,0:T(8,128)(2,1)}, bf16[2,128,512]{2,1,0:T(8,128)(2,1)S(1)}, u32[]{:S(2)}, u32[]{:S(2)}) collective-permute-start(bf16[2,128,512]{2,1,0:T(8,128)(2,1)} %collective-permute-done.9.refs_4_), channel_id=1, source_target_pairs={{0,224},{1,225},{2,226},{3,227},{4,228},{5,229},{6,230},{7,231},{8... | collective-permute-start | bytes 786440 | tf_op jit(solution)/shard_map/ppermute | solution.py:459
  88.5 1.3 copy-start.3
  89.8 1.3 copy-start.5
  108.9 19.5 %collective-permute-start.16 = (bf16[2,1376,128]{2,1,0:T(8,128)(2,1)S(1)}, bf16[2,1376,128]{2,1,0:T(8,128)(2,1)S(1)}, u32[]{:S(2)}, u32[]{:S(2)}) collective-permute-start(bf16[2,1376,128]{2,1,0:T(8,128)(2,1)S(1)} %get-tuple-element.48), channel_id=1, source_target_pairs={{0,8},{1,9},{2,10},{3,11},{4,12},{5,13},{6,14},{7,15},{8,0},{9,1},... | collective-permute-start | bytes 2113544 | tf_op jit(solution)/shard_map/ppermute | solution.py:46
  113.5 17.9 %collective-permute-start.13 = (bf16[2,1376,128]{2,1,0:T(8,128)(2,1)S(1)}, bf16[2,1376,128]{2,1,0:T(8,128)(2,1)S(1)}, u32[]{:S(2)}, u32[]{:S(2)}) collective-permute-start(bf16[2,1376,128]{2,1,0:T(8,128)(2,1)S(1)} %get-tuple-element.44), channel_id=1, source_target_pairs={{0,2},{1,3},{2,4},{3,5},{4,6},{5,7},{6,0},{7,1},{8,10},{9,11},{10,... | collective-permute-start | bytes 2113544 | tf_op jit(solution)/shard_map/ppermute | solution.py:46
  115.4 18.5 %collective-permute-start.14 = (bf16[2,1376,128]{2,1,0:T(8,128)(2,1)S(1)}, bf16[2,1376,128]{2,1,0:T(8,128)(2,1)S(1)}, u32[]{:S(2)}, u32[]{:S(2)}) collective-permute-start(bf16[2,1376,128]{2,1,0:T(8,128)(2,1)S(1)} %get-tuple-element.45), channel_id=1, source_target_pairs={{0,6},{1,7},{2,0},{3,1},{4,2},{5,3},{6,4},{7,5},{8,14},{9,15},{10,... | collective-permute-start | bytes 2113544 | tf_op jit(solution)/shard_map/ppermute | solution.py:46
  128.6 11.4 %collective-permute-start.17 = (bf16[1376,128]{1,0:T(8,128)(2,1)S(1)}, bf16[1376,128]{1,0:T(8,128)(2,1)S(1)}, u32[]{:S(2)}, u32[]{:S(2)}) collective-permute-start(bf16[1376,128]{1,0:T(8,128)(2,1)S(1)} %get-tuple-element.49), channel_id=1, source_target_pairs={{0,2},{1,3},{2,4},{3,5},{4,6},{5,7},{6,0},{7,1},{8,10},{9,11},{10,... | collective-permute-start | bytes 1056776 | tf_op jit(solution)/shard_map/ppermute | solution.py:46
  131.1 12.4 %collective-permute-start.21 = (bf16[1376,128]{1,0:T(8,128)(2,1)S(1)}, bf16[1376,128]{1,0:T(8,128)(2,1)S(1)}, u32[]{:S(2)}, u32[]{:S(2)}) collective-permute-start(bf16[1376,128]{1,0:T(8,128)(2,1)S(1)} %get-tuple-element.53), channel_id=1, source_target_pairs={{0,6},{1,7},{2,0},{3,1},{4,2},{5,3},{6,4},{7,5},{8,14},{9,15},{10,... | collective-permute-start | bytes 1056776 | tf_op jit(solution)/shard_map/ppermute | solution.py:46
  134.1 22.7 %collective-permute-start.15 = (bf16[2,1376,128]{2,1,0:T(8,128)(2,1)S(1)}, bf16[2,1376,128]{2,1,0:T(8,128)(2,1)S(1)}, u32[]{:S(2)}, u32[]{:S(2)}) collective-permute-start(bf16[2,1376,128]{2,1,0:T(8,128)(2,1)S(1)} %sum.4), channel_id=1, source_target_pairs={{0,8},{1,9},{2,10},{3,11},{4,12},{5,13},{6,14},{7,15},{8,0},{9,1},... | collective-permute-start | bytes 2113544 | tf_op jit(solution)/shard_map/ppermute | solution.py:46
  136.8 14.3 %collective-permute-start.19 = (bf16[1376,128]{1,0:T(8,128)(2,1)S(1)}, bf16[1376,128]{1,0:T(8,128)(2,1)S(1)}, u32[]{:S(2)}, u32[]{:S(2)}) collective-permute-start(bf16[1376,128]{1,0:T(8,128)(2,1)S(1)} %get-tuple-element.50), channel_id=1, source_target_pairs={{0,6},{1,7},{2,0},{3,1},{4,2},{5,3},{6,4},{7,5},{8,14},{9,15},{10,... | collective-permute-start | bytes 1056776 | tf_op jit(solution)/shard_map/ppermute | solution.py:46
  136.8 14.3 %collective-permute-start.20 = (bf16[1376,128]{1,0:T(8,128)(2,1)S(1)}, bf16[1376,128]{1,0:T(8,128)(2,1)S(1)}, u32[]{:S(2)}, u32[]{:S(2)}) collective-permute-start(bf16[1376,128]{1,0:T(8,128)(2,1)S(1)} %get-tuple-element.51), channel_id=1, source_target_pairs={{0,2},{1,3},{2,4},{3,5},{4,6},{5,7},{6,0},{7,1},{8,10},{9,11},{10,... | collective-permute-start | bytes 1056776 | tf_op jit(solution)/shard_map/ppermute | solution.py:46
  140.1 13.6 %collective-permute-start.18 = (bf16[1376,128]{1,0:T(8,128)(2,1)S(1)}, bf16[1376,128]{1,0:T(8,128)(2,1)S(1)}, u32[]{:S(2)}, u32[]{:S(2)}) collective-permute-start(bf16[1376,128]{1,0:T(8,128)(2,1)S(1)} %sum.6), channel_id=1, source_target_pairs={{0,2},{1,3},{2,4},{3,5},{4,6},{5,7},{6,0},{7,1},{8,10},{9,11},{10,... | collective-permute-start | bytes 1056776 | tf_op jit(solution)/shard_map/ppermute | solution.py:46
  143.6 13.2 %collective-permute-start.22 = (bf16[1376,128]{1,0:T(8,128)(2,1)S(1)}, bf16[1376,128]{1,0:T(8,128)(2,1)S(1)}, u32[]{:S(2)}, u32[]{:S(2)}) collective-permute-start(bf16[1376,128]{1,0:T(8,128)(2,1)S(1)} %sum.7), channel_id=1, source_target_pairs={{0,6},{1,7},{2,0},{3,1},{4,2},{5,3},{6,4},{7,5},{8,14},{9,15},{10,... | collective-permute-start | bytes 1056776 | tf_op jit(solution)/shard_map/ppermute | solution.py:46

commit v8 on v7

--- a/solution.py
+++ b/solution.py
@@ -136,7 +136,8 @@
             out_ref[copy, :, cols] = mixed
 
 
-def out_proj_kernel(offset, core_ref, mixed_hbm, w_hbm, start_ref, out_ref, mixed, w_buf, sem):
+def out_proj_kernel(offset, core_ref, mixed_hbm, w_hbm, start_ref, *refs):
+    *out_refs, mixed, w_buf, sem = refs
     first = jnp.bitwise_xor(core_ref[0], offset)
     copies = []
     for j in range(N_TP // 2):
@@ -155,7 +156,8 @@
         for copy in pair:
             copy.wait()
         acc = acc + dot(mixed[j], w_buf[j])
-    out_ref[...] = acc.astype(out_ref.dtype)
+    for out_ref in out_refs:
+        out_ref[...] = acc.astype(out_ref.dtype)
 
 
 def square_sums(values):
@@ -295,10 +297,10 @@
     return (z + steps, x, y, k) if z % 2 == 0 else (z - steps, x, y, k)
 
 
-def out_proj(offset, core, mixed, w_out, start, dtype):
+def out_proj(offset, core, mixed, w_out, start, dtype, copies):
     return pl.pallas_call(
         functools.partial(out_proj_kernel, offset),
-        out_shape=jax.ShapeDtypeStruct((ROWS, CH), dtype),
+        out_shape=[jax.ShapeDtypeStruct((ROWS, CH), dtype)] * copies,
         in_specs=[
             in_smem(),
             anywhere(),
@@ -440,8 +442,8 @@
     )
     mixed_oth = shift(mixed, k=1)
     core_arr = core.astype(jnp.int32)[None]
-    half = out_proj(0, core_arr, mixed, w_out, residual, F32)
-    stream = out_proj(1, core_arr, mixed_oth, w_out, half, BF16)
+    (half,) = out_proj(0, core_arr, mixed, w_out, residual, F32, 1)
+    stream_out, stream = out_proj(1, core_arr, mixed_oth, w_out, half, BF16, 2)
 
     first = lax.ppermute(stream, AXES, pairs_of(to_row_owner_first))
     second = lax.ppermute(stream, AXES, pairs_of(to_row_owner_second))
@@ -497,7 +499,7 @@
         "finish",
         (own_near, across, gate_1, gate_3, up_1, up_3),
     )
-    return stream, hidden_t.T
+    return stream_out, hidden_t.T
 
 
 def solution(mesh):

time: 159 us -> 158 us (level)
    unnamed x20 -> x18, local copies, waits for them, and re-layouts: 4.76 us -> 3.86 us
  transfers between devices with their start and end apart: 24 -> 24, of which waited for: 14 -> 13; matrix products, arithmetic and copies ran while one was open for 0% -> 0% of each run, Pallas kernels for 11% -> 11%
where the time goes in v8:
time: 158 us; the launch traced here: 157 us
  waiting for transfers between devices  56.4 us (36%)
  starting transfers between devices  34.4 us (22%)
  blocking collectives  32.3 us (20%)
  Pallas kernels  29.3 us (19%)
  local copies, waits for them, and re-layouts  3.94 us (2%)
    ppermute x14, waiting for transfers between devices, shift(): return lax.ppermute(arr, AXES, pairs)  24.1 us
    all_to_all x1, blocking collectives, shards(): lax.all_to_all(copies, 'tp', 0, 0, axis_index_groups=PLANE_GROUPS, tiled=...  19.4 us
    ppermute x14, starting transfers between devices, shift(): return lax.ppermute(arr, AXES, pairs)  16.4 us
    all_to_all x1, blocking collectives, shards(): conv_rows = lax.all_to_all(conv, 'ctx', 0, 0, tiled=True)  12.9 us
    pallas_call x5, Pallas kernels, mlp_part(): pl.pallas_call(functools.partial(mlp_kernel, slots, split), out_shape=[ja...  11.3 us
    all_to_all x1, waiting for transfers between devices, shards(): recv = lax.all_to_all(sent, 'ctx', 0, 0, tiled=True)  11 us
    all_to_all x1, starting transfers between devices, shards(): recv = lax.all_to_all(sent, 'ctx', 0, 0, tiled=True)  9.5 us
    ppermute x1, waiting for transfers between devices, shards(): lax.ppermute(two_second, AXES, pairs_of(functools.partial(along, -1)))  7.87 us
  transfers between devices with their start and end apart: 24, of which 13 were waited for; matrix products, arithmetic and copies ran while one was open for 0% of the time, Pallas kernels for 11%

profile of v8, /device:TPU:24, one launch (start us, length us, event | category | flops | bytes accessed | tf_op | source)
XLA Modules:
  0.0 157.1 jit_solution(17467582421352159928)
XLA Ops:
  0.6 0.0 copy-start.6
  0.7 0.1 collective-permute-start
  0.8 0.5 collective-permute-start.1
  1.2 1.9 %prep.1 = bf16[16,64,128]{2,1,0:T(8,128)(2,1)} custom-call(bf16[3,128,512]{2,1,0:T(8,128)(2,1)} %bitcast.25, f32[128,512]{1,0:T(8,128)} %filt_ref.1), custom_call_target="tpu_custom_call" | custom-call | tf_op jit(solution)/shard_map/prep/pallas_call | solution.py:413
  3.2 9.5 %all-to-all-start = ((bf16[16,64,128]{2,1,0:T(8,128)(2,1)}), bf16[16,64,128]{2,1,0:T(8,128)(2,1)S(1)}, u32[]{:S(2)}, u32[]{:S(2)}) async-start(bf16[16,64,128]{2,1,0:T(8,128)(2,1)} %prep.1), calls=%async_computation | async-start | bytes 524288 | tf_op jit(solution)/shard_map/all_to_all | solution.py:419
  12.7 0.1 collective-permute-start.2
  12.8 1.1 collective-permute-done.2.refs_6_.refs_4_
  13.9 11.0 %all-to-all-done.x_ref = bf16[16,64,128]{2,1,0:T(8,128)(2,1)S(1)} async-done(((bf16[16,64,128]{2,1,0:T(8,128)(2,1)}), bf16[16,64,128]{2,1,0:T(8,128)(2,1)S(1)}, u32[]{:S(2)}, u32[]{:S(2)}) %all-to-all-start) | async-done | bytes 262176 | tf_op jit(solution)/shard_map/all_to_all | solution.py:419
  24.9 0.0 collective-permute-done.wgx_ref
  24.9 1.1 copy-done.2
  26.1 0.0 collective-permute-done.1.wux_ref
  26.1 1.5 conv.1
  27.5 12.9 %all_to_all.15.conv_ref = bf16[16,32,128]{2,1,0:T(8,128)(2,1)} all-to-all(bf16[16,32,128]{2,1,0:T(8,128)(2,1)S(1)} %conv.1), channel_id=1, replica_groups=mesh['ctx'=16,'tp'=16] {'ctx'}, dimensions={0} | all-to-all | bytes 262144 | tf_op jit(solution)/shard_map/all_to_all | solution.py:432
  40.4 2.2 %mix.1 = bf16[8,128,512]{2,1,0:T(8,128)(2,1)} custom-call(bf16[16,32,128]{2,1,0:T(8,128)(2,1)} %all_to_all.15.conv_ref, bf16[3,128,512]{2,1,0:T(8,128)(2,1)} %bitcast.26, f32[1,512]{1,0:T(1,128)} %bitcast.28), custom_call_target="tpu_custom_call" | custom-call | tf_op jit(solution)/shard_map/mix/pallas_call | solution.py:433
  42.6 19.4 %all_to_all.16.mixed_hbm = bf16[8,128,512]{2,1,0:T(8,128)(2,1)S(1)} all-to-all(bf16[8,128,512]{2,1,0:T(8,128)(2,1)} %mix.1), channel_id=1, replica_groups={{0,2,4,6,8,10,12,14},{1,3,5,7,9,11,13,15},{16,18,20,22,24,26,28,30},{17..., dimensions={0} | all-to-all | bytes 2097152 | tf_op jit(solution)/shard_map/all_to_all | solution.py:440
  62.0 3.0 %out_proj.2.start_ref = f32[128,512]{1,0:T(8,128)S(1)} custom-call(s32[1]{0:T(128)} %bitcast.core_ref, bf16[8,128,512]{2,1,0:T(8,128)(2,1)S(1)} %all_to_all.16.mixed_hbm, bf16[8192,512]{1,0:T(8,128)(2,1)} %w_hbm.3, bf16[128,512]{1,0:T(8,128)(2,1)S(1)} %copy-done.7), custom_call_target="tpu_custom_call" | custom-call | flops 536870912 | bytes 5242880 | tf_op jit(solution)/shard_map/out_proj/pallas_call | solution.py:301
  65.0 0.0 collective-permute-done.3.mixed_hbm
  65.0 0.0 copy-start
  65.0 0.0 copy-start.1
  65.0 3.7 %out_proj.3 = (bf16[128,512]{1,0:T(8,128)(2,1)}, bf16[128,512]{1,0:T(8,128)(2,1)S(1)}) custom-call(s32[1]{0:T(128)} %bitcast.core_ref, bf16[8,128,512]{2,1,0:T(8,128)(2,1)} %collective-permute-done.3.mixed_hbm, bf16[8192,512]{1,0:T(8,128)(2,1)} %w_hbm.3, f32[128,512]{1,0:T(8,128)S(1)} %out_proj.2.start_ref), custom_call_target="tpu_custom_call" | custom-call | flops 536870912 | bytes 5242880 | tf_op jit(solution)/shard_map/out_proj/pallas_call | solution.py:301
  68.7 0.2 collective-permute-start.5
  68.9 0.7 collective-permute-start.4
  69.6 1.8 %collective-permute-done.5.first_ref = bf16[128,512]{1,0:T(8,128)(2,1)S(1)} collective-permute-done((bf16[128,512]{1,0:T(8,128)(2,1)S(1)}, bf16[128,512]{1,0:T(8,128)(2,1)S(1)}, u32[]{:S(2)}, u32[]{:S(2)}) %collective-permute-start.5) | collective-permute-done | bytes 131104 | tf_op jit(solution)/shard_map/ppermute | solution.py:448
  71.4 0.0 collective-permute-done.4.second_ref
  71.4 0.6 collective-permute-start.8
  72.0 3.6 %collective-permute-start.9 = (bf16[2,128,512]{2,1,0:T(8,128)(2,1)S(1)}, bf16[2,128,512]{2,1,0:T(8,128)(2,1)}, u32[]{:S(2)}, u32[]{:S(2)}) collective-permute-start(bf16[2,128,512]{2,1,0:T(8,128)(2,1)S(1)} %hold.1.refs_0_), channel_id=1, source_target_pairs={{0,192},{1,193},{2,194},{3,195},{4,196},{5,197},{6,198},{7,199},{8... | collective-permute-start | bytes 786440 | tf_op jit(solution)/shard_map/ppermute | solution.py:457
  75.7 0.1 stack.35
  75.7 0.6 collective-permute-start.7
  76.3 4.2 %collective-permute-done.8.refs_3_ = bf16[2,128,512]{2,1,0:T(8,128)(2,1)S(1)} collective-permute-done((bf16[2,128,512]{2,1,0:T(8,128)(2,1)S(1)}, bf16[2,128,512]{2,1,0:T(8,128)(2,1)S(1)}, u32[]{:S(2)}, u32[]{:S(2)}) %collective-permute-start.8) | collective-permute-done | bytes 262176 | tf_op jit(solution)/shard_map/ppermute | solution.py:456
  80.5 1.7 %collective-permute-start.10 = (bf16[2,128,512]{2,1,0:T(8,128)(2,1)S(1)}, bf16[2,128,512]{2,1,0:T(8,128)(2,1)S(1)}, u32[]{:S(2)}, u32[]{:S(2)}) collective-permute-start(bf16[2,128,512]{2,1,0:T(8,128)(2,1)S(1)} %collective-permute-done.8.refs_3_), channel_id=1, source_target_pairs={{0,32},{1,33},{2,34},{3,35},{4,36},{5,37},{6,38},{7,39},{8,40},{9,... | collective-permute-start | bytes 786440 | tf_op jit(solution)/shard_map/ppermute | solution.py:460
  82.1 3.4 %collective-permute-done.9.refs_4_ = bf16[2,128,512]{2,1,0:T(8,128)(2,1)} collective-permute-done((bf16[2,128,512]{2,1,0:T(8,128)(2,1)S(1)}, bf16[2,128,512]{2,1,0:T(8,128)(2,1)}, u32[]{:S(2)}, u32[]{:S(2)}) %collective-permute-start.9) | collective-permute-done | bytes 262176 | tf_op jit(solution)/shard_map/ppermute | solution.py:457
  85.6 1.2 collective-permute-start.11
  86.8 1.3 copy-done.3
  88.2 1.3 copy-done.5
  89.5 1.5 load.1
  91.1 4.0 %collective-permute-done.7.refs_2_ = bf16[2,128,512]{2,1,0:T(8,128)(2,1)S(1)} collective-permute-done((bf16[2,128,512]{2,1,0:T(8,128)(2,1)S(1)}, bf16[2,128,512]{2,1,0:T(8,128)(2,1)S(1)}, u32[]{:S(2)}, u32[]{:S(2)}) %collective-permute-start.7) | collective-permute-done | bytes 262176 | tf_op jit(solution)/shard_map/ppermute | solution.py:459
  95.0 1.8 %scale.2 = (bf16[5,128,1024]{2,1,0:T(8,128)(2,1)S(1)}, f32[5,8,128]{2,1,0:T(8,128)S(1)}) custom-call(bf16[2,128,512]{2,1,0:T(8,128)(2,1)S(1)} %hold.1.refs_0_, bf16[2,128,512]{2,1,0:T(8,128)(2,1)S(1)} %collective-permute-done.6.refs_1_, bf16[2,128,512]{2,1,0:T(8,128)(2,1)S(1)} %collective-permute-done.7.refs_2_, ...), custom_call_target="tpu_custom_call" | custom-call | flops 20971520 | bytes 2621440 | tf_op jit(solution)/shard_map/scale/pallas_call | solution.py:353
  96.8 7.9 %collective-permute-done.11.refs_1_ = bf16[2,128,512]{2,1,0:T(8,128)(2,1)S(1)} collective-permute-done((bf16[2,128,512]{2,1,0:T(8,128)(2,1)}, bf16[2,128,512]{2,1,0:T(8,128)(2,1)S(1)}, u32[]{:S(2)}, u32[]{:S(2)}) %collective-permute-start.11) | collective-permute-done | bytes 262176 | tf_op jit(solution)/shard_map/ppermute | solution.py:461
  104.7 0.6 scale.3
  105.2 2.2 %mlp.5 = (bf16[2,1376,128]{2,1,0:T(8,128)(2,1)S(1)}, s32[8]{0:T(128)S(1)}) custom-call(s32[8]{0:T(128)S(1)} %fusion.5.idx_ref, bf16[5,128,1024]{2,1,0:T(8,128)(2,1)S(1)} %get-tuple-element.34.refs_0_, f32[5,8,128]{2,1,0:T(8,128)S(1)} %get-tuple-element.35.refs_1_, bf16[3,128,1024]{2,1,0:T(8,128)(2,1)S(1)} %get-tuple-element.36.refs_2_, ...), custom_call_target="tpu_custom_call" | custom-call | flops 100000000 | bytes 524288 | tf_op jit(solution)/shard_map/mlp/pallas_call | solution.py:371
  107.5 2.5 %collective-permute-start.16 = (bf16[2,1376,128]{2,1,0:T(8,128)(2,1)S(1)}, bf16[2,1376,128]{2,1,0:T(8,128)(2,1)S(1)}, u32[]{:S(2)}, u32[]{:S(2)}) collective-permute-start(bf16[2,1376,128]{2,1,0:T(8,128)(2,1)S(1)} %get-tuple-element.52), channel_id=1, source_target_pairs={{0,8},{1,9},{2,10},{3,11},{4,12},{5,13},{6,14},{7,15},{8,0},{9,1},... | collective-permute-start | bytes 2113544 | tf_op jit(solution)/shard_map/ppermute | solution.py:46
  110.0 2.3 %mlp.6 = (bf16[2,1376,128]{2,1,0:T(8,128)(2,1)S(1)}, bf16[2,1376,128]{2,1,0:T(8,128)(2,1)S(1)}, s32[8]{0:T(128)S(1)}) custom-call(s32[8]{0:T(128)S(1)} %get-tuple-element.42.idx_ref, bf16[5,128,1024]{2,1,0:T(8,128)(2,1)S(1)} %get-tuple-element.34.refs_0_, f32[5,8,128]{2,1,0:T(8,128)S(1)} %get-tuple-element.35.refs_1_, ...), custom_call_target="tpu_custom_call" | custom-call | flops 100000000 | bytes 524288 | tf_op jit(solution)/shard_map/mlp/pallas_call | solution.py:371
  112.3 1.9 %collective-permute-start.13 = (bf16[2,1376,128]{2,1,0:T(8,128)(2,1)S(1)}, bf16[2,1376,128]{2,1,0:T(8,128)(2,1)S(1)}, u32[]{:S(2)}, u32[]{:S(2)}) collective-permute-start(bf16[2,1376,128]{2,1,0:T(8,128)(2,1)S(1)} %get-tuple-element.48), channel_id=1, source_target_pairs={{0,2},{1,3},{2,4},{3,5},{4,6},{5,7},{6,0},{7,1},{8,10},{9,11},{10,... | collective-permute-start | bytes 2113544 | tf_op jit(solution)/shard_map/ppermute | solution.py:46
  114.2 0.2 collective-permute-start.14
  114.4 2.3 %mlp.7 = (bf16[1376,128]{1,0:T(8,128)(2,1)S(1)}, bf16[1376,128]{1,0:T(8,128)(2,1)S(1)}, bf16[1376,128]{1,0:T(8,128)(2,1)S(1)}, bf16[1376,128]{1,0:T(8,128)(2,1)S(1)}, s32[8]{0:T(128)S(1)}) custom-call(s32[8]{0:T(128)S(1)} %get-tuple-element.43.idx_ref, bf16[5,128,1024]{2,1,0:T(8,128)(2,1)S(1)} %get-tuple-element.34.refs_0_, ...), custom_call_target="tpu_custom_call" | custom-call | flops 100000000 | bytes 524288 | tf_op jit(solution)/shard_map/mlp/pallas_call | solution.py:371
  116.7 2.3 %mlp.8 = (bf16[2,1376,128]{2,1,0:T(8,128)(2,1)S(1)}, bf16[2,1376,128]{2,1,0:T(8,128)(2,1)S(1)}, s32[8]{0:T(128)S(1)}) custom-call(s32[8]{0:T(128)S(1)} %get-tuple-element.44.idx_ref, bf16[5,128,1024]{2,1,0:T(8,128)(2,1)S(1)} %get-tuple-element.34.refs_0_, f32[5,8,128]{2,1,0:T(8,128)S(1)} %get-tuple-element.35.refs_1_, ...), custom_call_target="tpu_custom_call" | custom-call | flops 100000000 | bytes 524288 | tf_op jit(solution)/shard_map/mlp/pallas_call | solution.py:371
  119.0 8.3 %collective-permute-done.16.right_ref = bf16[2,1376,128]{2,1,0:T(8,128)(2,1)S(1)} collective-permute-done((bf16[2,1376,128]{2,1,0:T(8,128)(2,1)S(1)}, bf16[2,1376,128]{2,1,0:T(8,128)(2,1)S(1)}, u32[]{:S(2)}, u32[]{:S(2)}) %collective-permute-start.16) | collective-permute-done | bytes 704544 | tf_op jit(solution)/shard_map/ppermute | solution.py:46
  127.3 0.2 sum.5
  127.4 2.5 %collective-permute-start.17 = (bf16[1376,128]{1,0:T(8,128)(2,1)S(1)}, bf16[1376,128]{1,0:T(8,128)(2,1)S(1)}, u32[]{:S(2)}, u32[]{:S(2)}) collective-permute-start(bf16[1376,128]{1,0:T(8,128)(2,1)S(1)} %get-tuple-element.53), channel_id=1, source_target_pairs={{0,2},{1,3},{2,4},{3,5},{4,6},{5,7},{6,0},{7,1},{8,10},{9,11},{10,... | collective-permute-start | bytes 1056776 | tf_op jit(solution)/shard_map/ppermute | solution.py:46
  129.9 2.7 %collective-permute-done.14.refs_2_ = bf16[2,1376,128]{2,1,0:T(8,128)(2,1)S(1)} collective-permute-done((bf16[2,1376,128]{2,1,0:T(8,128)(2,1)S(1)}, bf16[2,1376,128]{2,1,0:T(8,128)(2,1)S(1)}, u32[]{:S(2)}, u32[]{:S(2)}) %collective-permute-start.14) | collective-permute-done | bytes 704544 | tf_op jit(solution)/shard_map/ppermute | solution.py:46
  132.6 0.3 sum.4
  132.9 2.8 %collective-permute-start.15 = (bf16[2,1376,128]{2,1,0:T(8,128)(2,1)S(1)}, bf16[2,1376,128]{2,1,0:T(8,128)(2,1)S(1)}, u32[]{:S(2)}, u32[]{:S(2)}) collective-permute-start(bf16[2,1376,128]{2,1,0:T(8,128)(2,1)S(1)} %sum.4), channel_id=1, source_target_pairs={{0,8},{1,9},{2,10},{3,11},{4,12},{5,13},{6,14},{7,15},{8,0},{9,1},... | collective-permute-start | bytes 2113544 | tf_op jit(solution)/shard_map/ppermute | solution.py:46
  135.6 0.0 collective-permute-start.19
  135.7 3.2 %collective-permute-start.20 = (bf16[1376,128]{1,0:T(8,128)(2,1)S(1)}, bf16[1376,128]{1,0:T(8,128)(2,1)S(1)}, u32[]{:S(2)}, u32[]{:S(2)}) collective-permute-start(bf16[1376,128]{1,0:T(8,128)(2,1)S(1)} %get-tuple-element.55), channel_id=1, source_target_pairs={{0,2},{1,3},{2,4},{3,5},{4,6},{5,7},{6,0},{7,1},{8,10},{9,11},{10,... | collective-permute-start | bytes 1056776 | tf_op jit(solution)/shard_map/ppermute | solution.py:46
  138.9 0.1 sum.6
  139.0 2.5 %collective-permute-start.18 = (bf16[1376,128]{1,0:T(8,128)(2,1)S(1)}, bf16[1376,128]{1,0:T(8,128)(2,1)S(1)}, u32[]{:S(2)}, u32[]{:S(2)}) collective-permute-start(bf16[1376,128]{1,0:T(8,128)(2,1)S(1)} %sum.6), channel_id=1, source_target_pairs={{0,2},{1,3},{2,4},{3,5},{4,6},{5,7},{6,0},{7,1},{8,10},{9,11},{10,... | collective-permute-start | bytes 1056776 | tf_op jit(solution)/shard_map/ppermute | solution.py:46
  141.5 0.8 collective-permute-done.21.refs_1_
  142.3 0.1 sum.7
  142.4 0.1 collective-permute-start.22
  142.5 2.2 %mlp.9 = (bf16[2,1376,128]{2,1,0:T(8,128)(2,1)S(1)}, s32[8]{0:T(128)}) custom-call(s32[8]{0:T(128)S(1)} %get-tuple-element.45.idx_ref, bf16[5,128,1024]{2,1,0:T(8,128)(2,1)S(1)} %get-tuple-element.34.refs_0_, f32[5,8,128]{2,1,0:T(8,128)S(1)} %get-tuple-element.35.refs_1_, bf16[3,128,1024]{2,1,0:T(8,128)(2,1)S(1)} %get-tuple-element.36.refs_2_, ...), custom_call_target="tpu_custom_call" | custom-call | flops 100000000 | bytes 524288 | tf_op jit(solution)/shard_map/mlp/pallas_call | solution.py:371
  144.7 5.2 %collective-permute-done.19.gate_3_ref = bf16[1376,128]{1,0:T(8,128)(2,1)S(1)} collective-permute-done((bf16[1376,128]{1,0:T(8,128)(2,1)S(1)}, bf16[1376,128]{1,0:T(8,128)(2,1)S(1)}, u32[]{:S(2)}, u32[]{:S(2)}) %collective-permute-start.19) | collective-permute-done | bytes 352288 | tf_op jit(solution)/shard_map/ppermute | solution.py:46
  149.9 2.7 %collective-permute-done.18.gate_1_ref = bf16[1376,128]{1,0:T(8,128)(2,1)S(1)} collective-permute-done((bf16[1376,128]{1,0:T(8,128)(2,1)S(1)}, bf16[1376,128]{1,0:T(8,128)(2,1)S(1)}, u32[]{:S(2)}, u32[]{:S(2)}) %collective-permute-start.18) | collective-permute-done | bytes 352288 | tf_op jit(solution)/shard_map/ppermute | solution.py:46
  152.5 3.3 %collective-permute-done.22.up_3_ref = bf16[1376,128]{1,0:T(8,128)(2,1)S(1)} collective-permute-done((bf16[1376,128]{1,0:T(8,128)(2,1)S(1)}, bf16[1376,128]{1,0:T(8,128)(2,1)S(1)}, u32[]{:S(2)}, u32[]{:S(2)}) %collective-permute-start.22) | collective-permute-done | bytes 352288 | tf_op jit(solution)/shard_map/ppermute | solution.py:46
  155.8 1.3 finish.1
  (26 shorter events, 0.1 us)
Async XLA Ops:
  0.6 25.4 %copy-start.6 = (bf16[128,1024]{1,0:T(8,128)(2,1)S(1)}, bf16[128,1024]{1,0:T(8,128)(2,1)}, u32[]{:S(2)}) copy-start(bf16[128,1024]{1,0:T(8,128)(2,1)} %constant.165.clone.tab_ref) | copy-start | bytes 786436
  0.6 12.0 %copy-start.8 = (f32[512]{0:T(512)S(1)}, f32[512]{0:T(512)}, u32[]{:S(2)}) copy-start(f32[512]{0:T(512)} %param.14) | copy-start | bytes 6148
  0.7 24.3 %collective-permute-start = (bf16[1368,512]{1,0:T(8,128)(2,1)}, bf16[1368,512]{1,0:T(8,128)(2,1)S(1)}, u32[]{:S(2)}, u32[]{:S(2)}) collective-permute-start(bf16[1368,512]{1,0:T(8,128)(2,1)} %bitcast.18), channel_id=1, source_target_pairs={{0,1},{1,0},{2,3},{3,2},{4,5},{5,4},{6,7},{7,6},{8,9},{9,8},{10,11... | collective-permute-start | bytes 4202504 | tf_op jit(solution)/shard_map/ppermute | solution.py:46
  0.8 25.3 %collective-permute-start.1 = (bf16[1368,512]{1,0:T(8,128)(2,1)}, bf16[1368,512]{1,0:T(8,128)(2,1)S(1)}, u32[]{:S(2)}, u32[]{:S(2)}) collective-permute-start(bf16[1368,512]{1,0:T(8,128)(2,1)} %bitcast.20), channel_id=1, source_target_pairs={{0,1},{1,0},{2,3},{3,2},{4,5},{5,4},{6,7},{7,6},{8,9},{9,8},{10,11... | collective-permute-start | bytes 4202504 | tf_op jit(solution)/shard_map/ppermute | solution.py:46
  3.2 21.8 %all-to-all-start = ((bf16[16,64,128]{2,1,0:T(8,128)(2,1)}), bf16[16,64,128]{2,1,0:T(8,128)(2,1)S(1)}, u32[]{:S(2)}, u32[]{:S(2)}) async-start(bf16[16,64,128]{2,1,0:T(8,128)(2,1)} %prep.1), calls=%async_computation | async-start | bytes 524288 | tf_op jit(solution)/shard_map/all_to_all | solution.py:419
  12.7 1.2 collective-permute-start.2
  24.9 1.1 copy-start.2
  26.1 36.0 %copy-start.4 = (bf16[1368,512]{1,0:T(8,128)(2,1)}, bf16[1368,512]{1,0:T(8,128)(2,1)S(1)}, u32[]{:S(2)}) copy-start(bf16[1368,512]{1,0:T(8,128)(2,1)S(1)} %collective-permute-done.1.wux_ref) | copy-start | bytes 4202500
  42.6 19.4 %copy-start.7 = (bf16[128,512]{1,0:T(8,128)(2,1)S(1)}, bf16[128,512]{1,0:T(8,128)(2,1)}, u32[]{:S(2)}) copy-start(bf16[128,512]{1,0:T(8,128)(2,1)} %start_ref.1) | copy-start | bytes 393220
  62.0 3.0 %collective-permute-start.3 = (bf16[8,128,512]{2,1,0:T(8,128)(2,1)S(1)}, bf16[8,128,512]{2,1,0:T(8,128)(2,1)}, u32[]{:S(2)}, u32[]{:S(2)}) collective-permute-start(bf16[8,128,512]{2,1,0:T(8,128)(2,1)S(1)} %all_to_all.16.mixed_hbm), channel_id=1, source_target_pairs={{0,1},{1,0},{2,3},{3,2},{4,5},{5,4},{6,7},{7,6},{8,9},{9,8},{10,11... | collective-permute-start | bytes 3145736 | tf_op jit(solution)/shard_map/ppermute | solution.py:46
  65.0 21.8 %copy-start = (bf16[512,1368]{0,1:T(8,128)(2,1)S(1)}, bf16[512,1368]{0,1:T(8,128)(2,1)}, u32[]{:S(2)}) copy-start(bf16[512,1368]{0,1:T(8,128)(2,1)} %param.15) | copy-start | bytes 4202500
  65.0 21.8 %copy-start.1 = (bf16[512,1368]{0,1:T(8,128)(2,1)S(1)}, bf16[512,1368]{0,1:T(8,128)(2,1)}, u32[]{:S(2)}) copy-start(bf16[512,1368]{0,1:T(8,128)(2,1)} %param.16) | copy-start | bytes 4202500
  68.7 2.7 %collective-permute-start.5 = (bf16[128,512]{1,0:T(8,128)(2,1)S(1)}, bf16[128,512]{1,0:T(8,128)(2,1)S(1)}, u32[]{:S(2)}, u32[]{:S(2)}) collective-permute-start(bf16[128,512]{1,0:T(8,128)(2,1)S(1)} %get-tuple-element.32.stream_ref), channel_id=1, source_target_pairs={{0,16},{1,0},{2,18},{3,2},{4,20},{5,4},{6,22},{7,6},{8,24},{9,8},{... | collective-permute-start | bytes 393224 | tf_op jit(solution)/shard_map/ppermute | solution.py:448
  68.9 2.5 %collective-permute-start.4 = (bf16[128,512]{1,0:T(8,128)(2,1)S(1)}, bf16[128,512]{1,0:T(8,128)(2,1)S(1)}, u32[]{:S(2)}, u32[]{:S(2)}) collective-permute-start(bf16[128,512]{1,0:T(8,128)(2,1)S(1)} %get-tuple-element.32.stream_ref), channel_id=1, source_target_pairs={{1,16},{3,18},{5,20},{7,22},{9,24},{11,26},{13,28},{15,30},{16,1},... | collective-permute-start | bytes 393224 | tf_op jit(solution)/shard_map/ppermute | solution.py:449
  71.4 9.0 %collective-permute-start.8 = (bf16[2,128,512]{2,1,0:T(8,128)(2,1)S(1)}, bf16[2,128,512]{2,1,0:T(8,128)(2,1)S(1)}, u32[]{:S(2)}, u32[]{:S(2)}) collective-permute-start(bf16[2,128,512]{2,1,0:T(8,128)(2,1)S(1)} %hold.1.refs_0_), channel_id=1, source_target_pairs={{0,64},{1,65},{2,66},{3,67},{4,68},{5,69},{6,70},{7,71},{8,72},{9,... | collective-permute-start | bytes 786440 | tf_op jit(solution)/shard_map/ppermute | solution.py:456
  72.0 13.5 %collective-permute-start.9 = (bf16[2,128,512]{2,1,0:T(8,128)(2,1)S(1)}, bf16[2,128,512]{2,1,0:T(8,128)(2,1)}, u32[]{:S(2)}, u32[]{:S(2)}) collective-permute-start(bf16[2,128,512]{2,1,0:T(8,128)(2,1)S(1)} %hold.1.refs_0_), channel_id=1, source_target_pairs={{0,192},{1,193},{2,194},{3,195},{4,196},{5,197},{6,198},{7,199},{8... | collective-permute-start | bytes 786440 | tf_op jit(solution)/shard_map/ppermute | solution.py:457
  75.7 19.3 %collective-permute-start.7 = (bf16[2,128,512]{2,1,0:T(8,128)(2,1)S(1)}, bf16[2,128,512]{2,1,0:T(8,128)(2,1)S(1)}, u32[]{:S(2)}, u32[]{:S(2)}) collective-permute-start(bf16[2,128,512]{2,1,0:T(8,128)(2,1)S(1)} %hold.1.refs_0_), channel_id=1, source_target_pairs={{0,224},{1,225},{2,226},{3,227},{4,228},{5,229},{6,230},{7,231},{8... | collective-permute-start | bytes 786440 | tf_op jit(solution)/shard_map/ppermute | solution.py:459
  76.3 18.7 %collective-permute-start.6 = (bf16[2,128,512]{2,1,0:T(8,128)(2,1)S(1)}, bf16[2,128,512]{2,1,0:T(8,128)(2,1)S(1)}, u32[]{:S(2)}, u32[]{:S(2)}) collective-permute-start(bf16[2,128,512]{2,1,0:T(8,128)(2,1)S(1)} %hold.1.refs_0_), channel_id=1, source_target_pairs={{0,32},{1,33},{2,34},{3,35},{4,36},{5,37},{6,38},{7,39},{8,40},{9,... | collective-permute-start | bytes 786440 | tf_op jit(solution)/shard_map/ppermute | solution.py:458
  80.5 24.2 %collective-permute-start.12 = (bf16[2,128,512]{2,1,0:T(8,128)(2,1)S(1)}, bf16[2,128,512]{2,1,0:T(8,128)(2,1)S(1)}, u32[]{:S(2)}, u32[]{:S(2)}) collective-permute-start(bf16[2,128,512]{2,1,0:T(8,128)(2,1)S(1)} %collective-permute-done.8.refs_3_), channel_id=1, source_target_pairs={{0,64},{1,65},{2,66},{3,67},{4,68},{5,69},{6,70},{7,71},{8,72},{9,... | collective-permute-start | bytes 786440 | tf_op jit(solution)/shard_map/ppermute | solution.py:462
  80.5 24.2 %collective-permute-start.10 = (bf16[2,128,512]{2,1,0:T(8,128)(2,1)S(1)}, bf16[2,128,512]{2,1,0:T(8,128)(2,1)S(1)}, u32[]{:S(2)}, u32[]{:S(2)}) collective-permute-start(bf16[2,128,512]{2,1,0:T(8,128)(2,1)S(1)} %collective-permute-done.8.refs_3_), channel_id=1, source_target_pairs={{0,32},{1,33},{2,34},{3,35},{4,36},{5,37},{6,38},{7,39},{8,40},{9,... | collective-permute-start | bytes 786440 | tf_op jit(solution)/shard_map/ppermute | solution.py:460
  85.6 19.1 %collective-permute-start.11 = (bf16[2,128,512]{2,1,0:T(8,128)(2,1)}, bf16[2,128,512]{2,1,0:T(8,128)(2,1)S(1)}, u32[]{:S(2)}, u32[]{:S(2)}) collective-permute-start(bf16[2,128,512]{2,1,0:T(8,128)(2,1)} %collective-permute-done.9.refs_4_), channel_id=1, source_target_pairs={{0,224},{1,225},{2,226},{3,227},{4,228},{5,229},{6,230},{7,231},{8... | collective-permute-start | bytes 786440 | tf_op jit(solution)/shard_map/ppermute | solution.py:461
  86.8 1.3 copy-start.3
  88.2 1.3 copy-start.5
  107.5 19.8 %collective-permute-start.16 = (bf16[2,1376,128]{2,1,0:T(8,128)(2,1)S(1)}, bf16[2,1376,128]{2,1,0:T(8,128)(2,1)S(1)}, u32[]{:S(2)}, u32[]{:S(2)}) collective-permute-start(bf16[2,1376,128]{2,1,0:T(8,128)(2,1)S(1)} %get-tuple-element.52), channel_id=1, source_target_pairs={{0,8},{1,9},{2,10},{3,11},{4,12},{5,13},{6,14},{7,15},{8,0},{9,1},... | collective-permute-start | bytes 2113544 | tf_op jit(solution)/shard_map/ppermute | solution.py:46
  112.3 17.7 %collective-permute-start.13 = (bf16[2,1376,128]{2,1,0:T(8,128)(2,1)S(1)}, bf16[2,1376,128]{2,1,0:T(8,128)(2,1)S(1)}, u32[]{:S(2)}, u32[]{:S(2)}) collective-permute-start(bf16[2,1376,128]{2,1,0:T(8,128)(2,1)S(1)} %get-tuple-element.48), channel_id=1, source_target_pairs={{0,2},{1,3},{2,4},{3,5},{4,6},{5,7},{6,0},{7,1},{8,10},{9,11},{10,... | collective-permute-start | bytes 2113544 | tf_op jit(solution)/shard_map/ppermute | solution.py:46
  114.2 18.4 %collective-permute-start.14 = (bf16[2,1376,128]{2,1,0:T(8,128)(2,1)S(1)}, bf16[2,1376,128]{2,1,0:T(8,128)(2,1)S(1)}, u32[]{:S(2)}, u32[]{:S(2)}) collective-permute-start(bf16[2,1376,128]{2,1,0:T(8,128)(2,1)S(1)} %get-tuple-element.49), channel_id=1, source_target_pairs={{0,6},{1,7},{2,0},{3,1},{4,2},{5,3},{6,4},{7,5},{8,14},{9,15},{10,... | collective-permute-start | bytes 2113544 | tf_op jit(solution)/shard_map/ppermute | solution.py:46
  127.4 11.5 %collective-permute-start.17 = (bf16[1376,128]{1,0:T(8,128)(2,1)S(1)}, bf16[1376,128]{1,0:T(8,128)(2,1)S(1)}, u32[]{:S(2)}, u32[]{:S(2)}) collective-permute-start(bf16[1376,128]{1,0:T(8,128)(2,1)S(1)} %get-tuple-element.53), channel_id=1, source_target_pairs={{0,2},{1,3},{2,4},{3,5},{4,6},{5,7},{6,0},{7,1},{8,10},{9,11},{10,... | collective-permute-start | bytes 1056776 | tf_op jit(solution)/shard_map/ppermute | solution.py:46
  129.9 12.4 %collective-permute-start.21 = (bf16[1376,128]{1,0:T(8,128)(2,1)S(1)}, bf16[1376,128]{1,0:T(8,128)(2,1)S(1)}, u32[]{:S(2)}, u32[]{:S(2)}) collective-permute-start(bf16[1376,128]{1,0:T(8,128)(2,1)S(1)} %get-tuple-element.57), channel_id=1, source_target_pairs={{0,6},{1,7},{2,0},{3,1},{4,2},{5,3},{6,4},{7,5},{8,14},{9,15},{10,... | collective-permute-start | bytes 1056776 | tf_op jit(solution)/shard_map/ppermute | solution.py:46
  132.9 23.0 %collective-permute-start.15 = (bf16[2,1376,128]{2,1,0:T(8,128)(2,1)S(1)}, bf16[2,1376,128]{2,1,0:T(8,128)(2,1)S(1)}, u32[]{:S(2)}, u32[]{:S(2)}) collective-permute-start(bf16[2,1376,128]{2,1,0:T(8,128)(2,1)S(1)} %sum.4), channel_id=1, source_target_pairs={{0,8},{1,9},{2,10},{3,11},{4,12},{5,13},{6,14},{7,15},{8,0},{9,1},... | collective-permute-start | bytes 2113544 | tf_op jit(solution)/shard_map/ppermute | solution.py:46
  135.6 14.2 %collective-permute-start.19 = (bf16[1376,128]{1,0:T(8,128)(2,1)S(1)}, bf16[1376,128]{1,0:T(8,128)(2,1)S(1)}, u32[]{:S(2)}, u32[]{:S(2)}) collective-permute-start(bf16[1376,128]{1,0:T(8,128)(2,1)S(1)} %get-tuple-element.54), channel_id=1, source_target_pairs={{0,6},{1,7},{2,0},{3,1},{4,2},{5,3},{6,4},{7,5},{8,14},{9,15},{10,... | collective-permute-start | bytes 1056776 | tf_op jit(solution)/shard_map/ppermute | solution.py:46
  135.7 14.2 %collective-permute-start.20 = (bf16[1376,128]{1,0:T(8,128)(2,1)S(1)}, bf16[1376,128]{1,0:T(8,128)(2,1)S(1)}, u32[]{:S(2)}, u32[]{:S(2)}) collective-permute-start(bf16[1376,128]{1,0:T(8,128)(2,1)S(1)} %get-tuple-element.55), channel_id=1, source_target_pairs={{0,2},{1,3},{2,4},{3,5},{4,6},{5,7},{6,0},{7,1},{8,10},{9,11},{10,... | collective-permute-start | bytes 1056776 | tf_op jit(solution)/shard_map/ppermute | solution.py:46
  139.0 13.6 %collective-permute-start.18 = (bf16[1376,128]{1,0:T(8,128)(2,1)S(1)}, bf16[1376,128]{1,0:T(8,128)(2,1)S(1)}, u32[]{:S(2)}, u32[]{:S(2)}) collective-permute-start(bf16[1376,128]{1,0:T(8,128)(2,1)S(1)} %sum.6), channel_id=1, source_target_pairs={{0,2},{1,3},{2,4},{3,5},{4,6},{5,7},{6,0},{7,1},{8,10},{9,11},{10,... | collective-permute-start | bytes 1056776 | tf_op jit(solution)/shard_map/ppermute | solution.py:46
  142.4 13.4 %collective-permute-start.22 = (bf16[1376,128]{1,0:T(8,128)(2,1)S(1)}, bf16[1376,128]{1,0:T(8,128)(2,1)S(1)}, u32[]{:S(2)}, u32[]{:S(2)}) collective-permute-start(bf16[1376,128]{1,0:T(8,128)(2,1)S(1)} %sum.7), channel_id=1, source_target_pairs={{0,6},{1,7},{2,0},{3,1},{4,2},{5,3},{6,4},{7,5},{8,14},{9,15},{10,... | collective-permute-start | bytes 1056776 | tf_op jit(solution)/shard_map/ppermute | solution.py:46

commit v9 on v8

--- a/solution.py
+++ b/solution.py
@@ -136,28 +136,37 @@
             out_ref[copy, :, cols] = mixed
 
 
-def out_proj_kernel(offset, core_ref, mixed_hbm, w_hbm, start_ref, *refs):
-    *out_refs, mixed, w_buf, sem = refs
-    first = jnp.bitwise_xor(core_ref[0], offset)
+def out_proj_first_kernel(
+    core_ref, mixed_hbm, w_hbm, start_ref, out_ref, w_next, mixed, w_buf, sem
+):
+    core = core_ref[0]
     copies = []
     for j in range(N_TP // 2):
-        rows = pl.ds(pl.multiple_of((2 * j + first) * CH, CH), CH)
-        copies.append(
-            (
-                pltpu.make_async_copy(mixed_hbm.at[j], mixed.at[j], sem.at[0, j]),
-                pltpu.make_async_copy(w_hbm.at[rows], w_buf.at[j], sem.at[1, j]),
-            )
-        )
-    for pair in copies:
-        for copy in pair:
-            copy.start()
+        rows = pl.ds(pl.multiple_of((2 * j + core) * CH, CH), CH)
+        copies.append(pltpu.make_async_copy(mixed_hbm.at[j], mixed.at[j], sem.at[0, j]))
+        copies.append(pltpu.make_async_copy(w_hbm.at[rows], w_buf.at[j], sem.at[1, j]))
+    later = []
+    for j in range(N_TP // 2):
+        rows = pl.ds(pl.multiple_of((2 * j + 1 - core) * CH, CH), CH)
+        later.append(pltpu.make_async_copy(w_hbm.at[rows], w_next.at[j], sem.at[2, j]))
+    for copy in copies + later:
+        copy.start()
     acc = start_ref[...].astype(F32)
-    for j, pair in enumerate(copies):
-        for copy in pair:
-            copy.wait()
+    for j in range(N_TP // 2):
+        copies[2 * j].wait()
+        copies[2 * j + 1].wait()
         acc = acc + dot(mixed[j], w_buf[j])
-    for out_ref in out_refs:
-        out_ref[...] = acc.astype(out_ref.dtype)
+    out_ref[...] = acc
+    for copy in later:
+        copy.wait()
+
+
+def out_proj_second_kernel(mixed_ref, w_ref, start_ref, out_ref, keep_ref):
+    acc = start_ref[...]
+    for j in range(N_TP // 2):
+        acc = acc + dot(mixed_ref[j], w_ref[j])
+    out_ref[...] = acc.astype(BF16)
+    keep_ref[...] = acc.astype(BF16)
 
 
 def square_sums(values):
@@ -297,27 +306,42 @@
     return (z + steps, x, y, k) if z % 2 == 0 else (z - steps, x, y, k)
 
 
-def out_proj(offset, core, mixed, w_out, start, dtype, copies):
+def out_proj_first(core, mixed, w_out, start):
+    vmem = pl.BlockSpec(memory_space=pltpu.VMEM)
     return pl.pallas_call(
-        functools.partial(out_proj_kernel, offset),
-        out_shape=[jax.ShapeDtypeStruct((ROWS, CH), dtype)] * copies,
-        in_specs=[
-            in_smem(),
-            anywhere(),
-            pl.BlockSpec(memory_space=pltpu.HBM),
-            pl.BlockSpec(memory_space=pltpu.VMEM),
+        out_proj_first_kernel,
+        out_shape=[
+            jax.ShapeDtypeStruct((ROWS, CH), F32),
+            jax.ShapeDtypeStruct((N_TP // 2, CH, CH), BF16),
         ],
+        in_specs=[in_smem(), anywhere(), anywhere(), vmem],
+        out_specs=[vmem] * 2,
         scratch_shapes=[
             pltpu.VMEM((N_TP // 2, ROWS, CH), BF16),
             pltpu.VMEM((N_TP // 2, CH, CH), BF16),
-            pltpu.SemaphoreType.DMA((2, N_TP // 2)),
+            pltpu.SemaphoreType.DMA((3, N_TP // 2)),
         ],
-        compiler_params=params(51),
+        compiler_params=params(45),
         cost_estimate=pl.CostEstimate(
-            flops=2 * ROWS * CH * N_TP // 2 * CH, bytes_accessed=5 << 20, transcendentals=0
+            flops=2 * ROWS * CH * N_TP // 2 * CH, bytes_accessed=9 << 20, transcendentals=0
         ),
-        name="out_proj",
+        name="out_proj_first",
     )(core, mixed, w_out, start)
+
+
+def out_proj_second(mixed, weights, start):
+    vmem = pl.BlockSpec(memory_space=pltpu.VMEM)
+    return pl.pallas_call(
+        out_proj_second_kernel,
+        out_shape=[jax.ShapeDtypeStruct((ROWS, CH), BF16)] * 2,
+        in_specs=[vmem] * 3,
+        out_specs=[vmem] * 2,
+        compiler_params=params(16),
+        cost_estimate=pl.CostEstimate(
+            flops=2 * ROWS * CH * N_TP // 2 * CH, bytes_accessed=1 << 20, transcendentals=0
+        ),
+        name="out_proj_second",
+    )(mixed, weights, start)
 
 
 def hold(here, *parts):
@@ -417,7 +441,7 @@
         name="prep",
     )(feat, filters)
     recv = lax.all_to_all(sent, "ctx", 0, 0, tiled=True)
-    recv, wg_oth, wu_oth, gain_oth = lax.optimization_barrier((recv, wg_oth, wu_oth, gain_oth))
+    recv, gain_oth = lax.optimization_barrier((recv, gain_oth))
     conv = pl.pallas_call(
         conv_kernel,
         out_shape=jax.ShapeDtypeStruct((N_CTX, SUB, ROWS), BF16),
@@ -442,9 +466,10 @@
     )
     mixed_oth = shift(mixed, k=1)
     core_arr = core.astype(jnp.int32)[None]
-    (half,) = out_proj(0, core_arr, mixed, w_out, residual, F32, 1)
-    stream_out, stream = out_proj(1, core_arr, mixed_oth, w_out, half, BF16, 2)
-
+    half, w_next = out_proj_first(core_arr, mixed, w_out, residual)
+    stream_out, stream = out_proj_second(mixed_oth, w_next, half)
+
+    stream, wg_oth, wu_oth = lax.optimization_barrier((stream, wg_oth, wu_oth))
     first = lax.ppermute(stream, AXES, pairs_of(to_row_owner_first))
     second = lax.ppermute(stream, AXES, pairs_of(to_row_owner_second))
     here = (x_lo == core).astype(jnp.int32)[None]

time: 158 us -> 156 us (0.987)
  blocking collectives: 32.3 us -> 12.9 us
  waiting for transfers between devices: 56.4 us -> 71.5 us
  starting transfers between devices: 34.4 us -> 38 us
    all_to_all x1 -> x0, blocking collectives: 19.4 us -> none  [shards(): lax.all_to_all(copies, 'tp', 0, 0, axis_index_groups=PLANE_GROUPS, tiled=...]
    all_to_all x0 -> x1, waiting for transfers between devices: none -> 11 us  [shards(): lax.all_to_all(copies, 'tp', 0, 0, axis_index_groups=PLANE_GROUPS, tiled=...]
    all_to_all x0 -> x1, starting transfers between devices: none -> 6.99 us  [shards(): lax.all_to_all(copies, 'tp', 0, 0, axis_index_groups=PLANE_GROUPS, tiled=...]
    ppermute x14, starting transfers between devices: 16.4 us -> 13 us  [shift(): return lax.ppermute(arr, AXES, pairs)]
    unnamed x18 -> x14, local copies, waits for them, and re-layouts: 3.86 us -> 3.11 us
  transfers between devices with their start and end apart: 24 -> 25, of which waited for: 13 -> 15; matrix products, arithmetic and copies ran while one was open for 0% -> 0% of each run, Pallas kernels for 11% -> 13%
where the time goes in v9:
time: 156 us
  waiting for transfers between devices  71.5 us (46%)
  starting transfers between devices  38 us (24%)
  Pallas kernels  29.3 us (19%)
  blocking collectives  12.9 us (8%)
  local copies, waits for them, and re-layouts  3.2 us (2%)
    ppermute x14, waiting for transfers between devices, shift(): return lax.ppermute(arr, AXES, pairs)  25.7 us
    ppermute x14, starting transfers between devices, shift(): return lax.ppermute(arr, AXES, pairs)  13 us
    all_to_all x1, blocking collectives, shards(): conv_rows = lax.all_to_all(conv, 'ctx', 0, 0, tiled=True)  12.9 us
    pallas_call x5, Pallas kernels, mlp_part(): pl.pallas_call(functools.partial(mlp_kernel, slots, split), out_shape=[ja...  11.4 us
    all_to_all x1, waiting for transfers between devices, shards(): lax.all_to_all(copies, 'tp', 0, 0, axis_index_groups=PLANE_GROUPS, tiled=...  11 us
    all_to_all x1, waiting for transfers between devices, shards(): recv = lax.all_to_all(sent, 'ctx', 0, 0, tiled=True)  10.8 us
    all_to_all x1, starting transfers between devices, shards(): recv = lax.all_to_all(sent, 'ctx', 0, 0, tiled=True)  9.5 us
    ppermute x1, waiting for transfers between devices, shards(): lax.ppermute(two_second, AXES, pairs_of(functools.partial(along, -1)))  7.97 us
  transfers between devices with their start and end apart: 25, of which 15 were waited for; matrix products, arithmetic and copies ran while one was open for 0% of the time, Pallas kernels for 13%

profile of v9, /device:TPU:24, one launch (start us, length us, event | category | flops | bytes accessed | tf_op | source)
XLA Modules:
  0.0 155.8 jit_solution(1307565389301004184)
XLA Ops:
  0.6 0.0 copy-start.4
  0.7 2.0 %prep.1 = bf16[16,64,128]{2,1,0:T(8,128)(2,1)} custom-call(bf16[3,128,512]{2,1,0:T(8,128)(2,1)} %bitcast.25, f32[128,512]{1,0:T(8,128)} %filt_ref.1), custom_call_target="tpu_custom_call" | custom-call | tf_op jit(solution)/shard_map/prep/pallas_call | solution.py:437
  2.6 9.5 %all-to-all-start = ((bf16[16,64,128]{2,1,0:T(8,128)(2,1)}), bf16[16,64,128]{2,1,0:T(8,128)(2,1)S(1)}, u32[]{:S(2)}, u32[]{:S(2)}) async-start(bf16[16,64,128]{2,1,0:T(8,128)(2,1)} %prep.1), calls=%async_computation | async-start | bytes 524288 | tf_op jit(solution)/shard_map/all_to_all | solution.py:443
  12.1 0.1 collective-permute-start
  12.2 1.1 collective-permute-done.refs_6_.refs_4_
  13.4 10.8 %all-to-all-done.x_ref = bf16[16,64,128]{2,1,0:T(8,128)(2,1)S(1)} async-done(((bf16[16,64,128]{2,1,0:T(8,128)(2,1)}), bf16[16,64,128]{2,1,0:T(8,128)(2,1)S(1)}, u32[]{:S(2)}, u32[]{:S(2)}) %all-to-all-start) | async-done | bytes 262176 | tf_op jit(solution)/shard_map/all_to_all | solution.py:443
  24.2 1.5 conv.1
  25.6 12.9 %all_to_all.15.conv_ref = bf16[16,32,128]{2,1,0:T(8,128)(2,1)} all-to-all(bf16[16,32,128]{2,1,0:T(8,128)(2,1)S(1)} %conv.1), channel_id=1, replica_groups=mesh['ctx'=16,'tp'=16] {'ctx'}, dimensions={0} | all-to-all | bytes 262144 | tf_op jit(solution)/shard_map/all_to_all | solution.py:456
  38.6 2.2 %mix.1 = bf16[8,128,512]{2,1,0:T(8,128)(2,1)} custom-call(bf16[16,32,128]{2,1,0:T(8,128)(2,1)} %all_to_all.15.conv_ref, bf16[3,128,512]{2,1,0:T(8,128)(2,1)} %bitcast.26, f32[1,512]{1,0:T(1,128)} %bitcast.28), custom_call_target="tpu_custom_call" | custom-call | tf_op jit(solution)/shard_map/mix/pallas_call | solution.py:457
  40.8 7.0 %all-to-all-start.2 = ((bf16[8,128,512]{2,1,0:T(8,128)(2,1)}), bf16[8,128,512]{2,1,0:T(8,128)(2,1)S(1)}, u32[]{:S(2)}, u32[]{:S(2)}) async-start(bf16[8,128,512]{2,1,0:T(8,128)(2,1)} %mix.1), calls=%async_computation.2 | async-start | bytes 2097152 | tf_op jit(solution)/shard_map/all_to_all | solution.py:464
  47.8 0.0 collective-permute-start.2
  47.8 0.5 collective-permute-start.3
  48.3 11.0 %all-to-all-done.2.mixed_hbm = bf16[8,128,512]{2,1,0:T(8,128)(2,1)S(1)} async-done(((bf16[8,128,512]{2,1,0:T(8,128)(2,1)}), bf16[8,128,512]{2,1,0:T(8,128)(2,1)S(1)}, u32[]{:S(2)}, u32[]{:S(2)}) %all-to-all-start.2) | async-done | bytes 1048608 | tf_op jit(solution)/shard_map/all_to_all | solution.py:464
  59.3 0.9 copy-done.5
  60.2 4.0 %out_proj_first.1 = (f32[128,512]{1,0:T(8,128)S(1)}, bf16[8,512,512]{2,1,0:T(8,128)(2,1)S(1)}) custom-call(s32[1]{0:T(128)} %bitcast.3.core_ref, bf16[8,128,512]{2,1,0:T(8,128)(2,1)S(1)} %all-to-all-done.2.mixed_hbm, bf16[8192,512]{1,0:T(8,128)(2,1)} %w_hbm.1, bf16[128,512]{1,0:T(8,128)(2,1)S(1)} %copy-done.5), custom_call_target="tpu_custom_call" | custom-call | flops 536870912 | bytes 9437184 | tf_op jit(solution)/shard_map/out_proj_first/pallas_call | solution.py:311
  64.2 0.0 collective-permute-done.1.mixed_ref
  64.2 1.0 copy-done.2
  65.2 1.2 copy-done.3
  66.4 1.4 out_proj_second.1
  67.8 0.0 collective-permute-done.2.wgx_ref
  67.8 0.0 collective-permute-done.3.wux_ref
  67.8 0.9 collective-permute-start.5
  68.7 0.7 collective-permute-start.4
  69.4 1.8 %collective-permute-done.5.first_ref = bf16[128,512]{1,0:T(8,128)(2,1)S(1)} collective-permute-done((bf16[128,512]{1,0:T(8,128)(2,1)S(1)}, bf16[128,512]{1,0:T(8,128)(2,1)S(1)}, u32[]{:S(2)}, u32[]{:S(2)}) %collective-permute-start.5) | collective-permute-done | bytes 131104 | tf_op jit(solution)/shard_map/ppermute | solution.py:473
  71.3 0.5 collective-permute-start.8
  71.7 3.8 %collective-permute-start.9 = (bf16[2,128,512]{2,1,0:T(8,128)(2,1)S(1)}, bf16[2,128,512]{2,1,0:T(8,128)(2,1)}, u32[]{:S(2)}, u32[]{:S(2)}) collective-permute-start(bf16[2,128,512]{2,1,0:T(8,128)(2,1)S(1)} %hold.1.refs_0_), channel_id=1, source_target_pairs={{0,192},{1,193},{2,194},{3,195},{4,196},{5,197},{6,198},{7,199},{8... | collective-permute-start | bytes 786440 | tf_op jit(solution)/shard_map/ppermute | solution.py:482
  75.5 0.1 stack.35
  75.6 0.1 collective-permute-start.7
  75.6 0.1 collective-permute-start.6
  75.7 4.7 %collective-permute-done.8.refs_3_ = bf16[2,128,512]{2,1,0:T(8,128)(2,1)S(1)} collective-permute-done((bf16[2,128,512]{2,1,0:T(8,128)(2,1)S(1)}, bf16[2,128,512]{2,1,0:T(8,128)(2,1)S(1)}, u32[]{:S(2)}, u32[]{:S(2)}) %collective-permute-start.8) | collective-permute-done | bytes 262176 | tf_op jit(solution)/shard_map/ppermute | solution.py:481
  80.4 1.2 collective-permute-start.10
  81.5 4.6 %collective-permute-done.9.refs_4_ = bf16[2,128,512]{2,1,0:T(8,128)(2,1)} collective-permute-done((bf16[2,128,512]{2,1,0:T(8,128)(2,1)S(1)}, bf16[2,128,512]{2,1,0:T(8,128)(2,1)}, u32[]{:S(2)}, u32[]{:S(2)}) %collective-permute-start.9) | collective-permute-done | bytes 262176 | tf_op jit(solution)/shard_map/ppermute | solution.py:482
  86.1 1.4 collective-permute-start.11
  87.6 2.7 %load.1 = (bf16[1368,1024]{1,0:T(8,128)(2,1)S(1)}, bf16[1368,1024]{1,0:T(8,128)(2,1)S(1)}, bf16[16,512]{1,0:T(8,128)(2,1)}) custom-call(bf16[1368,512]{1,0:T(8,128)(2,1)S(1)} %bitcast.19, bf16[1368,512]{1,0:T(8,128)(2,1)} %collective-permute-done.2.wgx_ref, bf16[1368,512]{1,0:T(8,128)(2,1)S(1)} %bitcast.21, ...), custom_call_target="tpu_custom_call" | custom-call | flops 1 | bytes 12582912 | tf_op jit(solution)/shard_map/load/pallas_call | solution.py:362
  90.3 5.0 %collective-permute-done.7.refs_2_ = bf16[2,128,512]{2,1,0:T(8,128)(2,1)S(1)} collective-permute-done((bf16[2,128,512]{2,1,0:T(8,128)(2,1)S(1)}, bf16[2,128,512]{2,1,0:T(8,128)(2,1)S(1)}, u32[]{:S(2)}, u32[]{:S(2)}) %collective-permute-start.7) | collective-permute-done | bytes 262176 | tf_op jit(solution)/shard_map/ppermute | solution.py:484
  95.3 1.8 %scale.2 = (bf16[5,128,1024]{2,1,0:T(8,128)(2,1)S(1)}, f32[5,8,128]{2,1,0:T(8,128)S(1)}) custom-call(bf16[2,128,512]{2,1,0:T(8,128)(2,1)S(1)} %hold.1.refs_0_, bf16[2,128,512]{2,1,0:T(8,128)(2,1)S(1)} %collective-permute-done.6.refs_1_, bf16[2,128,512]{2,1,0:T(8,128)(2,1)S(1)} %collective-permute-done.7.refs_2_, ...), custom_call_target="tpu_custom_call" | custom-call | flops 20971520 | bytes 2621440 | tf_op jit(solution)/shard_map/scale/pallas_call | solution.py:377
  97.0 8.0 %collective-permute-done.11.refs_1_ = bf16[2,128,512]{2,1,0:T(8,128)(2,1)S(1)} collective-permute-done((bf16[2,128,512]{2,1,0:T(8,128)(2,1)}, bf16[2,128,512]{2,1,0:T(8,128)(2,1)S(1)}, u32[]{:S(2)}, u32[]{:S(2)}) %collective-permute-start.11) | collective-permute-done | bytes 262176 | tf_op jit(solution)/shard_map/ppermute | solution.py:486
  105.0 0.6 scale.3
  105.6 2.2 %mlp.5 = (bf16[2,1376,128]{2,1,0:T(8,128)(2,1)S(1)}, s32[8]{0:T(128)S(1)}) custom-call(s32[8]{0:T(128)S(1)} %fusion.5.idx_ref, bf16[5,128,1024]{2,1,0:T(8,128)(2,1)S(1)} %get-tuple-element.40.refs_0_, f32[5,8,128]{2,1,0:T(8,128)S(1)} %get-tuple-element.41.refs_1_, bf16[3,128,1024]{2,1,0:T(8,128)(2,1)S(1)} %get-tuple-element.42.refs_2_, ...), custom_call_target="tpu_custom_call" | custom-call | flops 100000000 | bytes 524288 | tf_op jit(solution)/shard_map/mlp/pallas_call | solution.py:395
  107.8 1.4 collective-permute-start.16
  109.2 2.3 %mlp.6 = (bf16[2,1376,128]{2,1,0:T(8,128)(2,1)S(1)}, bf16[2,1376,128]{2,1,0:T(8,128)(2,1)S(1)}, s32[8]{0:T(128)S(1)}) custom-call(s32[8]{0:T(128)S(1)} %get-tuple-element.48.idx_ref, bf16[5,128,1024]{2,1,0:T(8,128)(2,1)S(1)} %get-tuple-element.40.refs_0_, f32[5,8,128]{2,1,0:T(8,128)S(1)} %get-tuple-element.41.refs_1_, ...), custom_call_target="tpu_custom_call" | custom-call | flops 100000000 | bytes 524288 | tf_op jit(solution)/shard_map/mlp/pallas_call | solution.py:395
  111.6 1.9 %collective-permute-start.13 = (bf16[2,1376,128]{2,1,0:T(8,128)(2,1)S(1)}, bf16[2,1376,128]{2,1,0:T(8,128)(2,1)S(1)}, u32[]{:S(2)}, u32[]{:S(2)}) collective-permute-start(bf16[2,1376,128]{2,1,0:T(8,128)(2,1)S(1)} %get-tuple-element.54), channel_id=1, source_target_pairs={{0,2},{1,3},{2,4},{3,5},{4,6},{5,7},{6,0},{7,1},{8,10},{9,11},{10,... | collective-permute-start | bytes 2113544 | tf_op jit(solution)/shard_map/ppermute | solution.py:46
  113.4 0.2 collective-permute-start.14
  113.7 2.3 %mlp.7 = (bf16[1376,128]{1,0:T(8,128)(2,1)S(1)}, bf16[1376,128]{1,0:T(8,128)(2,1)S(1)}, bf16[1376,128]{1,0:T(8,128)(2,1)S(1)}, bf16[1376,128]{1,0:T(8,128)(2,1)S(1)}, s32[8]{0:T(128)S(1)}) custom-call(s32[8]{0:T(128)S(1)} %get-tuple-element.49.idx_ref, bf16[5,128,1024]{2,1,0:T(8,128)(2,1)S(1)} %get-tuple-element.40.refs_0_, ...), custom_call_target="tpu_custom_call" | custom-call | flops 100000000 | bytes 524288 | tf_op jit(solution)/shard_map/mlp/pallas_call | solution.py:395
  116.0 2.3 %mlp.8 = (bf16[2,1376,128]{2,1,0:T(8,128)(2,1)S(1)}, bf16[2,1376,128]{2,1,0:T(8,128)(2,1)S(1)}, s32[8]{0:T(128)S(1)}) custom-call(s32[8]{0:T(128)S(1)} %get-tuple-element.50.idx_ref, bf16[5,128,1024]{2,1,0:T(8,128)(2,1)S(1)} %get-tuple-element.40.refs_0_, f32[5,8,128]{2,1,0:T(8,128)S(1)} %get-tuple-element.41.refs_1_, ...), custom_call_target="tpu_custom_call" | custom-call | flops 100000000 | bytes 524288 | tf_op jit(solution)/shard_map/mlp/pallas_call | solution.py:395
  118.3 8.9 %collective-permute-done.16.right_ref = bf16[2,1376,128]{2,1,0:T(8,128)(2,1)S(1)} collective-permute-done((bf16[2,1376,128]{2,1,0:T(8,128)(2,1)S(1)}, bf16[2,1376,128]{2,1,0:T(8,128)(2,1)S(1)}, u32[]{:S(2)}, u32[]{:S(2)}) %collective-permute-start.16) | collective-permute-done | bytes 704544 | tf_op jit(solution)/shard_map/ppermute | solution.py:46
  127.2 0.2 sum.5
  127.4 1.4 collective-permute-start.17
  128.8 0.7 collective-permute-start.21
  129.5 2.6 %collective-permute-done.14.refs_2_ = bf16[2,1376,128]{2,1,0:T(8,128)(2,1)S(1)} collective-permute-done((bf16[2,1376,128]{2,1,0:T(8,128)(2,1)S(1)}, bf16[2,1376,128]{2,1,0:T(8,128)(2,1)S(1)}, u32[]{:S(2)}, u32[]{:S(2)}) %collective-permute-start.14) | collective-permute-done | bytes 704544 | tf_op jit(solution)/shard_map/ppermute | solution.py:46
  132.1 0.3 sum.4
  132.4 1.8 %collective-permute-start.15 = (bf16[2,1376,128]{2,1,0:T(8,128)(2,1)S(1)}, bf16[2,1376,128]{2,1,0:T(8,128)(2,1)S(1)}, u32[]{:S(2)}, u32[]{:S(2)}) collective-permute-start(bf16[2,1376,128]{2,1,0:T(8,128)(2,1)S(1)} %sum.4), channel_id=1, source_target_pairs={{0,8},{1,9},{2,10},{3,11},{4,12},{5,13},{6,14},{7,15},{8,0},{9,1},... | collective-permute-start | bytes 2113544 | tf_op jit(solution)/shard_map/ppermute | solution.py:46
  134.1 3.2 %collective-permute-start.20 = (bf16[1376,128]{1,0:T(8,128)(2,1)S(1)}, bf16[1376,128]{1,0:T(8,128)(2,1)S(1)}, u32[]{:S(2)}, u32[]{:S(2)}) collective-permute-start(bf16[1376,128]{1,0:T(8,128)(2,1)S(1)} %get-tuple-element.61), channel_id=1, source_target_pairs={{0,2},{1,3},{2,4},{3,5},{4,6},{5,7},{6,0},{7,1},{8,10},{9,11},{10,... | collective-permute-start | bytes 1056776 | tf_op jit(solution)/shard_map/ppermute | solution.py:46
  137.4 1.3 collective-permute-done.17.refs_1_
  138.6 0.1 sum.6
  138.7 1.7 %collective-permute-start.18 = (bf16[1376,128]{1,0:T(8,128)(2,1)S(1)}, bf16[1376,128]{1,0:T(8,128)(2,1)S(1)}, u32[]{:S(2)}, u32[]{:S(2)}) collective-permute-start(bf16[1376,128]{1,0:T(8,128)(2,1)S(1)} %sum.6), channel_id=1, source_target_pairs={{0,2},{1,3},{2,4},{3,5},{4,6},{5,7},{6,0},{7,1},{8,10},{9,11},{10,... | collective-permute-start | bytes 1056776 | tf_op jit(solution)/shard_map/ppermute | solution.py:46
  140.4 0.8 collective-permute-done.21.refs_1_
  141.2 0.1 sum.7
  141.3 0.1 collective-permute-start.22
  141.3 2.2 %mlp.9 = (bf16[2,1376,128]{2,1,0:T(8,128)(2,1)S(1)}, s32[8]{0:T(128)}) custom-call(s32[8]{0:T(128)S(1)} %get-tuple-element.51.idx_ref, bf16[5,128,1024]{2,1,0:T(8,128)(2,1)S(1)} %get-tuple-element.40.refs_0_, f32[5,8,128]{2,1,0:T(8,128)S(1)} %get-tuple-element.41.refs_1_, bf16[3,128,1024]{2,1,0:T(8,128)(2,1)S(1)} %get-tuple-element.42.refs_2_, ...), custom_call_target="tpu_custom_call" | custom-call | flops 100000000 | bytes 524288 | tf_op jit(solution)/shard_map/mlp/pallas_call | solution.py:395
  143.6 5.1 %collective-permute-done.19.gate_3_ref = bf16[1376,128]{1,0:T(8,128)(2,1)S(1)} collective-permute-done((bf16[1376,128]{1,0:T(8,128)(2,1)S(1)}, bf16[1376,128]{1,0:T(8,128)(2,1)S(1)}, u32[]{:S(2)}, u32[]{:S(2)}) %collective-permute-start.19) | collective-permute-done | bytes 352288 | tf_op jit(solution)/shard_map/ppermute | solution.py:46
  148.7 3.2 %collective-permute-done.18.gate_1_ref = bf16[1376,128]{1,0:T(8,128)(2,1)S(1)} collective-permute-done((bf16[1376,128]{1,0:T(8,128)(2,1)S(1)}, bf16[1376,128]{1,0:T(8,128)(2,1)S(1)}, u32[]{:S(2)}, u32[]{:S(2)}) %collective-permute-start.18) | collective-permute-done | bytes 352288 | tf_op jit(solution)/shard_map/ppermute | solution.py:46
  152.0 2.5 %collective-permute-done.22.up_3_ref = bf16[1376,128]{1,0:T(8,128)(2,1)S(1)} collective-permute-done((bf16[1376,128]{1,0:T(8,128)(2,1)S(1)}, bf16[1376,128]{1,0:T(8,128)(2,1)S(1)}, u32[]{:S(2)}, u32[]{:S(2)}) %collective-permute-start.22) | collective-permute-done | bytes 352288 | tf_op jit(solution)/shard_map/ppermute | solution.py:46
  154.5 1.3 finish.1
  (23 shorter events, 0.1 us)
Async XLA Ops:
  0.6 23.5 %copy-start.4 = (bf16[128,1024]{1,0:T(8,128)(2,1)S(1)}, bf16[128,1024]{1,0:T(8,128)(2,1)}, u32[]{:S(2)}) copy-start(bf16[128,1024]{1,0:T(8,128)(2,1)} %constant.165.clone.tab_ref) | copy-start | bytes 786436
  0.6 11.5 %copy-start.6 = (f32[512]{0:T(512)S(1)}, f32[512]{0:T(512)}, u32[]{:S(2)}) copy-start(f32[512]{0:T(512)} %param.14) | copy-start | bytes 6148
  2.6 21.5 %all-to-all-start = ((bf16[16,64,128]{2,1,0:T(8,128)(2,1)}), bf16[16,64,128]{2,1,0:T(8,128)(2,1)S(1)}, u32[]{:S(2)}, u32[]{:S(2)}) async-start(bf16[16,64,128]{2,1,0:T(8,128)(2,1)} %prep.1), calls=%async_computation | async-start | bytes 524288 | tf_op jit(solution)/shard_map/all_to_all | solution.py:443
  12.1 1.2 collective-permute-start
  40.8 7.0 %copy-start = (bf16[512,1368]{0,1:T(8,128)(2,1)S(1)}, bf16[512,1368]{0,1:T(8,128)(2,1)}, u32[]{:S(2)}) copy-start(bf16[512,1368]{0,1:T(8,128)(2,1)} %param.15) | copy-start | bytes 4202500
  40.8 18.5 %all-to-all-start.2 = ((bf16[8,128,512]{2,1,0:T(8,128)(2,1)}), bf16[8,128,512]{2,1,0:T(8,128)(2,1)S(1)}, u32[]{:S(2)}, u32[]{:S(2)}) async-start(bf16[8,128,512]{2,1,0:T(8,128)(2,1)} %mix.1), calls=%async_computation.2 | async-start | bytes 2097152 | tf_op jit(solution)/shard_map/all_to_all | solution.py:464
  47.8 20.0 %collective-permute-start.2 = (bf16[1368,512]{1,0:T(8,128)(2,1)S(1)}, bf16[1368,512]{1,0:T(8,128)(2,1)}, u32[]{:S(2)}, u32[]{:S(2)}) collective-permute-start(bf16[1368,512]{1,0:T(8,128)(2,1)S(1)} %bitcast.18), channel_id=1, source_target_pairs={{0,1},{1,0},{2,3},{3,2},{4,5},{5,4},{6,7},{7,6},{8,9},{9,8},{10,11... | collective-permute-start | bytes 4202504 | tf_op jit(solution)/shard_map/ppermute | solution.py:46
  47.8 20.0 %collective-permute-start.3 = (bf16[1368,512]{1,0:T(8,128)(2,1)}, bf16[1368,512]{1,0:T(8,128)(2,1)}, u32[]{:S(2)}, u32[]{:S(2)}) collective-permute-start(bf16[1368,512]{1,0:T(8,128)(2,1)} %bitcast.20), channel_id=1, source_target_pairs={{0,1},{1,0},{2,3},{3,2},{4,5},{5,4},{6,7},{7,6},{8,9},{9,8},{10,11... | collective-permute-start | bytes 4202504 | tf_op jit(solution)/shard_map/ppermute | solution.py:46
  59.3 4.9 %collective-permute-start.1 = (bf16[8,128,512]{2,1,0:T(8,128)(2,1)S(1)}, bf16[8,128,512]{2,1,0:T(8,128)(2,1)S(1)}, u32[]{:S(2)}, u32[]{:S(2)}) collective-permute-start(bf16[8,128,512]{2,1,0:T(8,128)(2,1)S(1)} %all-to-all-done.2.mixed_hbm), channel_id=1, source_target_pairs={{0,1},{1,0},{2,3},{3,2},{4,5},{5,4},{6,7},{7,6},{8,9},{9,8},{10,11... | collective-permute-start | bytes 3145736 | tf_op jit(solution)/shard_map/ppermute | solution.py:46
  59.3 0.9 copy-start.5
  64.2 1.0 copy-start.2
  65.2 1.2 copy-start.3
  66.4 21.2 %copy-start.1 = (bf16[512,1368]{0,1:T(8,128)(2,1)S(1)}, bf16[512,1368]{0,1:T(8,128)(2,1)}, u32[]{:S(2)}) copy-start(bf16[512,1368]{0,1:T(8,128)(2,1)} %param.16) | copy-start | bytes 4202500
  67.8 3.4 %collective-permute-start.5 = (bf16[128,512]{1,0:T(8,128)(2,1)S(1)}, bf16[128,512]{1,0:T(8,128)(2,1)S(1)}, u32[]{:S(2)}, u32[]{:S(2)}) collective-permute-start(bf16[128,512]{1,0:T(8,128)(2,1)S(1)} %get-tuple-element.38.stream_ref), channel_id=1, source_target_pairs={{0,16},{1,0},{2,18},{3,2},{4,20},{5,4},{6,22},{7,6},{8,24},{9,8},{... | collective-permute-start | bytes 393224 | tf_op jit(solution)/shard_map/ppermute | solution.py:473
  68.7 2.5 %collective-permute-start.4 = (bf16[128,512]{1,0:T(8,128)(2,1)S(1)}, bf16[128,512]{1,0:T(8,128)(2,1)S(1)}, u32[]{:S(2)}, u32[]{:S(2)}) collective-permute-start(bf16[128,512]{1,0:T(8,128)(2,1)S(1)} %get-tuple-element.38.stream_ref), channel_id=1, source_target_pairs={{1,16},{3,18},{5,20},{7,22},{9,24},{11,26},{13,28},{15,30},{16,1},... | collective-permute-start | bytes 393224 | tf_op jit(solution)/shard_map/ppermute | solution.py:474
  71.3 9.1 %collective-permute-start.8 = (bf16[2,128,512]{2,1,0:T(8,128)(2,1)S(1)}, bf16[2,128,512]{2,1,0:T(8,128)(2,1)S(1)}, u32[]{:S(2)}, u32[]{:S(2)}) collective-permute-start(bf16[2,128,512]{2,1,0:T(8,128)(2,1)S(1)} %hold.1.refs_0_), channel_id=1, source_target_pairs={{0,64},{1,65},{2,66},{3,67},{4,68},{5,69},{6,70},{7,71},{8,72},{9,... | collective-permute-start | bytes 786440 | tf_op jit(solution)/shard_map/ppermute | solution.py:481
  71.7 14.4 %collective-permute-start.9 = (bf16[2,128,512]{2,1,0:T(8,128)(2,1)S(1)}, bf16[2,128,512]{2,1,0:T(8,128)(2,1)}, u32[]{:S(2)}, u32[]{:S(2)}) collective-permute-start(bf16[2,128,512]{2,1,0:T(8,128)(2,1)S(1)} %hold.1.refs_0_), channel_id=1, source_target_pairs={{0,192},{1,193},{2,194},{3,195},{4,196},{5,197},{6,198},{7,199},{8... | collective-permute-start | bytes 786440 | tf_op jit(solution)/shard_map/ppermute | solution.py:482
  75.6 19.7 %collective-permute-start.7 = (bf16[2,128,512]{2,1,0:T(8,128)(2,1)S(1)}, bf16[2,128,512]{2,1,0:T(8,128)(2,1)S(1)}, u32[]{:S(2)}, u32[]{:S(2)}) collective-permute-start(bf16[2,128,512]{2,1,0:T(8,128)(2,1)S(1)} %hold.1.refs_0_), channel_id=1, source_target_pairs={{0,224},{1,225},{2,226},{3,227},{4,228},{5,229},{6,230},{7,231},{8... | collective-permute-start | bytes 786440 | tf_op jit(solution)/shard_map/ppermute | solution.py:484
  75.6 19.6 %collective-permute-start.6 = (bf16[2,128,512]{2,1,0:T(8,128)(2,1)S(1)}, bf16[2,128,512]{2,1,0:T(8,128)(2,1)S(1)}, u32[]{:S(2)}, u32[]{:S(2)}) collective-permute-start(bf16[2,128,512]{2,1,0:T(8,128)(2,1)S(1)} %hold.1.refs_0_), channel_id=1, source_target_pairs={{0,32},{1,33},{2,34},{3,35},{4,36},{5,37},{6,38},{7,39},{8,40},{9,... | collective-permute-start | bytes 786440 | tf_op jit(solution)/shard_map/ppermute | solution.py:483
  80.3 24.7 %collective-permute-start.12 = (bf16[2,128,512]{2,1,0:T(8,128)(2,1)S(1)}, bf16[2,128,512]{2,1,0:T(8,128)(2,1)S(1)}, u32[]{:S(2)}, u32[]{:S(2)}) collective-permute-start(bf16[2,128,512]{2,1,0:T(8,128)(2,1)S(1)} %collective-permute-done.8.refs_3_), channel_id=1, source_target_pairs={{0,64},{1,65},{2,66},{3,67},{4,68},{5,69},{6,70},{7,71},{8,72},{9,... | collective-permute-start | bytes 786440 | tf_op jit(solution)/shard_map/ppermute | solution.py:487
  80.4 24.7 %collective-permute-start.10 = (bf16[2,128,512]{2,1,0:T(8,128)(2,1)S(1)}, bf16[2,128,512]{2,1,0:T(8,128)(2,1)S(1)}, u32[]{:S(2)}, u32[]{:S(2)}) collective-permute-start(bf16[2,128,512]{2,1,0:T(8,128)(2,1)S(1)} %collective-permute-done.8.refs_3_), channel_id=1, source_target_pairs={{0,32},{1,33},{2,34},{3,35},{4,36},{5,37},{6,38},{7,39},{8,40},{9,... | collective-permute-start | bytes 786440 | tf_op jit(solution)/shard_map/ppermute | solution.py:485
  86.1 18.9 %collective-permute-start.11 = (bf16[2,128,512]{2,1,0:T(8,128)(2,1)}, bf16[2,128,512]{2,1,0:T(8,128)(2,1)S(1)}, u32[]{:S(2)}, u32[]{:S(2)}) collective-permute-start(bf16[2,128,512]{2,1,0:T(8,128)(2,1)} %collective-permute-done.9.refs_4_), channel_id=1, source_target_pairs={{0,224},{1,225},{2,226},{3,227},{4,228},{5,229},{6,230},{7,231},{8... | collective-permute-start | bytes 786440 | tf_op jit(solution)/shard_map/ppermute | solution.py:486
  107.8 19.4 %collective-permute-start.16 = (bf16[2,1376,128]{2,1,0:T(8,128)(2,1)S(1)}, bf16[2,1376,128]{2,1,0:T(8,128)(2,1)S(1)}, u32[]{:S(2)}, u32[]{:S(2)}) collective-permute-start(bf16[2,1376,128]{2,1,0:T(8,128)(2,1)S(1)} %get-tuple-element.58), channel_id=1, source_target_pairs={{0,8},{1,9},{2,10},{3,11},{4,12},{5,13},{6,14},{7,15},{8,0},{9,1},... | collective-permute-start | bytes 2113544 | tf_op jit(solution)/shard_map/ppermute | solution.py:46
  111.6 17.9 %collective-permute-start.13 = (bf16[2,1376,128]{2,1,0:T(8,128)(2,1)S(1)}, bf16[2,1376,128]{2,1,0:T(8,128)(2,1)S(1)}, u32[]{:S(2)}, u32[]{:S(2)}) collective-permute-start(bf16[2,1376,128]{2,1,0:T(8,128)(2,1)S(1)} %get-tuple-element.54), channel_id=1, source_target_pairs={{0,2},{1,3},{2,4},{3,5},{4,6},{5,7},{6,0},{7,1},{8,10},{9,11},{10,... | collective-permute-start | bytes 2113544 | tf_op jit(solution)/shard_map/ppermute | solution.py:46
  113.4 18.7 %collective-permute-start.14 = (bf16[2,1376,128]{2,1,0:T(8,128)(2,1)S(1)}, bf16[2,1376,128]{2,1,0:T(8,128)(2,1)S(1)}, u32[]{:S(2)}, u32[]{:S(2)}) collective-permute-start(bf16[2,1376,128]{2,1,0:T(8,128)(2,1)S(1)} %get-tuple-element.55), channel_id=1, source_target_pairs={{0,6},{1,7},{2,0},{3,1},{4,2},{5,3},{6,4},{7,5},{8,14},{9,15},{10,... | collective-permute-start | bytes 2113544 | tf_op jit(solution)/shard_map/ppermute | solution.py:46
  127.4 11.3 %collective-permute-start.17 = (bf16[1376,128]{1,0:T(8,128)(2,1)S(1)}, bf16[1376,128]{1,0:T(8,128)(2,1)S(1)}, u32[]{:S(2)}, u32[]{:S(2)}) collective-permute-start(bf16[1376,128]{1,0:T(8,128)(2,1)S(1)} %get-tuple-element.59), channel_id=1, source_target_pairs={{0,2},{1,3},{2,4},{3,5},{4,6},{5,7},{6,0},{7,1},{8,10},{9,11},{10,... | collective-permute-start | bytes 1056776 | tf_op jit(solution)/shard_map/ppermute | solution.py:46
  128.8 12.4 %collective-permute-start.21 = (bf16[1376,128]{1,0:T(8,128)(2,1)S(1)}, bf16[1376,128]{1,0:T(8,128)(2,1)S(1)}, u32[]{:S(2)}, u32[]{:S(2)}) collective-permute-start(bf16[1376,128]{1,0:T(8,128)(2,1)S(1)} %get-tuple-element.63), channel_id=1, source_target_pairs={{0,6},{1,7},{2,0},{3,1},{4,2},{5,3},{6,4},{7,5},{8,14},{9,15},{10,... | collective-permute-start | bytes 1056776 | tf_op jit(solution)/shard_map/ppermute | solution.py:46
  132.4 22.2 %collective-permute-start.15 = (bf16[2,1376,128]{2,1,0:T(8,128)(2,1)S(1)}, bf16[2,1376,128]{2,1,0:T(8,128)(2,1)S(1)}, u32[]{:S(2)}, u32[]{:S(2)}) collective-permute-start(bf16[2,1376,128]{2,1,0:T(8,128)(2,1)S(1)} %sum.4), channel_id=1, source_target_pairs={{0,8},{1,9},{2,10},{3,11},{4,12},{5,13},{6,14},{7,15},{8,0},{9,1},... | collective-permute-start | bytes 2113544 | tf_op jit(solution)/shard_map/ppermute | solution.py:46
  134.1 14.6 %collective-permute-start.19 = (bf16[1376,128]{1,0:T(8,128)(2,1)S(1)}, bf16[1376,128]{1,0:T(8,128)(2,1)S(1)}, u32[]{:S(2)}, u32[]{:S(2)}) collective-permute-start(bf16[1376,128]{1,0:T(8,128)(2,1)S(1)} %get-tuple-element.60), channel_id=1, source_target_pairs={{0,6},{1,7},{2,0},{3,1},{4,2},{5,3},{6,4},{7,5},{8,14},{9,15},{10,... | collective-permute-start | bytes 1056776 | tf_op jit(solution)/shard_map/ppermute | solution.py:46
  134.1 14.6 %collective-permute-start.20 = (bf16[1376,128]{1,0:T(8,128)(2,1)S(1)}, bf16[1376,128]{1,0:T(8,128)(2,1)S(1)}, u32[]{:S(2)}, u32[]{:S(2)}) collective-permute-start(bf16[1376,128]{1,0:T(8,128)(2,1)S(1)} %get-tuple-element.61), channel_id=1, source_target_pairs={{0,2},{1,3},{2,4},{3,5},{4,6},{5,7},{6,0},{7,1},{8,10},{9,11},{10,... | collective-permute-start | bytes 1056776 | tf_op jit(solution)/shard_map/ppermute | solution.py:46
  138.7 13.3 %collective-permute-start.18 = (bf16[1376,128]{1,0:T(8,128)(2,1)S(1)}, bf16[1376,128]{1,0:T(8,128)(2,1)S(1)}, u32[]{:S(2)}, u32[]{:S(2)}) collective-permute-start(bf16[1376,128]{1,0:T(8,128)(2,1)S(1)} %sum.6), channel_id=1, source_target_pairs={{0,2},{1,3},{2,4},{3,5},{4,6},{5,7},{6,0},{7,1},{8,10},{9,11},{10,... | collective-permute-start | bytes 1056776 | tf_op jit(solution)/shard_map/ppermute | solution.py:46
  141.3 13.3 %collective-permute-start.22 = (bf16[1376,128]{1,0:T(8,128)(2,1)S(1)}, bf16[1376,128]{1,0:T(8,128)(2,1)S(1)}, u32[]{:S(2)}, u32[]{:S(2)}) collective-permute-start(bf16[1376,128]{1,0:T(8,128)(2,1)S(1)} %sum.7), channel_id=1, source_target_pairs={{0,6},{1,7},{2,0},{3,1},{4,2},{5,3},{6,4},{7,5},{8,14},{9,15},{10,... | collective-permute-start | bytes 1056776 | tf_op jit(solution)/shard_map/ppermute | solution.py:46

commit v10 on v9

--- a/solution.py
+++ b/solution.py
@@ -137,7 +137,7 @@
 
 
 def out_proj_first_kernel(
-    core_ref, mixed_hbm, w_hbm, start_ref, out_ref, w_next, mixed, w_buf, sem
+    core_ref, mixed_hbm, w_hbm, start_hbm, out_ref, w_next, mixed, w_buf, start, sem, start_sem
 ):
     core = core_ref[0]
     copies = []
@@ -149,9 +149,11 @@
     for j in range(N_TP // 2):
         rows = pl.ds(pl.multiple_of((2 * j + 1 - core) * CH, CH), CH)
         later.append(pltpu.make_async_copy(w_hbm.at[rows], w_next.at[j], sem.at[2, j]))
-    for copy in copies + later:
+    start_copy = pltpu.make_async_copy(start_hbm, start, start_sem)
+    for copy in [start_copy] + copies + later:
         copy.start()
-    acc = start_ref[...].astype(F32)
+    start_copy.wait()
+    acc = start[...].astype(F32)
     for j in range(N_TP // 2):
         copies[2 * j].wait()
         copies[2 * j + 1].wait()
@@ -161,10 +163,15 @@
         copy.wait()
 
 
-def out_proj_second_kernel(mixed_ref, w_ref, start_ref, out_ref, keep_ref):
+def out_proj_second_kernel(mixed_hbm, w_ref, start_ref, out_ref, keep_ref, mixed, sem):
+    copies = []
+    for j in range(N_TP // 2):
+        copies.append(pltpu.make_async_copy(mixed_hbm.at[j], mixed.at[j], sem.at[j]))
+        copies[-1].start()
     acc = start_ref[...]
-    for j in range(N_TP // 2):
-        acc = acc + dot(mixed_ref[j], w_ref[j])
+    for j, copy in enumerate(copies):
+        copy.wait()
+        acc = acc + dot(mixed[j], w_ref[j])
     out_ref[...] = acc.astype(BF16)
     keep_ref[...] = acc.astype(BF16)
 
@@ -314,14 +321,16 @@
             jax.ShapeDtypeStruct((ROWS, CH), F32),
             jax.ShapeDtypeStruct((N_TP // 2, CH, CH), BF16),
         ],
-        in_specs=[in_smem(), anywhere(), anywhere(), vmem],
+        in_specs=[in_smem(), anywhere(), anywhere(), anywhere()],
         out_specs=[vmem] * 2,
         scratch_shapes=[
             pltpu.VMEM((N_TP // 2, ROWS, CH), BF16),
             pltpu.VMEM((N_TP // 2, CH, CH), BF16),
+            pltpu.VMEM((ROWS, CH), BF16),
             pltpu.SemaphoreType.DMA((3, N_TP // 2)),
+            pltpu.SemaphoreType.DMA,
         ],
-        compiler_params=params(45),
+        compiler_params=params(43),
         cost_estimate=pl.CostEstimate(
             flops=2 * ROWS * CH * N_TP // 2 * CH, bytes_accessed=9 << 20, transcendentals=0
         ),
@@ -334,8 +343,12 @@
     return pl.pallas_call(
         out_proj_second_kernel,
         out_shape=[jax.ShapeDtypeStruct((ROWS, CH), BF16)] * 2,
-        in_specs=[vmem] * 3,
+        in_specs=[anywhere(), vmem, vmem],
         out_specs=[vmem] * 2,
+        scratch_shapes=[
+            pltpu.VMEM((N_TP // 2, ROWS, CH), BF16),
+            pltpu.SemaphoreType.DMA((N_TP // 2,)),
+        ],
         compiler_params=params(16),
         cost_estimate=pl.CostEstimate(
             flops=2 * ROWS * CH * N_TP // 2 * CH, bytes_accessed=1 << 20, transcendentals=0

time: 156 us -> 158 us (1.013)
  Pallas kernels: 29.3 us -> 31.2 us
    pallas_call x1, Pallas kernels: 1.37 us -> 3.14 us  [out_proj_second(): pl.pallas_call(out_proj_second_kernel, out_shape=[jax.ShapeDtypeStruct((R...]
  transfers between devices with their start and end apart: 25 -> 25, of which waited for: 15 -> 15; matrix products, arithmetic and copies ran while one was open for 0% -> 0% of each run, Pallas kernels for 13% -> 14%
where the time goes in v10:
time: 158 us
  waiting for transfers between devices  71.5 us (45%)
  starting transfers between devices  38.2 us (24%)
  Pallas kernels  31.2 us (20%)
  blocking collectives  12.9 us (8%)
  local copies, waits for them, and re-layouts  3.2 us (2%)
    ppermute x14, waiting for transfers between devices, shift(): return lax.ppermute(arr, AXES, pairs)  25.6 us
    ppermute x14, starting transfers between devices, shift(): return lax.ppermute(arr, AXES, pairs)  13 us
    all_to_all x1, blocking collectives, shards(): conv_rows = lax.all_to_all(conv, 'ctx', 0, 0, tiled=True)  12.9 us
    pallas_call x5, Pallas kernels, mlp_part(): pl.pallas_call(functools.partial(mlp_kernel, slots, split), out_shape=[ja...  11.4 us
    all_to_all x1, waiting for transfers between devices, shards(): lax.all_to_all(copies, 'tp', 0, 0, axis_index_groups=PLANE_GROUPS, tiled=...  11 us
    all_to_all x1, waiting for transfers between devices, shards(): recv = lax.all_to_all(sent, 'ctx', 0, 0, tiled=True)  10.8 us
    all_to_all x1, starting transfers between devices, shards(): recv = lax.all_to_all(sent, 'ctx', 0, 0, tiled=True)  9.5 us
    ppermute x1, waiting for transfers between devices, shards(): lax.ppermute(two_second, AXES, pairs_of(functools.partial(along, -1)))  7.98 us
  transfers between devices with their start and end apart: 25, of which 15 were waited for; matrix products, arithmetic and copies ran while one was open for 0% of the time, Pallas kernels for 14%

profile of v10, /device:TPU:24, one launch (start us, length us, event | category | flops | bytes accessed | tf_op | source)
XLA Modules:
  0.0 157.9 jit_solution(7348935225419058747)
XLA Ops:
  0.6 0.0 copy-start.4
  0.7 2.0 %prep.1 = bf16[16,64,128]{2,1,0:T(8,128)(2,1)} custom-call(bf16[3,128,512]{2,1,0:T(8,128)(2,1)} %bitcast.25, f32[128,512]{1,0:T(8,128)} %filt_ref.1), custom_call_target="tpu_custom_call" | custom-call | tf_op jit(solution)/shard_map/prep/pallas_call | solution.py:450
  2.6 9.5 %all-to-all-start = ((bf16[16,64,128]{2,1,0:T(8,128)(2,1)}), bf16[16,64,128]{2,1,0:T(8,128)(2,1)S(1)}, u32[]{:S(2)}, u32[]{:S(2)}) async-start(bf16[16,64,128]{2,1,0:T(8,128)(2,1)} %prep.1), calls=%async_computation | async-start | bytes 524288 | tf_op jit(solution)/shard_map/all_to_all | solution.py:456
  12.1 0.1 collective-permute-start
  12.2 1.1 collective-permute-done.refs_6_.refs_4_
  13.4 10.8 %all-to-all-done.x_ref = bf16[16,64,128]{2,1,0:T(8,128)(2,1)S(1)} async-done(((bf16[16,64,128]{2,1,0:T(8,128)(2,1)}), bf16[16,64,128]{2,1,0:T(8,128)(2,1)S(1)}, u32[]{:S(2)}, u32[]{:S(2)}) %all-to-all-start) | async-done | bytes 262176 | tf_op jit(solution)/shard_map/all_to_all | solution.py:456
  24.2 1.5 conv.1
  25.6 12.9 %all_to_all.15.conv_ref = bf16[16,32,128]{2,1,0:T(8,128)(2,1)} all-to-all(bf16[16,32,128]{2,1,0:T(8,128)(2,1)S(1)} %conv.1), channel_id=1, replica_groups=mesh['ctx'=16,'tp'=16] {'ctx'}, dimensions={0} | all-to-all | bytes 262144 | tf_op jit(solution)/shard_map/all_to_all | solution.py:469
  38.6 2.2 %mix.1 = bf16[8,128,512]{2,1,0:T(8,128)(2,1)} custom-call(bf16[16,32,128]{2,1,0:T(8,128)(2,1)} %all_to_all.15.conv_ref, bf16[3,128,512]{2,1,0:T(8,128)(2,1)} %bitcast.26, f32[1,512]{1,0:T(1,128)} %bitcast.28), custom_call_target="tpu_custom_call" | custom-call | tf_op jit(solution)/shard_map/mix/pallas_call | solution.py:470
  40.8 7.0 %all-to-all-start.2 = ((bf16[8,128,512]{2,1,0:T(8,128)(2,1)}), bf16[8,128,512]{2,1,0:T(8,128)(2,1)S(1)}, u32[]{:S(2)}, u32[]{:S(2)}) async-start(bf16[8,128,512]{2,1,0:T(8,128)(2,1)} %mix.1), calls=%async_computation.2 | async-start | bytes 2097152 | tf_op jit(solution)/shard_map/all_to_all | solution.py:477
  47.8 0.0 collective-permute-start.2
  47.8 0.5 collective-permute-start.3
  48.3 11.0 %all-to-all-done.2.mixed_hbm = bf16[8,128,512]{2,1,0:T(8,128)(2,1)S(1)} async-done(((bf16[8,128,512]{2,1,0:T(8,128)(2,1)}), bf16[8,128,512]{2,1,0:T(8,128)(2,1)S(1)}, u32[]{:S(2)}, u32[]{:S(2)}) %all-to-all-start.2) | async-done | bytes 1048608 | tf_op jit(solution)/shard_map/all_to_all | solution.py:477
  59.3 0.9 copy-done.5
  60.2 4.2 %out_proj_first.1 = (f32[128,512]{1,0:T(8,128)S(1)}, bf16[8,512,512]{2,1,0:T(8,128)(2,1)S(1)}) custom-call(s32[1]{0:T(128)} %bitcast.3.core_ref, bf16[8,128,512]{2,1,0:T(8,128)(2,1)S(1)} %all-to-all-done.2.mixed_hbm, bf16[8192,512]{1,0:T(8,128)(2,1)} %w_hbm.1, bf16[128,512]{1,0:T(8,128)(2,1)S(1)} %copy-done.5), custom_call_target="tpu_custom_call" | custom-call | flops 536870912 | bytes 9437184 | tf_op jit(solution)/shard_map/out_proj_first/pallas_call | solution.py:318
  64.4 1.0 copy-done.2
  65.4 1.2 copy-done.3
  66.6 3.1 %out_proj_second.1 = (bf16[128,512]{1,0:T(8,128)(2,1)}, bf16[128,512]{1,0:T(8,128)(2,1)S(1)}) custom-call(bf16[8,128,512]{2,1,0:T(8,128)(2,1)S(1)} %copy-done.3, bf16[8,512,512]{2,1,0:T(8,128)(2,1)S(1)} %get-tuple-element.34.w_ref, f32[128,512]{1,0:T(8,128)S(1)} %get-tuple-element.35.start_ref), custom_call_target="tpu_custom_call" | custom-call | flops 536870912 | bytes 1048576 | tf_op jit(solution)/shard_map/out_proj_second/pallas_call | solution.py:343
  69.8 1.0 collective-permute-start.5
  70.8 0.7 collective-permute-start.4
  71.4 1.8 %collective-permute-done.5.first_ref = bf16[128,512]{1,0:T(8,128)(2,1)S(1)} collective-permute-done((bf16[128,512]{1,0:T(8,128)(2,1)S(1)}, bf16[128,512]{1,0:T(8,128)(2,1)S(1)}, u32[]{:S(2)}, u32[]{:S(2)}) %collective-permute-start.5) | collective-permute-done | bytes 131104 | tf_op jit(solution)/shard_map/ppermute | solution.py:486
  73.3 0.0 collective-permute-done.4.second_ref
  73.3 0.5 collective-permute-start.8
  73.8 3.8 %collective-permute-start.9 = (bf16[2,128,512]{2,1,0:T(8,128)(2,1)S(1)}, bf16[2,128,512]{2,1,0:T(8,128)(2,1)}, u32[]{:S(2)}, u32[]{:S(2)}) collective-permute-start(bf16[2,128,512]{2,1,0:T(8,128)(2,1)S(1)} %hold.1.refs_0_), channel_id=1, source_target_pairs={{0,192},{1,193},{2,194},{3,195},{4,196},{5,197},{6,198},{7,199},{8... | collective-permute-start | bytes 786440 | tf_op jit(solution)/shard_map/ppermute | solution.py:495
  77.5 0.1 stack.35
  77.6 0.1 collective-permute-start.7
  77.7 0.0 collective-permute-start.6
  77.7 4.6 %collective-permute-done.8.refs_3_ = bf16[2,128,512]{2,1,0:T(8,128)(2,1)S(1)} collective-permute-done((bf16[2,128,512]{2,1,0:T(8,128)(2,1)S(1)}, bf16[2,128,512]{2,1,0:T(8,128)(2,1)S(1)}, u32[]{:S(2)}, u32[]{:S(2)}) %collective-permute-start.8) | collective-permute-done | bytes 262176 | tf_op jit(solution)/shard_map/ppermute | solution.py:494
  82.4 1.2 collective-permute-start.10
  83.6 4.6 %collective-permute-done.9.refs_4_ = bf16[2,128,512]{2,1,0:T(8,128)(2,1)} collective-permute-done((bf16[2,128,512]{2,1,0:T(8,128)(2,1)S(1)}, bf16[2,128,512]{2,1,0:T(8,128)(2,1)}, u32[]{:S(2)}, u32[]{:S(2)}) %collective-permute-start.9) | collective-permute-done | bytes 262176 | tf_op jit(solution)/shard_map/ppermute | solution.py:495
  88.2 1.4 collective-permute-start.11
  89.6 2.7 %load.1 = (bf16[1368,1024]{1,0:T(8,128)(2,1)S(1)}, bf16[1368,1024]{1,0:T(8,128)(2,1)S(1)}, bf16[16,512]{1,0:T(8,128)(2,1)}) custom-call(bf16[1368,512]{1,0:T(8,128)(2,1)S(1)} %bitcast.19, bf16[1368,512]{1,0:T(8,128)(2,1)} %collective-permute-done.2.wgx_ref, bf16[1368,512]{1,0:T(8,128)(2,1)S(1)} %bitcast.21, ...), custom_call_target="tpu_custom_call" | custom-call | flops 1 | bytes 12582912 | tf_op jit(solution)/shard_map/load/pallas_call | solution.py:375
  92.3 5.0 %collective-permute-done.7.refs_2_ = bf16[2,128,512]{2,1,0:T(8,128)(2,1)S(1)} collective-permute-done((bf16[2,128,512]{2,1,0:T(8,128)(2,1)S(1)}, bf16[2,128,512]{2,1,0:T(8,128)(2,1)S(1)}, u32[]{:S(2)}, u32[]{:S(2)}) %collective-permute-start.7) | collective-permute-done | bytes 262176 | tf_op jit(solution)/shard_map/ppermute | solution.py:497
  97.3 0.0 collective-permute-done.6.refs_1_
  97.3 1.8 %scale.2 = (bf16[5,128,1024]{2,1,0:T(8,128)(2,1)S(1)}, f32[5,8,128]{2,1,0:T(8,128)S(1)}) custom-call(bf16[2,128,512]{2,1,0:T(8,128)(2,1)S(1)} %hold.1.refs_0_, bf16[2,128,512]{2,1,0:T(8,128)(2,1)S(1)} %collective-permute-done.6.refs_1_, bf16[2,128,512]{2,1,0:T(8,128)(2,1)S(1)} %collective-permute-done.7.refs_2_, ...), custom_call_target="tpu_custom_call" | custom-call | flops 20971520 | bytes 2621440 | tf_op jit(solution)/shard_map/scale/pallas_call | solution.py:390
  99.1 8.0 %collective-permute-done.11.refs_1_ = bf16[2,128,512]{2,1,0:T(8,128)(2,1)S(1)} collective-permute-done((bf16[2,128,512]{2,1,0:T(8,128)(2,1)}, bf16[2,128,512]{2,1,0:T(8,128)(2,1)S(1)}, u32[]{:S(2)}, u32[]{:S(2)}) %collective-permute-start.11) | collective-permute-done | bytes 262176 | tf_op jit(solution)/shard_map/ppermute | solution.py:499
  107.1 0.6 scale.3
  107.6 2.2 %mlp.5 = (bf16[2,1376,128]{2,1,0:T(8,128)(2,1)S(1)}, s32[8]{0:T(128)S(1)}) custom-call(s32[8]{0:T(128)S(1)} %fusion.5.idx_ref, bf16[5,128,1024]{2,1,0:T(8,128)(2,1)S(1)} %get-tuple-element.40.refs_0_, f32[5,8,128]{2,1,0:T(8,128)S(1)} %get-tuple-element.41.refs_1_, bf16[3,128,1024]{2,1,0:T(8,128)(2,1)S(1)} %get-tuple-element.42.refs_2_, ...), custom_call_target="tpu_custom_call" | custom-call | flops 100000000 | bytes 524288 | tf_op jit(solution)/shard_map/mlp/pallas_call | solution.py:408
  109.9 1.4 collective-permute-start.16
  111.3 2.3 %mlp.6 = (bf16[2,1376,128]{2,1,0:T(8,128)(2,1)S(1)}, bf16[2,1376,128]{2,1,0:T(8,128)(2,1)S(1)}, s32[8]{0:T(128)S(1)}) custom-call(s32[8]{0:T(128)S(1)} %get-tuple-element.48.idx_ref, bf16[5,128,1024]{2,1,0:T(8,128)(2,1)S(1)} %get-tuple-element.40.refs_0_, f32[5,8,128]{2,1,0:T(8,128)S(1)} %get-tuple-element.41.refs_1_, ...), custom_call_target="tpu_custom_call" | custom-call | flops 100000000 | bytes 524288 | tf_op jit(solution)/shard_map/mlp/pallas_call | solution.py:408
  113.6 1.8 %collective-permute-start.13 = (bf16[2,1376,128]{2,1,0:T(8,128)(2,1)S(1)}, bf16[2,1376,128]{2,1,0:T(8,128)(2,1)S(1)}, u32[]{:S(2)}, u32[]{:S(2)}) collective-permute-start(bf16[2,1376,128]{2,1,0:T(8,128)(2,1)S(1)} %get-tuple-element.54), channel_id=1, source_target_pairs={{0,2},{1,3},{2,4},{3,5},{4,6},{5,7},{6,0},{7,1},{8,10},{9,11},{10,... | collective-permute-start | bytes 2113544 | tf_op jit(solution)/shard_map/ppermute | solution.py:46
  115.5 0.3 collective-permute-start.14
  115.7 2.3 %mlp.7 = (bf16[1376,128]{1,0:T(8,128)(2,1)S(1)}, bf16[1376,128]{1,0:T(8,128)(2,1)S(1)}, bf16[1376,128]{1,0:T(8,128)(2,1)S(1)}, bf16[1376,128]{1,0:T(8,128)(2,1)S(1)}, s32[8]{0:T(128)S(1)}) custom-call(s32[8]{0:T(128)S(1)} %get-tuple-element.49.idx_ref, bf16[5,128,1024]{2,1,0:T(8,128)(2,1)S(1)} %get-tuple-element.40.refs_0_, ...), custom_call_target="tpu_custom_call" | custom-call | flops 100000000 | bytes 524288 | tf_op jit(solution)/shard_map/mlp/pallas_call | solution.py:408
  118.0 2.3 %mlp.8 = (bf16[2,1376,128]{2,1,0:T(8,128)(2,1)S(1)}, bf16[2,1376,128]{2,1,0:T(8,128)(2,1)S(1)}, s32[8]{0:T(128)S(1)}) custom-call(s32[8]{0:T(128)S(1)} %get-tuple-element.50.idx_ref, bf16[5,128,1024]{2,1,0:T(8,128)(2,1)S(1)} %get-tuple-element.40.refs_0_, f32[5,8,128]{2,1,0:T(8,128)S(1)} %get-tuple-element.41.refs_1_, ...), custom_call_target="tpu_custom_call" | custom-call | flops 100000000 | bytes 524288 | tf_op jit(solution)/shard_map/mlp/pallas_call | solution.py:408
  120.3 8.9 %collective-permute-done.16.right_ref = bf16[2,1376,128]{2,1,0:T(8,128)(2,1)S(1)} collective-permute-done((bf16[2,1376,128]{2,1,0:T(8,128)(2,1)S(1)}, bf16[2,1376,128]{2,1,0:T(8,128)(2,1)S(1)}, u32[]{:S(2)}, u32[]{:S(2)}) %collective-permute-start.16) | collective-permute-done | bytes 704544 | tf_op jit(solution)/shard_map/ppermute | solution.py:46
  129.3 0.2 sum.5
  129.4 1.4 collective-permute-start.17
  130.8 0.7 collective-permute-start.21
  131.5 2.6 %collective-permute-done.14.refs_2_ = bf16[2,1376,128]{2,1,0:T(8,128)(2,1)S(1)} collective-permute-done((bf16[2,1376,128]{2,1,0:T(8,128)(2,1)S(1)}, bf16[2,1376,128]{2,1,0:T(8,128)(2,1)S(1)}, u32[]{:S(2)}, u32[]{:S(2)}) %collective-permute-start.14) | collective-permute-done | bytes 704544 | tf_op jit(solution)/shard_map/ppermute | solution.py:46
  134.1 0.3 sum.4
  134.4 1.8 %collective-permute-start.15 = (bf16[2,1376,128]{2,1,0:T(8,128)(2,1)S(1)}, bf16[2,1376,128]{2,1,0:T(8,128)(2,1)S(1)}, u32[]{:S(2)}, u32[]{:S(2)}) collective-permute-start(bf16[2,1376,128]{2,1,0:T(8,128)(2,1)S(1)} %sum.4), channel_id=1, source_target_pairs={{0,8},{1,9},{2,10},{3,11},{4,12},{5,13},{6,14},{7,15},{8,0},{9,1},... | collective-permute-start | bytes 2113544 | tf_op jit(solution)/shard_map/ppermute | solution.py:46
  136.2 0.0 collective-permute-start.19
  136.2 3.2 %collective-permute-start.20 = (bf16[1376,128]{1,0:T(8,128)(2,1)S(1)}, bf16[1376,128]{1,0:T(8,128)(2,1)S(1)}, u32[]{:S(2)}, u32[]{:S(2)}) collective-permute-start(bf16[1376,128]{1,0:T(8,128)(2,1)S(1)} %get-tuple-element.61), channel_id=1, source_target_pairs={{0,2},{1,3},{2,4},{3,5},{4,6},{5,7},{6,0},{7,1},{8,10},{9,11},{10,... | collective-permute-start | bytes 1056776 | tf_op jit(solution)/shard_map/ppermute | solution.py:46
  139.4 1.3 collective-permute-done.17.refs_1_
  140.7 0.1 sum.6
  140.8 1.7 %collective-permute-start.18 = (bf16[1376,128]{1,0:T(8,128)(2,1)S(1)}, bf16[1376,128]{1,0:T(8,128)(2,1)S(1)}, u32[]{:S(2)}, u32[]{:S(2)}) collective-permute-start(bf16[1376,128]{1,0:T(8,128)(2,1)S(1)} %sum.6), channel_id=1, source_target_pairs={{0,2},{1,3},{2,4},{3,5},{4,6},{5,7},{6,0},{7,1},{8,10},{9,11},{10,... | collective-permute-start | bytes 1056776 | tf_op jit(solution)/shard_map/ppermute | solution.py:46
  142.5 0.7 collective-permute-done.21.refs_1_
  143.2 0.1 sum.7
  143.3 0.1 collective-permute-start.22
  143.4 2.2 %mlp.9 = (bf16[2,1376,128]{2,1,0:T(8,128)(2,1)S(1)}, s32[8]{0:T(128)}) custom-call(s32[8]{0:T(128)S(1)} %get-tuple-element.51.idx_ref, bf16[5,128,1024]{2,1,0:T(8,128)(2,1)S(1)} %get-tuple-element.40.refs_0_, f32[5,8,128]{2,1,0:T(8,128)S(1)} %get-tuple-element.41.refs_1_, bf16[3,128,1024]{2,1,0:T(8,128)(2,1)S(1)} %get-tuple-element.42.refs_2_, ...), custom_call_target="tpu_custom_call" | custom-call | flops 100000000 | bytes 524288 | tf_op jit(solution)/shard_map/mlp/pallas_call | solution.py:408
  145.6 5.1 %collective-permute-done.19.gate_3_ref = bf16[1376,128]{1,0:T(8,128)(2,1)S(1)} collective-permute-done((bf16[1376,128]{1,0:T(8,128)(2,1)S(1)}, bf16[1376,128]{1,0:T(8,128)(2,1)S(1)}, u32[]{:S(2)}, u32[]{:S(2)}) %collective-permute-start.19) | collective-permute-done | bytes 352288 | tf_op jit(solution)/shard_map/ppermute | solution.py:46
  150.8 3.3 %collective-permute-done.18.gate_1_ref = bf16[1376,128]{1,0:T(8,128)(2,1)S(1)} collective-permute-done((bf16[1376,128]{1,0:T(8,128)(2,1)S(1)}, bf16[1376,128]{1,0:T(8,128)(2,1)S(1)}, u32[]{:S(2)}, u32[]{:S(2)}) %collective-permute-start.18) | collective-permute-done | bytes 352288 | tf_op jit(solution)/shard_map/ppermute | solution.py:46
  154.0 2.5 %collective-permute-done.22.up_3_ref = bf16[1376,128]{1,0:T(8,128)(2,1)S(1)} collective-permute-done((bf16[1376,128]{1,0:T(8,128)(2,1)S(1)}, bf16[1376,128]{1,0:T(8,128)(2,1)S(1)}, u32[]{:S(2)}, u32[]{:S(2)}) %collective-permute-start.22) | collective-permute-done | bytes 352288 | tf_op jit(solution)/shard_map/ppermute | solution.py:46
  156.6 1.3 finish.1
  (23 shorter events, 0.1 us)
Async XLA Ops:
  0.6 23.5 %copy-start.4 = (bf16[128,1024]{1,0:T(8,128)(2,1)S(1)}, bf16[128,1024]{1,0:T(8,128)(2,1)}, u32[]{:S(2)}) copy-start(bf16[128,1024]{1,0:T(8,128)(2,1)} %constant.165.clone.tab_ref) | copy-start | bytes 786436
  0.6 11.5 %copy-start.6 = (f32[512]{0:T(512)S(1)}, f32[512]{0:T(512)}, u32[]{:S(2)}) copy-start(f32[512]{0:T(512)} %param.14) | copy-start | bytes 6148
  2.6 21.5 %all-to-all-start = ((bf16[16,64,128]{2,1,0:T(8,128)(2,1)}), bf16[16,64,128]{2,1,0:T(8,128)(2,1)S(1)}, u32[]{:S(2)}, u32[]{:S(2)}) async-start(bf16[16,64,128]{2,1,0:T(8,128)(2,1)} %prep.1), calls=%async_computation | async-start | bytes 524288 | tf_op jit(solution)/shard_map/all_to_all | solution.py:456
  12.1 1.2 collective-permute-start
  40.8 7.0 %copy-start = (bf16[512,1368]{0,1:T(8,128)(2,1)S(1)}, bf16[512,1368]{0,1:T(8,128)(2,1)}, u32[]{:S(2)}) copy-start(bf16[512,1368]{0,1:T(8,128)(2,1)} %param.15) | copy-start | bytes 4202500
  40.8 18.5 %all-to-all-start.2 = ((bf16[8,128,512]{2,1,0:T(8,128)(2,1)}), bf16[8,128,512]{2,1,0:T(8,128)(2,1)S(1)}, u32[]{:S(2)}, u32[]{:S(2)}) async-start(bf16[8,128,512]{2,1,0:T(8,128)(2,1)} %mix.1), calls=%async_computation.2 | async-start | bytes 2097152 | tf_op jit(solution)/shard_map/all_to_all | solution.py:477
  47.8 22.0 %collective-permute-start.2 = (bf16[1368,512]{1,0:T(8,128)(2,1)S(1)}, bf16[1368,512]{1,0:T(8,128)(2,1)}, u32[]{:S(2)}, u32[]{:S(2)}) collective-permute-start(bf16[1368,512]{1,0:T(8,128)(2,1)S(1)} %bitcast.18), channel_id=1, source_target_pairs={{0,1},{1,0},{2,3},{3,2},{4,5},{5,4},{6,7},{7,6},{8,9},{9,8},{10,11... | collective-permute-start | bytes 4202504 | tf_op jit(solution)/shard_map/ppermute | solution.py:46
  47.8 22.0 %collective-permute-start.3 = (bf16[1368,512]{1,0:T(8,128)(2,1)}, bf16[1368,512]{1,0:T(8,128)(2,1)}, u32[]{:S(2)}, u32[]{:S(2)}) collective-permute-start(bf16[1368,512]{1,0:T(8,128)(2,1)} %bitcast.20), channel_id=1, source_target_pairs={{0,1},{1,0},{2,3},{3,2},{4,5},{5,4},{6,7},{7,6},{8,9},{9,8},{10,11... | collective-permute-start | bytes 4202504 | tf_op jit(solution)/shard_map/ppermute | solution.py:46
  59.3 5.1 %collective-permute-start.1 = (bf16[8,128,512]{2,1,0:T(8,128)(2,1)S(1)}, bf16[8,128,512]{2,1,0:T(8,128)(2,1)S(1)}, u32[]{:S(2)}, u32[]{:S(2)}) collective-permute-start(bf16[8,128,512]{2,1,0:T(8,128)(2,1)S(1)} %all-to-all-done.2.mixed_hbm), channel_id=1, source_target_pairs={{0,1},{1,0},{2,3},{3,2},{4,5},{5,4},{6,7},{7,6},{8,9},{9,8},{10,11... | collective-permute-start | bytes 3145736 | tf_op jit(solution)/shard_map/ppermute | solution.py:46
  59.3 0.9 copy-start.5
  64.4 1.0 copy-start.2
  65.4 1.2 copy-start.3
  66.6 23.0 %copy-start.1 = (bf16[512,1368]{0,1:T(8,128)(2,1)S(1)}, bf16[512,1368]{0,1:T(8,128)(2,1)}, u32[]{:S(2)}) copy-start(bf16[512,1368]{0,1:T(8,128)(2,1)} %param.16) | copy-start | bytes 4202500
  69.8 3.5 %collective-permute-start.5 = (bf16[128,512]{1,0:T(8,128)(2,1)S(1)}, bf16[128,512]{1,0:T(8,128)(2,1)S(1)}, u32[]{:S(2)}, u32[]{:S(2)}) collective-permute-start(bf16[128,512]{1,0:T(8,128)(2,1)S(1)} %get-tuple-element.38.stream_ref), channel_id=1, source_target_pairs={{0,16},{1,0},{2,18},{3,2},{4,20},{5,4},{6,22},{7,6},{8,24},{9,8},{... | collective-permute-start | bytes 393224 | tf_op jit(solution)/shard_map/ppermute | solution.py:486
  70.8 2.5 %collective-permute-start.4 = (bf16[128,512]{1,0:T(8,128)(2,1)S(1)}, bf16[128,512]{1,0:T(8,128)(2,1)S(1)}, u32[]{:S(2)}, u32[]{:S(2)}) collective-permute-start(bf16[128,512]{1,0:T(8,128)(2,1)S(1)} %get-tuple-element.38.stream_ref), channel_id=1, source_target_pairs={{1,16},{3,18},{5,20},{7,22},{9,24},{11,26},{13,28},{15,30},{16,1},... | collective-permute-start | bytes 393224 | tf_op jit(solution)/shard_map/ppermute | solution.py:487
  73.3 9.1 %collective-permute-start.8 = (bf16[2,128,512]{2,1,0:T(8,128)(2,1)S(1)}, bf16[2,128,512]{2,1,0:T(8,128)(2,1)S(1)}, u32[]{:S(2)}, u32[]{:S(2)}) collective-permute-start(bf16[2,128,512]{2,1,0:T(8,128)(2,1)S(1)} %hold.1.refs_0_), channel_id=1, source_target_pairs={{0,64},{1,65},{2,66},{3,67},{4,68},{5,69},{6,70},{7,71},{8,72},{9,... | collective-permute-start | bytes 786440 | tf_op jit(solution)/shard_map/ppermute | solution.py:494
  73.8 14.4 %collective-permute-start.9 = (bf16[2,128,512]{2,1,0:T(8,128)(2,1)S(1)}, bf16[2,128,512]{2,1,0:T(8,128)(2,1)}, u32[]{:S(2)}, u32[]{:S(2)}) collective-permute-start(bf16[2,128,512]{2,1,0:T(8,128)(2,1)S(1)} %hold.1.refs_0_), channel_id=1, source_target_pairs={{0,192},{1,193},{2,194},{3,195},{4,196},{5,197},{6,198},{7,199},{8... | collective-permute-start | bytes 786440 | tf_op jit(solution)/shard_map/ppermute | solution.py:495
  77.6 19.7 %collective-permute-start.7 = (bf16[2,128,512]{2,1,0:T(8,128)(2,1)S(1)}, bf16[2,128,512]{2,1,0:T(8,128)(2,1)S(1)}, u32[]{:S(2)}, u32[]{:S(2)}) collective-permute-start(bf16[2,128,512]{2,1,0:T(8,128)(2,1)S(1)} %hold.1.refs_0_), channel_id=1, source_target_pairs={{0,224},{1,225},{2,226},{3,227},{4,228},{5,229},{6,230},{7,231},{8... | collective-permute-start | bytes 786440 | tf_op jit(solution)/shard_map/ppermute | solution.py:497
  77.7 19.6 %collective-permute-start.6 = (bf16[2,128,512]{2,1,0:T(8,128)(2,1)S(1)}, bf16[2,128,512]{2,1,0:T(8,128)(2,1)S(1)}, u32[]{:S(2)}, u32[]{:S(2)}) collective-permute-start(bf16[2,128,512]{2,1,0:T(8,128)(2,1)S(1)} %hold.1.refs_0_), channel_id=1, source_target_pairs={{0,32},{1,33},{2,34},{3,35},{4,36},{5,37},{6,38},{7,39},{8,40},{9,... | collective-permute-start | bytes 786440 | tf_op jit(solution)/shard_map/ppermute | solution.py:496
  82.4 24.7 %collective-permute-start.12 = (bf16[2,128,512]{2,1,0:T(8,128)(2,1)S(1)}, bf16[2,128,512]{2,1,0:T(8,128)(2,1)S(1)}, u32[]{:S(2)}, u32[]{:S(2)}) collective-permute-start(bf16[2,128,512]{2,1,0:T(8,128)(2,1)S(1)} %collective-permute-done.8.refs_3_), channel_id=1, source_target_pairs={{0,64},{1,65},{2,66},{3,67},{4,68},{5,69},{6,70},{7,71},{8,72},{9,... | collective-permute-start | bytes 786440 | tf_op jit(solution)/shard_map/ppermute | solution.py:500
  82.4 24.7 %collective-permute-start.10 = (bf16[2,128,512]{2,1,0:T(8,128)(2,1)S(1)}, bf16[2,128,512]{2,1,0:T(8,128)(2,1)S(1)}, u32[]{:S(2)}, u32[]{:S(2)}) collective-permute-start(bf16[2,128,512]{2,1,0:T(8,128)(2,1)S(1)} %collective-permute-done.8.refs_3_), channel_id=1, source_target_pairs={{0,32},{1,33},{2,34},{3,35},{4,36},{5,37},{6,38},{7,39},{8,40},{9,... | collective-permute-start | bytes 786440 | tf_op jit(solution)/shard_map/ppermute | solution.py:498
  88.2 18.9 %collective-permute-start.11 = (bf16[2,128,512]{2,1,0:T(8,128)(2,1)}, bf16[2,128,512]{2,1,0:T(8,128)(2,1)S(1)}, u32[]{:S(2)}, u32[]{:S(2)}) collective-permute-start(bf16[2,128,512]{2,1,0:T(8,128)(2,1)} %collective-permute-done.9.refs_4_), channel_id=1, source_target_pairs={{0,224},{1,225},{2,226},{3,227},{4,228},{5,229},{6,230},{7,231},{8... | collective-permute-start | bytes 786440 | tf_op jit(solution)/shard_map/ppermute | solution.py:499
  109.9 19.4 %collective-permute-start.16 = (bf16[2,1376,128]{2,1,0:T(8,128)(2,1)S(1)}, bf16[2,1376,128]{2,1,0:T(8,128)(2,1)S(1)}, u32[]{:S(2)}, u32[]{:S(2)}) collective-permute-start(bf16[2,1376,128]{2,1,0:T(8,128)(2,1)S(1)} %get-tuple-element.58), channel_id=1, source_target_pairs={{0,8},{1,9},{2,10},{3,11},{4,12},{5,13},{6,14},{7,15},{8,0},{9,1},... | collective-permute-start | bytes 2113544 | tf_op jit(solution)/shard_map/ppermute | solution.py:46
  113.6 17.9 %collective-permute-start.13 = (bf16[2,1376,128]{2,1,0:T(8,128)(2,1)S(1)}, bf16[2,1376,128]{2,1,0:T(8,128)(2,1)S(1)}, u32[]{:S(2)}, u32[]{:S(2)}) collective-permute-start(bf16[2,1376,128]{2,1,0:T(8,128)(2,1)S(1)} %get-tuple-element.54), channel_id=1, source_target_pairs={{0,2},{1,3},{2,4},{3,5},{4,6},{5,7},{6,0},{7,1},{8,10},{9,11},{10,... | collective-permute-start | bytes 2113544 | tf_op jit(solution)/shard_map/ppermute | solution.py:46
  115.5 18.7 %collective-permute-start.14 = (bf16[2,1376,128]{2,1,0:T(8,128)(2,1)S(1)}, bf16[2,1376,128]{2,1,0:T(8,128)(2,1)S(1)}, u32[]{:S(2)}, u32[]{:S(2)}) collective-permute-start(bf16[2,1376,128]{2,1,0:T(8,128)(2,1)S(1)} %get-tuple-element.55), channel_id=1, source_target_pairs={{0,6},{1,7},{2,0},{3,1},{4,2},{5,3},{6,4},{7,5},{8,14},{9,15},{10,... | collective-permute-start | bytes 2113544 | tf_op jit(solution)/shard_map/ppermute | solution.py:46
  129.4 11.3 %collective-permute-start.17 = (bf16[1376,128]{1,0:T(8,128)(2,1)S(1)}, bf16[1376,128]{1,0:T(8,128)(2,1)S(1)}, u32[]{:S(2)}, u32[]{:S(2)}) collective-permute-start(bf16[1376,128]{1,0:T(8,128)(2,1)S(1)} %get-tuple-element.59), channel_id=1, source_target_pairs={{0,2},{1,3},{2,4},{3,5},{4,6},{5,7},{6,0},{7,1},{8,10},{9,11},{10,... | collective-permute-start | bytes 1056776 | tf_op jit(solution)/shard_map/ppermute | solution.py:46
  130.8 12.4 %collective-permute-start.21 = (bf16[1376,128]{1,0:T(8,128)(2,1)S(1)}, bf16[1376,128]{1,0:T(8,128)(2,1)S(1)}, u32[]{:S(2)}, u32[]{:S(2)}) collective-permute-start(bf16[1376,128]{1,0:T(8,128)(2,1)S(1)} %get-tuple-element.63), channel_id=1, source_target_pairs={{0,6},{1,7},{2,0},{3,1},{4,2},{5,3},{6,4},{7,5},{8,14},{9,15},{10,... | collective-permute-start | bytes 1056776 | tf_op jit(solution)/shard_map/ppermute | solution.py:46
  134.4 22.2 %collective-permute-start.15 = (bf16[2,1376,128]{2,1,0:T(8,128)(2,1)S(1)}, bf16[2,1376,128]{2,1,0:T(8,128)(2,1)S(1)}, u32[]{:S(2)}, u32[]{:S(2)}) collective-permute-start(bf16[2,1376,128]{2,1,0:T(8,128)(2,1)S(1)} %sum.4), channel_id=1, source_target_pairs={{0,8},{1,9},{2,10},{3,11},{4,12},{5,13},{6,14},{7,15},{8,0},{9,1},... | collective-permute-start | bytes 2113544 | tf_op jit(solution)/shard_map/ppermute | solution.py:46
  136.2 14.6 %collective-permute-start.19 = (bf16[1376,128]{1,0:T(8,128)(2,1)S(1)}, bf16[1376,128]{1,0:T(8,128)(2,1)S(1)}, u32[]{:S(2)}, u32[]{:S(2)}) collective-permute-start(bf16[1376,128]{1,0:T(8,128)(2,1)S(1)} %get-tuple-element.60), channel_id=1, source_target_pairs={{0,6},{1,7},{2,0},{3,1},{4,2},{5,3},{6,4},{7,5},{8,14},{9,15},{10,... | collective-permute-start | bytes 1056776 | tf_op jit(solution)/shard_map/ppermute | solution.py:46
  136.2 14.6 %collective-permute-start.20 = (bf16[1376,128]{1,0:T(8,128)(2,1)S(1)}, bf16[1376,128]{1,0:T(8,128)(2,1)S(1)}, u32[]{:S(2)}, u32[]{:S(2)}) collective-permute-start(bf16[1376,128]{1,0:T(8,128)(2,1)S(1)} %get-tuple-element.61), channel_id=1, source_target_pairs={{0,2},{1,3},{2,4},{3,5},{4,6},{5,7},{6,0},{7,1},{8,10},{9,11},{10,... | collective-permute-start | bytes 1056776 | tf_op jit(solution)/shard_map/ppermute | solution.py:46
  140.8 13.3 %collective-permute-start.18 = (bf16[1376,128]{1,0:T(8,128)(2,1)S(1)}, bf16[1376,128]{1,0:T(8,128)(2,1)S(1)}, u32[]{:S(2)}, u32[]{:S(2)}) collective-permute-start(bf16[1376,128]{1,0:T(8,128)(2,1)S(1)} %sum.6), channel_id=1, source_target_pairs={{0,2},{1,3},{2,4},{3,5},{4,6},{5,7},{6,0},{7,1},{8,10},{9,11},{10,... | collective-permute-start | bytes 1056776 | tf_op jit(solution)/shard_map/ppermute | solution.py:46
  143.3 13.3 %collective-permute-start.22 = (bf16[1376,128]{1,0:T(8,128)(2,1)S(1)}, bf16[1376,128]{1,0:T(8,128)(2,1)S(1)}, u32[]{:S(2)}, u32[]{:S(2)}) collective-permute-start(bf16[1376,128]{1,0:T(8,128)(2,1)S(1)} %sum.7), channel_id=1, source_target_pairs={{0,6},{1,7},{2,0},{3,1},{4,2},{5,3},{6,4},{7,5},{8,14},{9,15},{10,... | collective-permute-start | bytes 1056776 | tf_op jit(solution)/shard_map/ppermute | solution.py:46

commit v11 on v8

--- a/solution.py
+++ b/solution.py
@@ -417,7 +417,7 @@
         name="prep",
     )(feat, filters)
     recv = lax.all_to_all(sent, "ctx", 0, 0, tiled=True)
-    recv, wg_oth, wu_oth, gain_oth = lax.optimization_barrier((recv, wg_oth, wu_oth, gain_oth))
+    recv, gain_oth = lax.optimization_barrier((recv, gain_oth))
     conv = pl.pallas_call(
         conv_kernel,
         out_shape=jax.ShapeDtypeStruct((N_CTX, SUB, ROWS), BF16),
@@ -445,6 +445,7 @@
     (half,) = out_proj(0, core_arr, mixed, w_out, residual, F32, 1)
     stream_out, stream = out_proj(1, core_arr, mixed_oth, w_out, half, BF16, 2)
 
+    stream, wg_oth, wu_oth = lax.optimization_barrier((stream, wg_oth, wu_oth))
     first = lax.ppermute(stream, AXES, pairs_of(to_row_owner_first))
     second = lax.ppermute(stream, AXES, pairs_of(to_row_owner_second))
     here = (x_lo == core).astype(jnp.int32)[None]

time: 158 us -> 158 us (level)
  blocking collectives: 32.3 us -> 12.9 us
  waiting for transfers between devices: 56.4 us -> 71.5 us
  starting transfers between devices: 34.4 us -> 38.1 us
    all_to_all x1 -> x0, blocking collectives: 19.4 us -> none  [shards(): lax.all_to_all(copies, 'tp', 0, 0, axis_index_groups=PLANE_GROUPS, tiled=...]
    all_to_all x0 -> x1, waiting for transfers between devices: none -> 11 us  [shards(): lax.all_to_all(copies, 'tp', 0, 0, axis_index_groups=PLANE_GROUPS, tiled=...]
    all_to_all x0 -> x1, starting transfers between devices: none -> 6.99 us  [shards(): lax.all_to_all(copies, 'tp', 0, 0, axis_index_groups=PLANE_GROUPS, tiled=...]
    ppermute x14, starting transfers between devices: 16.4 us -> 13 us  [shift(): return lax.ppermute(arr, AXES, pairs)]
    ppermute x14, waiting for transfers between devices: 24.1 us -> 25.7 us  [shift(): return lax.ppermute(arr, AXES, pairs)]
    unnamed x18 -> x14, local copies, waits for them, and re-layouts: 3.86 us -> 3.1 us
  transfers between devices with their start and end apart: 24 -> 25, of which waited for: 13 -> 15; matrix products, arithmetic and copies ran while one was open for 0% -> 0% of each run, Pallas kernels for 11% -> 13%
where the time goes in v11:
time: 158 us; the launch traced here: 157 us
  waiting for transfers between devices  71.5 us (45%)
  starting transfers between devices  38.1 us (24%)
  Pallas kernels  30.4 us (19%)
  blocking collectives  12.9 us (8%)
  local copies, waits for them, and re-layouts  3.19 us (2%)
    ppermute x14, waiting for transfers between devices, shift(): return lax.ppermute(arr, AXES, pairs)  25.7 us
    ppermute x14, starting transfers between devices, shift(): return lax.ppermute(arr, AXES, pairs)  13 us
    all_to_all x1, blocking collectives, shards(): conv_rows = lax.all_to_all(conv, 'ctx', 0, 0, tiled=True)  12.9 us
    pallas_call x5, Pallas kernels, mlp_part(): pl.pallas_call(functools.partial(mlp_kernel, slots, split), out_shape=[ja...  11.4 us
    all_to_all x1, waiting for transfers between devices, shards(): lax.all_to_all(copies, 'tp', 0, 0, axis_index_groups=PLANE_GROUPS, tiled=...  11 us
    all_to_all x1, waiting for transfers between devices, shards(): recv = lax.all_to_all(sent, 'ctx', 0, 0, tiled=True)  10.8 us
    all_to_all x1, starting transfers between devices, shards(): recv = lax.all_to_all(sent, 'ctx', 0, 0, tiled=True)  9.5 us
    ppermute x1, waiting for transfers between devices, shards(): lax.ppermute(two_second, AXES, pairs_of(functools.partial(along, -1)))  7.98 us
  transfers between devices with their start and end apart: 25, of which 15 were waited for; matrix products, arithmetic and copies ran while one was open for 0% of the time, Pallas kernels for 13%

profile of v11, /device:TPU:24, one launch (start us, length us, event | category | flops | bytes accessed | tf_op | source)
XLA Modules:
  0.0 157.1 jit_solution(16425099903251750509)
XLA Ops:
  0.6 0.0 copy-start.4
  0.7 2.0 %prep.1 = bf16[16,64,128]{2,1,0:T(8,128)(2,1)} custom-call(bf16[3,128,512]{2,1,0:T(8,128)(2,1)} %bitcast.25, f32[128,512]{1,0:T(8,128)} %filt_ref.1), custom_call_target="tpu_custom_call" | custom-call | tf_op jit(solution)/shard_map/prep/pallas_call | solution.py:413
  2.6 9.5 %all-to-all-start = ((bf16[16,64,128]{2,1,0:T(8,128)(2,1)}), bf16[16,64,128]{2,1,0:T(8,128)(2,1)S(1)}, u32[]{:S(2)}, u32[]{:S(2)}) async-start(bf16[16,64,128]{2,1,0:T(8,128)(2,1)} %prep.1), calls=%async_computation | async-start | bytes 524288 | tf_op jit(solution)/shard_map/all_to_all | solution.py:419
  12.1 0.1 collective-permute-start
  12.2 1.1 collective-permute-done.refs_6_.refs_4_
  13.4 10.8 %all-to-all-done.x_ref = bf16[16,64,128]{2,1,0:T(8,128)(2,1)S(1)} async-done(((bf16[16,64,128]{2,1,0:T(8,128)(2,1)}), bf16[16,64,128]{2,1,0:T(8,128)(2,1)S(1)}, u32[]{:S(2)}, u32[]{:S(2)}) %all-to-all-start) | async-done | bytes 262176 | tf_op jit(solution)/shard_map/all_to_all | solution.py:419
  24.2 1.5 conv.1
  25.6 12.9 %all_to_all.15.conv_ref = bf16[16,32,128]{2,1,0:T(8,128)(2,1)} all-to-all(bf16[16,32,128]{2,1,0:T(8,128)(2,1)S(1)} %conv.1), channel_id=1, replica_groups=mesh['ctx'=16,'tp'=16] {'ctx'}, dimensions={0} | all-to-all | bytes 262144 | tf_op jit(solution)/shard_map/all_to_all | solution.py:432
  38.6 2.2 %mix.1 = bf16[8,128,512]{2,1,0:T(8,128)(2,1)} custom-call(bf16[16,32,128]{2,1,0:T(8,128)(2,1)} %all_to_all.15.conv_ref, bf16[3,128,512]{2,1,0:T(8,128)(2,1)} %bitcast.26, f32[1,512]{1,0:T(1,128)} %bitcast.28), custom_call_target="tpu_custom_call" | custom-call | tf_op jit(solution)/shard_map/mix/pallas_call | solution.py:433
  40.8 7.0 %all-to-all-start.2 = ((bf16[8,128,512]{2,1,0:T(8,128)(2,1)}), bf16[8,128,512]{2,1,0:T(8,128)(2,1)S(1)}, u32[]{:S(2)}, u32[]{:S(2)}) async-start(bf16[8,128,512]{2,1,0:T(8,128)(2,1)} %mix.1), calls=%async_computation.2 | async-start | bytes 2097152 | tf_op jit(solution)/shard_map/all_to_all | solution.py:440
  47.7 0.5 collective-permute-start.3
  48.3 11.0 %all-to-all-done.2.mixed_hbm = bf16[8,128,512]{2,1,0:T(8,128)(2,1)S(1)} async-done(((bf16[8,128,512]{2,1,0:T(8,128)(2,1)}), bf16[8,128,512]{2,1,0:T(8,128)(2,1)S(1)}, u32[]{:S(2)}, u32[]{:S(2)}) %all-to-all-start.2) | async-done | bytes 1048608 | tf_op jit(solution)/shard_map/all_to_all | solution.py:440
  59.3 0.9 copy-done.5
  60.2 2.9 %out_proj.2.start_ref = f32[128,512]{1,0:T(8,128)S(1)} custom-call(s32[1]{0:T(128)} %bitcast.core_ref, bf16[8,128,512]{2,1,0:T(8,128)(2,1)S(1)} %all-to-all-done.2.mixed_hbm, bf16[8192,512]{1,0:T(8,128)(2,1)} %w_hbm.3, bf16[128,512]{1,0:T(8,128)(2,1)S(1)} %copy-done.5), custom_call_target="tpu_custom_call" | custom-call | flops 536870912 | bytes 5242880 | tf_op jit(solution)/shard_map/out_proj/pallas_call | solution.py:301
  63.1 1.0 copy-done.2
  64.1 1.2 copy-done.3
  65.3 3.6 %out_proj.3 = (bf16[128,512]{1,0:T(8,128)(2,1)}, bf16[128,512]{1,0:T(8,128)(2,1)S(1)}) custom-call(s32[1]{0:T(128)} %bitcast.core_ref, bf16[8,128,512]{2,1,0:T(8,128)(2,1)S(1)} %copy-done.3, bf16[8192,512]{1,0:T(8,128)(2,1)} %w_hbm.3, f32[128,512]{1,0:T(8,128)S(1)} %out_proj.2.start_ref), custom_call_target="tpu_custom_call" | custom-call | flops 536870912 | bytes 5242880 | tf_op jit(solution)/shard_map/out_proj/pallas_call | solution.py:301
  68.9 0.0 collective-permute-done.2.wgx_ref
  68.9 1.0 collective-permute-start.5
  69.9 0.7 collective-permute-start.4
  70.6 1.8 %collective-permute-done.5.first_ref = bf16[128,512]{1,0:T(8,128)(2,1)S(1)} collective-permute-done((bf16[128,512]{1,0:T(8,128)(2,1)S(1)}, bf16[128,512]{1,0:T(8,128)(2,1)S(1)}, u32[]{:S(2)}, u32[]{:S(2)}) %collective-permute-start.5) | collective-permute-done | bytes 131104 | tf_op jit(solution)/shard_map/ppermute | solution.py:449
  72.5 0.5 collective-permute-start.8
  73.0 3.7 %collective-permute-start.9 = (bf16[2,128,512]{2,1,0:T(8,128)(2,1)S(1)}, bf16[2,128,512]{2,1,0:T(8,128)(2,1)}, u32[]{:S(2)}, u32[]{:S(2)}) collective-permute-start(bf16[2,128,512]{2,1,0:T(8,128)(2,1)S(1)} %hold.1.refs_0_), channel_id=1, source_target_pairs={{0,192},{1,193},{2,194},{3,195},{4,196},{5,197},{6,198},{7,199},{8... | collective-permute-start | bytes 786440 | tf_op jit(solution)/shard_map/ppermute | solution.py:458
  76.7 0.1 stack.35
  76.8 0.1 collective-permute-start.7
  76.9 0.0 collective-permute-start.6
  76.9 4.6 %collective-permute-done.8.refs_3_ = bf16[2,128,512]{2,1,0:T(8,128)(2,1)S(1)} collective-permute-done((bf16[2,128,512]{2,1,0:T(8,128)(2,1)S(1)}, bf16[2,128,512]{2,1,0:T(8,128)(2,1)S(1)}, u32[]{:S(2)}, u32[]{:S(2)}) %collective-permute-start.8) | collective-permute-done | bytes 262176 | tf_op jit(solution)/shard_map/ppermute | solution.py:457
  81.6 1.2 collective-permute-start.10
  82.8 4.6 %collective-permute-done.9.refs_4_ = bf16[2,128,512]{2,1,0:T(8,128)(2,1)} collective-permute-done((bf16[2,128,512]{2,1,0:T(8,128)(2,1)S(1)}, bf16[2,128,512]{2,1,0:T(8,128)(2,1)}, u32[]{:S(2)}, u32[]{:S(2)}) %collective-permute-start.9) | collective-permute-done | bytes 262176 | tf_op jit(solution)/shard_map/ppermute | solution.py:458
  87.4 1.4 collective-permute-start.11
  88.8 2.7 %load.1 = (bf16[1368,1024]{1,0:T(8,128)(2,1)S(1)}, bf16[1368,1024]{1,0:T(8,128)(2,1)S(1)}, bf16[16,512]{1,0:T(8,128)(2,1)}) custom-call(bf16[1368,512]{1,0:T(8,128)(2,1)S(1)} %bitcast.19, bf16[1368,512]{1,0:T(8,128)(2,1)} %collective-permute-done.2.wgx_ref, bf16[1368,512]{1,0:T(8,128)(2,1)S(1)} %bitcast.21, ...), custom_call_target="tpu_custom_call" | custom-call | flops 1 | bytes 12582912 | tf_op jit(solution)/shard_map/load/pallas_call | solution.py:338
  91.5 5.0 %collective-permute-done.7.refs_2_ = bf16[2,128,512]{2,1,0:T(8,128)(2,1)S(1)} collective-permute-done((bf16[2,128,512]{2,1,0:T(8,128)(2,1)S(1)}, bf16[2,128,512]{2,1,0:T(8,128)(2,1)S(1)}, u32[]{:S(2)}, u32[]{:S(2)}) %collective-permute-start.7) | collective-permute-done | bytes 262176 | tf_op jit(solution)/shard_map/ppermute | solution.py:460
  96.5 1.8 %scale.2 = (bf16[5,128,1024]{2,1,0:T(8,128)(2,1)S(1)}, f32[5,8,128]{2,1,0:T(8,128)S(1)}) custom-call(bf16[2,128,512]{2,1,0:T(8,128)(2,1)S(1)} %hold.1.refs_0_, bf16[2,128,512]{2,1,0:T(8,128)(2,1)S(1)} %collective-permute-done.6.refs_1_, bf16[2,128,512]{2,1,0:T(8,128)(2,1)S(1)} %collective-permute-done.7.refs_2_, ...), custom_call_target="tpu_custom_call" | custom-call | flops 20971520 | bytes 2621440 | tf_op jit(solution)/shard_map/scale/pallas_call | solution.py:353
  98.3 8.0 %collective-permute-done.11.refs_1_ = bf16[2,128,512]{2,1,0:T(8,128)(2,1)S(1)} collective-permute-done((bf16[2,128,512]{2,1,0:T(8,128)(2,1)}, bf16[2,128,512]{2,1,0:T(8,128)(2,1)S(1)}, u32[]{:S(2)}, u32[]{:S(2)}) %collective-permute-start.11) | collective-permute-done | bytes 262176 | tf_op jit(solution)/shard_map/ppermute | solution.py:462
  106.2 0.0 collective-permute-done.12.refs_2_
  106.2 0.0 collective-permute-done.10.refs_0_
  106.2 0.6 scale.3
  106.8 2.2 %mlp.5 = (bf16[2,1376,128]{2,1,0:T(8,128)(2,1)S(1)}, s32[8]{0:T(128)S(1)}) custom-call(s32[8]{0:T(128)S(1)} %fusion.5.idx_ref, bf16[5,128,1024]{2,1,0:T(8,128)(2,1)S(1)} %get-tuple-element.36.refs_0_, f32[5,8,128]{2,1,0:T(8,128)S(1)} %get-tuple-element.37.refs_1_, bf16[3,128,1024]{2,1,0:T(8,128)(2,1)S(1)} %get-tuple-element.38.refs_2_, ...), custom_call_target="tpu_custom_call" | custom-call | flops 100000000 | bytes 524288 | tf_op jit(solution)/shard_map/mlp/pallas_call | solution.py:371
  109.1 1.4 collective-permute-start.16
  110.5 2.3 %mlp.6 = (bf16[2,1376,128]{2,1,0:T(8,128)(2,1)S(1)}, bf16[2,1376,128]{2,1,0:T(8,128)(2,1)S(1)}, s32[8]{0:T(128)S(1)}) custom-call(s32[8]{0:T(128)S(1)} %get-tuple-element.44.idx_ref, bf16[5,128,1024]{2,1,0:T(8,128)(2,1)S(1)} %get-tuple-element.36.refs_0_, f32[5,8,128]{2,1,0:T(8,128)S(1)} %get-tuple-element.37.refs_1_, ...), custom_call_target="tpu_custom_call" | custom-call | flops 100000000 | bytes 524288 | tf_op jit(solution)/shard_map/mlp/pallas_call | solution.py:371
  112.8 1.9 %collective-permute-start.13 = (bf16[2,1376,128]{2,1,0:T(8,128)(2,1)S(1)}, bf16[2,1376,128]{2,1,0:T(8,128)(2,1)S(1)}, u32[]{:S(2)}, u32[]{:S(2)}) collective-permute-start(bf16[2,1376,128]{2,1,0:T(8,128)(2,1)S(1)} %get-tuple-element.50), channel_id=1, source_target_pairs={{0,2},{1,3},{2,4},{3,5},{4,6},{5,7},{6,0},{7,1},{8,10},{9,11},{10,... | collective-permute-start | bytes 2113544 | tf_op jit(solution)/shard_map/ppermute | solution.py:46
  114.6 0.3 collective-permute-start.14
  114.9 2.3 %mlp.7 = (bf16[1376,128]{1,0:T(8,128)(2,1)S(1)}, bf16[1376,128]{1,0:T(8,128)(2,1)S(1)}, bf16[1376,128]{1,0:T(8,128)(2,1)S(1)}, bf16[1376,128]{1,0:T(8,128)(2,1)S(1)}, s32[8]{0:T(128)S(1)}) custom-call(s32[8]{0:T(128)S(1)} %get-tuple-element.45.idx_ref, bf16[5,128,1024]{2,1,0:T(8,128)(2,1)S(1)} %get-tuple-element.36.refs_0_, ...), custom_call_target="tpu_custom_call" | custom-call | flops 100000000 | bytes 524288 | tf_op jit(solution)/shard_map/mlp/pallas_call | solution.py:371
  117.2 2.3 %mlp.8 = (bf16[2,1376,128]{2,1,0:T(8,128)(2,1)S(1)}, bf16[2,1376,128]{2,1,0:T(8,128)(2,1)S(1)}, s32[8]{0:T(128)S(1)}) custom-call(s32[8]{0:T(128)S(1)} %get-tuple-element.46.idx_ref, bf16[5,128,1024]{2,1,0:T(8,128)(2,1)S(1)} %get-tuple-element.36.refs_0_, f32[5,8,128]{2,1,0:T(8,128)S(1)} %get-tuple-element.37.refs_1_, ...), custom_call_target="tpu_custom_call" | custom-call | flops 100000000 | bytes 524288 | tf_op jit(solution)/shard_map/mlp/pallas_call | solution.py:371
  119.5 8.9 %collective-permute-done.16.right_ref = bf16[2,1376,128]{2,1,0:T(8,128)(2,1)S(1)} collective-permute-done((bf16[2,1376,128]{2,1,0:T(8,128)(2,1)S(1)}, bf16[2,1376,128]{2,1,0:T(8,128)(2,1)S(1)}, u32[]{:S(2)}, u32[]{:S(2)}) %collective-permute-start.16) | collective-permute-done | bytes 704544 | tf_op jit(solution)/shard_map/ppermute | solution.py:46
  128.5 0.2 sum.5
  128.6 1.4 collective-permute-start.17
  130.0 0.7 collective-permute-start.21
  130.7 2.6 %collective-permute-done.14.refs_2_ = bf16[2,1376,128]{2,1,0:T(8,128)(2,1)S(1)} collective-permute-done((bf16[2,1376,128]{2,1,0:T(8,128)(2,1)S(1)}, bf16[2,1376,128]{2,1,0:T(8,128)(2,1)S(1)}, u32[]{:S(2)}, u32[]{:S(2)}) %collective-permute-start.14) | collective-permute-done | bytes 704544 | tf_op jit(solution)/shard_map/ppermute | solution.py:46
  133.3 0.3 sum.4
  133.6 1.8 %collective-permute-start.15 = (bf16[2,1376,128]{2,1,0:T(8,128)(2,1)S(1)}, bf16[2,1376,128]{2,1,0:T(8,128)(2,1)S(1)}, u32[]{:S(2)}, u32[]{:S(2)}) collective-permute-start(bf16[2,1376,128]{2,1,0:T(8,128)(2,1)S(1)} %sum.4), channel_id=1, source_target_pairs={{0,8},{1,9},{2,10},{3,11},{4,12},{5,13},{6,14},{7,15},{8,0},{9,1},... | collective-permute-start | bytes 2113544 | tf_op jit(solution)/shard_map/ppermute | solution.py:46
  135.3 0.0 collective-permute-start.19
  135.3 3.2 %collective-permute-start.20 = (bf16[1376,128]{1,0:T(8,128)(2,1)S(1)}, bf16[1376,128]{1,0:T(8,128)(2,1)S(1)}, u32[]{:S(2)}, u32[]{:S(2)}) collective-permute-start(bf16[1376,128]{1,0:T(8,128)(2,1)S(1)} %get-tuple-element.57), channel_id=1, source_target_pairs={{0,2},{1,3},{2,4},{3,5},{4,6},{5,7},{6,0},{7,1},{8,10},{9,11},{10,... | collective-permute-start | bytes 1056776 | tf_op jit(solution)/shard_map/ppermute | solution.py:46
  138.6 1.3 collective-permute-done.17.refs_1_
  139.9 0.1 sum.6
  140.0 1.7 %collective-permute-start.18 = (bf16[1376,128]{1,0:T(8,128)(2,1)S(1)}, bf16[1376,128]{1,0:T(8,128)(2,1)S(1)}, u32[]{:S(2)}, u32[]{:S(2)}) collective-permute-start(bf16[1376,128]{1,0:T(8,128)(2,1)S(1)} %sum.6), channel_id=1, source_target_pairs={{0,2},{1,3},{2,4},{3,5},{4,6},{5,7},{6,0},{7,1},{8,10},{9,11},{10,... | collective-permute-start | bytes 1056776 | tf_op jit(solution)/shard_map/ppermute | solution.py:46
  141.7 0.8 collective-permute-done.21.refs_1_
  142.4 0.1 sum.7
  142.5 0.1 collective-permute-start.22
  142.6 2.2 %mlp.9 = (bf16[2,1376,128]{2,1,0:T(8,128)(2,1)S(1)}, s32[8]{0:T(128)}) custom-call(s32[8]{0:T(128)S(1)} %get-tuple-element.47.idx_ref, bf16[5,128,1024]{2,1,0:T(8,128)(2,1)S(1)} %get-tuple-element.36.refs_0_, f32[5,8,128]{2,1,0:T(8,128)S(1)} %get-tuple-element.37.refs_1_, bf16[3,128,1024]{2,1,0:T(8,128)(2,1)S(1)} %get-tuple-element.38.refs_2_, ...), custom_call_target="tpu_custom_call" | custom-call | flops 100000000 | bytes 524288 | tf_op jit(solution)/shard_map/mlp/pallas_call | solution.py:371
  144.8 5.1 %collective-permute-done.19.gate_3_ref = bf16[1376,128]{1,0:T(8,128)(2,1)S(1)} collective-permute-done((bf16[1376,128]{1,0:T(8,128)(2,1)S(1)}, bf16[1376,128]{1,0:T(8,128)(2,1)S(1)}, u32[]{:S(2)}, u32[]{:S(2)}) %collective-permute-start.19) | collective-permute-done | bytes 352288 | tf_op jit(solution)/shard_map/ppermute | solution.py:46
  150.0 3.3 %collective-permute-done.18.gate_1_ref = bf16[1376,128]{1,0:T(8,128)(2,1)S(1)} collective-permute-done((bf16[1376,128]{1,0:T(8,128)(2,1)S(1)}, bf16[1376,128]{1,0:T(8,128)(2,1)S(1)}, u32[]{:S(2)}, u32[]{:S(2)}) %collective-permute-start.18) | collective-permute-done | bytes 352288 | tf_op jit(solution)/shard_map/ppermute | solution.py:46
  153.3 2.5 %collective-permute-done.22.up_3_ref = bf16[1376,128]{1,0:T(8,128)(2,1)S(1)} collective-permute-done((bf16[1376,128]{1,0:T(8,128)(2,1)S(1)}, bf16[1376,128]{1,0:T(8,128)(2,1)S(1)}, u32[]{:S(2)}, u32[]{:S(2)}) %collective-permute-start.22) | collective-permute-done | bytes 352288 | tf_op jit(solution)/shard_map/ppermute | solution.py:46
  155.8 1.3 finish.1
  (23 shorter events, 0.1 us)
Async XLA Ops:
  0.6 23.5 %copy-start.4 = (bf16[128,1024]{1,0:T(8,128)(2,1)S(1)}, bf16[128,1024]{1,0:T(8,128)(2,1)}, u32[]{:S(2)}) copy-start(bf16[128,1024]{1,0:T(8,128)(2,1)} %constant.165.clone.tab_ref) | copy-start | bytes 786436
  0.6 11.5 %copy-start.6 = (f32[512]{0:T(512)S(1)}, f32[512]{0:T(512)}, u32[]{:S(2)}) copy-start(f32[512]{0:T(512)} %param.14) | copy-start | bytes 6148
  2.6 21.5 %all-to-all-start = ((bf16[16,64,128]{2,1,0:T(8,128)(2,1)}), bf16[16,64,128]{2,1,0:T(8,128)(2,1)S(1)}, u32[]{:S(2)}, u32[]{:S(2)}) async-start(bf16[16,64,128]{2,1,0:T(8,128)(2,1)} %prep.1), calls=%async_computation | async-start | bytes 524288 | tf_op jit(solution)/shard_map/all_to_all | solution.py:419
  12.1 1.2 collective-permute-start
  40.7 7.0 %copy-start = (bf16[512,1368]{0,1:T(8,128)(2,1)S(1)}, bf16[512,1368]{0,1:T(8,128)(2,1)}, u32[]{:S(2)}) copy-start(bf16[512,1368]{0,1:T(8,128)(2,1)} %param.15) | copy-start | bytes 4202500
  40.8 18.5 %all-to-all-start.2 = ((bf16[8,128,512]{2,1,0:T(8,128)(2,1)}), bf16[8,128,512]{2,1,0:T(8,128)(2,1)S(1)}, u32[]{:S(2)}, u32[]{:S(2)}) async-start(bf16[8,128,512]{2,1,0:T(8,128)(2,1)} %mix.1), calls=%async_computation.2 | async-start | bytes 2097152 | tf_op jit(solution)/shard_map/all_to_all | solution.py:440
  47.7 21.2 %collective-permute-start.2 = (bf16[1368,512]{1,0:T(8,128)(2,1)S(1)}, bf16[1368,512]{1,0:T(8,128)(2,1)}, u32[]{:S(2)}, u32[]{:S(2)}) collective-permute-start(bf16[1368,512]{1,0:T(8,128)(2,1)S(1)} %bitcast.18), channel_id=1, source_target_pairs={{0,1},{1,0},{2,3},{3,2},{4,5},{5,4},{6,7},{7,6},{8,9},{9,8},{10,11... | collective-permute-start | bytes 4202504 | tf_op jit(solution)/shard_map/ppermute | solution.py:46
  47.7 21.2 %collective-permute-start.3 = (bf16[1368,512]{1,0:T(8,128)(2,1)}, bf16[1368,512]{1,0:T(8,128)(2,1)}, u32[]{:S(2)}, u32[]{:S(2)}) collective-permute-start(bf16[1368,512]{1,0:T(8,128)(2,1)} %bitcast.20), channel_id=1, source_target_pairs={{0,1},{1,0},{2,3},{3,2},{4,5},{5,4},{6,7},{7,6},{8,9},{9,8},{10,11... | collective-permute-start | bytes 4202504 | tf_op jit(solution)/shard_map/ppermute | solution.py:46
  59.3 3.8 %collective-permute-start.1 = (bf16[8,128,512]{2,1,0:T(8,128)(2,1)S(1)}, bf16[8,128,512]{2,1,0:T(8,128)(2,1)S(1)}, u32[]{:S(2)}, u32[]{:S(2)}) collective-permute-start(bf16[8,128,512]{2,1,0:T(8,128)(2,1)S(1)} %all-to-all-done.2.mixed_hbm), channel_id=1, source_target_pairs={{0,1},{1,0},{2,3},{3,2},{4,5},{5,4},{6,7},{7,6},{8,9},{9,8},{10,11... | collective-permute-start | bytes 3145736 | tf_op jit(solution)/shard_map/ppermute | solution.py:46
  59.3 0.9 copy-start.5
  63.1 1.0 copy-start.2
  64.1 1.2 copy-start.3
  65.3 23.5 %copy-start.1 = (bf16[512,1368]{0,1:T(8,128)(2,1)S(1)}, bf16[512,1368]{0,1:T(8,128)(2,1)}, u32[]{:S(2)}) copy-start(bf16[512,1368]{0,1:T(8,128)(2,1)} %param.16) | copy-start | bytes 4202500
  68.9 3.5 %collective-permute-start.5 = (bf16[128,512]{1,0:T(8,128)(2,1)S(1)}, bf16[128,512]{1,0:T(8,128)(2,1)S(1)}, u32[]{:S(2)}, u32[]{:S(2)}) collective-permute-start(bf16[128,512]{1,0:T(8,128)(2,1)S(1)} %get-tuple-element.34.stream_ref), channel_id=1, source_target_pairs={{0,16},{1,0},{2,18},{3,2},{4,20},{5,4},{6,22},{7,6},{8,24},{9,8},{... | collective-permute-start | bytes 393224 | tf_op jit(solution)/shard_map/ppermute | solution.py:449
  69.9 2.5 %collective-permute-start.4 = (bf16[128,512]{1,0:T(8,128)(2,1)S(1)}, bf16[128,512]{1,0:T(8,128)(2,1)S(1)}, u32[]{:S(2)}, u32[]{:S(2)}) collective-permute-start(bf16[128,512]{1,0:T(8,128)(2,1)S(1)} %get-tuple-element.34.stream_ref), channel_id=1, source_target_pairs={{1,16},{3,18},{5,20},{7,22},{9,24},{11,26},{13,28},{15,30},{16,1},... | collective-permute-start | bytes 393224 | tf_op jit(solution)/shard_map/ppermute | solution.py:450
  72.5 9.1 %collective-permute-start.8 = (bf16[2,128,512]{2,1,0:T(8,128)(2,1)S(1)}, bf16[2,128,512]{2,1,0:T(8,128)(2,1)S(1)}, u32[]{:S(2)}, u32[]{:S(2)}) collective-permute-start(bf16[2,128,512]{2,1,0:T(8,128)(2,1)S(1)} %hold.1.refs_0_), channel_id=1, source_target_pairs={{0,64},{1,65},{2,66},{3,67},{4,68},{5,69},{6,70},{7,71},{8,72},{9,... | collective-permute-start | bytes 786440 | tf_op jit(solution)/shard_map/ppermute | solution.py:457
  73.0 14.4 %collective-permute-start.9 = (bf16[2,128,512]{2,1,0:T(8,128)(2,1)S(1)}, bf16[2,128,512]{2,1,0:T(8,128)(2,1)}, u32[]{:S(2)}, u32[]{:S(2)}) collective-permute-start(bf16[2,128,512]{2,1,0:T(8,128)(2,1)S(1)} %hold.1.refs_0_), channel_id=1, source_target_pairs={{0,192},{1,193},{2,194},{3,195},{4,196},{5,197},{6,198},{7,199},{8... | collective-permute-start | bytes 786440 | tf_op jit(solution)/shard_map/ppermute | solution.py:458
  76.8 19.7 %collective-permute-start.7 = (bf16[2,128,512]{2,1,0:T(8,128)(2,1)S(1)}, bf16[2,128,512]{2,1,0:T(8,128)(2,1)S(1)}, u32[]{:S(2)}, u32[]{:S(2)}) collective-permute-start(bf16[2,128,512]{2,1,0:T(8,128)(2,1)S(1)} %hold.1.refs_0_), channel_id=1, source_target_pairs={{0,224},{1,225},{2,226},{3,227},{4,228},{5,229},{6,230},{7,231},{8... | collective-permute-start | bytes 786440 | tf_op jit(solution)/shard_map/ppermute | solution.py:460
  76.9 19.6 %collective-permute-start.6 = (bf16[2,128,512]{2,1,0:T(8,128)(2,1)S(1)}, bf16[2,128,512]{2,1,0:T(8,128)(2,1)S(1)}, u32[]{:S(2)}, u32[]{:S(2)}) collective-permute-start(bf16[2,128,512]{2,1,0:T(8,128)(2,1)S(1)} %hold.1.refs_0_), channel_id=1, source_target_pairs={{0,32},{1,33},{2,34},{3,35},{4,36},{5,37},{6,38},{7,39},{8,40},{9,... | collective-permute-start | bytes 786440 | tf_op jit(solution)/shard_map/ppermute | solution.py:459
  81.6 24.7 %collective-permute-start.12 = (bf16[2,128,512]{2,1,0:T(8,128)(2,1)S(1)}, bf16[2,128,512]{2,1,0:T(8,128)(2,1)S(1)}, u32[]{:S(2)}, u32[]{:S(2)}) collective-permute-start(bf16[2,128,512]{2,1,0:T(8,128)(2,1)S(1)} %collective-permute-done.8.refs_3_), channel_id=1, source_target_pairs={{0,64},{1,65},{2,66},{3,67},{4,68},{5,69},{6,70},{7,71},{8,72},{9,... | collective-permute-start | bytes 786440 | tf_op jit(solution)/shard_map/ppermute | solution.py:463
  81.6 24.7 %collective-permute-start.10 = (bf16[2,128,512]{2,1,0:T(8,128)(2,1)S(1)}, bf16[2,128,512]{2,1,0:T(8,128)(2,1)S(1)}, u32[]{:S(2)}, u32[]{:S(2)}) collective-permute-start(bf16[2,128,512]{2,1,0:T(8,128)(2,1)S(1)} %collective-permute-done.8.refs_3_), channel_id=1, source_target_pairs={{0,32},{1,33},{2,34},{3,35},{4,36},{5,37},{6,38},{7,39},{8,40},{9,... | collective-permute-start | bytes 786440 | tf_op jit(solution)/shard_map/ppermute | solution.py:461
  87.4 18.9 %collective-permute-start.11 = (bf16[2,128,512]{2,1,0:T(8,128)(2,1)}, bf16[2,128,512]{2,1,0:T(8,128)(2,1)S(1)}, u32[]{:S(2)}, u32[]{:S(2)}) collective-permute-start(bf16[2,128,512]{2,1,0:T(8,128)(2,1)} %collective-permute-done.9.refs_4_), channel_id=1, source_target_pairs={{0,224},{1,225},{2,226},{3,227},{4,228},{5,229},{6,230},{7,231},{8... | collective-permute-start | bytes 786440 | tf_op jit(solution)/shard_map/ppermute | solution.py:462
  109.1 19.4 %collective-permute-start.16 = (bf16[2,1376,128]{2,1,0:T(8,128)(2,1)S(1)}, bf16[2,1376,128]{2,1,0:T(8,128)(2,1)S(1)}, u32[]{:S(2)}, u32[]{:S(2)}) collective-permute-start(bf16[2,1376,128]{2,1,0:T(8,128)(2,1)S(1)} %get-tuple-element.54), channel_id=1, source_target_pairs={{0,8},{1,9},{2,10},{3,11},{4,12},{5,13},{6,14},{7,15},{8,0},{9,1},... | collective-permute-start | bytes 2113544 | tf_op jit(solution)/shard_map/ppermute | solution.py:46
  112.8 17.9 %collective-permute-start.13 = (bf16[2,1376,128]{2,1,0:T(8,128)(2,1)S(1)}, bf16[2,1376,128]{2,1,0:T(8,128)(2,1)S(1)}, u32[]{:S(2)}, u32[]{:S(2)}) collective-permute-start(bf16[2,1376,128]{2,1,0:T(8,128)(2,1)S(1)} %get-tuple-element.50), channel_id=1, source_target_pairs={{0,2},{1,3},{2,4},{3,5},{4,6},{5,7},{6,0},{7,1},{8,10},{9,11},{10,... | collective-permute-start | bytes 2113544 | tf_op jit(solution)/shard_map/ppermute | solution.py:46
  114.6 18.7 %collective-permute-start.14 = (bf16[2,1376,128]{2,1,0:T(8,128)(2,1)S(1)}, bf16[2,1376,128]{2,1,0:T(8,128)(2,1)S(1)}, u32[]{:S(2)}, u32[]{:S(2)}) collective-permute-start(bf16[2,1376,128]{2,1,0:T(8,128)(2,1)S(1)} %get-tuple-element.51), channel_id=1, source_target_pairs={{0,6},{1,7},{2,0},{3,1},{4,2},{5,3},{6,4},{7,5},{8,14},{9,15},{10,... | collective-permute-start | bytes 2113544 | tf_op jit(solution)/shard_map/ppermute | solution.py:46
  128.6 11.3 %collective-permute-start.17 = (bf16[1376,128]{1,0:T(8,128)(2,1)S(1)}, bf16[1376,128]{1,0:T(8,128)(2,1)S(1)}, u32[]{:S(2)}, u32[]{:S(2)}) collective-permute-start(bf16[1376,128]{1,0:T(8,128)(2,1)S(1)} %get-tuple-element.55), channel_id=1, source_target_pairs={{0,2},{1,3},{2,4},{3,5},{4,6},{5,7},{6,0},{7,1},{8,10},{9,11},{10,... | collective-permute-start | bytes 1056776 | tf_op jit(solution)/shard_map/ppermute | solution.py:46
  130.0 12.4 %collective-permute-start.21 = (bf16[1376,128]{1,0:T(8,128)(2,1)S(1)}, bf16[1376,128]{1,0:T(8,128)(2,1)S(1)}, u32[]{:S(2)}, u32[]{:S(2)}) collective-permute-start(bf16[1376,128]{1,0:T(8,128)(2,1)S(1)} %get-tuple-element.59), channel_id=1, source_target_pairs={{0,6},{1,7},{2,0},{3,1},{4,2},{5,3},{6,4},{7,5},{8,14},{9,15},{10,... | collective-permute-start | bytes 1056776 | tf_op jit(solution)/shard_map/ppermute | solution.py:46
  133.6 22.2 %collective-permute-start.15 = (bf16[2,1376,128]{2,1,0:T(8,128)(2,1)S(1)}, bf16[2,1376,128]{2,1,0:T(8,128)(2,1)S(1)}, u32[]{:S(2)}, u32[]{:S(2)}) collective-permute-start(bf16[2,1376,128]{2,1,0:T(8,128)(2,1)S(1)} %sum.4), channel_id=1, source_target_pairs={{0,8},{1,9},{2,10},{3,11},{4,12},{5,13},{6,14},{7,15},{8,0},{9,1},... | collective-permute-start | bytes 2113544 | tf_op jit(solution)/shard_map/ppermute | solution.py:46
  135.3 14.6 %collective-permute-start.19 = (bf16[1376,128]{1,0:T(8,128)(2,1)S(1)}, bf16[1376,128]{1,0:T(8,128)(2,1)S(1)}, u32[]{:S(2)}, u32[]{:S(2)}) collective-permute-start(bf16[1376,128]{1,0:T(8,128)(2,1)S(1)} %get-tuple-element.56), channel_id=1, source_target_pairs={{0,6},{1,7},{2,0},{3,1},{4,2},{5,3},{6,4},{7,5},{8,14},{9,15},{10,... | collective-permute-start | bytes 1056776 | tf_op jit(solution)/shard_map/ppermute | solution.py:46
  135.3 14.6 %collective-permute-start.20 = (bf16[1376,128]{1,0:T(8,128)(2,1)S(1)}, bf16[1376,128]{1,0:T(8,128)(2,1)S(1)}, u32[]{:S(2)}, u32[]{:S(2)}) collective-permute-start(bf16[1376,128]{1,0:T(8,128)(2,1)S(1)} %get-tuple-element.57), channel_id=1, source_target_pairs={{0,2},{1,3},{2,4},{3,5},{4,6},{5,7},{6,0},{7,1},{8,10},{9,11},{10,... | collective-permute-start | bytes 1056776 | tf_op jit(solution)/shard_map/ppermute | solution.py:46
  140.0 13.3 %collective-permute-start.18 = (bf16[1376,128]{1,0:T(8,128)(2,1)S(1)}, bf16[1376,128]{1,0:T(8,128)(2,1)S(1)}, u32[]{:S(2)}, u32[]{:S(2)}) collective-permute-start(bf16[1376,128]{1,0:T(8,128)(2,1)S(1)} %sum.6), channel_id=1, source_target_pairs={{0,2},{1,3},{2,4},{3,5},{4,6},{5,7},{6,0},{7,1},{8,10},{9,11},{10,... | collective-permute-start | bytes 1056776 | tf_op jit(solution)/shard_map/ppermute | solution.py:46
  142.5 13.3 %collective-permute-start.22 = (bf16[1376,128]{1,0:T(8,128)(2,1)S(1)}, bf16[1376,128]{1,0:T(8,128)(2,1)S(1)}, u32[]{:S(2)}, u32[]{:S(2)}) collective-permute-start(bf16[1376,128]{1,0:T(8,128)(2,1)S(1)} %sum.7), channel_id=1, source_target_pairs={{0,6},{1,7},{2,0},{3,1},{4,2},{5,3},{6,4},{7,5},{8,14},{9,15},{10,... | collective-permute-start | bytes 1056776 | tf_op jit(solution)/shard_map/ppermute | solution.py:46

commit v12 on v11

--- a/solution.py
+++ b/solution.py
@@ -312,7 +312,7 @@
             pltpu.VMEM((N_TP // 2, CH, CH), BF16),
             pltpu.SemaphoreType.DMA((2, N_TP // 2)),
         ],
-        compiler_params=params(51),
+        compiler_params=params(53),
         cost_estimate=pl.CostEstimate(
             flops=2 * ROWS * CH * N_TP // 2 * CH, bytes_accessed=5 << 20, transcendentals=0
         ),

time: 158 us -> 155 us (0.981)
  local copies, waits for them, and re-layouts: 3.19 us -> 0.11 us
    unnamed x14 -> x10, local copies, waits for them, and re-layouts: 3.1 us -> 0.02 us
  transfers between devices with their start and end apart: 25 -> 25, of which waited for: 15 -> 16; matrix products, arithmetic and copies ran while one was open for 0% -> 0% of each run, Pallas kernels for 13% -> 13%
where the time goes in v12:
time: 155 us; the launch traced here: 154 us
  waiting for transfers between devices  71.7 us (46%)
  starting transfers between devices  38.1 us (25%)
  Pallas kernels  30.4 us (20%)
  blocking collectives  12.9 us (8%)
    ppermute x14, waiting for transfers between devices, shift(): return lax.ppermute(arr, AXES, pairs)  25.8 us
    ppermute x14, starting transfers between devices, shift(): return lax.ppermute(arr, AXES, pairs)  13 us
    all_to_all x1, blocking collectives, shards(): conv_rows = lax.all_to_all(conv, 'ctx', 0, 0, tiled=True)  12.9 us
    pallas_call x5, Pallas kernels, mlp_part(): pl.pallas_call(functools.partial(mlp_kernel, slots, split), out_shape=[ja...  11.4 us
    all_to_all x1, waiting for transfers between devices, shards(): lax.all_to_all(copies, 'tp', 0, 0, axis_index_groups=PLANE_GROUPS, tiled=...  11.1 us
    all_to_all x1, waiting for transfers between devices, shards(): recv = lax.all_to_all(sent, 'ctx', 0, 0, tiled=True)  10.8 us
    all_to_all x1, starting transfers between devices, shards(): recv = lax.all_to_all(sent, 'ctx', 0, 0, tiled=True)  9.5 us
    ppermute x1, waiting for transfers between devices, shards(): lax.ppermute(two_second, AXES, pairs_of(functools.partial(along, -1)))  7.97 us
  transfers between devices with their start and end apart: 25, of which 16 were waited for; matrix products, arithmetic and copies ran while one was open for 0% of the time, Pallas kernels for 13%

profile of v12, /device:TPU:24, one launch (start us, length us, event | category | flops | bytes accessed | tf_op | source)
XLA Modules:
  0.0 154.2 jit_solution(9386230457874281974)
XLA Ops:
  0.6 0.0 copy-start.2
  0.7 2.0 %prep.1 = bf16[16,64,128]{2,1,0:T(8,128)(2,1)} custom-call(bf16[3,128,512]{2,1,0:T(8,128)(2,1)} %bitcast.25, f32[128,512]{1,0:T(8,128)} %filt_ref.1), custom_call_target="tpu_custom_call" | custom-call | tf_op jit(solution)/shard_map/prep/pallas_call | solution.py:413
  2.6 9.5 %all-to-all-start = ((bf16[16,64,128]{2,1,0:T(8,128)(2,1)}), bf16[16,64,128]{2,1,0:T(8,128)(2,1)S(1)}, u32[]{:S(2)}, u32[]{:S(2)}) async-start(bf16[16,64,128]{2,1,0:T(8,128)(2,1)} %prep.1), calls=%async_computation | async-start | bytes 524288 | tf_op jit(solution)/shard_map/all_to_all | solution.py:419
  12.1 0.1 collective-permute-start
  12.2 1.1 collective-permute-done.refs_6_.refs_4_
  13.4 10.8 %all-to-all-done.x_ref = bf16[16,64,128]{2,1,0:T(8,128)(2,1)S(1)} async-done(((bf16[16,64,128]{2,1,0:T(8,128)(2,1)}), bf16[16,64,128]{2,1,0:T(8,128)(2,1)S(1)}, u32[]{:S(2)}, u32[]{:S(2)}) %all-to-all-start) | async-done | bytes 262176 | tf_op jit(solution)/shard_map/all_to_all | solution.py:419
  24.2 1.5 conv.1
  25.6 12.9 %all_to_all.15.conv_ref = bf16[16,32,128]{2,1,0:T(8,128)(2,1)} all-to-all(bf16[16,32,128]{2,1,0:T(8,128)(2,1)S(1)} %conv.1), channel_id=1, replica_groups=mesh['ctx'=16,'tp'=16] {'ctx'}, dimensions={0} | all-to-all | bytes 262144 | tf_op jit(solution)/shard_map/all_to_all | solution.py:432
  38.6 2.3 %mix.1 = bf16[8,128,512]{2,1,0:T(8,128)(2,1)} custom-call(bf16[16,32,128]{2,1,0:T(8,128)(2,1)} %all_to_all.15.conv_ref, bf16[3,128,512]{2,1,0:T(8,128)(2,1)} %bitcast.26, f32[1,512]{1,0:T(1,128)} %bitcast.28), custom_call_target="tpu_custom_call" | custom-call | tf_op jit(solution)/shard_map/mix/pallas_call | solution.py:433
  40.9 7.0 %all-to-all-start.2 = ((bf16[8,128,512]{2,1,0:T(8,128)(2,1)}), bf16[8,128,512]{2,1,0:T(8,128)(2,1)}, u32[]{:S(2)}, u32[]{:S(2)}) async-start(bf16[8,128,512]{2,1,0:T(8,128)(2,1)} %mix.1), calls=%async_computation.2 | async-start | bytes 2097152 | tf_op jit(solution)/shard_map/all_to_all | solution.py:440
  47.9 0.0 collective-permute-start.2
  47.9 0.5 collective-permute-start.3
  48.4 11.1 %all-to-all-done.2.mixed_hbm = bf16[8,128,512]{2,1,0:T(8,128)(2,1)} async-done(((bf16[8,128,512]{2,1,0:T(8,128)(2,1)}), bf16[8,128,512]{2,1,0:T(8,128)(2,1)}, u32[]{:S(2)}, u32[]{:S(2)}) %all-to-all-start.2) | async-done | bytes 1048608 | tf_op jit(solution)/shard_map/all_to_all | solution.py:440
  59.5 0.0 collective-permute-start.1
  59.5 2.9 %out_proj.2.start_ref = f32[128,512]{1,0:T(8,128)S(1)} custom-call(s32[1]{0:T(128)} %bitcast.core_ref, bf16[8,128,512]{2,1,0:T(8,128)(2,1)} %all-to-all-done.2.mixed_hbm, bf16[8192,512]{1,0:T(8,128)(2,1)} %w_hbm.3, bf16[128,512]{1,0:T(8,128)(2,1)S(1)} %copy-done.3), custom_call_target="tpu_custom_call" | custom-call | flops 536870912 | bytes 5242880 | tf_op jit(solution)/shard_map/out_proj/pallas_call | solution.py:301
  62.4 0.1 collective-permute-done.1.mixed_hbm
  62.5 3.5 %out_proj.3 = (bf16[128,512]{1,0:T(8,128)(2,1)}, bf16[128,512]{1,0:T(8,128)(2,1)S(1)}) custom-call(s32[1]{0:T(128)} %bitcast.core_ref, bf16[8,128,512]{2,1,0:T(8,128)(2,1)} %collective-permute-done.1.mixed_hbm, bf16[8192,512]{1,0:T(8,128)(2,1)} %w_hbm.3, f32[128,512]{1,0:T(8,128)S(1)} %out_proj.2.start_ref), custom_call_target="tpu_custom_call" | custom-call | flops 536870912 | bytes 5242880 | tf_op jit(solution)/shard_map/out_proj/pallas_call | solution.py:301
  66.1 0.0 collective-permute-done.2.wgx_ref
  66.1 0.0 collective-permute-done.3.wux_ref
  66.1 1.0 collective-permute-start.5
  67.1 0.7 collective-permute-start.4
  67.8 1.8 %collective-permute-done.5.first_ref = bf16[128,512]{1,0:T(8,128)(2,1)S(1)} collective-permute-done((bf16[128,512]{1,0:T(8,128)(2,1)S(1)}, bf16[128,512]{1,0:T(8,128)(2,1)S(1)}, u32[]{:S(2)}, u32[]{:S(2)}) %collective-permute-start.5) | collective-permute-done | bytes 131104 | tf_op jit(solution)/shard_map/ppermute | solution.py:449
  69.6 0.5 collective-permute-start.8
  70.1 3.7 %collective-permute-start.9 = (bf16[2,128,512]{2,1,0:T(8,128)(2,1)S(1)}, bf16[2,128,512]{2,1,0:T(8,128)(2,1)}, u32[]{:S(2)}, u32[]{:S(2)}) collective-permute-start(bf16[2,128,512]{2,1,0:T(8,128)(2,1)S(1)} %hold.1.refs_0_), channel_id=1, source_target_pairs={{0,192},{1,193},{2,194},{3,195},{4,196},{5,197},{6,198},{7,199},{8... | collective-permute-start | bytes 786440 | tf_op jit(solution)/shard_map/ppermute | solution.py:458
  73.8 0.1 stack.35
  73.9 0.1 collective-permute-start.7
  74.0 0.0 collective-permute-start.6
  74.1 4.7 %collective-permute-done.8.refs_3_ = bf16[2,128,512]{2,1,0:T(8,128)(2,1)S(1)} collective-permute-done((bf16[2,128,512]{2,1,0:T(8,128)(2,1)S(1)}, bf16[2,128,512]{2,1,0:T(8,128)(2,1)S(1)}, u32[]{:S(2)}, u32[]{:S(2)}) %collective-permute-start.8) | collective-permute-done | bytes 262176 | tf_op jit(solution)/shard_map/ppermute | solution.py:457
  78.7 0.0 collective-permute-start.12
  78.7 1.2 collective-permute-start.10
  80.0 4.6 %collective-permute-done.9.refs_4_ = bf16[2,128,512]{2,1,0:T(8,128)(2,1)} collective-permute-done((bf16[2,128,512]{2,1,0:T(8,128)(2,1)S(1)}, bf16[2,128,512]{2,1,0:T(8,128)(2,1)}, u32[]{:S(2)}, u32[]{:S(2)}) %collective-permute-start.9) | collective-permute-done | bytes 262176 | tf_op jit(solution)/shard_map/ppermute | solution.py:458
  84.5 1.4 collective-permute-start.11
  85.9 2.7 %load.1 = (bf16[1368,1024]{1,0:T(8,128)(2,1)S(1)}, bf16[1368,1024]{1,0:T(8,128)(2,1)S(1)}, bf16[16,512]{1,0:T(8,128)(2,1)}) custom-call(bf16[1368,512]{1,0:T(8,128)(2,1)S(1)} %bitcast.19, bf16[1368,512]{1,0:T(8,128)(2,1)} %collective-permute-done.2.wgx_ref, bf16[1368,512]{1,0:T(8,128)(2,1)S(1)} %bitcast.21, ...), custom_call_target="tpu_custom_call" | custom-call | flops 1 | bytes 12582912 | tf_op jit(solution)/shard_map/load/pallas_call | solution.py:338
  88.6 5.0 %collective-permute-done.7.refs_2_ = bf16[2,128,512]{2,1,0:T(8,128)(2,1)S(1)} collective-permute-done((bf16[2,128,512]{2,1,0:T(8,128)(2,1)S(1)}, bf16[2,128,512]{2,1,0:T(8,128)(2,1)S(1)}, u32[]{:S(2)}, u32[]{:S(2)}) %collective-permute-start.7) | collective-permute-done | bytes 262176 | tf_op jit(solution)/shard_map/ppermute | solution.py:460
  93.6 1.8 %scale.2 = (bf16[5,128,1024]{2,1,0:T(8,128)(2,1)S(1)}, f32[5,8,128]{2,1,0:T(8,128)S(1)}) custom-call(bf16[2,128,512]{2,1,0:T(8,128)(2,1)S(1)} %hold.1.refs_0_, bf16[2,128,512]{2,1,0:T(8,128)(2,1)S(1)} %collective-permute-done.6.refs_1_, bf16[2,128,512]{2,1,0:T(8,128)(2,1)S(1)} %collective-permute-done.7.refs_2_, ...), custom_call_target="tpu_custom_call" | custom-call | flops 20971520 | bytes 2621440 | tf_op jit(solution)/shard_map/scale/pallas_call | solution.py:353
  95.4 8.0 %collective-permute-done.11.refs_1_ = bf16[2,128,512]{2,1,0:T(8,128)(2,1)S(1)} collective-permute-done((bf16[2,128,512]{2,1,0:T(8,128)(2,1)}, bf16[2,128,512]{2,1,0:T(8,128)(2,1)S(1)}, u32[]{:S(2)}, u32[]{:S(2)}) %collective-permute-start.11) | collective-permute-done | bytes 262176 | tf_op jit(solution)/shard_map/ppermute | solution.py:462
  103.4 0.0 collective-permute-done.12.refs_2_
  103.4 0.6 scale.3
  103.9 2.2 %mlp.5 = (bf16[2,1376,128]{2,1,0:T(8,128)(2,1)S(1)}, s32[8]{0:T(128)S(1)}) custom-call(s32[8]{0:T(128)S(1)} %fusion.5.idx_ref, bf16[5,128,1024]{2,1,0:T(8,128)(2,1)S(1)} %get-tuple-element.36.refs_0_, f32[5,8,128]{2,1,0:T(8,128)S(1)} %get-tuple-element.37.refs_1_, bf16[3,128,1024]{2,1,0:T(8,128)(2,1)S(1)} %get-tuple-element.38.refs_2_, ...), custom_call_target="tpu_custom_call" | custom-call | flops 100000000 | bytes 524288 | tf_op jit(solution)/shard_map/mlp/pallas_call | solution.py:371
  106.2 1.4 collective-permute-start.16
  107.6 2.3 %mlp.6 = (bf16[2,1376,128]{2,1,0:T(8,128)(2,1)S(1)}, bf16[2,1376,128]{2,1,0:T(8,128)(2,1)S(1)}, s32[8]{0:T(128)S(1)}) custom-call(s32[8]{0:T(128)S(1)} %get-tuple-element.44.idx_ref, bf16[5,128,1024]{2,1,0:T(8,128)(2,1)S(1)} %get-tuple-element.36.refs_0_, f32[5,8,128]{2,1,0:T(8,128)S(1)} %get-tuple-element.37.refs_1_, ...), custom_call_target="tpu_custom_call" | custom-call | flops 100000000 | bytes 524288 | tf_op jit(solution)/shard_map/mlp/pallas_call | solution.py:371
  109.9 1.9 %collective-permute-start.13 = (bf16[2,1376,128]{2,1,0:T(8,128)(2,1)S(1)}, bf16[2,1376,128]{2,1,0:T(8,128)(2,1)S(1)}, u32[]{:S(2)}, u32[]{:S(2)}) collective-permute-start(bf16[2,1376,128]{2,1,0:T(8,128)(2,1)S(1)} %get-tuple-element.50), channel_id=1, source_target_pairs={{0,2},{1,3},{2,4},{3,5},{4,6},{5,7},{6,0},{7,1},{8,10},{9,11},{10,... | collective-permute-start | bytes 2113544 | tf_op jit(solution)/shard_map/ppermute | solution.py:46
  111.8 0.2 collective-permute-start.14
  112.1 2.3 %mlp.7 = (bf16[1376,128]{1,0:T(8,128)(2,1)S(1)}, bf16[1376,128]{1,0:T(8,128)(2,1)S(1)}, bf16[1376,128]{1,0:T(8,128)(2,1)S(1)}, bf16[1376,128]{1,0:T(8,128)(2,1)S(1)}, s32[8]{0:T(128)S(1)}) custom-call(s32[8]{0:T(128)S(1)} %get-tuple-element.45.idx_ref, bf16[5,128,1024]{2,1,0:T(8,128)(2,1)S(1)} %get-tuple-element.36.refs_0_, ...), custom_call_target="tpu_custom_call" | custom-call | flops 100000000 | bytes 524288 | tf_op jit(solution)/shard_map/mlp/pallas_call | solution.py:371
  114.4 2.3 %mlp.8 = (bf16[2,1376,128]{2,1,0:T(8,128)(2,1)S(1)}, bf16[2,1376,128]{2,1,0:T(8,128)(2,1)S(1)}, s32[8]{0:T(128)S(1)}) custom-call(s32[8]{0:T(128)S(1)} %get-tuple-element.46.idx_ref, bf16[5,128,1024]{2,1,0:T(8,128)(2,1)S(1)} %get-tuple-element.36.refs_0_, f32[5,8,128]{2,1,0:T(8,128)S(1)} %get-tuple-element.37.refs_1_, ...), custom_call_target="tpu_custom_call" | custom-call | flops 100000000 | bytes 524288 | tf_op jit(solution)/shard_map/mlp/pallas_call | solution.py:371
  116.7 8.9 %collective-permute-done.16.right_ref = bf16[2,1376,128]{2,1,0:T(8,128)(2,1)S(1)} collective-permute-done((bf16[2,1376,128]{2,1,0:T(8,128)(2,1)S(1)}, bf16[2,1376,128]{2,1,0:T(8,128)(2,1)S(1)}, u32[]{:S(2)}, u32[]{:S(2)}) %collective-permute-start.16) | collective-permute-done | bytes 704544 | tf_op jit(solution)/shard_map/ppermute | solution.py:46
  125.6 0.2 sum.5
  125.8 1.4 collective-permute-start.17
  127.2 0.7 collective-permute-start.21
  127.9 2.6 %collective-permute-done.14.refs_2_ = bf16[2,1376,128]{2,1,0:T(8,128)(2,1)S(1)} collective-permute-done((bf16[2,1376,128]{2,1,0:T(8,128)(2,1)S(1)}, bf16[2,1376,128]{2,1,0:T(8,128)(2,1)S(1)}, u32[]{:S(2)}, u32[]{:S(2)}) %collective-permute-start.14) | collective-permute-done | bytes 704544 | tf_op jit(solution)/shard_map/ppermute | solution.py:46
  130.5 0.3 sum.4
  130.7 1.8 %collective-permute-start.15 = (bf16[2,1376,128]{2,1,0:T(8,128)(2,1)S(1)}, bf16[2,1376,128]{2,1,0:T(8,128)(2,1)S(1)}, u32[]{:S(2)}, u32[]{:S(2)}) collective-permute-start(bf16[2,1376,128]{2,1,0:T(8,128)(2,1)S(1)} %sum.4), channel_id=1, source_target_pairs={{0,8},{1,9},{2,10},{3,11},{4,12},{5,13},{6,14},{7,15},{8,0},{9,1},... | collective-permute-start | bytes 2113544 | tf_op jit(solution)/shard_map/ppermute | solution.py:46
  132.5 3.2 %collective-permute-start.20 = (bf16[1376,128]{1,0:T(8,128)(2,1)S(1)}, bf16[1376,128]{1,0:T(8,128)(2,1)S(1)}, u32[]{:S(2)}, u32[]{:S(2)}) collective-permute-start(bf16[1376,128]{1,0:T(8,128)(2,1)S(1)} %get-tuple-element.57), channel_id=1, source_target_pairs={{0,2},{1,3},{2,4},{3,5},{4,6},{5,7},{6,0},{7,1},{8,10},{9,11},{10,... | collective-permute-start | bytes 1056776 | tf_op jit(solution)/shard_map/ppermute | solution.py:46
  135.7 1.3 collective-permute-done.17.refs_1_
  137.0 0.1 sum.6
  137.1 1.7 %collective-permute-start.18 = (bf16[1376,128]{1,0:T(8,128)(2,1)S(1)}, bf16[1376,128]{1,0:T(8,128)(2,1)S(1)}, u32[]{:S(2)}, u32[]{:S(2)}) collective-permute-start(bf16[1376,128]{1,0:T(8,128)(2,1)S(1)} %sum.6), channel_id=1, source_target_pairs={{0,2},{1,3},{2,4},{3,5},{4,6},{5,7},{6,0},{7,1},{8,10},{9,11},{10,... | collective-permute-start | bytes 1056776 | tf_op jit(solution)/shard_map/ppermute | solution.py:46
  138.8 0.7 collective-permute-done.21.refs_1_
  139.6 0.1 sum.7
  139.6 0.1 collective-permute-start.22
  139.7 2.2 %mlp.9 = (bf16[2,1376,128]{2,1,0:T(8,128)(2,1)S(1)}, s32[8]{0:T(128)}) custom-call(s32[8]{0:T(128)S(1)} %get-tuple-element.47.idx_ref, bf16[5,128,1024]{2,1,0:T(8,128)(2,1)S(1)} %get-tuple-element.36.refs_0_, f32[5,8,128]{2,1,0:T(8,128)S(1)} %get-tuple-element.37.refs_1_, bf16[3,128,1024]{2,1,0:T(8,128)(2,1)S(1)} %get-tuple-element.38.refs_2_, ...), custom_call_target="tpu_custom_call" | custom-call | flops 100000000 | bytes 524288 | tf_op jit(solution)/shard_map/mlp/pallas_call | solution.py:371
  142.0 5.1 %collective-permute-done.19.gate_3_ref = bf16[1376,128]{1,0:T(8,128)(2,1)S(1)} collective-permute-done((bf16[1376,128]{1,0:T(8,128)(2,1)S(1)}, bf16[1376,128]{1,0:T(8,128)(2,1)S(1)}, u32[]{:S(2)}, u32[]{:S(2)}) %collective-permute-start.19) | collective-permute-done | bytes 352288 | tf_op jit(solution)/shard_map/ppermute | solution.py:46
  147.1 3.3 %collective-permute-done.18.gate_1_ref = bf16[1376,128]{1,0:T(8,128)(2,1)S(1)} collective-permute-done((bf16[1376,128]{1,0:T(8,128)(2,1)S(1)}, bf16[1376,128]{1,0:T(8,128)(2,1)S(1)}, u32[]{:S(2)}, u32[]{:S(2)}) %collective-permute-start.18) | collective-permute-done | bytes 352288 | tf_op jit(solution)/shard_map/ppermute | solution.py:46
  150.4 2.5 %collective-permute-done.22.up_3_ref = bf16[1376,128]{1,0:T(8,128)(2,1)S(1)} collective-permute-done((bf16[1376,128]{1,0:T(8,128)(2,1)S(1)}, bf16[1376,128]{1,0:T(8,128)(2,1)S(1)}, u32[]{:S(2)}, u32[]{:S(2)}) %collective-permute-start.22) | collective-permute-done | bytes 352288 | tf_op jit(solution)/shard_map/ppermute | solution.py:46
  152.9 1.3 finish.1
  (19 shorter events, 0.1 us)
Async XLA Ops:
  0.6 23.5 %copy-start.2 = (bf16[128,1024]{1,0:T(8,128)(2,1)S(1)}, bf16[128,1024]{1,0:T(8,128)(2,1)}, u32[]{:S(2)}) copy-start(bf16[128,1024]{1,0:T(8,128)(2,1)} %constant.165.clone.tab_ref) | copy-start | bytes 786436
  0.6 11.5 %copy-start.4 = (f32[512]{0:T(512)S(1)}, f32[512]{0:T(512)}, u32[]{:S(2)}) copy-start(f32[512]{0:T(512)} %param.14) | copy-start | bytes 6148
  2.6 21.5 %all-to-all-start = ((bf16[16,64,128]{2,1,0:T(8,128)(2,1)}), bf16[16,64,128]{2,1,0:T(8,128)(2,1)S(1)}, u32[]{:S(2)}, u32[]{:S(2)}) async-start(bf16[16,64,128]{2,1,0:T(8,128)(2,1)} %prep.1), calls=%async_computation | async-start | bytes 524288 | tf_op jit(solution)/shard_map/all_to_all | solution.py:419
  12.1 1.2 collective-permute-start
  38.6 9.3 %copy-start.1 = (bf16[512,1368]{0,1:T(8,128)(2,1)S(1)}, bf16[512,1368]{0,1:T(8,128)(2,1)}, u32[]{:S(2)}) copy-start(bf16[512,1368]{0,1:T(8,128)(2,1)} %param.16) | copy-start | bytes 4202500
  40.9 7.0 %copy-start = (bf16[512,1368]{0,1:T(8,128)(2,1)S(1)}, bf16[512,1368]{0,1:T(8,128)(2,1)}, u32[]{:S(2)}) copy-start(bf16[512,1368]{0,1:T(8,128)(2,1)} %param.15) | copy-start | bytes 4202500
  40.9 18.6 %copy-start.3 = (bf16[128,512]{1,0:T(8,128)(2,1)S(1)}, bf16[128,512]{1,0:T(8,128)(2,1)}, u32[]{:S(2)}) copy-start(bf16[128,512]{1,0:T(8,128)(2,1)} %start_ref.1) | copy-start | bytes 393220
  40.9 18.6 %all-to-all-start.2 = ((bf16[8,128,512]{2,1,0:T(8,128)(2,1)}), bf16[8,128,512]{2,1,0:T(8,128)(2,1)}, u32[]{:S(2)}, u32[]{:S(2)}) async-start(bf16[8,128,512]{2,1,0:T(8,128)(2,1)} %mix.1), calls=%async_computation.2 | async-start | bytes 2097152 | tf_op jit(solution)/shard_map/all_to_all | solution.py:440
  47.9 18.2 %collective-permute-start.2 = (bf16[1368,512]{1,0:T(8,128)(2,1)S(1)}, bf16[1368,512]{1,0:T(8,128)(2,1)}, u32[]{:S(2)}, u32[]{:S(2)}) collective-permute-start(bf16[1368,512]{1,0:T(8,128)(2,1)S(1)} %bitcast.18), channel_id=1, source_target_pairs={{0,1},{1,0},{2,3},{3,2},{4,5},{5,4},{6,7},{7,6},{8,9},{9,8},{10,11... | collective-permute-start | bytes 4202504 | tf_op jit(solution)/shard_map/ppermute | solution.py:46
  47.9 18.2 %collective-permute-start.3 = (bf16[1368,512]{1,0:T(8,128)(2,1)S(1)}, bf16[1368,512]{1,0:T(8,128)(2,1)}, u32[]{:S(2)}, u32[]{:S(2)}) collective-permute-start(bf16[1368,512]{1,0:T(8,128)(2,1)S(1)} %bitcast.20), channel_id=1, source_target_pairs={{0,1},{1,0},{2,3},{3,2},{4,5},{5,4},{6,7},{7,6},{8,9},{9,8},{10,11... | collective-permute-start | bytes 4202504 | tf_op jit(solution)/shard_map/ppermute | solution.py:46
  59.5 3.0 %collective-permute-start.1 = (bf16[8,128,512]{2,1,0:T(8,128)(2,1)}, bf16[8,128,512]{2,1,0:T(8,128)(2,1)}, u32[]{:S(2)}, u32[]{:S(2)}) collective-permute-start(bf16[8,128,512]{2,1,0:T(8,128)(2,1)} %all-to-all-done.2.mixed_hbm), channel_id=1, source_target_pairs={{0,1},{1,0},{2,3},{3,2},{4,5},{5,4},{6,7},{7,6},{8,9},{9,8},{10,11... | collective-permute-start | bytes 3145736 | tf_op jit(solution)/shard_map/ppermute | solution.py:46
  66.1 3.5 %collective-permute-start.5 = (bf16[128,512]{1,0:T(8,128)(2,1)S(1)}, bf16[128,512]{1,0:T(8,128)(2,1)S(1)}, u32[]{:S(2)}, u32[]{:S(2)}) collective-permute-start(bf16[128,512]{1,0:T(8,128)(2,1)S(1)} %get-tuple-element.34.stream_ref), channel_id=1, source_target_pairs={{0,16},{1,0},{2,18},{3,2},{4,20},{5,4},{6,22},{7,6},{8,24},{9,8},{... | collective-permute-start | bytes 393224 | tf_op jit(solution)/shard_map/ppermute | solution.py:449
  67.1 2.5 %collective-permute-start.4 = (bf16[128,512]{1,0:T(8,128)(2,1)S(1)}, bf16[128,512]{1,0:T(8,128)(2,1)S(1)}, u32[]{:S(2)}, u32[]{:S(2)}) collective-permute-start(bf16[128,512]{1,0:T(8,128)(2,1)S(1)} %get-tuple-element.34.stream_ref), channel_id=1, source_target_pairs={{1,16},{3,18},{5,20},{7,22},{9,24},{11,26},{13,28},{15,30},{16,1},... | collective-permute-start | bytes 393224 | tf_op jit(solution)/shard_map/ppermute | solution.py:450
  69.6 9.1 %collective-permute-start.8 = (bf16[2,128,512]{2,1,0:T(8,128)(2,1)S(1)}, bf16[2,128,512]{2,1,0:T(8,128)(2,1)S(1)}, u32[]{:S(2)}, u32[]{:S(2)}) collective-permute-start(bf16[2,128,512]{2,1,0:T(8,128)(2,1)S(1)} %hold.1.refs_0_), channel_id=1, source_target_pairs={{0,64},{1,65},{2,66},{3,67},{4,68},{5,69},{6,70},{7,71},{8,72},{9,... | collective-permute-start | bytes 786440 | tf_op jit(solution)/shard_map/ppermute | solution.py:457
  70.1 14.4 %collective-permute-start.9 = (bf16[2,128,512]{2,1,0:T(8,128)(2,1)S(1)}, bf16[2,128,512]{2,1,0:T(8,128)(2,1)}, u32[]{:S(2)}, u32[]{:S(2)}) collective-permute-start(bf16[2,128,512]{2,1,0:T(8,128)(2,1)S(1)} %hold.1.refs_0_), channel_id=1, source_target_pairs={{0,192},{1,193},{2,194},{3,195},{4,196},{5,197},{6,198},{7,199},{8... | collective-permute-start | bytes 786440 | tf_op jit(solution)/shard_map/ppermute | solution.py:458
  73.9 19.7 %collective-permute-start.7 = (bf16[2,128,512]{2,1,0:T(8,128)(2,1)S(1)}, bf16[2,128,512]{2,1,0:T(8,128)(2,1)S(1)}, u32[]{:S(2)}, u32[]{:S(2)}) collective-permute-start(bf16[2,128,512]{2,1,0:T(8,128)(2,1)S(1)} %hold.1.refs_0_), channel_id=1, source_target_pairs={{0,224},{1,225},{2,226},{3,227},{4,228},{5,229},{6,230},{7,231},{8... | collective-permute-start | bytes 786440 | tf_op jit(solution)/shard_map/ppermute | solution.py:460
  74.0 19.6 %collective-permute-start.6 = (bf16[2,128,512]{2,1,0:T(8,128)(2,1)S(1)}, bf16[2,128,512]{2,1,0:T(8,128)(2,1)S(1)}, u32[]{:S(2)}, u32[]{:S(2)}) collective-permute-start(bf16[2,128,512]{2,1,0:T(8,128)(2,1)S(1)} %hold.1.refs_0_), channel_id=1, source_target_pairs={{0,32},{1,33},{2,34},{3,35},{4,36},{5,37},{6,38},{7,39},{8,40},{9,... | collective-permute-start | bytes 786440 | tf_op jit(solution)/shard_map/ppermute | solution.py:459
  78.7 24.7 %collective-permute-start.12 = (bf16[2,128,512]{2,1,0:T(8,128)(2,1)S(1)}, bf16[2,128,512]{2,1,0:T(8,128)(2,1)S(1)}, u32[]{:S(2)}, u32[]{:S(2)}) collective-permute-start(bf16[2,128,512]{2,1,0:T(8,128)(2,1)S(1)} %collective-permute-done.8.refs_3_), channel_id=1, source_target_pairs={{0,64},{1,65},{2,66},{3,67},{4,68},{5,69},{6,70},{7,71},{8,72},{9,... | collective-permute-start | bytes 786440 | tf_op jit(solution)/shard_map/ppermute | solution.py:463
  78.7 24.7 %collective-permute-start.10 = (bf16[2,128,512]{2,1,0:T(8,128)(2,1)S(1)}, bf16[2,128,512]{2,1,0:T(8,128)(2,1)S(1)}, u32[]{:S(2)}, u32[]{:S(2)}) collective-permute-start(bf16[2,128,512]{2,1,0:T(8,128)(2,1)S(1)} %collective-permute-done.8.refs_3_), channel_id=1, source_target_pairs={{0,32},{1,33},{2,34},{3,35},{4,36},{5,37},{6,38},{7,39},{8,40},{9,... | collective-permute-start | bytes 786440 | tf_op jit(solution)/shard_map/ppermute | solution.py:461
  84.5 18.9 %collective-permute-start.11 = (bf16[2,128,512]{2,1,0:T(8,128)(2,1)}, bf16[2,128,512]{2,1,0:T(8,128)(2,1)S(1)}, u32[]{:S(2)}, u32[]{:S(2)}) collective-permute-start(bf16[2,128,512]{2,1,0:T(8,128)(2,1)} %collective-permute-done.9.refs_4_), channel_id=1, source_target_pairs={{0,224},{1,225},{2,226},{3,227},{4,228},{5,229},{6,230},{7,231},{8... | collective-permute-start | bytes 786440 | tf_op jit(solution)/shard_map/ppermute | solution.py:462
  106.2 19.4 %collective-permute-start.16 = (bf16[2,1376,128]{2,1,0:T(8,128)(2,1)S(1)}, bf16[2,1376,128]{2,1,0:T(8,128)(2,1)S(1)}, u32[]{:S(2)}, u32[]{:S(2)}) collective-permute-start(bf16[2,1376,128]{2,1,0:T(8,128)(2,1)S(1)} %get-tuple-element.54), channel_id=1, source_target_pairs={{0,8},{1,9},{2,10},{3,11},{4,12},{5,13},{6,14},{7,15},{8,0},{9,1},... | collective-permute-start | bytes 2113544 | tf_op jit(solution)/shard_map/ppermute | solution.py:46
  109.9 17.9 %collective-permute-start.13 = (bf16[2,1376,128]{2,1,0:T(8,128)(2,1)S(1)}, bf16[2,1376,128]{2,1,0:T(8,128)(2,1)S(1)}, u32[]{:S(2)}, u32[]{:S(2)}) collective-permute-start(bf16[2,1376,128]{2,1,0:T(8,128)(2,1)S(1)} %get-tuple-element.50), channel_id=1, source_target_pairs={{0,2},{1,3},{2,4},{3,5},{4,6},{5,7},{6,0},{7,1},{8,10},{9,11},{10,... | collective-permute-start | bytes 2113544 | tf_op jit(solution)/shard_map/ppermute | solution.py:46
  111.8 18.7 %collective-permute-start.14 = (bf16[2,1376,128]{2,1,0:T(8,128)(2,1)S(1)}, bf16[2,1376,128]{2,1,0:T(8,128)(2,1)S(1)}, u32[]{:S(2)}, u32[]{:S(2)}) collective-permute-start(bf16[2,1376,128]{2,1,0:T(8,128)(2,1)S(1)} %get-tuple-element.51), channel_id=1, source_target_pairs={{0,6},{1,7},{2,0},{3,1},{4,2},{5,3},{6,4},{7,5},{8,14},{9,15},{10,... | collective-permute-start | bytes 2113544 | tf_op jit(solution)/shard_map/ppermute | solution.py:46
  125.8 11.3 %collective-permute-start.17 = (bf16[1376,128]{1,0:T(8,128)(2,1)S(1)}, bf16[1376,128]{1,0:T(8,128)(2,1)S(1)}, u32[]{:S(2)}, u32[]{:S(2)}) collective-permute-start(bf16[1376,128]{1,0:T(8,128)(2,1)S(1)} %get-tuple-element.55), channel_id=1, source_target_pairs={{0,2},{1,3},{2,4},{3,5},{4,6},{5,7},{6,0},{7,1},{8,10},{9,11},{10,... | collective-permute-start | bytes 1056776 | tf_op jit(solution)/shard_map/ppermute | solution.py:46
  127.2 12.4 %collective-permute-start.21 = (bf16[1376,128]{1,0:T(8,128)(2,1)S(1)}, bf16[1376,128]{1,0:T(8,128)(2,1)S(1)}, u32[]{:S(2)}, u32[]{:S(2)}) collective-permute-start(bf16[1376,128]{1,0:T(8,128)(2,1)S(1)} %get-tuple-element.59), channel_id=1, source_target_pairs={{0,6},{1,7},{2,0},{3,1},{4,2},{5,3},{6,4},{7,5},{8,14},{9,15},{10,... | collective-permute-start | bytes 1056776 | tf_op jit(solution)/shard_map/ppermute | solution.py:46
  130.7 22.2 %collective-permute-start.15 = (bf16[2,1376,128]{2,1,0:T(8,128)(2,1)S(1)}, bf16[2,1376,128]{2,1,0:T(8,128)(2,1)S(1)}, u32[]{:S(2)}, u32[]{:S(2)}) collective-permute-start(bf16[2,1376,128]{2,1,0:T(8,128)(2,1)S(1)} %sum.4), channel_id=1, source_target_pairs={{0,8},{1,9},{2,10},{3,11},{4,12},{5,13},{6,14},{7,15},{8,0},{9,1},... | collective-permute-start | bytes 2113544 | tf_op jit(solution)/shard_map/ppermute | solution.py:46
  132.5 14.6 %collective-permute-start.19 = (bf16[1376,128]{1,0:T(8,128)(2,1)S(1)}, bf16[1376,128]{1,0:T(8,128)(2,1)S(1)}, u32[]{:S(2)}, u32[]{:S(2)}) collective-permute-start(bf16[1376,128]{1,0:T(8,128)(2,1)S(1)} %get-tuple-element.56), channel_id=1, source_target_pairs={{0,6},{1,7},{2,0},{3,1},{4,2},{5,3},{6,4},{7,5},{8,14},{9,15},{10,... | collective-permute-start | bytes 1056776 | tf_op jit(solution)/shard_map/ppermute | solution.py:46
  132.5 14.6 %collective-permute-start.20 = (bf16[1376,128]{1,0:T(8,128)(2,1)S(1)}, bf16[1376,128]{1,0:T(8,128)(2,1)S(1)}, u32[]{:S(2)}, u32[]{:S(2)}) collective-permute-start(bf16[1376,128]{1,0:T(8,128)(2,1)S(1)} %get-tuple-element.57), channel_id=1, source_target_pairs={{0,2},{1,3},{2,4},{3,5},{4,6},{5,7},{6,0},{7,1},{8,10},{9,11},{10,... | collective-permute-start | bytes 1056776 | tf_op jit(solution)/shard_map/ppermute | solution.py:46
  137.1 13.3 %collective-permute-start.18 = (bf16[1376,128]{1,0:T(8,128)(2,1)S(1)}, bf16[1376,128]{1,0:T(8,128)(2,1)S(1)}, u32[]{:S(2)}, u32[]{:S(2)}) collective-permute-start(bf16[1376,128]{1,0:T(8,128)(2,1)S(1)} %sum.6), channel_id=1, source_target_pairs={{0,2},{1,3},{2,4},{3,5},{4,6},{5,7},{6,0},{7,1},{8,10},{9,11},{10,... | collective-permute-start | bytes 1056776 | tf_op jit(solution)/shard_map/ppermute | solution.py:46
  139.6 13.3 %collective-permute-start.22 = (bf16[1376,128]{1,0:T(8,128)(2,1)S(1)}, bf16[1376,128]{1,0:T(8,128)(2,1)S(1)}, u32[]{:S(2)}, u32[]{:S(2)}) collective-permute-start(bf16[1376,128]{1,0:T(8,128)(2,1)S(1)} %sum.7), channel_id=1, source_target_pairs={{0,6},{1,7},{2,0},{3,1},{4,2},{5,3},{6,4},{7,5},{8,14},{9,15},{10,... | collective-permute-start | bytes 1056776 | tf_op jit(solution)/shard_map/ppermute | solution.py:46

commit v13 on v12

--- a/solution.py
+++ b/solution.py
@@ -475,8 +475,7 @@
 
     weights = (gate_w, up_w)
     both, half = (2, FF_PAD, ROWS), (FF_PAD, ROWS)
-    (two_far,), then = mlp_part((5,), idx, rows, weights)
-    (one_far, three_far), then = mlp_part((3, 7), then, rows, weights)
+    (two_far, one_far, three_far), then = mlp_part((5, 3, 7), idx, rows, weights)
     near, then = mlp_part((2, 6), then, rows, weights, split=True)
     (two_near, own_far), then = mlp_part((4, 1), then, rows, weights)
     (own_near,), _ = mlp_part((0,), then, rows, weights)

time: 155 us -> 156 us (level)
    pallas_call x5 -> x4, Pallas kernels: 11.4 us -> 10.6 us  [mlp_part(): pl.pallas_call(functools.partial(mlp_kernel, slots, split), out_shape=[ja...]
  transfers between devices with their start and end apart: 25 -> 25, of which waited for: 16 -> 14; matrix products, arithmetic and copies ran while one was open for 0% -> 0% of each run, Pallas kernels for 13% -> 12%
where the time goes in v13:
time: 156 us; the launch traced here: 155 us
  waiting for transfers between devices  72.9 us (47%)
  starting transfers between devices  39 us (25%)
  Pallas kernels  29.7 us (19%)
  blocking collectives  12.9 us (8%)
    ppermute x14, waiting for transfers between devices, shift(): return lax.ppermute(arr, AXES, pairs)  26.9 us
    ppermute x14, starting transfers between devices, shift(): return lax.ppermute(arr, AXES, pairs)  13.9 us
    all_to_all x1, blocking collectives, shards(): conv_rows = lax.all_to_all(conv, 'ctx', 0, 0, tiled=True)  12.9 us
    all_to_all x1, waiting for transfers between devices, shards(): lax.all_to_all(copies, 'tp', 0, 0, axis_index_groups=PLANE_GROUPS, tiled=...  11.1 us
    all_to_all x1, waiting for transfers between devices, shards(): recv = lax.all_to_all(sent, 'ctx', 0, 0, tiled=True)  10.8 us
    pallas_call x4, Pallas kernels, mlp_part(): pl.pallas_call(functools.partial(mlp_kernel, slots, split), out_shape=[ja...  10.6 us
    all_to_all x1, starting transfers between devices, shards(): recv = lax.all_to_all(sent, 'ctx', 0, 0, tiled=True)  9.5 us
    ppermute x1, waiting for transfers between devices, shards(): lax.ppermute(two_second, AXES, pairs_of(functools.partial(along, -1)))  7.97 us
  transfers between devices with their start and end apart: 25, of which 14 were waited for; matrix products, arithmetic and copies ran while one was open for 0% of the time, Pallas kernels for 12%

profile of v13, /device:TPU:24, one launch (start us, length us, event | category | flops | bytes accessed | tf_op | source)
XLA Modules:
  0.0 155.4 jit_solution(10864667348462576645)
XLA Ops:
  0.6 0.0 copy-start.2
  0.7 2.0 %prep.1 = bf16[16,64,128]{2,1,0:T(8,128)(2,1)} custom-call(bf16[3,128,512]{2,1,0:T(8,128)(2,1)} %bitcast.25, f32[128,512]{1,0:T(8,128)} %filt_ref.1), custom_call_target="tpu_custom_call" | custom-call | tf_op jit(solution)/shard_map/prep/pallas_call | solution.py:413
  2.6 9.5 %all-to-all-start = ((bf16[16,64,128]{2,1,0:T(8,128)(2,1)}), bf16[16,64,128]{2,1,0:T(8,128)(2,1)S(1)}, u32[]{:S(2)}, u32[]{:S(2)}) async-start(bf16[16,64,128]{2,1,0:T(8,128)(2,1)} %prep.1), calls=%async_computation | async-start | bytes 524288 | tf_op jit(solution)/shard_map/all_to_all | solution.py:419
  12.1 0.1 collective-permute-start
  12.2 1.1 collective-permute-done.refs_6_.refs_4_
  13.4 10.8 %all-to-all-done.x_ref = bf16[16,64,128]{2,1,0:T(8,128)(2,1)S(1)} async-done(((bf16[16,64,128]{2,1,0:T(8,128)(2,1)}), bf16[16,64,128]{2,1,0:T(8,128)(2,1)S(1)}, u32[]{:S(2)}, u32[]{:S(2)}) %all-to-all-start) | async-done | bytes 262176 | tf_op jit(solution)/shard_map/all_to_all | solution.py:419
  24.2 1.5 conv.1
  25.6 12.9 %all_to_all.15.conv_ref = bf16[16,32,128]{2,1,0:T(8,128)(2,1)} all-to-all(bf16[16,32,128]{2,1,0:T(8,128)(2,1)S(1)} %conv.1), channel_id=1, replica_groups=mesh['ctx'=16,'tp'=16] {'ctx'}, dimensions={0} | all-to-all | bytes 262144 | tf_op jit(solution)/shard_map/all_to_all | solution.py:432
  38.6 2.3 %mix.1 = bf16[8,128,512]{2,1,0:T(8,128)(2,1)} custom-call(bf16[16,32,128]{2,1,0:T(8,128)(2,1)} %all_to_all.15.conv_ref, bf16[3,128,512]{2,1,0:T(8,128)(2,1)} %bitcast.26, f32[1,512]{1,0:T(1,128)} %bitcast.28), custom_call_target="tpu_custom_call" | custom-call | tf_op jit(solution)/shard_map/mix/pallas_call | solution.py:433
  40.9 7.0 %all-to-all-start.2 = ((bf16[8,128,512]{2,1,0:T(8,128)(2,1)}), bf16[8,128,512]{2,1,0:T(8,128)(2,1)}, u32[]{:S(2)}, u32[]{:S(2)}) async-start(bf16[8,128,512]{2,1,0:T(8,128)(2,1)} %mix.1), calls=%async_computation.2 | async-start | bytes 2097152 | tf_op jit(solution)/shard_map/all_to_all | solution.py:440
  47.9 0.0 collective-permute-start.2
  47.9 0.5 collective-permute-start.3
  48.4 11.1 %all-to-all-done.2.mixed_hbm = bf16[8,128,512]{2,1,0:T(8,128)(2,1)} async-done(((bf16[8,128,512]{2,1,0:T(8,128)(2,1)}), bf16[8,128,512]{2,1,0:T(8,128)(2,1)}, u32[]{:S(2)}, u32[]{:S(2)}) %all-to-all-start.2) | async-done | bytes 1048608 | tf_op jit(solution)/shard_map/all_to_all | solution.py:440
  59.5 2.9 %out_proj.2.start_ref = f32[128,512]{1,0:T(8,128)S(1)} custom-call(s32[1]{0:T(128)} %bitcast.core_ref, bf16[8,128,512]{2,1,0:T(8,128)(2,1)} %all-to-all-done.2.mixed_hbm, bf16[8192,512]{1,0:T(8,128)(2,1)} %w_hbm.3, bf16[128,512]{1,0:T(8,128)(2,1)S(1)} %copy-done.3), custom_call_target="tpu_custom_call" | custom-call | flops 536870912 | bytes 5242880 | tf_op jit(solution)/shard_map/out_proj/pallas_call | solution.py:301
  62.4 0.1 collective-permute-done.1.mixed_hbm
  62.5 3.5 %out_proj.3 = (bf16[128,512]{1,0:T(8,128)(2,1)}, bf16[128,512]{1,0:T(8,128)(2,1)S(1)}) custom-call(s32[1]{0:T(128)} %bitcast.core_ref, bf16[8,128,512]{2,1,0:T(8,128)(2,1)} %collective-permute-done.1.mixed_hbm, bf16[8192,512]{1,0:T(8,128)(2,1)} %w_hbm.3, f32[128,512]{1,0:T(8,128)S(1)} %out_proj.2.start_ref), custom_call_target="tpu_custom_call" | custom-call | flops 536870912 | bytes 5242880 | tf_op jit(solution)/shard_map/out_proj/pallas_call | solution.py:301
  66.1 0.0 collective-permute-done.3.wux_ref
  66.1 1.0 collective-permute-start.5
  67.1 0.7 collective-permute-start.4
  67.8 1.8 %collective-permute-done.5.first_ref = bf16[128,512]{1,0:T(8,128)(2,1)S(1)} collective-permute-done((bf16[128,512]{1,0:T(8,128)(2,1)S(1)}, bf16[128,512]{1,0:T(8,128)(2,1)S(1)}, u32[]{:S(2)}, u32[]{:S(2)}) %collective-permute-start.5) | collective-permute-done | bytes 131104 | tf_op jit(solution)/shard_map/ppermute | solution.py:449
  69.6 0.0 collective-permute-done.4.second_ref
  69.6 0.5 collective-permute-start.8
  70.1 3.8 %collective-permute-start.9 = (bf16[2,128,512]{2,1,0:T(8,128)(2,1)S(1)}, bf16[2,128,512]{2,1,0:T(8,128)(2,1)}, u32[]{:S(2)}, u32[]{:S(2)}) collective-permute-start(bf16[2,128,512]{2,1,0:T(8,128)(2,1)S(1)} %hold.1.refs_0_), channel_id=1, source_target_pairs={{0,192},{1,193},{2,194},{3,195},{4,196},{5,197},{6,198},{7,199},{8... | collective-permute-start | bytes 786440 | tf_op jit(solution)/shard_map/ppermute | solution.py:458
  73.8 0.1 stack.35
  73.9 0.1 collective-permute-start.7
  74.0 0.0 collective-permute-start.6
  74.1 4.7 %collective-permute-done.8.refs_3_ = bf16[2,128,512]{2,1,0:T(8,128)(2,1)S(1)} collective-permute-done((bf16[2,128,512]{2,1,0:T(8,128)(2,1)S(1)}, bf16[2,128,512]{2,1,0:T(8,128)(2,1)S(1)}, u32[]{:S(2)}, u32[]{:S(2)}) %collective-permute-start.8) | collective-permute-done | bytes 262176 | tf_op jit(solution)/shard_map/ppermute | solution.py:457
  78.7 0.0 collective-permute-start.12
  78.7 1.2 collective-permute-start.10
  80.0 4.6 %collective-permute-done.9.refs_4_ = bf16[2,128,512]{2,1,0:T(8,128)(2,1)} collective-permute-done((bf16[2,128,512]{2,1,0:T(8,128)(2,1)S(1)}, bf16[2,128,512]{2,1,0:T(8,128)(2,1)}, u32[]{:S(2)}, u32[]{:S(2)}) %collective-permute-start.9) | collective-permute-done | bytes 262176 | tf_op jit(solution)/shard_map/ppermute | solution.py:458
  84.5 1.4 collective-permute-start.11
  85.9 2.7 %load.1 = (bf16[1368,1024]{1,0:T(8,128)(2,1)S(1)}, bf16[1368,1024]{1,0:T(8,128)(2,1)S(1)}, bf16[16,512]{1,0:T(8,128)(2,1)}) custom-call(bf16[1368,512]{1,0:T(8,128)(2,1)S(1)} %bitcast.19, bf16[1368,512]{1,0:T(8,128)(2,1)} %collective-permute-done.2.wgx_ref, bf16[1368,512]{1,0:T(8,128)(2,1)S(1)} %bitcast.21, ...), custom_call_target="tpu_custom_call" | custom-call | flops 1 | bytes 12582912 | tf_op jit(solution)/shard_map/load/pallas_call | solution.py:338
  88.6 5.0 %collective-permute-done.7.refs_2_ = bf16[2,128,512]{2,1,0:T(8,128)(2,1)S(1)} collective-permute-done((bf16[2,128,512]{2,1,0:T(8,128)(2,1)S(1)}, bf16[2,128,512]{2,1,0:T(8,128)(2,1)S(1)}, u32[]{:S(2)}, u32[]{:S(2)}) %collective-permute-start.7) | collective-permute-done | bytes 262176 | tf_op jit(solution)/shard_map/ppermute | solution.py:460
  93.6 0.0 collective-permute-done.6.refs_1_
  93.6 1.8 %scale.2 = (bf16[5,128,1024]{2,1,0:T(8,128)(2,1)S(1)}, f32[5,8,128]{2,1,0:T(8,128)S(1)}) custom-call(bf16[2,128,512]{2,1,0:T(8,128)(2,1)S(1)} %hold.1.refs_0_, bf16[2,128,512]{2,1,0:T(8,128)(2,1)S(1)} %collective-permute-done.6.refs_1_, bf16[2,128,512]{2,1,0:T(8,128)(2,1)S(1)} %collective-permute-done.7.refs_2_, ...), custom_call_target="tpu_custom_call" | custom-call | flops 20971520 | bytes 2621440 | tf_op jit(solution)/shard_map/scale/pallas_call | solution.py:353
  95.4 8.0 %collective-permute-done.11.refs_1_ = bf16[2,128,512]{2,1,0:T(8,128)(2,1)S(1)} collective-permute-done((bf16[2,128,512]{2,1,0:T(8,128)(2,1)}, bf16[2,128,512]{2,1,0:T(8,128)(2,1)S(1)}, u32[]{:S(2)}, u32[]{:S(2)}) %collective-permute-start.11) | collective-permute-done | bytes 262176 | tf_op jit(solution)/shard_map/ppermute | solution.py:462
  103.4 0.0 collective-permute-done.12.refs_2_
  103.4 0.0 collective-permute-done.10.refs_0_
  103.4 0.6 scale.3
  104.0 3.8 %mlp.4 = (bf16[2,1376,128]{2,1,0:T(8,128)(2,1)S(1)}, bf16[2,1376,128]{2,1,0:T(8,128)(2,1)S(1)}, bf16[2,1376,128]{2,1,0:T(8,128)(2,1)S(1)}, s32[8]{0:T(128)S(1)}) custom-call(s32[8]{0:T(128)S(1)} %fusion.5.idx_ref, bf16[5,128,1024]{2,1,0:T(8,128)(2,1)S(1)} %get-tuple-element.35.refs_0_, f32[5,8,128]{2,1,0:T(8,128)S(1)} %get-tuple-element.36.refs_1_, ...), custom_call_target="tpu_custom_call" | custom-call | flops 100000000 | bytes 524288 | tf_op jit(solution)/shard_map/mlp/pallas_call | solution.py:371
  107.7 1.4 collective-permute-start.16
  109.2 1.8 %collective-permute-start.13 = (bf16[2,1376,128]{2,1,0:T(8,128)(2,1)S(1)}, bf16[2,1376,128]{2,1,0:T(8,128)(2,1)S(1)}, u32[]{:S(2)}, u32[]{:S(2)}) collective-permute-start(bf16[2,1376,128]{2,1,0:T(8,128)(2,1)S(1)} %get-tuple-element.48), channel_id=1, source_target_pairs={{0,2},{1,3},{2,4},{3,5},{4,6},{5,7},{6,0},{7,1},{8,10},{9,11},{10,... | collective-permute-start | bytes 2113544 | tf_op jit(solution)/shard_map/ppermute | solution.py:46
  111.0 0.2 collective-permute-start.14
  111.2 2.3 %mlp.5 = (bf16[1376,128]{1,0:T(8,128)(2,1)S(1)}, bf16[1376,128]{1,0:T(8,128)(2,1)S(1)}, bf16[1376,128]{1,0:T(8,128)(2,1)S(1)}, bf16[1376,128]{1,0:T(8,128)(2,1)S(1)}, s32[8]{0:T(128)S(1)}) custom-call(s32[8]{0:T(128)S(1)} %get-tuple-element.43.idx_ref, bf16[5,128,1024]{2,1,0:T(8,128)(2,1)S(1)} %get-tuple-element.35.refs_0_, ...), custom_call_target="tpu_custom_call" | custom-call | flops 100000000 | bytes 524288 | tf_op jit(solution)/shard_map/mlp/pallas_call | solution.py:371
  113.5 2.3 %mlp.6 = (bf16[2,1376,128]{2,1,0:T(8,128)(2,1)S(1)}, bf16[2,1376,128]{2,1,0:T(8,128)(2,1)S(1)}, s32[8]{0:T(128)S(1)}) custom-call(s32[8]{0:T(128)S(1)} %get-tuple-element.44.idx_ref, bf16[5,128,1024]{2,1,0:T(8,128)(2,1)S(1)} %get-tuple-element.35.refs_0_, f32[5,8,128]{2,1,0:T(8,128)S(1)} %get-tuple-element.36.refs_1_, ...), custom_call_target="tpu_custom_call" | custom-call | flops 100000000 | bytes 524288 | tf_op jit(solution)/shard_map/mlp/pallas_call | solution.py:371
  115.8 11.3 %collective-permute-done.16.right_ref = bf16[2,1376,128]{2,1,0:T(8,128)(2,1)S(1)} collective-permute-done((bf16[2,1376,128]{2,1,0:T(8,128)(2,1)S(1)}, bf16[2,1376,128]{2,1,0:T(8,128)(2,1)S(1)}, u32[]{:S(2)}, u32[]{:S(2)}) %collective-permute-start.16) | collective-permute-done | bytes 704544 | tf_op jit(solution)/shard_map/ppermute | solution.py:46
  127.1 0.2 sum.5
  127.3 1.4 collective-permute-start.17
  128.7 0.7 collective-permute-start.21
  129.4 0.0 collective-permute-done.13.refs_1_
  129.4 0.3 sum.4
  129.7 1.8 %collective-permute-start.15 = (bf16[2,1376,128]{2,1,0:T(8,128)(2,1)S(1)}, bf16[2,1376,128]{2,1,0:T(8,128)(2,1)S(1)}, u32[]{:S(2)}, u32[]{:S(2)}) collective-permute-start(bf16[2,1376,128]{2,1,0:T(8,128)(2,1)S(1)} %sum.4), channel_id=1, source_target_pairs={{0,8},{1,9},{2,10},{3,11},{4,12},{5,13},{6,14},{7,15},{8,0},{9,1},... | collective-permute-start | bytes 2113544 | tf_op jit(solution)/shard_map/ppermute | solution.py:46
  131.5 0.0 collective-permute-start.19
  131.5 3.2 %collective-permute-start.20 = (bf16[1376,128]{1,0:T(8,128)(2,1)S(1)}, bf16[1376,128]{1,0:T(8,128)(2,1)S(1)}, u32[]{:S(2)}, u32[]{:S(2)}) collective-permute-start(bf16[1376,128]{1,0:T(8,128)(2,1)S(1)} %get-tuple-element.55), channel_id=1, source_target_pairs={{0,2},{1,3},{2,4},{3,5},{4,6},{5,7},{6,0},{7,1},{8,10},{9,11},{10,... | collective-permute-start | bytes 1056776 | tf_op jit(solution)/shard_map/ppermute | solution.py:46
  134.7 3.8 %collective-permute-done.17.refs_1_ = bf16[1376,128]{1,0:T(8,128)(2,1)S(1)} collective-permute-done((bf16[1376,128]{1,0:T(8,128)(2,1)S(1)}, bf16[1376,128]{1,0:T(8,128)(2,1)S(1)}, u32[]{:S(2)}, u32[]{:S(2)}) %collective-permute-start.17) | collective-permute-done | bytes 352288 | tf_op jit(solution)/shard_map/ppermute | solution.py:46
  138.6 0.1 sum.6
  138.6 2.6 %collective-permute-start.18 = (bf16[1376,128]{1,0:T(8,128)(2,1)S(1)}, bf16[1376,128]{1,0:T(8,128)(2,1)S(1)}, u32[]{:S(2)}, u32[]{:S(2)}) collective-permute-start(bf16[1376,128]{1,0:T(8,128)(2,1)S(1)} %sum.6), channel_id=1, source_target_pairs={{0,2},{1,3},{2,4},{3,5},{4,6},{5,7},{6,0},{7,1},{8,10},{9,11},{10,... | collective-permute-start | bytes 1056776 | tf_op jit(solution)/shard_map/ppermute | solution.py:46
  141.3 0.1 sum.7
  141.3 0.1 collective-permute-start.22
  141.4 2.2 %mlp.7 = (bf16[2,1376,128]{2,1,0:T(8,128)(2,1)S(1)}, s32[8]{0:T(128)}) custom-call(s32[8]{0:T(128)S(1)} %get-tuple-element.45.idx_ref, bf16[5,128,1024]{2,1,0:T(8,128)(2,1)S(1)} %get-tuple-element.35.refs_0_, f32[5,8,128]{2,1,0:T(8,128)S(1)} %get-tuple-element.36.refs_1_, bf16[3,128,1024]{2,1,0:T(8,128)(2,1)S(1)} %get-tuple-element.37.refs_2_, ...), custom_call_target="tpu_custom_call" | custom-call | flops 100000000 | bytes 524288 | tf_op jit(solution)/shard_map/mlp/pallas_call | solution.py:371
  143.7 5.0 %collective-permute-done.19.gate_3_ref = bf16[1376,128]{1,0:T(8,128)(2,1)S(1)} collective-permute-done((bf16[1376,128]{1,0:T(8,128)(2,1)S(1)}, bf16[1376,128]{1,0:T(8,128)(2,1)S(1)}, u32[]{:S(2)}, u32[]{:S(2)}) %collective-permute-start.19) | collective-permute-done | bytes 352288 | tf_op jit(solution)/shard_map/ppermute | solution.py:46
  148.6 3.3 %collective-permute-done.18.gate_1_ref = bf16[1376,128]{1,0:T(8,128)(2,1)S(1)} collective-permute-done((bf16[1376,128]{1,0:T(8,128)(2,1)S(1)}, bf16[1376,128]{1,0:T(8,128)(2,1)S(1)}, u32[]{:S(2)}, u32[]{:S(2)}) %collective-permute-start.18) | collective-permute-done | bytes 352288 | tf_op jit(solution)/shard_map/ppermute | solution.py:46
  151.9 2.3 %collective-permute-done.22.up_3_ref = bf16[1376,128]{1,0:T(8,128)(2,1)S(1)} collective-permute-done((bf16[1376,128]{1,0:T(8,128)(2,1)S(1)}, bf16[1376,128]{1,0:T(8,128)(2,1)S(1)}, u32[]{:S(2)}, u32[]{:S(2)}) %collective-permute-start.22) | collective-permute-done | bytes 352288 | tf_op jit(solution)/shard_map/ppermute | solution.py:46
  154.2 1.3 finish.1
  (18 shorter events, 0.1 us)
Async XLA Ops:
  0.6 23.5 %copy-start.2 = (bf16[128,1024]{1,0:T(8,128)(2,1)S(1)}, bf16[128,1024]{1,0:T(8,128)(2,1)}, u32[]{:S(2)}) copy-start(bf16[128,1024]{1,0:T(8,128)(2,1)} %constant.165.clone.tab_ref) | copy-start | bytes 786436
  0.6 11.5 %copy-start.4 = (f32[512]{0:T(512)S(1)}, f32[512]{0:T(512)}, u32[]{:S(2)}) copy-start(f32[512]{0:T(512)} %param.14) | copy-start | bytes 6148
  2.6 21.5 %all-to-all-start = ((bf16[16,64,128]{2,1,0:T(8,128)(2,1)}), bf16[16,64,128]{2,1,0:T(8,128)(2,1)S(1)}, u32[]{:S(2)}, u32[]{:S(2)}) async-start(bf16[16,64,128]{2,1,0:T(8,128)(2,1)} %prep.1), calls=%async_computation | async-start | bytes 524288 | tf_op jit(solution)/shard_map/all_to_all | solution.py:419
  12.1 1.2 collective-permute-start
  38.6 9.3 %copy-start.1 = (bf16[512,1368]{0,1:T(8,128)(2,1)S(1)}, bf16[512,1368]{0,1:T(8,128)(2,1)}, u32[]{:S(2)}) copy-start(bf16[512,1368]{0,1:T(8,128)(2,1)} %param.16) | copy-start | bytes 4202500
  40.9 7.0 %copy-start = (bf16[512,1368]{0,1:T(8,128)(2,1)S(1)}, bf16[512,1368]{0,1:T(8,128)(2,1)}, u32[]{:S(2)}) copy-start(bf16[512,1368]{0,1:T(8,128)(2,1)} %param.15) | copy-start | bytes 4202500
  40.9 18.6 %copy-start.3 = (bf16[128,512]{1,0:T(8,128)(2,1)S(1)}, bf16[128,512]{1,0:T(8,128)(2,1)}, u32[]{:S(2)}) copy-start(bf16[128,512]{1,0:T(8,128)(2,1)} %start_ref.1) | copy-start | bytes 393220
  40.9 18.6 %all-to-all-start.2 = ((bf16[8,128,512]{2,1,0:T(8,128)(2,1)}), bf16[8,128,512]{2,1,0:T(8,128)(2,1)}, u32[]{:S(2)}, u32[]{:S(2)}) async-start(bf16[8,128,512]{2,1,0:T(8,128)(2,1)} %mix.1), calls=%async_computation.2 | async-start | bytes 2097152 | tf_op jit(solution)/shard_map/all_to_all | solution.py:440
  47.9 18.2 %collective-permute-start.2 = (bf16[1368,512]{1,0:T(8,128)(2,1)S(1)}, bf16[1368,512]{1,0:T(8,128)(2,1)}, u32[]{:S(2)}, u32[]{:S(2)}) collective-permute-start(bf16[1368,512]{1,0:T(8,128)(2,1)S(1)} %bitcast.18), channel_id=1, source_target_pairs={{0,1},{1,0},{2,3},{3,2},{4,5},{5,4},{6,7},{7,6},{8,9},{9,8},{10,11... | collective-permute-start | bytes 4202504 | tf_op jit(solution)/shard_map/ppermute | solution.py:46
  47.9 18.2 %collective-permute-start.3 = (bf16[1368,512]{1,0:T(8,128)(2,1)S(1)}, bf16[1368,512]{1,0:T(8,128)(2,1)}, u32[]{:S(2)}, u32[]{:S(2)}) collective-permute-start(bf16[1368,512]{1,0:T(8,128)(2,1)S(1)} %bitcast.20), channel_id=1, source_target_pairs={{0,1},{1,0},{2,3},{3,2},{4,5},{5,4},{6,7},{7,6},{8,9},{9,8},{10,11... | collective-permute-start | bytes 4202504 | tf_op jit(solution)/shard_map/ppermute | solution.py:46
  59.5 3.0 %collective-permute-start.1 = (bf16[8,128,512]{2,1,0:T(8,128)(2,1)}, bf16[8,128,512]{2,1,0:T(8,128)(2,1)}, u32[]{:S(2)}, u32[]{:S(2)}) collective-permute-start(bf16[8,128,512]{2,1,0:T(8,128)(2,1)} %all-to-all-done.2.mixed_hbm), channel_id=1, source_target_pairs={{0,1},{1,0},{2,3},{3,2},{4,5},{5,4},{6,7},{7,6},{8,9},{9,8},{10,11... | collective-permute-start | bytes 3145736 | tf_op jit(solution)/shard_map/ppermute | solution.py:46
  66.1 3.5 %collective-permute-start.5 = (bf16[128,512]{1,0:T(8,128)(2,1)S(1)}, bf16[128,512]{1,0:T(8,128)(2,1)S(1)}, u32[]{:S(2)}, u32[]{:S(2)}) collective-permute-start(bf16[128,512]{1,0:T(8,128)(2,1)S(1)} %get-tuple-element.33.stream_ref), channel_id=1, source_target_pairs={{0,16},{1,0},{2,18},{3,2},{4,20},{5,4},{6,22},{7,6},{8,24},{9,8},{... | collective-permute-start | bytes 393224 | tf_op jit(solution)/shard_map/ppermute | solution.py:449
  67.1 2.5 %collective-permute-start.4 = (bf16[128,512]{1,0:T(8,128)(2,1)S(1)}, bf16[128,512]{1,0:T(8,128)(2,1)S(1)}, u32[]{:S(2)}, u32[]{:S(2)}) collective-permute-start(bf16[128,512]{1,0:T(8,128)(2,1)S(1)} %get-tuple-element.33.stream_ref), channel_id=1, source_target_pairs={{1,16},{3,18},{5,20},{7,22},{9,24},{11,26},{13,28},{15,30},{16,1},... | collective-permute-start | bytes 393224 | tf_op jit(solution)/shard_map/ppermute | solution.py:450
  69.6 9.1 %collective-permute-start.8 = (bf16[2,128,512]{2,1,0:T(8,128)(2,1)S(1)}, bf16[2,128,512]{2,1,0:T(8,128)(2,1)S(1)}, u32[]{:S(2)}, u32[]{:S(2)}) collective-permute-start(bf16[2,128,512]{2,1,0:T(8,128)(2,1)S(1)} %hold.1.refs_0_), channel_id=1, source_target_pairs={{0,64},{1,65},{2,66},{3,67},{4,68},{5,69},{6,70},{7,71},{8,72},{9,... | collective-permute-start | bytes 786440 | tf_op jit(solution)/shard_map/ppermute | solution.py:457
  70.1 14.4 %collective-permute-start.9 = (bf16[2,128,512]{2,1,0:T(8,128)(2,1)S(1)}, bf16[2,128,512]{2,1,0:T(8,128)(2,1)}, u32[]{:S(2)}, u32[]{:S(2)}) collective-permute-start(bf16[2,128,512]{2,1,0:T(8,128)(2,1)S(1)} %hold.1.refs_0_), channel_id=1, source_target_pairs={{0,192},{1,193},{2,194},{3,195},{4,196},{5,197},{6,198},{7,199},{8... | collective-permute-start | bytes 786440 | tf_op jit(solution)/shard_map/ppermute | solution.py:458
  73.9 19.7 %collective-permute-start.7 = (bf16[2,128,512]{2,1,0:T(8,128)(2,1)S(1)}, bf16[2,128,512]{2,1,0:T(8,128)(2,1)S(1)}, u32[]{:S(2)}, u32[]{:S(2)}) collective-permute-start(bf16[2,128,512]{2,1,0:T(8,128)(2,1)S(1)} %hold.1.refs_0_), channel_id=1, source_target_pairs={{0,224},{1,225},{2,226},{3,227},{4,228},{5,229},{6,230},{7,231},{8... | collective-permute-start | bytes 786440 | tf_op jit(solution)/shard_map/ppermute | solution.py:460
  74.0 19.6 %collective-permute-start.6 = (bf16[2,128,512]{2,1,0:T(8,128)(2,1)S(1)}, bf16[2,128,512]{2,1,0:T(8,128)(2,1)S(1)}, u32[]{:S(2)}, u32[]{:S(2)}) collective-permute-start(bf16[2,128,512]{2,1,0:T(8,128)(2,1)S(1)} %hold.1.refs_0_), channel_id=1, source_target_pairs={{0,32},{1,33},{2,34},{3,35},{4,36},{5,37},{6,38},{7,39},{8,40},{9,... | collective-permute-start | bytes 786440 | tf_op jit(solution)/shard_map/ppermute | solution.py:459
  78.7 24.6 %collective-permute-start.12 = (bf16[2,128,512]{2,1,0:T(8,128)(2,1)S(1)}, bf16[2,128,512]{2,1,0:T(8,128)(2,1)S(1)}, u32[]{:S(2)}, u32[]{:S(2)}) collective-permute-start(bf16[2,128,512]{2,1,0:T(8,128)(2,1)S(1)} %collective-permute-done.8.refs_3_), channel_id=1, source_target_pairs={{0,64},{1,65},{2,66},{3,67},{4,68},{5,69},{6,70},{7,71},{8,72},{9,... | collective-permute-start | bytes 786440 | tf_op jit(solution)/shard_map/ppermute | solution.py:463
  78.7 24.6 %collective-permute-start.10 = (bf16[2,128,512]{2,1,0:T(8,128)(2,1)S(1)}, bf16[2,128,512]{2,1,0:T(8,128)(2,1)S(1)}, u32[]{:S(2)}, u32[]{:S(2)}) collective-permute-start(bf16[2,128,512]{2,1,0:T(8,128)(2,1)S(1)} %collective-permute-done.8.refs_3_), channel_id=1, source_target_pairs={{0,32},{1,33},{2,34},{3,35},{4,36},{5,37},{6,38},{7,39},{8,40},{9,... | collective-permute-start | bytes 786440 | tf_op jit(solution)/shard_map/ppermute | solution.py:461
  84.5 18.9 %collective-permute-start.11 = (bf16[2,128,512]{2,1,0:T(8,128)(2,1)}, bf16[2,128,512]{2,1,0:T(8,128)(2,1)S(1)}, u32[]{:S(2)}, u32[]{:S(2)}) collective-permute-start(bf16[2,128,512]{2,1,0:T(8,128)(2,1)} %collective-permute-done.9.refs_4_), channel_id=1, source_target_pairs={{0,224},{1,225},{2,226},{3,227},{4,228},{5,229},{6,230},{7,231},{8... | collective-permute-start | bytes 786440 | tf_op jit(solution)/shard_map/ppermute | solution.py:462
  107.7 19.4 %collective-permute-start.16 = (bf16[2,1376,128]{2,1,0:T(8,128)(2,1)S(1)}, bf16[2,1376,128]{2,1,0:T(8,128)(2,1)S(1)}, u32[]{:S(2)}, u32[]{:S(2)}) collective-permute-start(bf16[2,1376,128]{2,1,0:T(8,128)(2,1)S(1)} %get-tuple-element.52), channel_id=1, source_target_pairs={{0,8},{1,9},{2,10},{3,11},{4,12},{5,13},{6,14},{7,15},{8,0},{9,1},... | collective-permute-start | bytes 2113544 | tf_op jit(solution)/shard_map/ppermute | solution.py:46
  109.2 20.2 %collective-permute-start.13 = (bf16[2,1376,128]{2,1,0:T(8,128)(2,1)S(1)}, bf16[2,1376,128]{2,1,0:T(8,128)(2,1)S(1)}, u32[]{:S(2)}, u32[]{:S(2)}) collective-permute-start(bf16[2,1376,128]{2,1,0:T(8,128)(2,1)S(1)} %get-tuple-element.48), channel_id=1, source_target_pairs={{0,2},{1,3},{2,4},{3,5},{4,6},{5,7},{6,0},{7,1},{8,10},{9,11},{10,... | collective-permute-start | bytes 2113544 | tf_op jit(solution)/shard_map/ppermute | solution.py:46
  111.0 18.5 %collective-permute-start.14 = (bf16[2,1376,128]{2,1,0:T(8,128)(2,1)S(1)}, bf16[2,1376,128]{2,1,0:T(8,128)(2,1)S(1)}, u32[]{:S(2)}, u32[]{:S(2)}) collective-permute-start(bf16[2,1376,128]{2,1,0:T(8,128)(2,1)S(1)} %get-tuple-element.49), channel_id=1, source_target_pairs={{0,6},{1,7},{2,0},{3,1},{4,2},{5,3},{6,4},{7,5},{8,14},{9,15},{10,... | collective-permute-start | bytes 2113544 | tf_op jit(solution)/shard_map/ppermute | solution.py:46
  127.3 11.3 %collective-permute-start.17 = (bf16[1376,128]{1,0:T(8,128)(2,1)S(1)}, bf16[1376,128]{1,0:T(8,128)(2,1)S(1)}, u32[]{:S(2)}, u32[]{:S(2)}) collective-permute-start(bf16[1376,128]{1,0:T(8,128)(2,1)S(1)} %get-tuple-element.53), channel_id=1, source_target_pairs={{0,2},{1,3},{2,4},{3,5},{4,6},{5,7},{6,0},{7,1},{8,10},{9,11},{10,... | collective-permute-start | bytes 1056776 | tf_op jit(solution)/shard_map/ppermute | solution.py:46
  128.7 12.6 %collective-permute-start.21 = (bf16[1376,128]{1,0:T(8,128)(2,1)S(1)}, bf16[1376,128]{1,0:T(8,128)(2,1)S(1)}, u32[]{:S(2)}, u32[]{:S(2)}) collective-permute-start(bf16[1376,128]{1,0:T(8,128)(2,1)S(1)} %get-tuple-element.57), channel_id=1, source_target_pairs={{0,6},{1,7},{2,0},{3,1},{4,2},{5,3},{6,4},{7,5},{8,14},{9,15},{10,... | collective-permute-start | bytes 1056776 | tf_op jit(solution)/shard_map/ppermute | solution.py:46
  129.7 24.5 %collective-permute-start.15 = (bf16[2,1376,128]{2,1,0:T(8,128)(2,1)S(1)}, bf16[2,1376,128]{2,1,0:T(8,128)(2,1)S(1)}, u32[]{:S(2)}, u32[]{:S(2)}) collective-permute-start(bf16[2,1376,128]{2,1,0:T(8,128)(2,1)S(1)} %sum.4), channel_id=1, source_target_pairs={{0,8},{1,9},{2,10},{3,11},{4,12},{5,13},{6,14},{7,15},{8,0},{9,1},... | collective-permute-start | bytes 2113544 | tf_op jit(solution)/shard_map/ppermute | solution.py:46
  131.5 17.2 %collective-permute-start.19 = (bf16[1376,128]{1,0:T(8,128)(2,1)S(1)}, bf16[1376,128]{1,0:T(8,128)(2,1)S(1)}, u32[]{:S(2)}, u32[]{:S(2)}) collective-permute-start(bf16[1376,128]{1,0:T(8,128)(2,1)S(1)} %get-tuple-element.54), channel_id=1, source_target_pairs={{0,6},{1,7},{2,0},{3,1},{4,2},{5,3},{6,4},{7,5},{8,14},{9,15},{10,... | collective-permute-start | bytes 1056776 | tf_op jit(solution)/shard_map/ppermute | solution.py:46
  131.5 17.2 %collective-permute-start.20 = (bf16[1376,128]{1,0:T(8,128)(2,1)S(1)}, bf16[1376,128]{1,0:T(8,128)(2,1)S(1)}, u32[]{:S(2)}, u32[]{:S(2)}) collective-permute-start(bf16[1376,128]{1,0:T(8,128)(2,1)S(1)} %get-tuple-element.55), channel_id=1, source_target_pairs={{0,2},{1,3},{2,4},{3,5},{4,6},{5,7},{6,0},{7,1},{8,10},{9,11},{10,... | collective-permute-start | bytes 1056776 | tf_op jit(solution)/shard_map/ppermute | solution.py:46
  138.6 13.3 %collective-permute-start.18 = (bf16[1376,128]{1,0:T(8,128)(2,1)S(1)}, bf16[1376,128]{1,0:T(8,128)(2,1)S(1)}, u32[]{:S(2)}, u32[]{:S(2)}) collective-permute-start(bf16[1376,128]{1,0:T(8,128)(2,1)S(1)} %sum.6), channel_id=1, source_target_pairs={{0,2},{1,3},{2,4},{3,5},{4,6},{5,7},{6,0},{7,1},{8,10},{9,11},{10,... | collective-permute-start | bytes 1056776 | tf_op jit(solution)/shard_map/ppermute | solution.py:46
  141.3 12.8 %collective-permute-start.22 = (bf16[1376,128]{1,0:T(8,128)(2,1)S(1)}, bf16[1376,128]{1,0:T(8,128)(2,1)S(1)}, u32[]{:S(2)}, u32[]{:S(2)}) collective-permute-start(bf16[1376,128]{1,0:T(8,128)(2,1)S(1)} %sum.7), channel_id=1, source_target_pairs={{0,6},{1,7},{2,0},{3,1},{4,2},{5,3},{6,4},{7,5},{8,14},{9,15},{10,... | collective-permute-start | bytes 1056776 | tf_op jit(solution)/shard_map/ppermute | solution.py:46
